TPU v7x, 32 devices: a whole 2x2x4 slice. The times are simulated.
32 devices in a mesh: exp: 8 (over z, y), dp: 4 (over x, core).
Axes of the slice: x: 2, y: 2, z: 4, core: 2. Of those that a mesh axis runs over, the one named last changes fastest.
Arguments:
- tokens: bfloat16 [4096, 768], P(('exp', 'dp')), may hold values from -6 to 6
- norm_gain: float32 [768], replicated, may hold values from 0.5 to 1.5
- w_query: bfloat16 [768, 768], replicated, may hold values from -0.21875 to 0.21875
- w_key: bfloat16 [768, 768], replicated, may hold values from -0.21875 to 0.21875
- w_value: bfloat16 [768, 768], replicated, may hold values from -0.21875 to 0.21875
- w_output: bfloat16 [768, 768], replicated, may hold values from -1.75 to 1.75
- rel_bias: float32 [32, 12], replicated, may hold values from -3 to 3
- ffn_gain: float32 [768], replicated, may hold values from 0.5 to 1.5
- w_router: bfloat16 [768, 8], replicated, may hold values from -0.375 to 0.375
- w_in: bfloat16 [8, 768, 3072], P('exp', None, 'dp'), may hold values from -0.21875 to 0.21875
- w_out: bfloat16 [8, 3072, 768], P('exp', 'dp'), may hold values from -2 to 2
- routes: int32 [4096, 1], P(('exp', 'dp')), may hold values from 0 to 7; in each aligned block of 128 rows (0 to 127, 128 to 255, ...) at most 40 rows name the same one
- lengths: int32 [32], P(('exp', 'dp')), may hold values from 32 to 128, as said below
- cotangent: bfloat16 [4096, 768], P(('exp', 'dp')), may hold values from -6 to 6
Outputs:
- output: bfloat16 [4096, 768], P(('exp', 'dp'))
- grad_input: bfloat16 [4096, 768], P(('exp', 'dp'))
- grad_norm_gain: float32 [768], replicated
- grad_query: float32 [768, 768], replicated
- grad_key: float32 [768, 768], replicated
- grad_value: float32 [768, 768], replicated
- grad_output_proj: float32 [768, 768], replicated
- grad_rel_bias: float32 [32, 12], replicated
- grad_ffn_gain: float32 [768], replicated
- grad_router: float32 [768, 8], replicated
- grad_w_in: float32 [8, 768, 3072], P('exp', None, 'dp')
- grad_w_out: float32 [8, 3072, 768], P('exp', 'dp')
Inputs may be any that keep to these rules, and one draw needn't show every extreme that they name: `lengths`: each sequence's live tokens come first; some sequence has all 128 live in every draw. `routes`: among the 128 tokens of one sequence no expert is named more than 2 * 20 times, and in every draw some expert is named exactly 2 * 20 times in some sequence.
All inputs are finite; a program needn't handle non-finite values.
Results may differ from a plain program's by a relative error of at most 0.014.
The roundings to bfloat16 on the way count: a program that leaves them out, or rounds other values in their place, can miss the bound.
Values may be sent and summed in bfloat16 or wider, within the bound.
No kernel may reach another device: no remote copies, remote signals or barrier semaphores. Data moves between devices by JAX's collectives and lax.ppermute only.
A program may use at most 128 MiB of HBM per device.

v0:
```python
import jax
import jax.numpy as jnp
from jax import lax
from jax.sharding import PartitionSpec as P

HEADS = 12
HEAD_DIM = 64
BUCKETS = 32


norm_eps = 1e-06
score_scale = 0.125
masked_score = -1e30
far_limits = (11, 16, 22, 32, 45, 64, 90)


def bucket_index(length):
    places = jnp.arange(length, dtype=jnp.int32)
    offset = places[None, :] - places[:, None]
    distance = jnp.abs(offset)
    far_bucket = jnp.full(distance.shape, 8, jnp.int32)
    for limit_value in far_limits:
        far_bucket = far_bucket + (distance >= limit_value).astype(jnp.int32)
    near_bucket = jnp.where(distance < 8, distance, far_bucket)
    return near_bucket + 16 * (offset > 0).astype(jnp.int32)


def dot_last(left_side, right_side):
    return lax.dot_general(
        left_side, right_side, (((1,), (1,)), ((), ())), preferred_element_type=jnp.float32
    )


def dot_first(left_side, right_side):
    return lax.dot_general(
        left_side, right_side, (((0,), (0,)), ((), ())), preferred_element_type=jnp.float32
    )


def gelu_grad(inner_sum, upstream):
    _, pullback = jax.vjp(jax.nn.gelu, inner_sum)
    return pullback(upstream)[0]


def norm_backward(values, factor, gain, grad_normed):
    scaled = gain * grad_normed
    grad_gain = jnp.sum(grad_normed * values * factor, axis=0)
    grad_values = factor * scaled - values * factor * factor * factor * jnp.mean(
        scaled * values, axis=-1, keepdims=True
    )
    return (grad_values, grad_gain)


def per_device(
    tokens,
    norm_gain,
    w_query,
    w_key,
    w_value,
    w_output,
    rel_bias,
    ffn_gain,
    w_router,
    w_in,
    w_out,
    routes,
    lengths,
    cotangent,
):
    length = tokens.shape[0]
    model_width = tokens.shape[1]
    exp_count = lax.axis_size("exp")
    capacity = max(2, (5 * length + 4 * exp_count - 1) // (4 * exp_count))
    inputs = tokens.astype(jnp.float32)
    live_mask = jnp.arange(length, dtype=jnp.int32) < lengths[0]
    factor_one = lax.rsqrt(jnp.mean(inputs * inputs, axis=-1, keepdims=True) + norm_eps)
    normed = (inputs * factor_one * norm_gain).astype(jnp.bfloat16)
    queries = jnp.dot(normed, w_query, preferred_element_type=jnp.float32).astype(jnp.bfloat16)
    keys_all = jnp.dot(normed, w_key, preferred_element_type=jnp.float32).astype(jnp.bfloat16)
    values_all = jnp.dot(normed, w_value, preferred_element_type=jnp.float32).astype(jnp.bfloat16)
    query_heads = queries.reshape(length, HEADS, HEAD_DIM)
    key_heads = keys_all.reshape(length, HEADS, HEAD_DIM)
    value_heads = values_all.reshape(length, HEADS, HEAD_DIM)
    buckets = bucket_index(length)
    bias_field = jnp.take(rel_bias, buckets, axis=0).transpose(2, 0, 1)

    def scores_of():
        scores = (
            jnp.einsum("qhe,khe->hqk", query_heads, key_heads, preferred_element_type=jnp.float32)
            * score_scale
            + bias_field
        )
        return jnp.where(live_mask[None, None, :], scores, masked_score)

    scores = scores_of()
    log_total = jax.nn.logsumexp(scores, axis=-1, keepdims=True)
    attn_weights = jnp.exp(scores - log_total).astype(jnp.bfloat16)
    attended = jnp.einsum(
        "hqk,khe->qhe", attn_weights, value_heads, preferred_element_type=jnp.float32
    )
    attended = attended.reshape(length, model_width).astype(jnp.bfloat16)
    hidden = inputs + jnp.dot(attended, w_output, preferred_element_type=jnp.float32)
    factor_two = lax.rsqrt(jnp.mean(hidden * hidden, axis=-1, keepdims=True) + norm_eps)
    normed_two = (hidden * factor_two * ffn_gain).astype(jnp.bfloat16)
    logits = jnp.dot(normed_two, w_router, preferred_element_type=jnp.float32)
    router_probs = jax.nn.softmax(logits, axis=-1)
    experts = w_router.shape[1]
    choose = routes[:, 0][:, None] == jnp.arange(experts, dtype=jnp.int32)
    choose_int = choose.astype(jnp.int32)
    running = jnp.cumsum(choose_int * live_mask[:, None].astype(jnp.int32), axis=0)
    slot_index = jnp.sum(running * choose_int, axis=1) - 1
    kept_mask = live_mask & (slot_index < capacity)
    dispatch = (
        choose[:, :, None]
        & (slot_index[:, None, None] == jnp.arange(capacity, dtype=jnp.int32))
        & kept_mask[:, None, None]
    )
    dispatch_low = dispatch.astype(jnp.bfloat16)
    gate_value = jnp.sum(jnp.where(choose, router_probs, 0.0), axis=1)
    packed = jnp.einsum(
        "tec,td->ecd", dispatch_low, normed_two, preferred_element_type=jnp.float32
    ).astype(jnp.bfloat16)
    received = lax.all_to_all(packed, "exp", split_axis=0, concat_axis=0, tiled=True)
    expert_rows = received.reshape(-1, model_width)
    whole_in, whole_out = (
        lax.all_gather(w_in, "dp", axis=2, tiled=True),
        lax.all_gather(w_out, "dp", axis=1, tiled=True),
    )
    inner_sum = jnp.dot(expert_rows, whole_in[0], preferred_element_type=jnp.float32)
    active = jax.nn.gelu(inner_sum).astype(jnp.bfloat16)
    result = jnp.dot(active, whole_out[0], preferred_element_type=jnp.float32).astype(jnp.bfloat16)
    returned_slots = lax.all_to_all(
        result.reshape(exp_count, capacity, model_width),
        "exp",
        split_axis=0,
        concat_axis=0,
        tiled=True,
    )
    returned = jnp.einsum(
        "tec,ecd->td", dispatch_low, returned_slots, preferred_element_type=jnp.float32
    )
    output = (hidden + gate_value[:, None] * returned).astype(jnp.bfloat16)
    grad_top = cotangent.astype(jnp.float32)
    scaled_grad = (gate_value[:, None] * grad_top).astype(jnp.bfloat16)
    grad_packed = jnp.einsum(
        "tec,td->ecd", dispatch_low, scaled_grad, preferred_element_type=jnp.float32
    )
    grad_slots = lax.all_to_all(
        grad_packed.astype(jnp.bfloat16), "exp", split_axis=0, concat_axis=0, tiled=True
    ).reshape(-1, model_width)
    d_active = dot_last(grad_slots, whole_out[0])
    grad_out_full = dot_first(active, grad_slots)
    d_inner = gelu_grad(inner_sum, d_active).astype(jnp.bfloat16)
    grad_in_full = dot_first(expert_rows, d_inner)
    d_rows = dot_last(d_inner, whole_in[0])
    grad_in, grad_out = (
        lax.psum_scatter(
            grad_in_full[None].astype(jnp.bfloat16), "dp", scatter_dimension=2, tiled=True
        ).astype(jnp.float32),
        lax.psum_scatter(
            grad_out_full[None].astype(jnp.bfloat16), "dp", scatter_dimension=1, tiled=True
        ).astype(jnp.float32),
    )
    grad_back = lax.all_to_all(
        d_rows.astype(jnp.bfloat16).reshape(exp_count, capacity, model_width),
        "exp",
        split_axis=0,
        concat_axis=0,
        tiled=True,
    )
    d_normed_two = jnp.einsum(
        "tec,ecd->td", dispatch_low, grad_back, preferred_element_type=jnp.float32
    )
    d_gate = jnp.sum(grad_top * returned, axis=1)
    d_router_probs = jnp.where(choose, d_gate[:, None], 0.0)
    d_logits = router_probs * (
        d_router_probs - jnp.sum(router_probs * d_router_probs, axis=1, keepdims=True)
    )
    d_logits = d_logits.astype(jnp.bfloat16)
    grad_router = dot_first(normed_two, d_logits)
    d_normed_two = d_normed_two + dot_last(d_logits, w_router)
    d_from_norm, grad_ffn = norm_backward(hidden, factor_two, ffn_gain, d_normed_two)
    d_hidden = grad_top + d_from_norm
    d_mixed = d_hidden.astype(jnp.bfloat16)
    grad_output = dot_first(attended, d_mixed)
    d_attended = dot_last(d_mixed, w_output).astype(jnp.bfloat16).reshape(length, HEADS, HEAD_DIM)
    probs_again = jnp.exp(scores_of() - log_total)
    weights_again = probs_again.astype(jnp.bfloat16)
    d_probs_attn = jnp.einsum(
        "qhe,khe->hqk", d_attended, value_heads, preferred_element_type=jnp.float32
    )
    grad_values = jnp.einsum(
        "hqk,qhe->khe", weights_again, d_attended, preferred_element_type=jnp.float32
    )
    grad_values = grad_values.astype(jnp.bfloat16).reshape(length, model_width)
    d_scores = probs_again * (
        d_probs_attn - jnp.sum(probs_again * d_probs_attn, axis=-1, keepdims=True)
    )
    d_scores = d_scores.astype(jnp.bfloat16)
    grad_queries = (
        jnp.einsum("hqk,khe->qhe", d_scores, key_heads, preferred_element_type=jnp.float32)
        * score_scale
    )
    grad_queries = grad_queries.astype(jnp.bfloat16).reshape(length, model_width)
    grad_keys = (
        jnp.einsum("hqk,qhe->khe", d_scores, query_heads, preferred_element_type=jnp.float32)
        * score_scale
    )
    grad_keys = grad_keys.astype(jnp.bfloat16).reshape(length, model_width)
    bucket_onehot = (buckets[:, :, None] == jnp.arange(BUCKETS, dtype=jnp.int32)).astype(
        jnp.bfloat16
    )
    grad_bias = jnp.einsum(
        "hqk,qkb->bh", d_scores, bucket_onehot, preferred_element_type=jnp.float32
    )
    grad_query = dot_first(normed, grad_queries)
    grad_key = dot_first(normed, grad_keys)
    grad_value = dot_first(normed, grad_values)
    d_normed = (
        dot_last(grad_queries, w_query)
        + dot_last(grad_keys, w_key)
        + dot_last(grad_values, w_value)
    )
    d_from_first, grad_norm = norm_backward(inputs, factor_one, norm_gain, d_normed)
    grad_input = (d_hidden + d_from_first).astype(jnp.bfloat16)
    grad_norm, grad_query, grad_key, grad_value, grad_output, grad_bias, grad_ffn, grad_router = (
        lax.psum(
            (
                grad_norm,
                grad_query,
                grad_key,
                grad_value,
                grad_output,
                grad_bias,
                grad_ffn,
                grad_router,
            ),
            ("exp", "dp"),
        )
    )
    return (
        output,
        grad_input,
        grad_norm,
        grad_query,
        grad_key,
        grad_value,
        grad_output,
        grad_bias,
        grad_ffn,
        grad_router,
        grad_in,
        grad_out,
    )


def solution(mesh):
    in_specs = (
        P(("exp", "dp"), None),
        P(),
        P(),
        P(),
        P(),
        P(),
        P(),
        P(),
        P(),
        P("exp", None, "dp"),
        P("exp", "dp", None),
        P(("exp", "dp"), None),
        P(("exp", "dp")),
        P(("exp", "dp"), None),
    )
    out_specs = (
        P(("exp", "dp"), None),
        P(("exp", "dp"), None),
        P(),
        P(),
        P(),
        P(),
        P(),
        P(),
        P(),
        P(),
        P("exp", None, "dp"),
        P("exp", "dp", None),
    )
    return jax.shard_map(
        per_device, mesh=mesh, in_specs=in_specs, out_specs=out_specs, check_vma=False
    )
```

profile of v0, /device:TPU:0, one launch (start us, length us, event | category | flops | bytes accessed | tf_op | source)
XLA Modules:
  0.0 449.4 jit_solution(10690610546697744693)
XLA Ops:
  7.3 0.7 all-gather.3.cloned.1.call-update
  8.0 0.7 all-gather.5.cloned.1.call-update
  10.5 1.7 convolution_convert_fusion.7
  13.1 54.5 %gather_fusion = f32[16384,12]{1,0:T(8,128)} fusion(f32[32,12]{1,0:T(8,128)S(1)} %copy.45, s32[16384]{0:T(1024)S(1)} %fusion.60), kind=kCustom, calls=%fused_computation | custom fusion | bytes 1638400 | tf_op jit(solution)/shard_map/jit(_take)/gather | solution.py:85
  67.5 6.6 %copy.47 = f32[128,128,12]{0,1,2:T(8,128)S(1)} copy(f32[128,128,12]{2,1,0:T(8,128)} %bitcast.97) | data formatting | bytes 1572864 | tf_op jit(solution)/shard_map/jit(_take)/gather | solution.py:85
  75.2 0.4 copy-done.2
  75.6 0.4 multiply_reduce_fusion.3
  76.5 17.4 %all_to_all.20 = bf16[8,20,768]{2,1,0:T(8,128)(2,1)S(1)} all-to-all(bf16[8,20,768]{2,1,0:T(8,128)(2,1)S(1)} %convolution_convert_fusion.3), channel_id=1, replica_groups=mesh['exp'=8,'dp'=4] {'exp'}, dimensions={0} | all-to-all | bytes 491520 | tf_op jit(solution)/shard_map/all_to_all | solution.py:123
  94.1 4.6 %fusion.6 = f32[160,3072]{1,0:T(8,128)} fusion(bf16[160,768]{1,0:T(8,128)(2,1)S(1)} %reshape.306, bf16[1,768,3072]{2,1,0:T(8,128)(2,1)} %all-gather.3.cloned.1.call-done), kind=kOutput, calls=%fused_computation.9 | convolution fusion | flops 754974720 | bytes 6930432 | tf_op jit(solution)/shard_map/dot_general | solution.py:129
  98.7 4.3 fusion.25
  103.0 0.8 reshape.307
  103.8 3.4 all-to-all-start.1
  107.5 8.6 %all-to-all-done.1 = bf16[8,20,768]{2,1,0:T(8,128)(2,1)S(1)} async-done(((bf16[8,20,768]{2,1,0:T(8,128)(2,1)}), bf16[8,20,768]{2,1,0:T(8,128)(2,1)S(1)}, u32[]{:S(2)}, u32[]{:S(2)}) %all-to-all-start.1) | async-done | bytes 245792 | tf_op jit(solution)/shard_map/all_to_all | solution.py:132
  116.1 1.0 fusion.43
  117.2 0.6 fusion.91
  118.0 13.1 %all_to_all.21 = bf16[8,20,768]{2,1,0:T(8,128)(2,1)S(1)} all-to-all(bf16[8,20,768]{2,1,0:T(8,128)(2,1)S(1)} %convolution_convert_fusion.2), channel_id=1, replica_groups=mesh['exp'=8,'dp'=4] {'exp'}, dimensions={0} | all-to-all | bytes 491520 | tf_op jit(solution)/shard_map/all_to_all | solution.py:148
  131.2 5.7 %fusion.9 = bf16[1,3072,768]{2,1,0:T(8,128)(2,1)} fusion(bf16[160,768]{1,0:T(8,128)(2,1)S(1)} %reshape.308, f32[160,3072]{1,0:T(8,128)} %fusion.6), kind=kOutput, calls=%fused_computation.12 | convolution fusion | flops 761757696 | bytes 6930432 | tf_op jit(solution)/shard_map/dot_general | solution.py:35
  137.2 5.2 %fusion.17 = bf16[160,3072]{1,0:T(8,128)(2,1)S(1)} fusion(f32[160,3072]{1,0:T(8,128)} %fusion.6, bf16[160,768]{1,0:T(8,128)(2,1)} %copy-done.28, bf16[1,3072,768]{2,1,0:T(8,128)(2,1)} %all-gather.5.cloned.1.call-done), kind=kOutput, calls=%fused_computation.23 | convolution fusion | flops 764805120 | bytes 7913472 | tf_op jit(solution)/shard_map/dot_general | solution.py:29
  142.4 3.6 fusion.8
  146.2 4.9 %fusion.22 = bf16[160,768]{1,0:T(8,128)(2,1)} fusion(bf16[160,3072]{1,0:T(8,128)(2,1)S(1)} %fusion.17, bf16[1,768,3072]{2,1,0:T(8,128)(2,1)} %all-gather.3.cloned.1.call-done), kind=kOutput, calls=%fused_computation.38 | convolution fusion | flops 755097600 | bytes 5947392 | tf_op jit(solution)/shard_map/dot_general | solution.py:29
  151.1 1.0 reshape.309
  152.1 13.6 %all_to_all.22 = bf16[8,20,768]{2,1,0:T(8,128)(2,1)S(1)} all-to-all(bf16[8,20,768]{2,1,0:T(8,128)(2,1)S(1)} %reshape.309), channel_id=1, replica_groups=mesh['exp'=8,'dp'=4] {'exp'}, dimensions={0} | all-to-all | bytes 491520 | tf_op jit(solution)/shard_map/all_to_all | solution.py:164
  165.8 1.1 convolution_bitcast_fusion
  166.8 1.7 multiply_reduce_fusion.1
  168.6 0.8 convert_add_fusion
  169.4 0.5 convolution_convert_fusion.5
  171.8 0.4 convolution_convert_fusion.4
  172.2 2.0 fusion.103
  174.2 2.0 fusion.105
  176.2 2.0 fusion.107
  178.1 1.9 fusion.54
  180.1 0.8 copy-done.8
  181.1 0.6 fusion.30
  181.6 0.5 fusion.114
  182.2 0.5 convolution_add_fusion.1
  182.8 0.7 fusion.47
  183.4 39.7 %all-reduce = (f32[768]{0:T(1024)}, f32[32,12]{0,1:T(8,128)}, f32[768]{0:T(1024)}, f32[768,8]{0,1:T(8,128)}) all-reduce(f32[768]{0:T(1024)S(1)} %get-tuple-element.14, f32[32,12]{0,1:T(8,128)S(1)} %fusion.30, f32[768]{0:T(1024)S(1)} %copy-done.36, f32[768,8]{0,1:T(8,128)S(1)} %fusion.97), channel_id=1, replica_groups=mesh['exp'=8,'dp'=4] {'exp','dp'}, use_global_device_ids=true, to_apply=%region_15.16 | all-reduce | flops 8064 | bytes 64512 | tf_op jit(solution)/shard_map/psum | solution.py:227
  223.1 0.9 fusion.41
  224.0 2.8 convert_element_type.304
  226.8 7.6 %reduce-scatter.3.cloned.1.call-done = bf16[1,768,768]{2,1,0:T(8,128)(2,1)} async-done(((bf16[1,768,3072]{2,1,0:T(8,128)(2,1)}), bf16[1,768,768]{2,1,0:T(8,128)(2,1)}) %reduce-scatter.3.cloned.1.call-update) | async-done | bytes 1179664 | tf_op jit(solution)/shard_map/reduce_scatter | solution.py:157
  234.4 2.8 convert_element_type.301
  237.2 195.8 %all-reduce.4.cloned.1.call-done = (f32[768,768]{1,0:T(8,128)}, f32[768,768]{1,0:T(8,128)}, f32[768,768]{1,0:T(8,128)}, f32[768,768]{1,0:T(8,128)}) async-done(((f32[768,768]{1,0:T(8,128)}, f32[768,768]{1,0:T(8,128)}, f32[768,768]{1,0:T(8,128)}, f32[768,768]{1,0:T(8,128)}), (f32[768,768]{1,0:T(8,128)}, f32[768,768]{1,0:T(8,128)}, f32[768,768]{1,0:T(8,128)}, ...) | async-done | bytes 9437200 | tf_op jit(solution)/shard_map/psum | solution.py:227
  433.1 3.4 copy.69
  436.4 1.4 copy.70
  437.9 1.1 copy-done.12
  439.0 1.4 copy.71
  440.4 1.1 copy-done.11
  441.5 1.4 copy.72
  (159 shorter events, 6.4 us)
Async XLA Ops:
  7.2 5.3 %copy-start = (bf16[768,768]{1,0:T(8,128)(2,1)S(1)}, bf16[768,768]{1,0:T(8,128)(2,1)}, u32[]{:S(2)}) copy-start(bf16[768,768]{1,0:T(8,128)(2,1)} %param.18) | copy-start | bytes 3538948
  7.2 2.2 copy-start.49
  7.2 2.3 copy-start.40
  7.2 2.6 copy-start.1
  7.2 2.7 copy-start.27
  7.2 2.7 copy-start.4
  7.2 86.8 %all-gather.3.cloned.1.call-start = ((), (), s32[]{:S(2)}) async-start(), calls=%async_computation.6 | async-start | bytes 5898240 | tf_op jit(solution)/shard_map/all_gather | solution.py:126
  8.0 90.7 %all-gather.5.cloned.1.call-start = ((), (), s32[]{:S(2)}) async-start(), calls=%async_computation.7 | async-start | bytes 5898240 | tf_op jit(solution)/shard_map/all_gather | solution.py:127
  10.0 2.4 copy-start.33
  10.5 63.8 %copy-start.16 = (bf16[128,768]{0,1:T(8,128)(2,1)}, bf16[128,768]{0,1:T(8,128)(2,1)S(1)}, u32[]{:S(2)}) copy-start(bf16[128,768]{0,1:T(8,128)(2,1)S(1)} %copy.43) | copy-start | bytes 589828
  12.4 61.9 %copy-start.18 = (bf16[128,768]{0,1:T(8,128)(2,1)}, bf16[128,768]{0,1:T(8,128)(2,1)S(1)}, u32[]{:S(2)}) copy-start(bf16[128,768]{0,1:T(8,128)(2,1)S(1)} %copy.44) | copy-start | bytes 589828
  13.0 62.0 %copy-start.20 = (bf16[128,768]{0,1:T(8,128)(2,1)}, bf16[128,768]{0,1:T(8,128)(2,1)S(1)}, u32[]{:S(2)}) copy-start(bf16[128,768]{0,1:T(8,128)(2,1)S(1)} %copy.42) | copy-start | bytes 589828
  74.3 2.0 copy-start.43
  74.8 1.4 copy-start.31
  76.1 18.0 %copy-start.51 = (f32[128]{0:T(128)}, f32[128]{0:T(128)S(1)}, u32[]{:S(2)}) copy-start(f32[128]{0:T(128)S(1)} %add_rsqrt_fusion) | copy-start | bytes 1540
  76.1 41.6 %copy-start.37 = (pred[128,8]{0,1:T(8,128)(4,1)}, pred[128,8]{0,1:T(8,128)(4,1)S(1)}, u32[]{:S(2)}) copy-start(pred[128,8]{0,1:T(8,128)(4,1)S(1)} %iota_compare_fusion.5) | copy-start | bytes 3076
  76.1 41.6 %copy-start.29 = (pred[128,20]{0,1:T(8,128)(4,1)}, pred[128,20]{0,1:T(8,128)(4,1)S(1)}, u32[]{:S(2)}) copy-start(pred[128,20]{0,1:T(8,128)(4,1)S(1)} %iota_compare_fusion.4) | copy-start | bytes 7684
  76.3 31.0 %copy-start.7 = (bf16[128,768]{1,0:T(8,128)(2,1)}, bf16[128,768]{1,0:T(8,128)(2,1)S(1)}, u32[]{:S(2)}) copy-start(bf16[128,768]{1,0:T(8,128)(2,1)S(1)} %multiply_convert_fusion.2) | copy-start | bytes 589828
  94.0 4.7 %copy-start.9 = (bf16[160,768]{1,0:T(8,128)(2,1)}, bf16[160,768]{1,0:T(8,128)(2,1)S(1)}, u32[]{:S(2)}) copy-start(bf16[160,768]{1,0:T(8,128)(2,1)S(1)} %reshape.306) | copy-start | bytes 737284
  98.7 8.6 %copy-start.30 = (bf16[768,8]{0,1:T(8,128)(2,1)S(1)}, bf16[768,8]{0,1:T(8,128)(2,1)}, u32[]{:S(2)}) copy-start(bf16[768,8]{0,1:T(8,128)(2,1)} %param.22) | copy-start | bytes 36868
  98.7 17.5 %copy-start.24 = (bf16[128,768]{1,0:T(8,128)(2,1)S(1)}, bf16[128,768]{1,0:T(8,128)(2,1)}, u32[]{:S(2)}) copy-start(bf16[128,768]{1,0:T(8,128)(2,1)} %param.27) | copy-start | bytes 589828
  98.7 17.5 %copy-start.44 = (pred[128]{0:T(512)(128)(4,1)S(1)}, pred[128]{0:T(512)(128)(4,1)}, u32[]{:S(2)}) copy-start(pred[128]{0:T(512)(128)(4,1)} %copy-done.43) | copy-start | bytes 388
  103.0 14.2 %copy-start.41 = (s32[128,1]{0,1:T(1,128)S(1)}, s32[128,1]{0,1:T(1,128)}, u32[]{:S(2)}) copy-start(s32[128,1]{0,1:T(1,128)} %param.25) | copy-start | bytes 1540
  103.8 12.4 %all-to-all-start.1 = ((bf16[8,20,768]{2,1,0:T(8,128)(2,1)}), bf16[8,20,768]{2,1,0:T(8,128)(2,1)S(1)}, u32[]{:S(2)}, u32[]{:S(2)}) async-start(bf16[8,20,768]{2,1,0:T(8,128)(2,1)} %reshape.307), calls=%async_computation.1 | async-start | bytes 589824 | tf_op jit(solution)/shard_map/all_to_all | solution.py:132
  107.2 116.8 %reduce-scatter.5.cloned.1.call-start = ((), (), s32[]{:S(2)}) async-start(), calls=%async_computation.9 | async-start | bytes 5898240 | tf_op jit(solution)/shard_map/reduce_scatter | solution.py:160
  107.4 29.5 %copy-start.38 = (f32[128]{0:T(128)}, f32[128]{0:T(128)S(1)}, u32[]{:S(2)}) copy-start(f32[128]{0:T(128)S(1)} %get-tuple-element.34) | copy-start | bytes 1540
  107.5 29.4 %copy-start.47 = (f32[128]{0:T(128)}, f32[128]{0:T(128)S(1)}, u32[]{:S(2)}) copy-start(f32[128]{0:T(128)S(1)} %fusion.96) | copy-start | bytes 1540
  117.2 19.8 %copy-start.45 = (f32[128]{0:T(128)}, f32[128]{0:T(128)S(1)}, u32[]{:S(2)}) copy-start(f32[128]{0:T(128)S(1)} %get-tuple-element.32) | copy-start | bytes 1540
  117.7 19.2 %copy-start.53 = (f32[128]{0:T(128)}, f32[128]{0:T(128)S(1)}, u32[]{:S(2)}) copy-start(f32[128]{0:T(128)S(1)} %get-tuple-element.17) | copy-start | bytes 1540
  131.2 5.7 %copy-start.28 = (bf16[160,768]{1,0:T(8,128)(2,1)}, bf16[160,768]{1,0:T(8,128)(2,1)S(1)}, u32[]{:S(2)}) copy-start(bf16[160,768]{1,0:T(8,128)(2,1)S(1)} %reshape.308) | copy-start | bytes 737284
  137.0 97.4 %reduce-scatter.3.cloned.1.call-start = ((), (), s32[]{:S(2)}) async-start(), calls=%async_computation.8 | async-start | bytes 5898240 | tf_op jit(solution)/shard_map/reduce_scatter | solution.py:157
  137.2 5.2 %copy-start.10 = (bf16[160,768]{1,0:T(8,128)(2,1)S(1)}, bf16[160,768]{1,0:T(8,128)(2,1)}, u32[]{:S(2)}) copy-start(bf16[160,768]{1,0:T(8,128)(2,1)} %copy-done.9) | copy-start | bytes 737284
  146.1 287.0 %all-reduce.4.cloned.1.call-start = ((), (), s32[]{:S(2)}) async-start(), calls=%async_computation.10 | async-start | bytes 18874368 | tf_op jit(solution)/shard_map/psum | solution.py:227
  151.1 17.5 %copy-start.25 = (bf16[128,768]{1,0:T(8,128)(2,1)S(1)}, bf16[128,768]{1,0:T(8,128)(2,1)}, u32[]{:S(2)}) copy-start(bf16[128,768]{1,0:T(8,128)(2,1)} %param.27) | copy-start | bytes 589828
  151.1 17.5 %copy-start.32 = (f32[768]{0:T(1024)S(1)}, f32[768]{0:T(1024)}, u32[]{:S(2)}) copy-start(f32[768]{0:T(1024)} %param.21) | copy-start | bytes 9220
  151.1 17.5 %copy-start.52 = (f32[128]{0:T(128)S(1)}, f32[128]{0:T(128)}, u32[]{:S(2)}) copy-start(f32[128]{0:T(128)} %copy-done.51) | copy-start | bytes 1540
  151.1 17.5 %copy-start.54 = (f32[128]{0:T(128)S(1)}, f32[128]{0:T(128)}, u32[]{:S(2)}) copy-start(f32[128]{0:T(128)} %copy-done.53) | copy-start | bytes 1540
  152.1 16.5 %copy-start.26 = (f32[128,768]{1,0:T(8,128)S(1)}, f32[128,768]{1,0:T(8,128)}, u32[]{:S(2)}) copy-start(f32[128,768]{1,0:T(8,128)} %get-tuple-element.33) | copy-start | bytes 1179652
  165.8 3.7 copy-start.3
  168.6 1.6 copy-start.21
  170.2 1.4 copy-start.19
  170.8 1.4 copy-start.34
  176.2 2.0 copy-start.15
  180.0 1.6 copy-start.5
  180.1 2.1 copy-start.6
  433.1 3.4 copy-start.13
  436.4 2.5 copy-start.12
  439.0 2.5 copy-start.11
  (13 other events, 13.1 us)
Sparse Core Ops, SparseCore 0:
  9.6 40.1 all-gather.2
  51.4 37.4 all-gather.4
  137.1 46.1 reduce-scatter.4
  185.8 48.5 reduce-scatter.2
  241.0 191.9 all-reduce.3
where the time goes:
time: 450 us; the launch traced here: 449 us
  waiting for transfers between devices  214 us (48%)
  blocking collectives  83.9 us (19%)
  local copies, waits for them, and re-layouts  75.6 us (17%)
  matrix products  48.3 us (11%)
  between operations  15.2 us (3%)
  other arithmetic  9.04 us (2%)
    psum x1, waiting for transfers between devices, per_device(): lax.psum((grad_norm, grad_query, grad_key, grad_value, grad_output, grad_...  196 us
    gather x2, local copies, waits for them, and re-layouts, per_device(): bias_field = jnp.take(rel_bias, buckets, axis=0).transpose(2, 0, 1)  61.1 us
    psum x1, blocking collectives, per_device(): lax.psum((grad_norm, grad_query, grad_key, grad_value, grad_output, grad_...  39.7 us
    all_to_all x1, blocking collectives, per_device(): lax.all_to_all(packed, 'exp', split_axis=0, concat_axis=0, tiled=True)  17.4 us
    dot_general x7, matrix products, dot_first(): lax.dot_general(left_side, right_side, (((0,), (0,)), ((), ())), preferre...  17.2 us
    dot_general x7, matrix products, dot_last(): lax.dot_general(left_side, right_side, (((1,), (1,)), ((), ())), preferre...  14.1 us
    all_to_all x1, blocking collectives, per_device(): lax.all_to_all(d_rows.astype(jnp.bfloat16).reshape(exp_count, capacity, m...  13.6 us
    all_to_all x1, blocking collectives, per_device(): lax.all_to_all(grad_packed.astype(jnp.bfloat16), 'exp', split_axis=0, con...  13.1 us
  transfers between devices with their start and end apart: 6, of which 3 were waited for; matrix products, arithmetic and copies ran while one was open for 24% of the time, Pallas kernels for 0%

commit v1 on v0

v1 whole, which is shorter than its diff:
```python
import jax
import jax.numpy as jnp
from jax import lax
from jax.sharding import Mesh
from jax.sharding import PartitionSpec as P

HEADS = 12
HEAD_DIM = 64
BUCKETS = 32
LANES = 128

norm_eps = 1e-06
score_scale = 0.125
masked_score = -1e30
far_limits = (11, 16, 22, 32, 45, 64, 90)

EXPERT_AXES = ("eh", "em", "ey", "dx")
GROUP_AXES = ("em", "ey", "dx", "dc")
TOKEN_AXES = ("eh", "em", "ey", "dx", "dc")


def bucket_of(offset):
    distance = jnp.abs(offset)
    far_bucket = jnp.full(distance.shape, 8, jnp.int32)
    for limit_value in far_limits:
        far_bucket = far_bucket + (distance >= limit_value).astype(jnp.int32)
    near_bucket = jnp.where(distance < 8, distance, far_bucket)
    return near_bucket + 16 * (offset > 0).astype(jnp.int32)


def bucket_index(length):
    places = jnp.arange(length, dtype=jnp.int32)
    return bucket_of(places[None, :] - places[:, None])


def dot_last(left_side, right_side):
    return lax.dot_general(
        left_side, right_side, (((1,), (1,)), ((), ())), preferred_element_type=jnp.float32
    )


def dot_first(left_side, right_side):
    return lax.dot_general(
        left_side, right_side, (((0,), (0,)), ((), ())), preferred_element_type=jnp.float32
    )


def gelu_grad(inner_sum, upstream):
    _, pullback = jax.vjp(jax.nn.gelu, inner_sum)
    return pullback(upstream)[0]


def norm_backward(values, factor, gain, grad_normed):
    scaled = gain * grad_normed
    grad_gain = jnp.sum(grad_normed * values * factor, axis=0)
    grad_values = factor * scaled - values * factor * factor * factor * jnp.mean(
        scaled * values, axis=-1, keepdims=True
    )
    return (grad_values, grad_gain)


def swap(array, axis):
    return lax.ppermute(array, axis, perm=[(0, 1), (1, 0)])


def in_order(own, other, axis):
    first = lax.axis_index(axis) == 0
    return jnp.stack([jnp.where(first, own, other), jnp.where(first, other, own)])


def gather_pair(array, axis):
    return in_order(array, swap(array, axis), axis)


def split_two(values):
    high = values.astype(jnp.bfloat16)
    low = (values - high.astype(jnp.float32)).astype(jnp.bfloat16)
    return high, low


def per_device(
    tokens,
    norm_gain,
    w_query,
    w_key,
    w_value,
    w_output,
    rel_bias,
    ffn_gain,
    w_router,
    w_in,
    w_out,
    routes,
    lengths,
    cotangent,
):
    low_type = jnp.bfloat16
    length, model_width = tokens.shape
    experts = w_router.shape[1]
    eh_count = lax.axis_size("eh")
    group = lax.axis_size(GROUP_AXES)
    capacity = max(2, (5 * length + 4 * experts - 1) // (4 * experts))

    w_in_own, w_out_own = w_in[0], w_out[0]
    w_in_other, w_out_other = swap(w_in_own, "dc"), swap(w_out_own, "dc")
    tokens_all = lax.all_gather(tokens, GROUP_AXES, axis=0, tiled=True)

    inputs = tokens.astype(jnp.float32)
    live_mask = jnp.arange(length, dtype=jnp.int32) < lengths[0]
    factor_one = lax.rsqrt(jnp.mean(inputs * inputs, axis=-1, keepdims=True) + norm_eps)
    normed = (inputs * factor_one * norm_gain).astype(low_type)
    queries = jnp.dot(normed, w_query, preferred_element_type=jnp.float32).astype(low_type)
    keys_all = jnp.dot(normed, w_key, preferred_element_type=jnp.float32).astype(low_type)
    values_all = jnp.dot(normed, w_value, preferred_element_type=jnp.float32).astype(low_type)
    query_heads = queries.reshape(length, HEADS, HEAD_DIM)
    key_heads = keys_all.reshape(length, HEADS, HEAD_DIM)
    value_heads = values_all.reshape(length, HEADS, HEAD_DIM)
    buckets = bucket_index(length)
    bucket_onehot = buckets[:, :, None] == jnp.arange(BUCKETS, dtype=jnp.int32)
    bias_field = jnp.einsum(
        "qkb,bh->hqk",
        bucket_onehot.astype(jnp.float32),
        rel_bias,
        precision=lax.Precision.HIGHEST,
        preferred_element_type=jnp.float32,
    )
    scores = (
        jnp.einsum("qhe,khe->hqk", query_heads, key_heads, preferred_element_type=jnp.float32)
        * score_scale
        + bias_field
    )
    scores = jnp.where(live_mask[None, None, :], scores, masked_score)
    probs = jax.nn.softmax(scores, axis=-1)
    attn_weights = probs.astype(low_type)
    attended = jnp.einsum(
        "hqk,khe->qhe", attn_weights, value_heads, preferred_element_type=jnp.float32
    )
    attended = attended.reshape(length, model_width).astype(low_type)
    attended_all = lax.all_gather(attended, GROUP_AXES, axis=0, tiled=True)
    hidden = inputs + jnp.dot(attended, w_output, preferred_element_type=jnp.float32)
    factor_two = lax.rsqrt(jnp.mean(hidden * hidden, axis=-1, keepdims=True) + norm_eps)
    normed_two = (hidden * factor_two * ffn_gain).astype(low_type)
    logits = jnp.dot(normed_two, w_router, preferred_element_type=jnp.float32)
    router_probs = jax.nn.softmax(logits, axis=-1)
    choose = routes[:, 0][:, None] == jnp.arange(experts, dtype=jnp.int32)
    choose_int = choose.astype(jnp.int32)
    running = jnp.cumsum(choose_int * live_mask[:, None].astype(jnp.int32), axis=0)
    slot_index = jnp.sum(running * choose_int, axis=1) - 1
    kept_mask = live_mask & (slot_index < capacity)
    dispatch = (
        choose[:, :, None]
        & (slot_index[:, None, None] == jnp.arange(capacity, dtype=jnp.int32))
        & kept_mask[:, None, None]
    )
    dispatch_low = dispatch.astype(low_type)
    gate_value = jnp.sum(jnp.where(choose, router_probs, 0.0), axis=1)
    grad_top = cotangent.astype(jnp.float32)
    scaled_grad = (gate_value[:, None] * grad_top).astype(low_type)
    packed = jnp.einsum(
        "tec,td->ecd", dispatch_low, normed_two, preferred_element_type=jnp.float32
    ).astype(low_type)
    grad_packed = jnp.einsum(
        "tec,td->ecd", dispatch_low, scaled_grad, preferred_element_type=jnp.float32
    ).astype(low_type)
    outgoing = jnp.concatenate([packed, grad_packed], axis=1)
    outgoing = jnp.broadcast_to(outgoing[:, None], (experts, 2) + outgoing.shape[1:])
    outgoing = outgoing.reshape((experts * 2,) + outgoing.shape[2:])
    incoming = lax.all_to_all(outgoing, EXPERT_AXES, split_axis=0, concat_axis=0, tiled=True)
    expert_rows = incoming[:, :capacity].reshape(-1, model_width)
    grad_slots = incoming[:, capacity:].reshape(-1, model_width)

    result, d_rows = 0.0, 0.0
    expert_grads = []
    for part_in, part_out in ((w_in_own, w_out_own), (w_in_other, w_out_other)):
        inner_sum = jnp.dot(expert_rows, part_in, preferred_element_type=jnp.float32)
        active = jax.nn.gelu(inner_sum).astype(low_type)
        result = result + jnp.dot(active, part_out, preferred_element_type=jnp.float32)
        d_active = dot_last(grad_slots, part_out)
        d_inner = gelu_grad(inner_sum, d_active).astype(low_type)
        d_rows = d_rows + dot_last(d_inner, part_in)
        expert_grads.append((dot_first(expert_rows, d_inner), dot_first(active, grad_slots)))
    sent_back = jnp.concatenate(
        [
            result.astype(low_type).reshape(-1, capacity, model_width),
            d_rows.astype(low_type).reshape(-1, capacity, model_width),
        ],
        axis=1,
    )
    came_back = lax.all_to_all(sent_back, EXPERT_AXES, split_axis=0, concat_axis=0, tiled=True)
    came_back = came_back.reshape(experts, 2, 2 * capacity, model_width).astype(jnp.float32)
    came_back = (came_back[:, 0] + came_back[:, 1]).astype(low_type)
    (in_own, out_own), (in_other, out_other) = expert_grads
    grad_in = in_own + swap(in_other.astype(low_type), "dc").astype(jnp.float32)
    grad_out = out_own + swap(out_other.astype(low_type), "dc").astype(jnp.float32)

    returned = jnp.einsum(
        "tec,ecd->td", dispatch_low, came_back[:, :capacity], preferred_element_type=jnp.float32
    )
    output = (hidden + gate_value[:, None] * returned).astype(low_type)
    d_normed_two = jnp.einsum(
        "tec,ecd->td", dispatch_low, came_back[:, capacity:], preferred_element_type=jnp.float32
    )
    d_gate = jnp.sum(grad_top * returned, axis=1)
    d_router_probs = jnp.where(choose, d_gate[:, None], 0.0)
    d_logits = router_probs * (
        d_router_probs - jnp.sum(router_probs * d_router_probs, axis=1, keepdims=True)
    )
    d_logits = d_logits.astype(low_type)
    grad_router = dot_first(normed_two, d_logits)
    d_normed_two = d_normed_two + dot_last(d_logits, w_router)
    d_from_norm, grad_ffn = norm_backward(hidden, factor_two, ffn_gain, d_normed_two)
    d_hidden = grad_top + d_from_norm
    d_mixed = d_hidden.astype(low_type)
    d_attended = dot_last(d_mixed, w_output).astype(low_type).reshape(length, HEADS, HEAD_DIM)
    d_probs_attn = jnp.einsum(
        "qhe,khe->hqk", d_attended, value_heads, preferred_element_type=jnp.float32
    )
    grad_values = jnp.einsum(
        "hqk,qhe->khe", attn_weights, d_attended, preferred_element_type=jnp.float32
    )
    grad_values = grad_values.astype(low_type).reshape(length, model_width)
    d_scores = probs * (d_probs_attn - jnp.sum(probs * d_probs_attn, axis=-1, keepdims=True))
    d_scores = d_scores.astype(low_type)
    grad_queries = (
        jnp.einsum("hqk,khe->qhe", d_scores, key_heads, preferred_element_type=jnp.float32)
        * score_scale
    )
    grad_queries = grad_queries.astype(low_type).reshape(length, model_width)
    grad_keys = (
        jnp.einsum("hqk,qhe->khe", d_scores, query_heads, preferred_element_type=jnp.float32)
        * score_scale
    )
    grad_keys = grad_keys.astype(low_type).reshape(length, model_width)
    grad_bias = jnp.einsum(
        "hqk,qkb->bh", d_scores, bucket_onehot.astype(low_type), preferred_element_type=jnp.float32
    )
    d_normed = (
        dot_last(grad_queries, w_query)
        + dot_last(grad_keys, w_key)
        + dot_last(grad_values, w_value)
    )
    d_from_first, grad_norm = norm_backward(inputs, factor_one, norm_gain, d_normed)
    grad_input = (d_hidden + d_from_first).astype(low_type)

    small_sizes = (model_width, model_width, BUCKETS * HEADS, model_width * experts)
    small = jnp.concatenate(
        [grad_norm, grad_ffn, grad_bias.reshape(-1), grad_router.reshape(-1)]
    )
    small_rows = -(-small.shape[0] // (LANES * group))
    small = jnp.pad(small, (0, small_rows * group * LANES - small.shape[0]))
    small_high, small_low = split_two(small.reshape(group, small_rows, LANES))
    block = 4 * model_width // group
    factors = jnp.concatenate([grad_queries, grad_keys, grad_values, d_mixed], axis=1)
    factors = factors.T.reshape(group, block, length)
    late = jnp.concatenate([factors, small_high, small_low], axis=1)
    late = lax.all_to_all(late, GROUP_AXES, split_axis=0, concat_axis=0, tiled=True)
    small = jnp.sum(late[:, block:].astype(jnp.float32), axis=0)
    small = small[:small_rows] + small[small_rows:]

    inputs_all = tokens_all.astype(jnp.float32)
    factor_all = lax.rsqrt(jnp.mean(inputs_all * inputs_all, axis=-1, keepdims=True) + norm_eps)
    normed_all = (inputs_all * factor_all * norm_gain).astype(low_type)
    which = lax.axis_index(GROUP_AXES) // (group // 4)
    left_all = jnp.where(which == 3, attended_all, normed_all)
    late_block = late[:, :block].transpose(1, 0, 2).reshape(block, group * length)
    grad_block = jnp.dot(late_block, left_all, preferred_element_type=jnp.float32)

    part = block // eh_count
    grad_block = grad_block.reshape(eh_count, part, model_width)
    if eh_count == 2:
        place = lax.axis_index("eh")
        mine = lax.dynamic_index_in_dim(grad_block, place, 0, keepdims=False)
        theirs = lax.dynamic_index_in_dim(grad_block, 1 - place, 0, keepdims=False)
        small_high, small_low = split_two(small)
        sent = jnp.concatenate(
            [theirs.astype(low_type).reshape(-1, LANES), small_high, small_low], axis=0
        )
        got = swap(sent, "eh").astype(jnp.float32)
        edge = part * model_width // LANES
        mine = mine.reshape(-1, LANES) + got[:edge]
        small = small + (got[edge : edge + small_rows] + got[edge + small_rows :])
    else:
        mine = lax.psum_scatter(grad_block, "eh", scatter_dimension=0, tiled=True)
        mine = mine.reshape(-1, LANES)
        small = lax.psum(small, "eh")
        edge = mine.shape[0]
    small_high, small_low = split_two(small)
    share = jnp.concatenate([mine.astype(low_type), small_high, small_low], axis=0)
    rows = share.shape[0]

    if eh_count == 2:
        share = gather_pair(share, "eh")
    else:
        share = lax.all_gather(share, "eh", axis=0, tiled=False)
    share = gather_pair(share, "em").reshape(2 * eh_count * rows, LANES)
    half = eh_count * rows
    first, second = share[:half], share[half:]
    first = gather_pair(first, "dx")
    second = gather_pair(second, "ey")
    first = gather_pair(first, "ey")
    second = gather_pair(second, "dx").transpose(1, 0, 2, 3)
    whole = jnp.stack([first, second])
    whole = gather_pair(whole, "dc")
    whole = whole.reshape(2, 2, 2, 2, eh_count, rows, LANES)
    whole = whole.transpose(1, 2, 3, 0, 4, 5, 6).reshape(group, eh_count, rows, LANES)
    grads = whole[:, :, :edge].reshape(4, model_width, model_width).transpose(0, 2, 1)
    grads = grads.astype(jnp.float32)
    small = whole[:, 0, edge:].astype(jnp.float32)
    small = (small[:, :small_rows] + small[:, small_rows:]).reshape(-1)
    pieces, at = [], 0
    for size in small_sizes:
        pieces.append(small[at : at + size])
        at += size
    return (
        output,
        grad_input,
        pieces[0],
        grads[0],
        grads[1],
        grads[2],
        grads[3],
        pieces[2].reshape(BUCKETS, HEADS),
        pieces[1],
        pieces[3].reshape(model_width, experts),
        grad_in[None],
        grad_out[None],
    )


def solution(mesh):
    exp_count, dp_count = mesh.shape["exp"], mesh.shape["dp"]
    fine = Mesh(
        mesh.devices.reshape(exp_count // 4, 2, 2, dp_count // 2, 2),
        TOKEN_AXES,
    )
    exp, dp = ("eh", "em", "ey"), ("dx", "dc")
    in_specs = (
        P(TOKEN_AXES, None),
        P(),
        P(),
        P(),
        P(),
        P(),
        P(),
        P(),
        P(),
        P(exp, None, dp),
        P(exp, dp, None),
        P(TOKEN_AXES, None),
        P(TOKEN_AXES),
        P(TOKEN_AXES, None),
    )
    out_specs = (
        P(TOKEN_AXES, None),
        P(TOKEN_AXES, None),
        P(),
        P(),
        P(),
        P(),
        P(),
        P(),
        P(),
        P(),
        P(exp, None, dp),
        P(exp, dp, None),
    )
    return jax.shard_map(
        per_device, mesh=fine, in_specs=in_specs, out_specs=out_specs, check_vma=False
    )
```

time: 450 us -> 275 us (0.61)
  waiting for transfers between devices: 214 us -> 104 us
  blocking collectives: 83.9 us -> 0 us
  starting transfers between devices: 3.8 us -> 26.4 us
  local copies, waits for them, and re-layouts: 75.6 us -> 59.1 us
  other arithmetic: 9.04 us -> 21.2 us
    psum x1 -> x0, waiting for transfers between devices: 196 us -> none  [per_device(): lax.psum((grad_norm, grad_query, grad_key, grad_value, grad_output, grad_...]
    gather x2 -> x0, local copies, waits for them, and re-layouts: 61.1 us -> none  [per_device(): bias_field = jnp.take(rel_bias, buckets, axis=0).transpose(2, 0, 1)]
    all_to_all x1 -> x3, waiting for transfers between devices: 8.64 us -> 60.2 us  [the longest x1 24.4 us: per_device(): lax.all_to_all(outgoing, EXPERT_AXES, split_axis=0, concat_axis=0, tiled=...]
    all_to_all x3 -> x0, blocking collectives: 44.2 us -> none  [the longest x1 17.4 us: per_device(): lax.all_to_all(packed, 'exp', split_axis=0, concat_axis=0, tiled=True)]
    ppermute x0 -> x12, waiting for transfers between devices: none -> 42.8 us  [swap(): return lax.ppermute(array, axis, perm=[(0, 1), (1, 0)])]
    psum x1 -> x0, blocking collectives: 39.7 us -> none  [per_device(): lax.psum((grad_norm, grad_query, grad_key, grad_value, grad_output, grad_...]
    convert_element_type x2 -> x6, local copies, waits for them, and re-layouts: 0.32 us -> 14.2 us  [the longest x1 11.3 us: per_device(): grads = grads.astype(jnp.float32)]
    all_to_all x1 -> x3, starting transfers between devices: 3.42 us -> 15.8 us  [the longest x1 8.31 us: per_device(): lax.all_to_all(outgoing, EXPERT_AXES, split_axis=0, concat_axis=0, tiled=...]
  transfers between devices with their start and end apart: 6 -> 17, of which waited for: 3 -> 10; matrix products, arithmetic and copies ran while one was open for 24% -> 23% of each run, Pallas kernels for 0% -> 0%
where the time goes in v1:
time: 275 us; the launch traced here: 273 us
  waiting for transfers between devices  104 us (38%)
  local copies, waits for them, and re-layouts  59.1 us (21%)
  matrix products  46.7 us (17%)
  starting transfers between devices  26.4 us (10%)
  other arithmetic  21.2 us (8%)
  between operations  16.1 us (6%)
    ppermute x12, waiting for transfers between devices, swap(): return lax.ppermute(array, axis, perm=[(0, 1), (1, 0)])  42.8 us
    all_to_all x1, waiting for transfers between devices, per_device(): lax.all_to_all(outgoing, EXPERT_AXES, split_axis=0, concat_axis=0, tiled=...  24.4 us
    all_to_all x1, waiting for transfers between devices, per_device(): lax.all_to_all(sent_back, EXPERT_AXES, split_axis=0, concat_axis=0, tiled...  22.2 us
    unnamed x166, local copies, waits for them, and re-layouts  20 us
    all_to_all x1, waiting for transfers between devices, per_device(): lax.all_to_all(late, GROUP_AXES, split_axis=0, concat_axis=0, tiled=True)  13.6 us
    dot_general x9, matrix products, dot_last(): lax.dot_general(left_side, right_side, (((1,), (1,)), ((), ())), preferre...  11.9 us
    convert_element_type x1, local copies, waits for them, and re-layouts, per_device(): grads = grads.astype(jnp.float32)  11.3 us
    dot_general x5, matrix products, dot_first(): lax.dot_general(left_side, right_side, (((0,), (0,)), ((), ())), preferre...  11.3 us
  transfers between devices with their start and end apart: 17, of which 10 were waited for; matrix products, arithmetic and copies ran while one was open for 23% of the time, Pallas kernels for 0%

profile of v1, /device:TPU:0, one launch (start us, length us, event | category | flops | bytes accessed | tf_op | source)
XLA Modules:
  0.0 273.2 jit_solution(15740701142474492709)
XLA Ops:
  8.5 1.8 convolution_convert_fusion.7
  15.9 1.8 convolution_convert_fusion.6
  21.3 8.3 %all-to-all-start = ((bf16[16,40,768]{2,1,0:T(8,128)(2,1)}), bf16[16,40,768]{2,1,0:T(8,128)(2,1)S(1)}, u32[]{:S(2)}, u32[]{:S(2)}) async-start(bf16[16,40,768]{2,1,0:T(8,128)(2,1)} %bitcast.11), calls=%async_computation | async-start | bytes 1966080 | tf_op jit(solution)/shard_map/all_to_all | solution.py:168
  31.0 24.4 %all-to-all-done = bf16[16,40,768]{2,1,0:T(8,128)(2,1)S(1)} async-done(((bf16[16,40,768]{2,1,0:T(8,128)(2,1)}), bf16[16,40,768]{2,1,0:T(8,128)(2,1)S(1)}, u32[]{:S(2)}, u32[]{:S(2)}) %all-to-all-start) | async-done | bytes 983072 | tf_op jit(solution)/shard_map/all_to_all | solution.py:168
  57.8 1.9 reshape.270
  62.8 1.8 fusion.121
  64.7 2.6 fusion.35
  68.0 2.8 %fusion.16 = bf16[320,768]{1,0:T(8,128)(2,1)} fusion(f32[320,768]{1,0:T(8,128)S(1)} %fusion.100, bf16[320,768]{1,0:T(8,128)(2,1)S(1)} %fusion.35, bf16[768,768]{1,0:T(8,128)(2,1)} %collective-permute-done), kind=kOutput, calls=%fused_computation.38 | convolution fusion | flops 377978880 | bytes 3145728 | tf_op jit(solution)/shard_map/dot_general | solution.py:37
  70.8 1.9 reshape.271
  72.7 2.1 fusion.96
  74.8 2.9 %fusion.15 = bf16[320,768]{1,0:T(8,128)(2,1)} fusion(f32[320,768]{1,0:T(8,128)S(1)} %fusion.96, bf16[768,768]{1,0:T(8,128)(2,1)} %collective-permute-done.1, f32[320,768]{1,0:T(8,128)S(1)} %copy-done.41), kind=kOutput, calls=%fused_computation.37 | convolution fusion | flops 380190720 | bytes 3637248 | tf_op jit(solution)/shard_map/dot_general | solution.py:177
  80.0 3.9 %all-to-all-start.1 = ((bf16[16,40,768]{2,1,0:T(8,128)(2,1)}), bf16[16,40,768]{2,1,0:T(8,128)(2,1)S(1)}, u32[]{:S(2)}, u32[]{:S(2)}) async-start(bf16[16,40,768]{2,1,0:T(8,128)(2,1)} %pad_maximum_fusion.2), calls=%async_computation.1 | async-start | bytes 1966080 | tf_op jit(solution)/shard_map/all_to_all | solution.py:189
  85.0 22.2 %all-to-all-done.1 = bf16[16,40,768]{2,1,0:T(8,128)(2,1)S(1)} async-done(((bf16[16,40,768]{2,1,0:T(8,128)(2,1)}), bf16[16,40,768]{2,1,0:T(8,128)(2,1)S(1)}, u32[]{:S(2)}, u32[]{:S(2)}) %all-to-all-start.1) | async-done | bytes 983072 | tf_op jit(solution)/shard_map/all_to_all | solution.py:189
  112.7 1.7 copy.59
  115.0 1.8 multiply_reduce_fusion
  117.7 1.8 convolution_convert_fusion.4
  123.3 2.2 maximum_bitcast_fusion.2
  125.5 2.3 copy.66
  127.8 1.6 fusion.122
  130.0 1.3 fusion.53
  132.3 3.6 %all-to-all-start.2 = ((bf16[16,200,128]{2,1,0:T(8,128)(2,1)}), bf16[16,200,128]{2,1,0:T(8,128)(2,1)S(1)}, u32[]{:S(2)}, u32[]{:S(2)}) async-start(bf16[16,200,128]{2,1,0:T(8,128)(2,1)} %pad_maximum_fusion.3), calls=%async_computation.2 | async-start | bytes 1638400 | tf_op jit(solution)/shard_map/all_to_all | solution.py:256
  136.0 13.6 %all-to-all-done.2 = bf16[16,200,128]{2,1,0:T(8,128)(2,1)S(1)} async-done(((bf16[16,200,128]{2,1,0:T(8,128)(2,1)}), bf16[16,200,128]{2,1,0:T(8,128)(2,1)S(1)}, u32[]{:S(2)}, u32[]{:S(2)}) %all-to-all-start.2) | async-done | bytes 819232 | tf_op jit(solution)/shard_map/all_to_all | solution.py:256
  151.5 2.6 fusion.1
  154.2 3.5 %fusion.6 = f32[2,96,768]{2,1,0:T(8,128)S(1)} fusion(bf16[2,96,2048]{2,1,0:T(8,128)(2,1)S(1)} %copy-done.47, bf16[2048,768]{1,0:T(8,128)(2,1)} %all-gather.3.cloned.1.call-done, bf16[2048,768]{1,0:T(8,128)(2,1)} %all-gather.5.cloned.1.call-done, f32[768]{0:T(1024)S(1)} %copy-done.52, f32[2048]{0:T(1024)S(1)} %add_rsqrt_fusion, pred[]{:T(512)S(6)} %eq.91), kind=kOutput, calls=%fused_computation.10 | convolution fusion | flops 611844096 | bytes 7678977 | tf_op jit(solution)/shard_map/dot_general | solution.py:266
  158.7 8.7 %collective-permute-done.2 = bf16[584,128]{1,0:T(8,128)(2,1)S(1)} collective-permute-done((bf16[584,128]{1,0:T(8,128)(2,1)S(1)}, bf16[584,128]{1,0:T(8,128)(2,1)S(1)}, u32[]{:S(2)}, u32[]{:S(2)}) %collective-permute-start.2) | collective-permute-done | bytes 149536 | tf_op jit(solution)/shard_map/ppermute | solution.py:63
  167.6 7.1 %collective-permute-done.3 = bf16[584,128]{1,0:T(8,128)(2,1)S(1)} collective-permute-done((bf16[584,128]{1,0:T(8,128)(2,1)S(1)}, bf16[584,128]{1,0:T(8,128)(2,1)S(1)}, u32[]{:S(2)}, u32[]{:S(2)}) %collective-permute-start.3) | collective-permute-done | bytes 149536 | tf_op jit(solution)/shard_map/ppermute | solution.py:63
  174.9 8.6 %collective-permute-done.4 = bf16[2,584,128]{2,1,0:T(8,128)(2,1)S(1)} collective-permute-done((bf16[2,584,128]{2,1,0:T(8,128)(2,1)S(1)}, bf16[2,584,128]{2,1,0:T(8,128)(2,1)S(1)}, u32[]{:S(2)}, u32[]{:S(2)}) %collective-permute-start.4) | collective-permute-done | bytes 299040 | tf_op jit(solution)/shard_map/ppermute | solution.py:63
  183.6 2.3 collective-permute-start.7
  185.9 1.9 collective-permute-start.5
  187.8 4.3 %collective-permute-done.7 = bf16[1168,128]{1,0:T(8,128)(2,1)S(1)} collective-permute-done((bf16[1168,128]{1,0:T(8,128)(2,1)S(1)}, bf16[1168,128]{1,0:T(8,128)(2,1)S(1)}, u32[]{:S(2)}, u32[]{:S(2)}) %collective-permute-start.7) | collective-permute-done | bytes 299040 | tf_op jit(solution)/shard_map/ppermute | solution.py:63
  192.2 2.2 collective-permute-start.8
  194.6 1.8 collective-permute-start.6
  196.4 10.4 %collective-permute-done.8 = bf16[2,1168,128]{2,1,0:T(8,128)(2,1)S(1)} collective-permute-done((bf16[2,1168,128]{2,1,0:T(8,128)(2,1)S(1)}, bf16[2,1168,128]{2,1,0:T(8,128)(2,1)S(1)}, u32[]{:S(2)}, u32[]{:S(2)}) %collective-permute-start.8) | collective-permute-done | bytes 598048 | tf_op jit(solution)/shard_map/ppermute | solution.py:63
  207.0 1.3 collective-permute-done.6
  208.5 1.6 pad_maximum_fusion.1
  210.3 1.8 convolution_convert_fusion.1
  212.6 1.9 convolution_convert_fusion
  214.6 2.4 collective-permute-done.10
  216.9 3.6 %add_bitcast_fusion.1 = f32[1,768,768]{2,1,0:T(8,128)} fusion(bf16[768,768]{1,0:T(8,128)(2,1)} %collective-permute-done.10, bf16[320,768]{1,0:T(8,128)(2,1)S(1)} %reshape.268, bf16[320,768]{1,0:T(8,128)(2,1)} %copy-done.29), kind=kOutput, calls=%fused_computation.20 | convolution fusion | flops 378667008 | bytes 4521984 | tf_op jit(solution)/shard_map/dot_general | solution.py:43
  220.6 3.7 %add_bitcast_fusion = f32[1,768,768]{2,1,0:T(8,128)} fusion(bf16[768,768]{1,0:T(8,128)(2,1)} %collective-permute-done.11, bf16[320,768]{1,0:T(8,128)(2,1)S(1)} %copy-done.28, f32[320,768]{1,0:T(8,128)S(1)} %copy-done.14), kind=kOutput, calls=%fused_computation.19 | convolution fusion | flops 380878848 | bytes 5013504 | tf_op jit(solution)/shard_map/dot_general | solution.py:43
  225.6 2.0 broadcast_select_fusion.1
  228.0 4.8 %slice_convert_fusion = f32[16,2,576,128]{3,2,1,0:T(8,128)} fusion(bf16[16,2,584,128]{3,2,1,0:T(8,128)(2,1)S(1)} %bitcast.186), kind=kLoop, calls=%fused_computation.7 | loop fusion | flops 2359296 | bytes 14155776 | tf_op jit(solution)/shard_map/convert_element_type | solution.py:307
  234.5 11.3 %reshape.286 = f32[4,768,768]{2,1,0:T(8,128)} reshape(f32[16,2,576,128]{3,2,1,0:T(8,128)} %slice_convert_fusion) | data formatting | bytes 18874368 | tf_op jit(solution)/shard_map/convert_element_type | solution.py:307
  245.8 6.9 %slice_bitcast_fusion = (f32[768,768]{0,1:T(8,128)S(1)}, f32[768,768]{0,1:T(8,128)}, f32[768,768]{0,1:T(8,128)}, f32[768,768]{0,1:T(8,128)}) fusion(f32[4,768,768]{1,2,0:T(8,128)} %bitcast.184), kind=kLoop, calls=%fused_computation.15 | loop fusion | bytes 18874368 | tf_op jit(solution)/shard_map/squeeze | solution.py:321
  252.7 3.0 %copy.73 = f32[768,768]{1,0:T(8,128)} copy(f32[768,768]{0,1:T(8,128)} %get-tuple-element.38) | data formatting | bytes 4718592
  255.8 3.0 %copy.74 = f32[768,768]{1,0:T(8,128)} copy(f32[768,768]{0,1:T(8,128)} %get-tuple-element.37) | data formatting | bytes 4718592
  258.8 3.0 %copy.75 = f32[768,768]{1,0:T(8,128)} copy(f32[768,768]{0,1:T(8,128)} %get-tuple-element.36) | data formatting | bytes 4718592
  261.8 1.9 copy.76
  (279 shorter events, 42.9 us)
Async XLA Ops:
  7.2 8.2 %copy-start = (bf16[768,768]{1,0:T(8,128)(2,1)S(1)}, bf16[768,768]{1,0:T(8,128)(2,1)}, u32[]{:S(2)}) copy-start(bf16[768,768]{1,0:T(8,128)(2,1)} %param.18) | copy-start | bytes 3538948
  7.2 3.3 %copy-start.2 = (bf16[128,768]{1,0:T(8,128)(2,1)S(1)}, bf16[128,768]{1,0:T(8,128)(2,1)}, u32[]{:S(2)}) copy-start(bf16[128,768]{1,0:T(8,128)(2,1)} %param.14) | copy-start | bytes 589828
  7.2 3.3 %copy-start.52 = (f32[768]{0:T(1024)S(1)}, f32[768]{0:T(1024)}, u32[]{:S(2)}) copy-start(f32[768]{0:T(1024)} %param.15) | copy-start | bytes 9220
  7.2 3.3 %copy-start.8 = (bf16[768,768]{1,0:T(8,128)(2,1)S(1)}, bf16[768,768]{1,0:T(8,128)(2,1)}, u32[]{:S(2)}) copy-start(bf16[768,768]{1,0:T(8,128)(2,1)} %param.16) | copy-start | bytes 3538948
  8.5 6.8 %copy-start.63 = (f32[128]{0:T(128)}, f32[128]{0:T(128)S(1)}, u32[]{:S(2)}) copy-start(f32[128]{0:T(128)S(1)} %add_rsqrt_fusion.2) | copy-start | bytes 1540
  11.7 8.1 %copy-start.65 = (pred[128,8]{0,1:T(8,128)(4,1)}, pred[128,8]{0,1:T(8,128)(4,1)S(1)}, u32[]{:S(2)}) copy-start(pred[128,8]{0,1:T(8,128)(4,1)S(1)} %iota_compare_fusion.7) | copy-start | bytes 3076
  12.2 7.7 %copy-start.73 = (pred[128]{0:T(512)(128)(4,1)}, pred[128]{0:T(512)(128)(4,1)S(1)}, u32[]{:S(2)}) copy-start(pred[128]{0:T(512)(128)(4,1)S(1)} %get-tuple-element.71) | copy-start | bytes 388
  21.3 34.0 %all-to-all-start = ((bf16[16,40,768]{2,1,0:T(8,128)(2,1)}), bf16[16,40,768]{2,1,0:T(8,128)(2,1)S(1)}, u32[]{:S(2)}, u32[]{:S(2)}) async-start(bf16[16,40,768]{2,1,0:T(8,128)(2,1)} %bitcast.11), calls=%async_computation | async-start | bytes 1966080 | tf_op jit(solution)/shard_map/all_to_all | solution.py:168
  29.6 121.8 %all-gather.5.cloned.1.call-start = ((), (), s32[]{:S(2)}) async-start(), calls=%async_computation.4 | async-start | bytes 3342336 | tf_op jit(solution)/shard_map/all_gather | solution.py:106
  30.4 32.4 %collective-permute-start = (bf16[768,768]{1,0:T(8,128)(2,1)}, bf16[768,768]{1,0:T(8,128)(2,1)}, u32[]{:S(2)}, u32[]{:S(2)}) collective-permute-start(bf16[768,768]{1,0:T(8,128)(2,1)} %bitcast.189), channel_id=1, source_target_pairs={{0,1},{1,0},{2,3},{3,2},{4,5},{5,4},{6,7},{7,6},{8,9},{9,8},{10,11... | collective-permute-start | bytes 3538952 | tf_op jit(solution)/shard_map/ppermute | solution.py:63
  30.5 34.2 %collective-permute-start.1 = (bf16[768,768]{1,0:T(8,128)(2,1)}, bf16[768,768]{1,0:T(8,128)(2,1)}, u32[]{:S(2)}, u32[]{:S(2)}) collective-permute-start(bf16[768,768]{1,0:T(8,128)(2,1)} %bitcast.220), channel_id=1, source_target_pairs={{0,1},{1,0},{2,3},{3,2},{4,5},{5,4},{6,7},{7,6},{8,9},{9,8},{10,11... | collective-permute-start | bytes 3538952 | tf_op jit(solution)/shard_map/ppermute | solution.py:63
  56.5 3.2 %copy-start.11 = (bf16[1,768,768]{2,1,0:T(8,128)(2,1)S(1)}, bf16[1,768,768]{2,1,0:T(8,128)(2,1)}, u32[]{:S(2)}) copy-start(bf16[1,768,768]{2,1,0:T(8,128)(2,1)} %param.23) | copy-start | bytes 3538948
  68.0 4.7 %copy-start.13 = (f32[320,768]{1,0:T(8,128)S(1)}, f32[320,768]{1,0:T(8,128)}, u32[]{:S(2)}) copy-start(f32[320,768]{1,0:T(8,128)} %copy-done.12) | copy-start | bytes 2949124
  74.8 4.0 %copy-start.25 = (bf16[16,20,768]{2,1,0:T(8,128)(2,1)S(1)}, bf16[16,20,768]{2,1,0:T(8,128)(2,1)}, u32[]{:S(2)}) copy-start(bf16[16,20,768]{2,1,0:T(8,128)(2,1)} %reshape.271) | copy-start | bytes 1474564
  78.9 5.3 %copy-start.44 = (bf16[12,64,128]{2,1,0:T(8,128)(2,1)S(1)}, bf16[12,64,128]{2,1,0:T(8,128)(2,1)}, u32[]{:S(2)}) copy-start(bf16[12,64,128]{2,1,0:T(8,128)(2,1)} %copy-done.43) | copy-start | bytes 589828
  80.0 27.2 %all-to-all-start.1 = ((bf16[16,40,768]{2,1,0:T(8,128)(2,1)}), bf16[16,40,768]{2,1,0:T(8,128)(2,1)S(1)}, u32[]{:S(2)}, u32[]{:S(2)}) async-start(bf16[16,40,768]{2,1,0:T(8,128)(2,1)} %pad_maximum_fusion.2), calls=%async_computation.1 | async-start | bytes 1966080 | tf_op jit(solution)/shard_map/all_to_all | solution.py:189
  83.9 70.2 %all-gather.3.cloned.1.call-start = ((), (), s32[]{:S(2)}) async-start(), calls=%async_computation.3 | async-start | bytes 3342336 | tf_op jit(solution)/shard_map/all_gather | solution.py:139
  108.4 3.1 %copy-start.7 = (bf16[768,768]{1,0:T(8,128)(2,1)S(1)}, bf16[768,768]{1,0:T(8,128)(2,1)}, u32[]{:S(2)}) copy-start(bf16[768,768]{1,0:T(8,128)(2,1)} %param.19) | copy-start | bytes 3538948
  109.9 4.5 %copy-start.77 = (f32[128]{0:T(128)}, f32[128]{0:T(128)S(1)}, u32[]{:S(2)}) copy-start(f32[128]{0:T(128)S(1)} %broadcast_multiply_fusion.1) | copy-start | bytes 1540
  110.6 3.8 %copy-start.62 = (f32[128]{0:T(128)S(1)}, f32[128]{0:T(128)}, u32[]{:S(2)}) copy-start(f32[128]{0:T(128)} %copy-done.60) | copy-start | bytes 1540
  110.6 3.8 %copy-start.71 = (f32[128]{0:T(128)S(1)}, f32[128]{0:T(128)}, u32[]{:S(2)}) copy-start(f32[128]{0:T(128)} %copy-done.70) | copy-start | bytes 1540
  111.5 3.0 %copy-start.24 = (bf16[128,768]{1,0:T(8,128)(2,1)S(1)}, bf16[128,768]{1,0:T(8,128)(2,1)}, u32[]{:S(2)}) copy-start(bf16[128,768]{1,0:T(8,128)(2,1)} %copy-done.23) | copy-start | bytes 589828
  111.5 3.4 %copy-start.57 = (f32[12,128]{1,0:T(8,128)S(1)}, f32[12,128]{1,0:T(8,128)}, u32[]{:S(2)}) copy-start(f32[12,128]{1,0:T(8,128)} %copy-done.56) | copy-start | bytes 18436
  117.7 3.4 %copy-start.33 = (bf16[128,768]{0,1:T(8,128)(2,1)S(1)}, bf16[128,768]{0,1:T(8,128)(2,1)}, u32[]{:S(2)}) copy-start(bf16[128,768]{0,1:T(8,128)(2,1)} %copy-done.32) | copy-start | bytes 589828
  123.3 4.5 %copy-start.9 = (bf16[768,768]{1,0:T(8,128)(2,1)S(1)}, bf16[768,768]{1,0:T(8,128)(2,1)}, u32[]{:S(2)}) copy-start(bf16[768,768]{1,0:T(8,128)(2,1)} %param.16) | copy-start | bytes 3538948
  132.3 17.3 %all-to-all-start.2 = ((bf16[16,200,128]{2,1,0:T(8,128)(2,1)}), bf16[16,200,128]{2,1,0:T(8,128)(2,1)S(1)}, u32[]{:S(2)}, u32[]{:S(2)}) async-start(bf16[16,200,128]{2,1,0:T(8,128)(2,1)} %pad_maximum_fusion.3), calls=%async_computation.2 | async-start | bytes 1638400 | tf_op jit(solution)/shard_map/all_to_all | solution.py:256
  151.4 2.7 copy-start.47
  157.8 9.6 %collective-permute-start.2 = (bf16[584,128]{1,0:T(8,128)(2,1)S(1)}, bf16[584,128]{1,0:T(8,128)(2,1)S(1)}, u32[]{:S(2)}, u32[]{:S(2)}) collective-permute-start(bf16[584,128]{1,0:T(8,128)(2,1)S(1)} %pad_maximum_fusion.8), channel_id=1, source_target_pairs={{0,16},{16,0},{1,17},{17,1},{2,18},{18,2},{3,19},{19,3},{4,20},{20... | collective-permute-start | bytes 448520 | tf_op jit(solution)/shard_map/ppermute | solution.py:63
  167.5 7.2 %collective-permute-start.3 = (bf16[584,128]{1,0:T(8,128)(2,1)S(1)}, bf16[584,128]{1,0:T(8,128)(2,1)S(1)}, u32[]{:S(2)}, u32[]{:S(2)}) collective-permute-start(bf16[584,128]{1,0:T(8,128)(2,1)S(1)} %pad_maximum_fusion.9), channel_id=1, source_target_pairs={{0,16},{16,0},{1,17},{17,1},{2,18},{18,2},{3,19},{19,3},{4,20},{20... | collective-permute-start | bytes 448520 | tf_op jit(solution)/shard_map/ppermute | solution.py:63
  174.8 8.7 %collective-permute-start.4 = (bf16[2,584,128]{2,1,0:T(8,128)(2,1)S(1)}, bf16[2,584,128]{2,1,0:T(8,128)(2,1)S(1)}, u32[]{:S(2)}, u32[]{:S(2)}) collective-permute-start(bf16[2,584,128]{2,1,0:T(8,128)(2,1)S(1)} %pad_maximum_fusion.7), channel_id=1, source_target_pairs={{0,8},{8,0},{1,9},{9,1},{2,10},{10,2},{3,11},{11,3},{4,12},{12,4},... | collective-permute-start | bytes 897032 | tf_op jit(solution)/shard_map/ppermute | solution.py:63
  183.6 8.5 %collective-permute-start.7 = (bf16[1168,128]{1,0:T(8,128)(2,1)S(1)}, bf16[1168,128]{1,0:T(8,128)(2,1)S(1)}, u32[]{:S(2)}, u32[]{:S(2)}) collective-permute-start(bf16[1168,128]{1,0:T(8,128)(2,1)S(1)} %bitcast.201), channel_id=1, source_target_pairs={{0,4},{4,0},{1,5},{5,1},{2,6},{6,2},{3,7},{7,3},{8,12},{12,8},{9,1... | collective-permute-start | bytes 897032 | tf_op jit(solution)/shard_map/ppermute | solution.py:63
  185.9 8.6 %collective-permute-start.5 = (bf16[1168,128]{1,0:T(8,128)(2,1)S(1)}, bf16[1168,128]{1,0:T(8,128)(2,1)S(1)}, u32[]{:S(2)}, u32[]{:S(2)}) collective-permute-start(bf16[1168,128]{1,0:T(8,128)(2,1)S(1)} %bitcast.200), channel_id=1, source_target_pairs={{0,2},{2,0},{1,3},{3,1},{4,6},{6,4},{5,7},{7,5},{8,10},{10,8},{9,1... | collective-permute-start | bytes 897032 | tf_op jit(solution)/shard_map/ppermute | solution.py:63
  192.2 14.6 %collective-permute-start.8 = (bf16[2,1168,128]{2,1,0:T(8,128)(2,1)S(1)}, bf16[2,1168,128]{2,1,0:T(8,128)(2,1)S(1)}, u32[]{:S(2)}, u32[]{:S(2)}) collective-permute-start(bf16[2,1168,128]{2,1,0:T(8,128)(2,1)S(1)} %pad_maximum_fusion.5), channel_id=1, source_target_pairs={{0,2},{2,0},{1,3},{3,1},{4,6},{6,4},{5,7},{7,5},{8,10},{10,8},{9,1... | collective-permute-start | bytes 1794056 | tf_op jit(solution)/shard_map/ppermute | solution.py:63
  194.6 13.7 %collective-permute-start.6 = (bf16[2,1168,128]{2,1,0:T(8,128)(2,1)S(1)}, bf16[2,1168,128]{2,1,0:T(8,128)(2,1)S(1)}, u32[]{:S(2)}, u32[]{:S(2)}) collective-permute-start(bf16[2,1168,128]{2,1,0:T(8,128)(2,1)S(1)} %pad_maximum_fusion.4), channel_id=1, source_target_pairs={{0,4},{4,0},{1,5},{5,1},{2,6},{6,2},{3,7},{7,3},{8,12},{12,8},{9,1... | collective-permute-start | bytes 1794056 | tf_op jit(solution)/shard_map/ppermute | solution.py:63
  210.3 15.2 %collective-permute-start.9 = (bf16[2,2,2,1168,128]{4,3,2,1,0:T(8,128)(2,1)}, bf16[2,2,2,1168,128]{4,3,2,1,0:T(8,128)(2,1)}, u32[]{:S(2)}, u32[]{:S(2)}) collective-permute-start(bf16[2,2,2,1168,128]{4,3,2,1,0:T(8,128)(2,1)} %pad_maximum_fusion.1), channel_id=1, source_target_pairs={{0,1},{1,0},{2,3},{3,2},{4,5},{5,4},{6,7},{7,6},{8,9},{9,8},{10,11... | collective-permute-start | bytes 7176200 | tf_op jit(solution)/shard_map/ppermute | solution.py:63
  212.1 4.8 %collective-permute-start.10 = (bf16[768,768]{1,0:T(8,128)(2,1)}, bf16[768,768]{1,0:T(8,128)(2,1)}, u32[]{:S(2)}, u32[]{:S(2)}) collective-permute-start(bf16[768,768]{1,0:T(8,128)(2,1)} %convolution_convert_fusion.1), channel_id=1, source_target_pairs={{0,1},{1,0},{2,3},{3,2},{4,5},{5,4},{6,7},{7,6},{8,9},{9,8},{10,11... | collective-permute-start | bytes 3538952 | tf_op jit(solution)/shard_map/ppermute | solution.py:63
  214.5 6.1 %collective-permute-start.11 = (bf16[768,768]{1,0:T(8,128)(2,1)}, bf16[768,768]{1,0:T(8,128)(2,1)}, u32[]{:S(2)}, u32[]{:S(2)}) collective-permute-start(bf16[768,768]{1,0:T(8,128)(2,1)} %convolution_convert_fusion), channel_id=1, source_target_pairs={{0,1},{1,0},{2,3},{3,2},{4,5},{5,4},{6,7},{7,6},{8,9},{9,8},{10,11... | collective-permute-start | bytes 3538952 | tf_op jit(solution)/shard_map/ppermute | solution.py:63
  214.5 6.1 %copy-start.14 = (f32[320,768]{1,0:T(8,128)S(1)}, f32[320,768]{1,0:T(8,128)}, u32[]{:S(2)}) copy-start(f32[320,768]{1,0:T(8,128)} %copy-done.12) | copy-start | bytes 2949124
  214.5 6.1 %copy-start.28 = (bf16[320,768]{1,0:T(8,128)(2,1)S(1)}, bf16[320,768]{1,0:T(8,128)(2,1)}, u32[]{:S(2)}) copy-start(bf16[320,768]{1,0:T(8,128)(2,1)} %reshape.270) | copy-start | bytes 1474564
  220.5 3.8 %copy-start.16 = (f32[128,768]{1,0:T(8,128)S(1)}, f32[128,768]{1,0:T(8,128)}, u32[]{:S(2)}) copy-start(f32[128,768]{1,0:T(8,128)} %copy-done.15) | copy-start | bytes 1179652
  220.5 3.8 %copy-start.22 = (bf16[128,768]{1,0:T(8,128)(2,1)S(1)}, bf16[128,768]{1,0:T(8,128)(2,1)}, u32[]{:S(2)}) copy-start(bf16[128,768]{1,0:T(8,128)(2,1)} %param.27) | copy-start | bytes 589828
  220.5 3.8 %copy-start.38 = (f32[128,768]{1,0:T(8,128)S(1)}, f32[128,768]{1,0:T(8,128)}, u32[]{:S(2)}) copy-start(f32[128,768]{1,0:T(8,128)} %get-tuple-element.66) | copy-start | bytes 1179652
  220.6 3.8 %copy-start.39 = (f32[128,768]{1,0:T(8,128)S(1)}, f32[128,768]{1,0:T(8,128)}, u32[]{:S(2)}) copy-start(f32[128,768]{1,0:T(8,128)} %get-tuple-element.70) | copy-start | bytes 1179652
  220.6 3.8 %copy-start.54 = (f32[768]{0:T(1024)S(1)}, f32[768]{0:T(1024)}, u32[]{:S(2)}) copy-start(f32[768]{0:T(1024)} %param.21) | copy-start | bytes 9220
  220.6 3.8 %copy-start.69 = (f32[128]{0:T(128)S(1)}, f32[128]{0:T(128)}, u32[]{:S(2)}) copy-start(f32[128]{0:T(128)} %copy-done.67) | copy-start | bytes 1540
  220.6 3.8 %copy-start.76 = (f32[128]{0:T(128)S(1)}, f32[128]{0:T(128)}, u32[]{:S(2)}) copy-start(f32[128]{0:T(128)} %copy-done.75) | copy-start | bytes 1540
  220.6 3.8 %copy-start.78 = (f32[128]{0:T(128)S(1)}, f32[128]{0:T(128)}, u32[]{:S(2)}) copy-start(f32[128]{0:T(128)} %copy-done.77) | copy-start | bytes 1540
  261.8 4.5 %copy-start.1 = (bf16[768,768]{1,0:T(8,128)(2,1)S(1)}, bf16[768,768]{1,0:T(8,128)(2,1)}, u32[]{:S(2)}) copy-start(bf16[768,768]{1,0:T(8,128)(2,1)} %param.18) | copy-start | bytes 3538948
  (49 other events, 77.2 us)
Sparse Core Ops, SparseCore 0:
  32.1 38.4 all-gather.4
  86.4 37.3 all-gather.2

commit v2 on v1

--- a/solution.py
+++ b/solution.py
@@ -1,6 +1,11 @@
+import functools
+
 import jax
 import jax.numpy as jnp
+import numpy as np
 from jax import lax
+from jax.experimental import pallas as pl
+from jax.experimental.pallas import tpu as pltpu
 from jax.sharding import Mesh
 from jax.sharding import PartitionSpec as P
 
@@ -45,11 +50,6 @@
     )
 
 
-def gelu_grad(inner_sum, upstream):
-    _, pullback = jax.vjp(jax.nn.gelu, inner_sum)
-    return pullback(upstream)[0]
-
-
 def norm_backward(values, factor, gain, grad_normed):
     scaled = gain * grad_normed
     grad_gain = jnp.sum(grad_normed * values * factor, axis=0)
@@ -63,19 +63,296 @@
     return lax.ppermute(array, axis, perm=[(0, 1), (1, 0)])
 
 
-def in_order(own, other, axis):
-    first = lax.axis_index(axis) == 0
-    return jnp.stack([jnp.where(first, own, other), jnp.where(first, other, own)])
-
-
-def gather_pair(array, axis):
-    return in_order(array, swap(array, axis), axis)
-
-
 def split_two(values):
     high = values.astype(jnp.bfloat16)
     low = (values - high.astype(jnp.float32)).astype(jnp.bfloat16)
     return high, low
+
+def whole_spec():
+    return pl.BlockSpec(memory_space=pltpu.VMEM)
+
+
+def any_spec():
+    return pl.BlockSpec(memory_space=pl.ANY)
+
+
+def params(mib):
+    return pltpu.CompilerParams(vmem_limit_bytes=mib * 1024 * 1024)
+
+
+def cost(flops, moved):
+    return pl.CostEstimate(flops=flops, bytes_accessed=moved, transcendentals=0)
+
+
+def shaped(dims, kind):
+    return jax.ShapeDtypeStruct(dims, kind)
+
+
+gelu_scale = 0.7978845608028654
+gelu_cubic = 0.044715
+
+
+def expert_kernel(
+    rows_ref, order_ref, in_a, out_a, in_b, out_b, back_ref, rows_out, grads_out, act_ref, inner_ref
+):
+    count = rows_ref.shape[0]
+    half = count // 2
+    lanes = lax.broadcasted_iota(jnp.int32, (count, count), 1)
+    sort = jnp.where(order_ref[:, 0:1] == lanes, 1.0, 0.0).astype(jnp.bfloat16)
+    unsort = jnp.where(order_ref[:, 1:2] == lanes, 1.0, 0.0).astype(jnp.bfloat16)
+    ordered = jnp.dot(sort, rows_ref[...], preferred_element_type=jnp.float32)
+    ordered = ordered.astype(jnp.bfloat16)
+    rows, slots = ordered[:half], ordered[half:]
+    rows_out[...] = rows
+    grads_out[...] = slots
+    result, d_rows = 0.0, 0.0
+    for part, (part_in, part_out) in enumerate(((in_a, out_a), (in_b, out_b))):
+        inner = jnp.dot(rows, part_in[...], preferred_element_type=jnp.float32)
+        upstream = dot_last(slots, part_out[...])
+        square = inner * inner
+        bent = jnp.tanh(gelu_scale * (inner + gelu_cubic * (square * inner)))
+        active = (inner * (0.5 * (1.0 + bent))).astype(jnp.bfloat16)
+        slope = 0.5 * (1.0 + bent) + 0.5 * inner * (1.0 - bent * bent) * (
+            gelu_scale * (1.0 + 3.0 * gelu_cubic * square)
+        )
+        d_inner = (upstream * slope).astype(jnp.bfloat16)
+        act_ref[part] = active
+        inner_ref[part] = d_inner
+        result = result + jnp.dot(active, part_out[...], preferred_element_type=jnp.float32)
+        d_rows = d_rows + dot_last(d_inner, part_in[...])
+    both = jnp.concatenate([result.astype(jnp.bfloat16), d_rows.astype(jnp.bfloat16)], axis=0)
+    back_ref[...] = jnp.dot(unsort, both, preferred_element_type=jnp.float32).astype(jnp.bfloat16)
+
+
+def expert_rows_of(rows, capacity, part_weights):
+    count, width = rows.shape
+    half = count // 2
+    place = np.arange(count)
+    sort = place % half // capacity * 2 * capacity + place // half * capacity + place % capacity
+    unsort = np.empty_like(sort)
+    unsort[sort] = place
+    order = jnp.asarray(np.stack([sort, unsort], axis=1), jnp.int32)
+    hidden_width = part_weights[0].shape[1]
+    low = jnp.bfloat16
+    return pl.pallas_call(
+        expert_kernel,
+        out_shape=(
+            shaped((count, width), low),
+            shaped((half, width), low),
+            shaped((half, width), low),
+            shaped((2, half, hidden_width), low),
+            shaped((2, half, hidden_width), low),
+        ),
+        in_specs=[whole_spec()] * 6,
+        out_specs=(whole_spec(),) * 5,
+        compiler_params=params(48),
+        cost_estimate=cost(16 * half * width * hidden_width, 12 * width * width),
+        name="expert_rows",
+    )(rows, order, *part_weights)
+
+
+def expert_grads_kernel(rows_ref, slots_ref, act_ref, inner_ref, own_in, own_out, sent_in, sent_out):
+    own_in[...] = dot_first(rows_ref[...], inner_ref[0])
+    sent_in[...] = dot_first(rows_ref[...], inner_ref[1]).astype(jnp.bfloat16)
+    own_out[...] = dot_first(act_ref[0], slots_ref[...])
+    sent_out[...] = dot_first(act_ref[1], slots_ref[...]).astype(jnp.bfloat16)
+
+
+def expert_grads_of(rows, slots, active, d_inner):
+    half, width = rows.shape
+    hidden_width = active.shape[2]
+    return pl.pallas_call(
+        expert_grads_kernel,
+        out_shape=(
+            shaped((width, hidden_width), jnp.float32),
+            shaped((hidden_width, width), jnp.float32),
+            shaped((width, hidden_width), jnp.bfloat16),
+            shaped((hidden_width, width), jnp.bfloat16),
+        ),
+        in_specs=[whole_spec()] * 4,
+        out_specs=(whole_spec(),) * 4,
+        compiler_params=params(48),
+        cost_estimate=cost(8 * half * width * hidden_width, 12 * width * width),
+        name="expert_grads",
+    )(rows, slots, active, d_inner)
+
+
+def block_kernel(place_ref, late_ref, left_ref, mine_ref, sent_ref, small_ref, held):
+    group, rows, length = late_ref.shape
+    part, width = held.shape[1], held.shape[2]
+    block = 2 * part
+    small_rows = small_ref.shape[0]
+    right = jnp.concatenate([late_ref[i, :block] for i in range(group)], axis=1)
+    total = jnp.dot(right, left_ref[...], preferred_element_type=jnp.float32)
+    held[0] = total[:part]
+    held[1] = total[part:]
+    place = place_ref[0]
+    mine, theirs = held[place], held[1 - place]
+    for chunk in range(width // LANES):
+        lanes = slice(chunk * LANES, (chunk + 1) * LANES)
+        mine_ref[chunk * part : (chunk + 1) * part] = mine[:, lanes]
+        sent_ref[chunk * part : (chunk + 1) * part] = theirs[:, lanes].astype(jnp.bfloat16)
+    tail = jnp.sum(late_ref[:, block:].astype(jnp.float32), axis=0)
+    small = tail[:small_rows] + tail[small_rows:]
+    small_ref[...] = small
+    high = small.astype(jnp.bfloat16).astype(jnp.float32)
+    both = jnp.concatenate([high, small - high], axis=0)
+    sent_ref[sent_ref.shape[0] - 2 * small_rows :] = both.astype(jnp.bfloat16)
+
+
+def block_of(place, late, left, small_rows):
+    group, rows, length = late.shape
+    width = left.shape[1]
+    part = (rows - 2 * small_rows) // 2
+    edge = part * width // LANES
+    return pl.pallas_call(
+        block_kernel,
+        out_shape=(
+            shaped((edge, LANES), jnp.float32),
+            shaped((edge + 2 * small_rows, LANES), jnp.bfloat16),
+            shaped((small_rows, LANES), jnp.float32),
+        ),
+        in_specs=[pl.BlockSpec(memory_space=pltpu.SMEM), whole_spec(), whole_spec()],
+        out_specs=(whole_spec(),) * 3,
+        scratch_shapes=[pltpu.VMEM((2, part, width), jnp.float32)],
+        compiler_params=params(48),
+        cost_estimate=cost(4 * part * width * group * length, 2 * left.size),
+        name="grad_block",
+    )(place, late, left)
+
+
+def share_kernel(mine_ref, small_ref, got_ref, share_ref):
+    edge, small_rows = mine_ref.shape[0], small_ref.shape[0]
+    share_ref[:edge] = (mine_ref[...] + got_ref[:edge].astype(jnp.float32)).astype(jnp.bfloat16)
+    tail = got_ref[edge:].astype(jnp.float32)
+    small = small_ref[...] + (tail[:small_rows] + tail[small_rows:])
+    high = small.astype(jnp.bfloat16).astype(jnp.float32)
+    share_ref[edge:] = jnp.concatenate([high, small - high], axis=0).astype(jnp.bfloat16)
+
+
+def share_of(mine, small, got):
+    return pl.pallas_call(
+        share_kernel,
+        out_shape=shaped(got.shape, jnp.bfloat16),
+        in_specs=[whole_spec()] * 3,
+        out_specs=whole_spec(),
+        compiler_params=params(16),
+        cost_estimate=cost(mine.size, 8 * mine.size),
+        name="share",
+    )(mine, small, got)
+
+
+def assemble_kernel(part, small_rows, bits_ref, *refs):
+    sources, outs, small_out = refs[:8], refs[8:12], refs[12]
+    held, made, in_sems, out_sems = refs[13:]
+    em, ey, dx, dc, eh = [bits_ref[i] for i in range(5)]
+    edge = held.shape[2] - 2 * small_rows
+    width = made.shape[1]
+    copies = [[] for _ in range(4)]
+    for far in range(2):
+        core = dc ^ far
+        for side, first in enumerate(("x", "x", "y", "y")):
+            source = sources[far * 4 + side]
+            for at in range(2):
+                if first == "x":
+                    weight, step = side, at
+                else:
+                    weight, step = 2 + at, side - 2
+                for other in range(2):
+                    to = ((dx ^ step) * 2 + core) * 2 + (eh ^ other)
+                    copies[weight].append(
+                        pltpu.make_async_copy(
+                            source.at[at, other],
+                            held.at[weight, to],
+                            in_sems.at[weight, len(copies[weight])],
+                        )
+                    )
+    for weight in range(4):
+        for copy in copies[weight]:
+            copy.start()
+    unit = lax.broadcasted_iota(jnp.int32, (LANES, LANES), 0)
+    unit = jnp.where(unit == lax.broadcasted_iota(jnp.int32, (LANES, LANES), 1), 1.0, 0.0)
+    unit = unit.astype(jnp.bfloat16)
+    for weight in range(4):
+        for copy in copies[weight]:
+            copy.wait()
+        for chunk in range(width // LANES):
+            columns = jnp.concatenate(
+                [held[weight, i, chunk * part : (chunk + 1) * part] for i in range(8)], axis=0
+            )
+            made[weight, chunk * LANES : (chunk + 1) * LANES] = dot_last(unit, columns)
+        truth = (em ^ (weight // 2)) * 2 + (ey ^ (weight % 2))
+        for i in range(4):
+            at = 2 * i
+            tail = held[weight, at, edge:].astype(jnp.float32)
+            small_out[truth, i] = tail[:small_rows] + tail[small_rows:]
+
+            @pl.when(truth == i)
+            def _():
+                pltpu.make_async_copy(made.at[weight], outs[i], out_sems.at[weight]).start()
+
+    for weight in range(4):
+        truth = (em ^ (weight // 2)) * 2 + (ey ^ (weight % 2))
+        for i in range(4):
+
+            @pl.when(truth == i)
+            def _():
+                pltpu.make_async_copy(made.at[weight], outs[i], out_sems.at[weight]).wait()
+
+
+def assemble(bits, sources, part, small_rows, width):
+    rows = sources[0].shape[2]
+    return pl.pallas_call(
+        functools.partial(assemble_kernel, part, small_rows),
+        out_shape=(shaped((width, width), jnp.float32),) * 4
+        + (shaped((4, 4, small_rows, LANES), jnp.float32),),
+        in_specs=[pl.BlockSpec(memory_space=pltpu.SMEM)] + [any_spec()] * 8,
+        out_specs=(any_spec(),) * 4 + (whole_spec(),),
+        scratch_shapes=[
+            pltpu.VMEM((4, 8, rows, LANES), jnp.bfloat16),
+            pltpu.VMEM((4, width, width), jnp.float32),
+            pltpu.SemaphoreType.DMA((4, 8)),
+            pltpu.SemaphoreType.DMA((4,)),
+        ],
+        compiler_params=params(48),
+        cost_estimate=cost(8 * LANES * width * width, 24 * width * width),
+        name="assemble",
+    )(bits, *sources)
+
+
+def gathered_grads(late, left_all, small_rows):
+    width = left_all.shape[1]
+    place = lax.axis_index("eh").astype(jnp.int32)
+    mine, sent, small = block_of(place[None], late, left_all, small_rows)
+    share = share_of(mine, small, swap(sent, "eh"))
+    near = jnp.stack([share, swap(share, "eh")])
+    far = swap(near, "em")
+    near_x = jnp.stack([near, swap(near, "dx")])
+    far_y = jnp.stack([far, swap(far, "ey")])
+    near_y = swap(near_x, "ey")
+    far_x = swap(far_y, "dx")
+    sources = (near_x, near_y, far_y, far_x)
+    sources = sources + tuple(swap(source, "dc") for source in sources)
+    bits = jnp.stack([lax.axis_index(axis) for axis in ("em", "ey", "dx", "dc", "eh")])
+    part = (late.shape[1] - 2 * small_rows) // 2
+    *grads, small = assemble(bits.astype(jnp.int32), sources, part, small_rows, width)
+    return grads, small
+
+
+def gathered_grads_plain(late, left_all, small_rows):
+    group, rows, length = late.shape
+    width = left_all.shape[1]
+    block = rows - 2 * small_rows
+    small = jnp.sum(late[:, block:].astype(jnp.float32), axis=0)
+    small = lax.psum(small[:small_rows] + small[small_rows:], "eh")
+    late_block = late[:, :block].transpose(1, 0, 2).reshape(block, group * length)
+    grad_block = jnp.dot(late_block, left_all, preferred_element_type=jnp.float32)
+    mine = lax.psum_scatter(grad_block, "eh", scatter_dimension=0, tiled=True)
+    grads = lax.all_gather(mine.astype(jnp.bfloat16), "eh", axis=0, tiled=True)
+    grads = lax.all_gather(grads, GROUP_AXES, axis=0, tiled=True)
+    small = lax.all_gather(small, GROUP_AXES, axis=0, tiled=True)
+    grads = grads.reshape(4, width, width).transpose(0, 2, 1).astype(jnp.float32)
+    return grads, small
 
 
 def per_device(
@@ -166,32 +443,22 @@
     outgoing = jnp.broadcast_to(outgoing[:, None], (experts, 2) + outgoing.shape[1:])
     outgoing = outgoing.reshape((experts * 2,) + outgoing.shape[2:])
     incoming = lax.all_to_all(outgoing, EXPERT_AXES, split_axis=0, concat_axis=0, tiled=True)
-    expert_rows = incoming[:, :capacity].reshape(-1, model_width)
-    grad_slots = incoming[:, capacity:].reshape(-1, model_width)
-
-    result, d_rows = 0.0, 0.0
-    expert_grads = []
-    for part_in, part_out in ((w_in_own, w_out_own), (w_in_other, w_out_other)):
-        inner_sum = jnp.dot(expert_rows, part_in, preferred_element_type=jnp.float32)
-        active = jax.nn.gelu(inner_sum).astype(low_type)
-        result = result + jnp.dot(active, part_out, preferred_element_type=jnp.float32)
-        d_active = dot_last(grad_slots, part_out)
-        d_inner = gelu_grad(inner_sum, d_active).astype(low_type)
-        d_rows = d_rows + dot_last(d_inner, part_in)
-        expert_grads.append((dot_first(expert_rows, d_inner), dot_first(active, grad_slots)))
-    sent_back = jnp.concatenate(
-        [
-            result.astype(low_type).reshape(-1, capacity, model_width),
-            d_rows.astype(low_type).reshape(-1, capacity, model_width),
-        ],
-        axis=1,
+    incoming = incoming.reshape(-1, model_width)
+    sent_back, expert_rows, grad_slots, active, d_inner = expert_rows_of(
+        incoming, capacity, (w_in_own, w_out_own, w_in_other, w_out_other)
+    )
+    sent_back = sent_back.reshape(2 * experts, 2 * capacity, model_width)
+    in_own, out_own, in_other, out_other = expert_grads_of(
+        expert_rows, grad_slots, active, d_inner
     )
     came_back = lax.all_to_all(sent_back, EXPERT_AXES, split_axis=0, concat_axis=0, tiled=True)
     came_back = came_back.reshape(experts, 2, 2 * capacity, model_width).astype(jnp.float32)
     came_back = (came_back[:, 0] + came_back[:, 1]).astype(low_type)
-    (in_own, out_own), (in_other, out_other) = expert_grads
-    grad_in = in_own + swap(in_other.astype(low_type), "dc").astype(jnp.float32)
-    grad_out = out_own + swap(out_other.astype(low_type), "dc").astype(jnp.float32)
+    came_back, in_own, out_own, in_other, out_other = lax.optimization_barrier(
+        (came_back, in_own, out_own, in_other, out_other)
+    )
+    grad_in = in_own + swap(in_other, "dc").astype(jnp.float32)
+    grad_out = out_own + swap(out_other, "dc").astype(jnp.float32)
 
     returned = jnp.einsum(
         "tec,ecd->td", dispatch_low, came_back[:, :capacity], preferred_element_type=jnp.float32
@@ -254,59 +521,17 @@
     factors = factors.T.reshape(group, block, length)
     late = jnp.concatenate([factors, small_high, small_low], axis=1)
     late = lax.all_to_all(late, GROUP_AXES, split_axis=0, concat_axis=0, tiled=True)
-    small = jnp.sum(late[:, block:].astype(jnp.float32), axis=0)
-    small = small[:small_rows] + small[small_rows:]
-
     inputs_all = tokens_all.astype(jnp.float32)
     factor_all = lax.rsqrt(jnp.mean(inputs_all * inputs_all, axis=-1, keepdims=True) + norm_eps)
     normed_all = (inputs_all * factor_all * norm_gain).astype(low_type)
     which = lax.axis_index(GROUP_AXES) // (group // 4)
     left_all = jnp.where(which == 3, attended_all, normed_all)
-    late_block = late[:, :block].transpose(1, 0, 2).reshape(block, group * length)
-    grad_block = jnp.dot(late_block, left_all, preferred_element_type=jnp.float32)
-
-    part = block // eh_count
-    grad_block = grad_block.reshape(eh_count, part, model_width)
+    late, left_all = lax.optimization_barrier((late, left_all))
     if eh_count == 2:
-        place = lax.axis_index("eh")
-        mine = lax.dynamic_index_in_dim(grad_block, place, 0, keepdims=False)
-        theirs = lax.dynamic_index_in_dim(grad_block, 1 - place, 0, keepdims=False)
-        small_high, small_low = split_two(small)
-        sent = jnp.concatenate(
-            [theirs.astype(low_type).reshape(-1, LANES), small_high, small_low], axis=0
-        )
-        got = swap(sent, "eh").astype(jnp.float32)
-        edge = part * model_width // LANES
-        mine = mine.reshape(-1, LANES) + got[:edge]
-        small = small + (got[edge : edge + small_rows] + got[edge + small_rows :])
+        grads, small = gathered_grads(late, left_all, small_rows)
     else:
-        mine = lax.psum_scatter(grad_block, "eh", scatter_dimension=0, tiled=True)
-        mine = mine.reshape(-1, LANES)
-        small = lax.psum(small, "eh")
-        edge = mine.shape[0]
-    small_high, small_low = split_two(small)
-    share = jnp.concatenate([mine.astype(low_type), small_high, small_low], axis=0)
-    rows = share.shape[0]
-
-    if eh_count == 2:
-        share = gather_pair(share, "eh")
-    else:
-        share = lax.all_gather(share, "eh", axis=0, tiled=False)
-    share = gather_pair(share, "em").reshape(2 * eh_count * rows, LANES)
-    half = eh_count * rows
-    first, second = share[:half], share[half:]
-    first = gather_pair(first, "dx")
-    second = gather_pair(second, "ey")
-    first = gather_pair(first, "ey")
-    second = gather_pair(second, "dx").transpose(1, 0, 2, 3)
-    whole = jnp.stack([first, second])
-    whole = gather_pair(whole, "dc")
-    whole = whole.reshape(2, 2, 2, 2, eh_count, rows, LANES)
-    whole = whole.transpose(1, 2, 3, 0, 4, 5, 6).reshape(group, eh_count, rows, LANES)
-    grads = whole[:, :, :edge].reshape(4, model_width, model_width).transpose(0, 2, 1)
-    grads = grads.astype(jnp.float32)
-    small = whole[:, 0, edge:].astype(jnp.float32)
-    small = (small[:, :small_rows] + small[:, small_rows:]).reshape(-1)
+        grads, small = gathered_grads_plain(late, left_all, small_rows)
+    small = small.reshape(-1)
     pieces, at = [], 0
     for size in small_sizes:
         pieces.append(small[at : at + size])

time: 275 us -> 215 us (0.78)
  local copies, waits for them, and re-layouts: 59.1 us -> 21.8 us
  matrix products: 46.7 us -> 15.9 us
  Pallas kernels: 0 us -> 24.1 us
  waiting for transfers between devices: 104 us -> 87.4 us
    pallas_call x0 -> x5, Pallas kernels: none -> 24.1 us  [the longest x1 10.4 us: assemble(): pl.pallas_call(functools.partial(assemble_kernel, part, small_rows), out_...]
    convert_element_type x3 -> x0, local copies, waits for them, and re-layouts: 11.5 us -> none  [the longest x1 11.3 us: per_device(): grads = grads.astype(jnp.float32)]
    dot_general x5 -> x1, matrix products: 11.3 us -> 0.23 us  [dot_first(): lax.dot_general(left_side, right_side, (((0,), (0,)), ((), ())), preferre...]
    dot_general x5 -> x0, matrix products: 10.8 us -> none  [the longest x2 4.96 us: per_device(): jnp.dot(active, part_out, preferred_element_type=jnp.float32)]
    dot_general x9 -> x5, matrix products: 11.9 us -> 4.85 us  [dot_last(): lax.dot_general(left_side, right_side, (((1,), (1,)), ((), ())), preferre...]
    squeeze x1 -> x0, local copies, waits for them, and re-layouts: 6.88 us -> none  [per_device(): grads[3]]
    all_to_all x1, waiting for transfers between devices: 13.6 us -> 6.87 us  [per_device(): lax.all_to_all(late, GROUP_AXES, split_axis=0, concat_axis=0, tiled=True)]
    reshape x5 -> x0, local copies, waits for them, and re-layouts: 6.3 us -> none  [the longest x1 1.94 us: per_device(): grad_slots = incoming[:, capacity:].reshape(-1, model_width)]
  transfers between devices with their start and end apart: 17 -> 20, of which waited for: 10 -> 11; matrix products, arithmetic and copies ran while one was open for 23% -> 22% of each run, Pallas kernels for 0% -> 6%
where the time goes in v2:
time: 215 us; the launch traced here: 214 us
  waiting for transfers between devices  87.4 us (41%)
  starting transfers between devices  25.7 us (12%)
  Pallas kernels  24.1 us (11%)
  other arithmetic  23.4 us (11%)
  local copies, waits for them, and re-layouts  21.8 us (10%)
  matrix products  15.9 us (7%)
  between operations  15.9 us (7%)
    ppermute x15, waiting for transfers between devices, swap(): return lax.ppermute(array, axis, perm=[(0, 1), (1, 0)])  40.9 us
    all_to_all x1, waiting for transfers between devices, per_device(): lax.all_to_all(outgoing, EXPERT_AXES, split_axis=0, concat_axis=0, tiled=...  20.7 us
    all_to_all x1, waiting for transfers between devices, per_device(): lax.all_to_all(sent_back, EXPERT_AXES, split_axis=0, concat_axis=0, tiled...  18.2 us
    unnamed x146, local copies, waits for them, and re-layouts  13.9 us
    pallas_call x1, Pallas kernels, assemble(): pl.pallas_call(functools.partial(assemble_kernel, part, small_rows), out_...  10.4 us
    ppermute x15, starting transfers between devices, swap(): return lax.ppermute(array, axis, perm=[(0, 1), (1, 0)])  8.86 us
    pallas_call x1, Pallas kernels, expert_rows_of(): pl.pallas_call(expert_kernel, out_shape=(shaped((count, width), low), sha...  8.42 us
    all_to_all x1, starting transfers between devices, per_device(): lax.all_to_all(outgoing, EXPERT_AXES, split_axis=0, concat_axis=0, tiled=...  8.31 us
  transfers between devices with their start and end apart: 20, of which 11 were waited for; matrix products, arithmetic and copies ran while one was open for 22% of the time, Pallas kernels for 6%

profile of v2, /device:TPU:0, one launch (start us, length us, event | category | flops | bytes accessed | tf_op | source)
XLA Modules:
  0.0 214.2 jit_solution(17975179295349101821)
XLA Ops:
  8.0 1.1 fusion.30
  11.5 1.8 convolution_convert_fusion.6
  14.4 0.8 copy.50
  17.0 1.1 fusion.83
  18.7 1.3 convolution_convert_fusion.4
  23.0 1.0 broadcast_in_dim.31
  24.0 8.3 %all-to-all-start = ((bf16[16,40,768]{2,1,0:T(8,128)(2,1)}), bf16[16,40,768]{2,1,0:T(8,128)(2,1)S(1)}, u32[]{:S(2)}, u32[]{:S(2)}) async-start(bf16[16,40,768]{2,1,0:T(8,128)(2,1)} %bitcast.11), calls=%async_computation | async-start | bytes 1966080 | tf_op jit(solution)/shard_map/all_to_all | solution.py:445
  32.9 3.5 %collective-permute-done.in_b = bf16[768,768]{1,0:T(8,128)(2,1)S(1)} collective-permute-done((bf16[768,768]{1,0:T(8,128)(2,1)}, bf16[768,768]{1,0:T(8,128)(2,1)S(1)}, u32[]{:S(2)}, u32[]{:S(2)}) %collective-permute-start) | collective-permute-done | bytes 1179680 | tf_op jit(solution)/shard_map/ppermute | solution.py:63
  36.4 1.0 copy-done.71
  37.6 20.7 %all-to-all-done = bf16[16,40,768]{2,1,0:T(8,128)(2,1)S(1)} async-done(((bf16[16,40,768]{2,1,0:T(8,128)(2,1)}), bf16[16,40,768]{2,1,0:T(8,128)(2,1)S(1)}, u32[]{:S(2)}, u32[]{:S(2)}) %all-to-all-start) | async-done | bytes 983072 | tf_op jit(solution)/shard_map/all_to_all | solution.py:445
  58.3 8.4 %expert_rows.1 = (bf16[640,768]{1,0:T(8,128)(2,1)}, bf16[320,768]{1,0:T(8,128)(2,1)S(1)}, bf16[320,768]{1,0:T(8,128)(2,1)S(1)}, bf16[2,320,768]{2,1,0:T(8,128)(2,1)S(1)}, bf16[2,320,768]{2,1,0:T(8,128)(2,1)S(1)}) custom-call(bf16[640,768]{1,0:T(8,128)(2,1)S(1)} %bitcast.111, s32[640,2]{1,0:T(8,128)S(1)} %copy-done.2, bf16[768,768]{1,0:T(8,128)(2,1)} %bitcast.145, ...), custom_call_target="tpu_custom_call" | custom-call | flops 3019898880 | bytes 7077888 | tf_op jit(solution)/shard_map/expert_rows/pallas_call | solution.py:137
  66.8 0.9 copy-done.3
  67.7 0.8 copy-done.5
  69.3 4.5 %all-to-all-start.1 = ((bf16[16,40,768]{2,1,0:T(8,128)(2,1)}), bf16[16,40,768]{2,1,0:T(8,128)(2,1)}, u32[]{:S(2)}, u32[]{:S(2)}) async-start(bf16[16,40,768]{2,1,0:T(8,128)(2,1)} %bitcast.15), calls=%async_computation.1 | async-start | bytes 1966080 | tf_op jit(solution)/shard_map/all_to_all | solution.py:454
  74.0 0.9 copy.71
  74.9 1.0 copy-done.6
  75.9 1.0 copy-done.8
  76.9 4.4 %expert_grads.1 = (f32[768,768]{1,0:T(8,128)}, f32[768,768]{1,0:T(8,128)}, bf16[768,768]{1,0:T(8,128)(2,1)}, bf16[768,768]{1,0:T(8,128)(2,1)}) custom-call(bf16[320,768]{1,0:T(8,128)(2,1)S(1)} %copy-done.6, bf16[320,768]{1,0:T(8,128)(2,1)S(1)} %copy-done.8, bf16[2,320,768]{2,1,0:T(8,128)(2,1)S(1)} %get-tuple-element.39.act_ref, ...), custom_call_target="tpu_custom_call" | custom-call | flops 1509949440 | bytes 7077888 | tf_op jit(solution)/shard_map/expert_grads/pallas_call | solution.py:164
  81.3 18.2 %all-to-all-done.1 = bf16[16,40,768]{2,1,0:T(8,128)(2,1)} async-done(((bf16[16,40,768]{2,1,0:T(8,128)(2,1)}), bf16[16,40,768]{2,1,0:T(8,128)(2,1)}, u32[]{:S(2)}, u32[]{:S(2)}) %all-to-all-start.1) | async-done | bytes 983072 | tf_op jit(solution)/shard_map/all_to_all | solution.py:454
  99.5 1.4 convert.1
  101.9 1.0 fusion.29
  103.2 0.8 reshape.241
  106.4 1.9 convolution_convert_fusion.2
  112.7 1.0 maximum_bitcast_fusion
  113.6 1.5 copy.67
  115.2 1.6 fusion.85
  117.4 1.8 fusion.33
  119.2 1.0 pad_maximum_fusion
  120.2 3.8 %all-to-all-start.2 = ((bf16[16,200,128]{2,1,0:T(8,128)(2,1)}), bf16[16,200,128]{2,1,0:T(8,128)(2,1)S(1)}, u32[]{:S(2)}, u32[]{:S(2)}) async-start(bf16[16,200,128]{2,1,0:T(8,128)(2,1)} %pad_maximum_fusion), calls=%async_computation.2 | async-start | bytes 1638400 | tf_op jit(solution)/shard_map/all_to_all | solution.py:523
  124.1 2.6 %fusion.1 = f32[2048]{0:T(1024)S(1)} fusion(bf16[2048,768]{1,0:T(8,128)(2,1)} %all-gather.5.cloned.1.call-done), kind=kLoop, calls=%fused_computation.3 | loop fusion | flops 4716544 | bytes 3153920 | tf_op jit(solution)/shard_map/reduce_sum | solution.py:525
  126.7 3.9 %fusion.4.left_ref = bf16[2048,768]{1,0:T(8,128)(2,1)} fusion(bf16[2048,768]{1,0:T(8,128)(2,1)} %all-gather.3.cloned.1.call-done, bf16[2048,768]{1,0:T(8,128)(2,1)} %all-gather.5.cloned.1.call-done, f32[768]{0:T(1024)S(1)} %copy-done.41, f32[2048]{0:T(1024)S(1)} %add_rsqrt_fusion, pred[]{:T(512)S(6)} %eq.69), kind=kLoop, calls=%fused_computation.6 | loop fusion | flops 7864320 | bytes 9448449 | tf_op jit(solution)/shard_map/jit(_where)/select_n | solution.py:528
  130.6 6.9 %all-to-all-done.2.late_ref = bf16[16,200,128]{2,1,0:T(8,128)(2,1)S(1)} async-done(((bf16[16,200,128]{2,1,0:T(8,128)(2,1)}), bf16[16,200,128]{2,1,0:T(8,128)(2,1)S(1)}, u32[]{:S(2)}, u32[]{:S(2)}) %all-to-all-start.2) | async-done | bytes 819232 | tf_op jit(solution)/shard_map/all_to_all | solution.py:523
  137.5 1.9 copy-done.1
  139.4 0.9 grad_block.1
  140.3 0.9 collective-permute-start.2
  141.2 8.6 %collective-permute-done.2.got_ref = bf16[584,128]{1,0:T(8,128)(2,1)S(1)} collective-permute-done((bf16[584,128]{1,0:T(8,128)(2,1)S(1)}, bf16[584,128]{1,0:T(8,128)(2,1)S(1)}, u32[]{:S(2)}, u32[]{:S(2)}) %collective-permute-start.2) | collective-permute-done | bytes 149536 | tf_op jit(solution)/shard_map/ppermute | solution.py:63
  149.9 7.2 %collective-permute-done.3 = bf16[584,128]{1,0:T(8,128)(2,1)S(1)} collective-permute-done((bf16[584,128]{1,0:T(8,128)(2,1)S(1)}, bf16[584,128]{1,0:T(8,128)(2,1)S(1)}, u32[]{:S(2)}, u32[]{:S(2)}) %collective-permute-start.3) | collective-permute-done | bytes 149536 | tf_op jit(solution)/shard_map/ppermute | solution.py:63
  157.4 1.8 collective-permute-start.4
  159.2 6.8 %collective-permute-done.6 = bf16[2,584,128]{2,1,0:T(8,128)(2,1)S(1)} collective-permute-done((bf16[2,584,128]{2,1,0:T(8,128)(2,1)S(1)}, bf16[2,584,128]{2,1,0:T(8,128)(2,1)S(1)}, u32[]{:S(2)}, u32[]{:S(2)}) %collective-permute-start.6) | collective-permute-done | bytes 299040 | tf_op jit(solution)/shard_map/ppermute | solution.py:63
  166.0 2.0 collective-permute-start.7
  168.8 7.3 %collective-permute-done.7 = bf16[2,584,128]{2,1,0:T(8,128)(2,1)S(1)} collective-permute-done((bf16[2,584,128]{2,1,0:T(8,128)(2,1)S(1)}, bf16[2,584,128]{2,1,0:T(8,128)(2,1)S(1)}, u32[]{:S(2)}, u32[]{:S(2)}) %collective-permute-start.7) | collective-permute-done | bytes 299040 | tf_op jit(solution)/shard_map/ppermute | solution.py:63
  176.1 2.1 collective-permute-start.8
  178.4 2.6 %fusion.27 = (bf16[128,768]{1,0:T(8,128)(2,1)}, bf16[128,768]{1,0:T(8,128)(2,1)}) fusion(bf16[128,768]{1,0:T(8,128)(2,1)S(1)} %copy-done.10, f32[128,768]{1,0:T(8,128)} %get-tuple-element.95, f32[128]{0:T(128)S(1)} %broadcast_multiply_fusion, f32[768]{0:T(1024)S(1)} %copy-done.41, f32[128]{0:T(128)S(1)} %copy-done.56, f32[128]{0:T(128)S(1)} %copy-done.69, ...), kind=kLoop, calls=%fused_computation.65 | loop fusion | flops 2162688 | bytes 2368000 | tf_op jit(solution)/shard_map/convert_element_type | solution.py:510
  181.5 5.8 %collective-permute-done.5.refs_1_ = bf16[2,2,584,128]{3,2,1,0:T(8,128)(2,1)S(1)} collective-permute-done((bf16[2,2,584,128]{3,2,1,0:T(8,128)(2,1)S(1)}, bf16[2,2,584,128]{3,2,1,0:T(8,128)(2,1)S(1)}, u32[]{:S(2)}, u32[]{:S(2)}) %collective-permute-start.5) | collective-permute-done | bytes 598048 | tf_op jit(solution)/shard_map/ppermute | solution.py:63
  187.3 1.4 collective-permute-done.8.refs_3_
  188.7 2.9 %add_bitcast_fusion.1 = f32[1,768,768]{2,1,0:T(8,128)} fusion(f32[768,768]{1,0:T(8,128)S(1)} %copy-done.26, bf16[768,768]{1,0:T(8,128)(2,1)} %collective-permute-done.13), kind=kLoop, calls=%fused_computation.8 | loop fusion | flops 1179648 | bytes 5898240 | tf_op jit(solution)/shard_map/broadcast_in_dim | solution.py:550
  191.6 2.9 %add_bitcast_fusion = f32[1,768,768]{2,1,0:T(8,128)} fusion(f32[768,768]{1,0:T(8,128)S(1)} %copy-done.25, bf16[768,768]{1,0:T(8,128)(2,1)} %collective-permute-done.14), kind=kLoop, calls=%fused_computation.7 | loop fusion | flops 1179648 | bytes 5898240 | tf_op jit(solution)/shard_map/broadcast_in_dim | solution.py:551
  194.5 10.4 %assemble.1 = (f32[768,768]{1,0:T(8,128)}, f32[768,768]{1,0:T(8,128)}, f32[768,768]{1,0:T(8,128)}, f32[768,768]{1,0:T(8,128)}, f32[4,4,4,128]{3,2,1,0:T(4,128)S(1)}) custom-call(s32[5]{0:T(128)S(1)} %stack.50.bits_ref, bf16[2,2,584,128]{3,2,1,0:T(8,128)(2,1)S(1)} %pad_maximum_fusion.1.refs_0_, bf16[2,2,584,128]{3,2,1,0:T(8,128)(2,1)S(1)} %collective-permute-done.5.refs_1_, ...), custom_call_target="tpu_custom_call" | custom-call | flops 603979776 | bytes 14155776 | tf_op jit(solution)/shard_map/assemble/pallas_call | solution.py:305
  (225 shorter events, 22.9 us)
Async XLA Ops:
  7.2 6.8 %copy-start = (bf16[768,768]{1,0:T(8,128)(2,1)S(1)}, bf16[768,768]{1,0:T(8,128)(2,1)}, u32[]{:S(2)}) copy-start(bf16[768,768]{1,0:T(8,128)(2,1)} %param.19) | copy-start | bytes 3538948
  7.2 6.2 %copy-start.9 = (bf16[128,768]{1,0:T(8,128)(2,1)S(1)}, bf16[128,768]{1,0:T(8,128)(2,1)}, u32[]{:S(2)}) copy-start(bf16[128,768]{1,0:T(8,128)(2,1)} %param.15) | copy-start | bytes 589828
  7.2 6.2 %copy-start.41 = (f32[768]{0:T(1024)S(1)}, f32[768]{0:T(1024)}, u32[]{:S(2)}) copy-start(f32[768]{0:T(1024)} %param.16) | copy-start | bytes 9220
  7.2 6.2 %copy-start.16 = (bf16[768,768]{1,0:T(8,128)(2,1)S(1)}, bf16[768,768]{1,0:T(8,128)(2,1)}, u32[]{:S(2)}) copy-start(bf16[768,768]{1,0:T(8,128)(2,1)} %param.18) | copy-start | bytes 3538948
  7.2 116.9 %all-gather.5.cloned.1.call-start = ((), (), s32[]{:S(2)}) async-start(), calls=%async_computation.4 | async-start | bytes 3342336 | tf_op jit(solution)/shard_map/all_gather | solution.py:383
  9.1 6.6 %copy-start.38 = (s32[128,128]{0,1:T(8,128)}, s32[128,128]{0,1:T(8,128)S(1)}, u32[]{:S(2)}) copy-start(s32[128,128]{0,1:T(8,128)S(1)} %fusion.42) | copy-start | bytes 196612
  9.8 4.2 %copy-start.54 = (f32[128]{0:T(128)}, f32[128]{0:T(128)S(1)}, u32[]{:S(2)}) copy-start(f32[128]{0:T(128)S(1)} %add_rsqrt_fusion.2) | copy-start | bytes 1540
  13.4 3.1 %copy-start.27 = (bf16[128,768]{0,1:T(8,128)(2,1)}, bf16[128,768]{0,1:T(8,128)(2,1)S(1)}, u32[]{:S(2)}) copy-start(bf16[128,768]{0,1:T(8,128)(2,1)S(1)} %copy.51) | copy-start | bytes 589828
  14.0 3.0 %copy-start.29 = (bf16[128,768]{0,1:T(8,128)(2,1)}, bf16[128,768]{0,1:T(8,128)(2,1)S(1)}, u32[]{:S(2)}) copy-start(bf16[128,768]{0,1:T(8,128)(2,1)S(1)} %copy.52) | copy-start | bytes 589828
  17.0 3.1 %copy-start.19 = (f32[12,128,128]{1,2,0:T(8,128)}, f32[12,128,128]{1,2,0:T(8,128)S(1)}, u32[]{:S(2)}) copy-start(f32[12,128,128]{1,2,0:T(8,128)S(1)} %fusion.10) | copy-start | bytes 2359300
  20.1 2.4 %copy-start.34 = (bf16[12,64,128]{2,1,0:T(8,128)(2,1)}, bf16[12,64,128]{2,1,0:T(8,128)(2,1)S(1)}, u32[]{:S(2)}) copy-start(bf16[12,64,128]{2,1,0:T(8,128)(2,1)S(1)} %convolution_convert_fusion.4) | copy-start | bytes 589828
  20.2 2.3 %copy-start.21 = (bf16[128,768]{1,0:T(8,128)(2,1)S(1)}, bf16[128,768]{1,0:T(8,128)(2,1)}, u32[]{:S(2)}) copy-start(bf16[128,768]{1,0:T(8,128)(2,1)} %param.28) | copy-start | bytes 589828
  22.9 35.4 %copy-start.2 = (s32[640,2]{1,0:T(8,128)S(1)}, s32[640,2]{1,0:T(8,128)}, u32[]{:S(2)}) copy-start(s32[640,2]{1,0:T(8,128)} %constant.91.clone.order_ref) | copy-start | bytes 15364
  24.0 34.4 %all-to-all-start = ((bf16[16,40,768]{2,1,0:T(8,128)(2,1)}), bf16[16,40,768]{2,1,0:T(8,128)(2,1)S(1)}, u32[]{:S(2)}, u32[]{:S(2)}) async-start(bf16[16,40,768]{2,1,0:T(8,128)(2,1)} %bitcast.11), calls=%async_computation | async-start | bytes 1966080 | tf_op jit(solution)/shard_map/all_to_all | solution.py:445
  32.3 4.1 %collective-permute-start = (bf16[768,768]{1,0:T(8,128)(2,1)}, bf16[768,768]{1,0:T(8,128)(2,1)S(1)}, u32[]{:S(2)}, u32[]{:S(2)}) collective-permute-start(bf16[768,768]{1,0:T(8,128)(2,1)} %bitcast.144), channel_id=1, source_target_pairs={{0,1},{1,0},{2,3},{3,2},{4,5},{5,4},{6,7},{7,6},{8,9},{9,8},{10,11... | collective-permute-start | bytes 3538952 | tf_op jit(solution)/shard_map/ppermute | solution.py:63
  32.4 5.2 %collective-permute-start.1 = (bf16[768,768]{1,0:T(8,128)(2,1)}, bf16[768,768]{1,0:T(8,128)(2,1)}, u32[]{:S(2)}, u32[]{:S(2)}) collective-permute-start(bf16[768,768]{1,0:T(8,128)(2,1)} %bitcast.146), channel_id=1, source_target_pairs={{0,1},{1,0},{2,3},{3,2},{4,5},{5,4},{6,7},{7,6},{8,9},{9,8},{10,11... | collective-permute-start | bytes 3538952 | tf_op jit(solution)/shard_map/ppermute | solution.py:63
  69.3 4.7 %copy-start.35 = (bf16[12,64,128]{2,1,0:T(8,128)(2,1)S(1)}, bf16[12,64,128]{2,1,0:T(8,128)(2,1)}, u32[]{:S(2)}) copy-start(bf16[12,64,128]{2,1,0:T(8,128)(2,1)} %copy-done.34) | copy-start | bytes 589828
  69.3 5.6 %copy-start.4 = (bf16[2,320,768]{2,1,0:T(8,128)(2,1)S(1)}, bf16[2,320,768]{2,1,0:T(8,128)(2,1)}, u32[]{:S(2)}) copy-start(bf16[2,320,768]{2,1,0:T(8,128)(2,1)} %copy-done.3) | copy-start | bytes 2949124
  69.3 30.3 %all-to-all-start.1 = ((bf16[16,40,768]{2,1,0:T(8,128)(2,1)}), bf16[16,40,768]{2,1,0:T(8,128)(2,1)}, u32[]{:S(2)}, u32[]{:S(2)}) async-start(bf16[16,40,768]{2,1,0:T(8,128)(2,1)} %bitcast.15), calls=%async_computation.1 | async-start | bytes 1966080 | tf_op jit(solution)/shard_map/all_to_all | solution.py:454
  73.7 53.0 %all-gather.3.cloned.1.call-start = ((), (), s32[]{:S(2)}) async-start(), calls=%async_computation.3 | async-start | bytes 3342336 | tf_op jit(solution)/shard_map/all_gather | solution.py:416
  101.1 3.1 %copy-start.12 = (f32[128,768]{1,0:T(8,128)S(1)}, f32[128,768]{1,0:T(8,128)}, u32[]{:S(2)}) copy-start(f32[128,768]{1,0:T(8,128)} %copy-done.11) | copy-start | bytes 1179652
  101.1 3.1 %copy-start.45 = (bf16[768,8]{0,1:T(8,128)(2,1)S(1)}, bf16[768,8]{0,1:T(8,128)(2,1)}, u32[]{:S(2)}) copy-start(bf16[768,8]{0,1:T(8,128)(2,1)} %param.23) | copy-start | bytes 36868
  101.1 3.1 %copy-start.60 = (f32[128]{0:T(128)S(1)}, f32[128]{0:T(128)}, u32[]{:S(2)}) copy-start(f32[128]{0:T(128)} %copy-done.59) | copy-start | bytes 1540
  112.6 2.5 %copy-start.15 = (bf16[768,768]{1,0:T(8,128)(2,1)S(1)}, bf16[768,768]{1,0:T(8,128)(2,1)}, u32[]{:S(2)}) copy-start(bf16[768,768]{1,0:T(8,128)(2,1)} %param.17) | copy-start | bytes 3538948
  115.2 2.2 %copy-start.10 = (bf16[128,768]{1,0:T(8,128)(2,1)S(1)}, bf16[128,768]{1,0:T(8,128)(2,1)}, u32[]{:S(2)}) copy-start(bf16[128,768]{1,0:T(8,128)(2,1)} %param.15) | copy-start | bytes 589828
  115.2 2.2 %copy-start.37 = (bf16[12,64,128]{2,1,0:T(8,128)(2,1)S(1)}, bf16[12,64,128]{2,1,0:T(8,128)(2,1)}, u32[]{:S(2)}) copy-start(bf16[12,64,128]{2,1,0:T(8,128)(2,1)} %copy-done.36) | copy-start | bytes 589828
  115.2 2.2 %copy-start.55 = (f32[128]{0:T(128)S(1)}, f32[128]{0:T(128)}, u32[]{:S(2)}) copy-start(f32[128]{0:T(128)} %copy-done.54) | copy-start | bytes 1540
  120.2 17.3 %all-to-all-start.2 = ((bf16[16,200,128]{2,1,0:T(8,128)(2,1)}), bf16[16,200,128]{2,1,0:T(8,128)(2,1)S(1)}, u32[]{:S(2)}, u32[]{:S(2)}) async-start(bf16[16,200,128]{2,1,0:T(8,128)(2,1)} %pad_maximum_fusion), calls=%async_computation.2 | async-start | bytes 1638400 | tf_op jit(solution)/shard_map/all_to_all | solution.py:523
  140.3 9.6 %collective-permute-start.2 = (bf16[584,128]{1,0:T(8,128)(2,1)S(1)}, bf16[584,128]{1,0:T(8,128)(2,1)S(1)}, u32[]{:S(2)}, u32[]{:S(2)}) collective-permute-start(bf16[584,128]{1,0:T(8,128)(2,1)S(1)} %get-tuple-element.50), channel_id=1, source_target_pairs={{0,16},{16,0},{1,17},{17,1},{2,18},{18,2},{3,19},{19,3},{4,20},{20... | collective-permute-start | bytes 448520 | tf_op jit(solution)/shard_map/ppermute | solution.py:63
  149.9 7.3 %collective-permute-start.3 = (bf16[584,128]{1,0:T(8,128)(2,1)S(1)}, bf16[584,128]{1,0:T(8,128)(2,1)S(1)}, u32[]{:S(2)}, u32[]{:S(2)}) collective-permute-start(bf16[584,128]{1,0:T(8,128)(2,1)S(1)} %share.1), channel_id=1, source_target_pairs={{0,16},{16,0},{1,17},{17,1},{2,18},{18,2},{3,19},{19,3},{4,20},{20... | collective-permute-start | bytes 448520 | tf_op jit(solution)/shard_map/ppermute | solution.py:63
  157.2 21.2 %copy-start.70 = (f32[128]{0:T(128)S(1)}, f32[128]{0:T(128)}, u32[]{:S(2)}) copy-start(f32[128]{0:T(128)} %get-tuple-element.75) | copy-start | bytes 1540
  157.2 21.2 %copy-start.56 = (f32[128]{0:T(128)S(1)}, f32[128]{0:T(128)}, u32[]{:S(2)}) copy-start(f32[128]{0:T(128)} %copy-done.54) | copy-start | bytes 1540
  157.2 21.2 %copy-start.61 = (f32[128]{0:T(128)S(1)}, f32[128]{0:T(128)}, u32[]{:S(2)}) copy-start(f32[128]{0:T(128)} %copy-done.59) | copy-start | bytes 1540
  157.2 21.2 %copy-start.67 = (f32[128]{0:T(128)S(1)}, f32[128]{0:T(128)}, u32[]{:S(2)}) copy-start(f32[128]{0:T(128)} %copy-done.66) | copy-start | bytes 1540
  157.2 21.2 %copy-start.69 = (f32[128]{0:T(128)S(1)}, f32[128]{0:T(128)}, u32[]{:S(2)}) copy-start(f32[128]{0:T(128)} %copy-done.68) | copy-start | bytes 1540
  157.3 8.8 %collective-permute-start.6 = (bf16[2,584,128]{2,1,0:T(8,128)(2,1)S(1)}, bf16[2,584,128]{2,1,0:T(8,128)(2,1)S(1)}, u32[]{:S(2)}, u32[]{:S(2)}) collective-permute-start(bf16[2,584,128]{2,1,0:T(8,128)(2,1)S(1)} %get-tuple-element.81), channel_id=1, source_target_pairs={{0,8},{8,0},{1,9},{9,1},{2,10},{10,2},{3,11},{11,3},{4,12},{12,4},... | collective-permute-start | bytes 897032 | tf_op jit(solution)/shard_map/ppermute | solution.py:63
  157.3 23.6 %collective-permute-start.13 = (bf16[768,768]{1,0:T(8,128)(2,1)}, bf16[768,768]{1,0:T(8,128)(2,1)}, u32[]{:S(2)}, u32[]{:S(2)}) collective-permute-start(bf16[768,768]{1,0:T(8,128)(2,1)} %get-tuple-element.57), channel_id=1, source_target_pairs={{0,1},{1,0},{2,3},{3,2},{4,5},{5,4},{6,7},{7,6},{8,9},{9,8},{10,11... | collective-permute-start | bytes 3538952 | tf_op jit(solution)/shard_map/ppermute | solution.py:63
  157.4 10.7 %collective-permute-start.4 = (bf16[2,584,128]{2,1,0:T(8,128)(2,1)S(1)}, bf16[2,584,128]{2,1,0:T(8,128)(2,1)S(1)}, u32[]{:S(2)}, u32[]{:S(2)}) collective-permute-start(bf16[2,584,128]{2,1,0:T(8,128)(2,1)S(1)} %get-tuple-element.81), channel_id=1, source_target_pairs={{0,2},{2,0},{1,3},{3,1},{4,6},{6,4},{5,7},{7,5},{8,10},{10,8},{9,1... | collective-permute-start | bytes 897032 | tf_op jit(solution)/shard_map/ppermute | solution.py:63
  166.0 10.1 %collective-permute-start.7 = (bf16[2,584,128]{2,1,0:T(8,128)(2,1)S(1)}, bf16[2,584,128]{2,1,0:T(8,128)(2,1)S(1)}, u32[]{:S(2)}, u32[]{:S(2)}) collective-permute-start(bf16[2,584,128]{2,1,0:T(8,128)(2,1)S(1)} %collective-permute-done.6), channel_id=1, source_target_pairs={{0,4},{4,0},{1,5},{5,1},{2,6},{6,2},{3,7},{7,3},{8,12},{12,8},{9,1... | collective-permute-start | bytes 897032 | tf_op jit(solution)/shard_map/ppermute | solution.py:63
  168.1 23.5 %collective-permute-start.14 = (bf16[768,768]{1,0:T(8,128)(2,1)}, bf16[768,768]{1,0:T(8,128)(2,1)}, u32[]{:S(2)}, u32[]{:S(2)}) collective-permute-start(bf16[768,768]{1,0:T(8,128)(2,1)} %get-tuple-element.59), channel_id=1, source_target_pairs={{0,1},{1,0},{2,3},{3,2},{4,5},{5,4},{6,7},{7,6},{8,9},{9,8},{10,11... | collective-permute-start | bytes 3538952 | tf_op jit(solution)/shard_map/ppermute | solution.py:63
  168.1 19.2 %collective-permute-start.5 = (bf16[2,2,584,128]{3,2,1,0:T(8,128)(2,1)S(1)}, bf16[2,2,584,128]{3,2,1,0:T(8,128)(2,1)S(1)}, u32[]{:S(2)}, u32[]{:S(2)}) collective-permute-start(bf16[2,2,584,128]{3,2,1,0:T(8,128)(2,1)S(1)} %pad_maximum_fusion.1.refs_0_), channel_id=1, source_target_pairs={{0,4},{4,0},{1,5},{5,1},{2,6},{6,2},{3,7},{7,3},{8,12},{12,8},{9,1... | collective-permute-start | bytes 1794056 | tf_op jit(solution)/shard_map/ppermute | solution.py:63
  176.1 12.5 %collective-permute-start.8 = (bf16[2,2,584,128]{3,2,1,0:T(8,128)(2,1)S(1)}, bf16[2,2,584,128]{3,2,1,0:T(8,128)(2,1)}, u32[]{:S(2)}, u32[]{:S(2)}) collective-permute-start(bf16[2,2,584,128]{3,2,1,0:T(8,128)(2,1)S(1)} %pad_maximum_fusion.2.refs_2_), channel_id=1, source_target_pairs={{0,2},{2,0},{1,3},{3,1},{4,6},{6,4},{5,7},{7,5},{8,10},{10,8},{9,1... | collective-permute-start | bytes 1794056 | tf_op jit(solution)/shard_map/ppermute | solution.py:63
  178.3 10.3 %copy-start.26 = (f32[768,768]{1,0:T(8,128)S(1)}, f32[768,768]{1,0:T(8,128)}, u32[]{:S(2)}) copy-start(f32[768,768]{1,0:T(8,128)} %get-tuple-element.56) | copy-start | bytes 7077892
  180.9 10.6 %copy-start.25 = (f32[768,768]{1,0:T(8,128)S(1)}, f32[768,768]{1,0:T(8,128)}, u32[]{:S(2)}) copy-start(f32[768,768]{1,0:T(8,128)} %get-tuple-element.58) | copy-start | bytes 7077892
  181.0 13.5 %collective-permute-start.9 = (bf16[2,2,584,128]{3,2,1,0:T(8,128)(2,1)S(1)}, bf16[2,2,584,128]{3,2,1,0:T(8,128)(2,1)S(1)}, u32[]{:S(2)}, u32[]{:S(2)}) collective-permute-start(bf16[2,2,584,128]{3,2,1,0:T(8,128)(2,1)S(1)} %pad_maximum_fusion.1.refs_0_), channel_id=1, source_target_pairs={{0,1},{1,0},{2,3},{3,2},{4,5},{5,4},{6,7},{7,6},{8,9},{9,8},{10,11... | collective-permute-start | bytes 1794056 | tf_op jit(solution)/shard_map/ppermute | solution.py:63
  181.0 13.5 %collective-permute-start.11 = (bf16[2,2,584,128]{3,2,1,0:T(8,128)(2,1)S(1)}, bf16[2,2,584,128]{3,2,1,0:T(8,128)(2,1)S(1)}, u32[]{:S(2)}, u32[]{:S(2)}) collective-permute-start(bf16[2,2,584,128]{3,2,1,0:T(8,128)(2,1)S(1)} %pad_maximum_fusion.2.refs_2_), channel_id=1, source_target_pairs={{0,1},{1,0},{2,3},{3,2},{4,5},{5,4},{6,7},{7,6},{8,9},{9,8},{10,11... | collective-permute-start | bytes 1794056 | tf_op jit(solution)/shard_map/ppermute | solution.py:63
  187.3 7.2 %collective-permute-start.10 = (bf16[2,2,584,128]{3,2,1,0:T(8,128)(2,1)S(1)}, bf16[2,2,584,128]{3,2,1,0:T(8,128)(2,1)S(1)}, u32[]{:S(2)}, u32[]{:S(2)}) collective-permute-start(bf16[2,2,584,128]{3,2,1,0:T(8,128)(2,1)S(1)} %collective-permute-done.5.refs_1_), channel_id=1, source_target_pairs={{0,1},{1,0},{2,3},{3,2},{4,5},{5,4},{6,7},{7,6},{8,9},{9,8},{10,11... | collective-permute-start | bytes 1794056 | tf_op jit(solution)/shard_map/ppermute | solution.py:63
  188.7 5.8 %collective-permute-start.12 = (bf16[2,2,584,128]{3,2,1,0:T(8,128)(2,1)}, bf16[2,2,584,128]{3,2,1,0:T(8,128)(2,1)S(1)}, u32[]{:S(2)}, u32[]{:S(2)}) collective-permute-start(bf16[2,2,584,128]{3,2,1,0:T(8,128)(2,1)} %collective-permute-done.8.refs_3_), channel_id=1, source_target_pairs={{0,1},{1,0},{2,3},{3,2},{4,5},{5,4},{6,7},{7,6},{8,9},{9,8},{10,11... | collective-permute-start | bytes 1794056 | tf_op jit(solution)/shard_map/ppermute | solution.py:63
  (44 other events, 56.2 us)
Sparse Core Ops, SparseCore 0:
  9.7 47.2 all-gather.4
  76.2 38.2 all-gather.2

commit v3 on v2

v3 whole, which is shorter than its diff:
```python
import functools

import jax
import jax.numpy as jnp
import numpy as np
from jax import lax
from jax.experimental import pallas as pl
from jax.experimental.pallas import tpu as pltpu
from jax.sharding import Mesh
from jax.sharding import PartitionSpec as P

HEADS = 12
HEAD_DIM = 64
BUCKETS = 32
LANES = 128
VMEM_MIB = 63

norm_eps = 1e-06
score_scale = 0.125
masked_score = -1e30
far_limits = (11, 16, 22, 32, 45, 64, 90)

EXPERT_AXES = ("eh", "em", "ey", "dx")
GROUP_AXES = ("em", "ey", "dx", "dc")
TOKEN_AXES = ("eh", "em", "ey", "dx", "dc")


def bucket_of(offset):
    distance = jnp.abs(offset)
    far_bucket = jnp.full(distance.shape, 8, jnp.int32)
    for limit_value in far_limits:
        far_bucket = far_bucket + (distance >= limit_value).astype(jnp.int32)
    near_bucket = jnp.where(distance < 8, distance, far_bucket)
    return near_bucket + 16 * (offset > 0).astype(jnp.int32)


def dot_last(left_side, right_side):
    return lax.dot_general(
        left_side, right_side, (((1,), (1,)), ((), ())), preferred_element_type=jnp.float32
    )


def dot_first(left_side, right_side):
    return lax.dot_general(
        left_side, right_side, (((0,), (0,)), ((), ())), preferred_element_type=jnp.float32
    )


def norm_backward(values, factor, gain, grad_normed):
    scaled = gain * grad_normed
    grad_gain = jnp.sum(grad_normed * values * factor, axis=0, keepdims=True)
    grad_values = factor * scaled - values * factor * factor * factor * jnp.mean(
        scaled * values, axis=-1, keepdims=True
    )
    return (grad_values, grad_gain)


def swap(array, axis):
    return lax.ppermute(array, axis, perm=[(0, 1), (1, 0)])


def whole_spec():
    return pl.BlockSpec(memory_space=pltpu.VMEM)


def any_spec():
    return pl.BlockSpec(memory_space=pl.ANY)


def params(mib):
    return pltpu.CompilerParams(vmem_limit_bytes=mib * 1024 * 1024)


def cost(flops, moved):
    return pl.CostEstimate(flops=flops, bytes_accessed=moved, transcendentals=0)


def shaped(dims, kind):
    return jax.ShapeDtypeStruct(dims, kind)


class Arriving:
    def __init__(self, source, held, sem):
        self.held, self.pending = held, pltpu.make_async_copy(source, held, sem)
        self.pending.start()

    def ref(self):
        if self.pending is not None:
            self.pending.wait()
            self.pending = None
        return self.held

    def __getitem__(self, index):
        return self.ref()[index]

    @property
    def shape(self):
        return self.held.shape


class Leaving:
    def __init__(self, held, target, sem):
        self.held, self.copy = held, pltpu.make_async_copy(held, target, sem)

    def __setitem__(self, index, value):
        self.held[index] = value

    def __getitem__(self, index):
        return self.held[index]

    @property
    def shape(self):
        return self.held.shape

    def send(self):
        self.copy.start()

    def finish(self):
        self.copy.wait()


class Staying:
    def __init__(self, held):
        self.held = held

    def __setitem__(self, index, value):
        self.held[index] = value

    def __getitem__(self, index):
        return self.held[index]

    @property
    def shape(self):
        return self.held.shape

    def send(self):
        pass


def staged(
    kernel,
    name,
    scalars,
    inputs,
    outputs,
    scratch,
    flops,
    moved,
    residents=(),
    kept=(),
    mib=VMEM_MIB,
):
    counts = (len(scalars), len(residents), len(inputs), len(kept), len(outputs))

    def body(*refs):
        refs = list(refs)
        take = lambda count: [refs.pop(0) for _ in range(count)]
        numbers, there, sources, staying, targets = [take(count) for count in counts]
        held_in, held_out = take(counts[2]), take(counts[4])
        sems = refs.pop(0)
        arriving = [
            Arriving(source, held, sems.at[i])
            for i, (source, held) in enumerate(zip(sources, held_in))
        ]
        leaving = [
            Leaving(held, target, sems.at[counts[2] + i])
            for i, (held, target) in enumerate(zip(held_out, targets))
        ]
        kernel(numbers, there + arriving, [Staying(ref) for ref in staying] + leaving, refs)
        for copy in leaving:
            copy.finish()

    return pl.pallas_call(
        body,
        out_shape=tuple(kept) + tuple(outputs),
        in_specs=[pl.BlockSpec(memory_space=pltpu.SMEM)] * counts[0]
        + [whole_spec()] * counts[1]
        + [any_spec()] * counts[2],
        out_specs=(whole_spec(),) * counts[3] + (any_spec(),) * counts[4],
        scratch_shapes=[pltpu.VMEM(x.shape, x.dtype) for x in inputs]
        + [pltpu.VMEM(x.shape, x.dtype) for x in outputs]
        + [pltpu.SemaphoreType.DMA((max(1, counts[2] + counts[4]),))]
        + list(scratch),
        compiler_params=params(mib),
        cost_estimate=cost(flops, moved),
        name=name,
    )(*scalars, *residents, *inputs)


def row_of(ref):
    return jnp.concatenate([ref[i : i + 1] for i in range(ref.shape[0])], axis=1)


def rms_factor(values):
    return lax.rsqrt(jnp.mean(values * values, axis=-1, keepdims=True) + norm_eps)


def pair_masks(rows):
    first = lax.broadcasted_iota(jnp.int32, (rows, LANES), 1) < HEAD_DIM
    return first


def stacked_heads(pair, first):
    zero = jnp.zeros_like(pair)
    return jnp.concatenate([jnp.where(first, pair, zero), jnp.where(first, zero, pair)], axis=0)


def offset_buckets(rows, length):
    lane = lax.broadcasted_iota(jnp.int32, (rows, 2 * length), 1)
    return bucket_of(jnp.where(lane < length, lane, lane - 2 * length))


def forward_kernel(numbers, inputs, outputs, scratch):
    (count_ref,) = numbers
    (
        tokens_ref,
        gain_ref,
        query_ref,
        key_ref,
        value_ref,
        bias_ref,
        routes_ref,
        output_ref,
        gain_two_ref,
        router_ref,
        cotangent_ref,
    ) = inputs
    (
        outgoing_ref,
        attended_ref,
        q_ref,
        k_ref,
        v_ref,
        probs_ref,
        hidden_ref,
        router_probs_ref,
        choose_ref,
        slot_ref,
    ) = outputs
    low = jnp.bfloat16
    length, width = tokens_ref.shape
    experts = router_ref.shape[0]
    capacity = outgoing_ref.shape[2] // 2
    inputs = tokens_ref[...].astype(jnp.float32)
    normed = (inputs * rms_factor(inputs) * row_of(gain_ref)).astype(low)
    for weight, out in ((query_ref, q_ref), (key_ref, k_ref), (value_ref, v_ref)):
        out[...] = jnp.dot(normed, weight[...], preferred_element_type=jnp.float32).astype(low)
        out.send()

    buckets = offset_buckets(BUCKETS, length)
    hot = buckets == lax.broadcasted_iota(jnp.int32, buckets.shape, 0)
    table = jnp.dot(
        bias_ref[...],
        jnp.where(hot, 1.0, 0.0),
        precision=lax.Precision.HIGHEST,
        preferred_element_type=jnp.float32,
    )
    live = lax.broadcasted_iota(jnp.int32, (length, length), 1) < count_ref[0]
    first = pair_masks(length)
    for pair in range(HEADS // 2):
        lanes = slice(pair * LANES, (pair + 1) * LANES)
        scores = dot_last(q_ref[:, lanes], stacked_heads(k_ref[:, lanes], first)) * score_scale
        weights = []
        for head in range(2):
            row = table[2 * pair + head : 2 * pair + head + 1]
            field = pltpu.roll(
                jnp.broadcast_to(row, (length, 2 * length)), 0, 1, stride=1, stride_axis=0
            )
            own = scores[:, head * length : (head + 1) * length] + field[:, :length]
            own = jnp.where(live, own, masked_score)
            own = jnp.exp(own - jnp.max(own, axis=1, keepdims=True))
            own = own / jnp.sum(own, axis=1, keepdims=True)
            probs_ref[pair, :, head * length : (head + 1) * length] = own
            weights.append(own.astype(low))
        both = jnp.concatenate(weights, axis=1)
        attended_ref[:, lanes] = jnp.dot(
            both, stacked_heads(v_ref[:, lanes], first), preferred_element_type=jnp.float32
        ).astype(low)

    attended_ref.send()
    probs_ref.send()
    hidden = inputs + jnp.dot(
        attended_ref[...], output_ref[...], preferred_element_type=jnp.float32
    )
    hidden_ref[...] = hidden
    hidden_ref.send()
    normed_two = (hidden * rms_factor(hidden) * row_of(gain_two_ref)).astype(low)
    logits = dot_last(normed_two, router_ref[...])
    router_probs = jnp.exp(logits - jnp.max(logits, axis=1, keepdims=True))
    router_probs = router_probs / jnp.sum(router_probs, axis=1, keepdims=True)
    router_probs_ref[...] = router_probs
    router_probs_ref.send()

    lane = lax.broadcasted_iota(jnp.int32, (length, length), 1)
    place = lax.broadcasted_iota(jnp.int32, (length, length), 0)
    routes = routes_ref[...]
    chosen = routes == lax.broadcasted_iota(jnp.int32, (experts, length), 0)
    chosen = jnp.where(chosen, 1.0, 0.0)
    alive = lax.broadcasted_iota(jnp.int32, (1, length), 1) < count_ref[0]
    before = jnp.where(place <= lane, 1.0, 0.0).astype(low)
    running = jnp.dot(
        (chosen * jnp.where(alive, 1.0, 0.0)).astype(low),
        before,
        preferred_element_type=jnp.float32,
    )
    slot = jnp.sum(running * chosen, axis=0, keepdims=True).astype(jnp.int32) - 1
    kept = alive & (slot < capacity)
    column = jnp.where(kept, routes * (2 * capacity) + slot, -2 * capacity)
    slot_ref[...] = column
    slot_ref.send()
    unit = jnp.where(place == lane, 1.0, 0.0).astype(low)
    choose = dot_last(unit, chosen.astype(low))
    choose_ref[...] = choose
    choose_ref.send()
    gate = jnp.sum(router_probs * choose, axis=1, keepdims=True)
    scaled = (gate * cotangent_ref[...].astype(jnp.float32)).astype(low)
    row = lax.broadcasted_iota(jnp.int32, (experts * 2 * capacity, length), 0)
    spread = jnp.concatenate(
        [
            jnp.where(row == column, 1.0, 0.0).astype(low),
            jnp.where(row == column + capacity, 1.0, 0.0).astype(low),
        ],
        axis=1,
    )
    packed = jnp.dot(
        spread,
        jnp.concatenate([normed_two, scaled], axis=0),
        preferred_element_type=jnp.float32,
    )
    for expert in range(experts):
        rows = packed[expert * 2 * capacity : (expert + 1) * 2 * capacity].astype(low)
        outgoing_ref[expert, 0] = rows
        outgoing_ref[expert, 1] = rows
    outgoing_ref.send()


def forward_of(count, tokens, gain, weights, bias, gain_two, router, routes, cotangent, capacity):
    length, width = tokens.shape
    experts = router.shape[0]
    low = jnp.bfloat16
    outputs = (
        shaped((experts, 2, 2 * capacity, width), low),
        shaped((length, width), low),
        shaped((length, width), low),
        shaped((length, width), low),
        shaped((length, width), low),
        shaped((HEADS // 2, length, 2 * length), jnp.float32),
        shaped((length, width), jnp.float32),
        shaped((length, experts), jnp.float32),
        shaped((length, experts), jnp.float32),
        shaped((1, length), jnp.int32),
    )
    query, key, value, output = weights
    inputs = (tokens, gain, query, key, value, bias, routes, output, gain_two, router, cotangent)
    return staged(
        forward_kernel,
        "forward",
        (count,),
        inputs,
        outputs,
        (),
        10 * length * width * width,
        10 * width * width,
    )


def backward_kernel(numbers, inputs, outputs, scratch):
    (
        came_ref,
        slot_ref,
        hidden_ref,
        router_probs_ref,
        choose_ref,
        cotangent_ref,
        gain_two_ref,
        router_ref,
        output_ref,
        v_ref,
        probs_ref,
        q_ref,
        k_ref,
        query_ref,
        key_ref,
        value_ref,
        tokens_ref,
        gain_ref,
    ) = inputs
    out_ref, grad_ref, late_ref = outputs
    turned, sums, tail = scratch
    low = jnp.bfloat16
    length, width = tokens_ref.shape
    experts = router_ref.shape[0]
    capacity = came_ref.shape[2] // 2
    group = late_ref.shape[0]
    small_rows = tail.shape[0] // group
    top = cotangent_ref[...].astype(jnp.float32)
    slots = experts * 2 * capacity
    came = came_ref[:, 0].astype(jnp.float32) + came_ref[:, 1].astype(jnp.float32)
    came = came.reshape(slots, width).astype(low)
    row = lax.broadcasted_iota(jnp.int32, (slots, length), 0)
    column = slot_ref[...]
    spread = jnp.concatenate(
        [
            jnp.where(row == column, 1.0, 0.0).astype(low),
            jnp.where(row == column + capacity, 1.0, 0.0).astype(low),
        ],
        axis=1,
    )
    back = dot_first(spread, came)
    returned, d_normed_two = back[:length], back[length:]
    hidden = hidden_ref[...]
    router_probs, choose = router_probs_ref[...], choose_ref[...]
    gate = jnp.sum(router_probs * choose, axis=1, keepdims=True)
    out_ref[...] = (hidden + gate * returned).astype(low)
    out_ref.send()
    d_gate = jnp.sum(top * returned, axis=1, keepdims=True)
    d_probs = choose * d_gate
    d_logits = router_probs * (
        d_probs - jnp.sum(router_probs * d_probs, axis=1, keepdims=True)
    )
    d_logits = d_logits.astype(low)
    factor = rms_factor(hidden)
    gain_two = row_of(gain_two_ref)
    normed_two = (hidden * factor * gain_two).astype(low)
    grad_router = dot_first(d_logits, normed_two)
    d_normed_two = d_normed_two + jnp.dot(
        d_logits, router_ref[...], preferred_element_type=jnp.float32
    )
    d_from_norm, grad_ffn = norm_backward(hidden, factor, gain_two, d_normed_two)
    d_hidden = top + d_from_norm
    d_mixed = d_hidden.astype(low)
    d_attended = dot_last(d_mixed, output_ref[...]).astype(low)
    flipped = d_mixed.T
    for head in range(HEADS):
        at = 3 * HEADS + head
        late_ref[at // 3, at % 3 * HEAD_DIM : (at % 3 + 1) * HEAD_DIM] = flipped[
            head * HEAD_DIM : (head + 1) * HEAD_DIM
        ]

    first = pair_masks(length)
    upper = lax.broadcasted_iota(jnp.int32, (LANES, length), 0) < HEAD_DIM
    lane = lax.broadcasted_iota(jnp.int32, (length, length), 1)
    place = lax.broadcasted_iota(jnp.int32, (length, length), 0)
    reverse = jnp.where(place + lane == length - 1, 1.0, 0.0).astype(low)
    for pair in range(HEADS // 2):
        lanes = slice(pair * LANES, (pair + 1) * LANES)
        upstream = d_attended[:, lanes]
        probs = probs_ref[pair]
        d_probs = dot_last(upstream, stacked_heads(v_ref[:, lanes], first))
        parts = []
        for head in range(2):
            span = slice(head * length, (head + 1) * length)
            own, grad = probs[:, span], d_probs[:, span]
            parts.append(own * (grad - jnp.sum(own * grad, axis=1, keepdims=True)))
        d_scores = jnp.concatenate(parts, axis=1).astype(low)
        d_values = dot_first(upstream, probs.astype(low))
        d_values = jnp.where(upper, d_values[:, :length], d_values[:, length:])
        d_keys = dot_first(q_ref[:, lanes], d_scores) * score_scale
        d_keys = jnp.where(upper, d_keys[:, :length], d_keys[:, length:])
        d_queries = jnp.dot(
            d_scores, stacked_heads(k_ref[:, lanes], first), preferred_element_type=jnp.float32
        )
        d_queries = (d_queries * score_scale).astype(low)
        for which, value in enumerate(
            (d_queries.T, d_keys.astype(low), d_values.astype(low))
        ):
            turned[which, lanes] = value
            for head in range(2):
                at = which * HEADS + 2 * pair + head
                late_ref[at // 3, at % 3 * HEAD_DIM : (at % 3 + 1) * HEAD_DIM] = value[
                    head * HEAD_DIM : (head + 1) * HEAD_DIM
                ]
        upside = jnp.dot(reverse, d_scores, preferred_element_type=jnp.float32)
        for head in range(2):
            own = upside[:, head * length : (head + 1) * length]
            own = jnp.concatenate([own, jnp.zeros_like(own)], axis=1)
            own = pltpu.roll(own, 0, 1, stride=1, stride_axis=0)
            at = 2 * pair + head
            sums[at % 4, at // 4 : at // 4 + 1] = jnp.sum(own, axis=0, keepdims=True)

    d_normed = 0.0
    for which, weight in enumerate((query_ref, key_ref, value_ref)):
        d_normed = d_normed + lax.dot_general(
            turned[which],
            weight[...],
            (((0,), (1,)), ((), ())),
            preferred_element_type=jnp.float32,
        )
    inputs = tokens_ref[...].astype(jnp.float32)
    d_first, grad_norm = norm_backward(
        inputs, rms_factor(inputs), row_of(gain_ref), d_normed
    )
    grad_ref[...] = (d_hidden + d_first).astype(low)
    grad_ref.send()

    shift = lax.broadcasted_iota(jnp.int32, (2 * length, LANES), 0) - (length - 1)
    bucket = bucket_of(shift)
    lane_wide = lax.broadcasted_iota(jnp.int32, (2 * length, LANES), 1)
    bias_rows = 0.0
    for quarter in range(4):
        hot = jnp.where(bucket + quarter * BUCKETS == lane_wide, 1.0, 0.0)
        bias_rows = bias_rows + jnp.dot(
            sums[quarter],
            hot,
            precision=lax.Precision.HIGHEST,
            preferred_element_type=jnp.float32,
        )
    chunks = width // LANES
    tail[...] = jnp.zeros_like(tail)
    for chunk in range(chunks):
        lanes = slice(chunk * LANES, (chunk + 1) * LANES)
        tail[chunk : chunk + 1] = grad_norm[:, lanes]
        tail[chunks + chunk : chunks + chunk + 1] = grad_ffn[:, lanes]
        for expert in range(experts):
            at = 2 * chunks + HEADS // 4 + expert * chunks + chunk
            tail[at : at + 1] = grad_router[expert : expert + 1, lanes]
    tail[2 * chunks : 2 * chunks + HEADS // 4] = bias_rows[: HEADS // 4]
    block = 4 * width // group
    for at in range(group):
        own = tail[at * small_rows : (at + 1) * small_rows]
        high = own.astype(low).astype(jnp.float32)
        late_ref[at, block:] = jnp.concatenate([high, own - high], axis=0).astype(low)
    late_ref.send()


def backward_of(came, tokens, gain, weights, gain_two, router, cotangent, saved, group):
    length, width = tokens.shape
    experts = router.shape[0]
    low = jnp.bfloat16
    small_rows = -(-small_count(width, experts) // group)
    block = 4 * width // group
    outputs = (
        shaped((length, width), low),
        shaped((length, width), low),
        shaped((group, block + 2 * small_rows, length), low),
    )
    scratch = (
        pltpu.VMEM((3, width, length), low),
        pltpu.VMEM((4, 8, 2 * length), jnp.float32),
        pltpu.VMEM((group * small_rows, LANES), jnp.float32),
    )
    query, key, value, output = weights
    q, k, v, probs, hidden, router_probs, choose, slot = saved
    inputs = (slot, hidden, router_probs, choose, cotangent, gain_two, router, output)
    inputs = inputs + (v, probs, q, k, query, key, value, tokens, gain)
    return staged(
        backward_kernel,
        "backward",
        (),
        inputs,
        outputs,
        scratch,
        10 * length * width * width,
        10 * width * width,
        residents=(came,),
        mib=62,
    )


def small_count(width, experts):
    return (2 + experts) * (width // LANES) + HEADS // 4


def pick_kernel(numbers, inputs, outputs, scratch):
    (which_ref,), (*pieces, tokens_ref) = numbers, inputs
    which = which_ref[0]
    pieces = [piece.ref() for piece in pieces]
    rows = pieces[0].shape[0]
    tokens_ref = tokens_ref.ref()
    if len(pieces) > 1:
        for part, piece in enumerate(pieces):
            outputs[0][part * rows : (part + 1) * rows] = piece[...]
        outputs[0].send()
    for out, turn in zip(outputs[-2:], (3, 2)):

        @pl.when(which == turn)
        def _():
            for part, piece in enumerate(pieces):
                out[part * rows : (part + 1) * rows] = piece[...]

        @pl.when(which != turn)
        def _():
            out[...] = tokens_ref[...]

        out.send()


def picked(which, pieces, tokens):
    outputs = (shaped(tokens.shape, tokens.dtype),) * (2 if len(pieces) == 1 else 3)
    return staged(
        pick_kernel,
        "picked",
        (which,),
        (*pieces, tokens),
        outputs,
        (),
        0,
        10 * tokens.size,
    )


def left_kernel(numbers, inputs, outputs, scratch):
    (which_ref,), (*pieces, gain_ref), (left_ref,) = numbers, inputs, outputs
    which = which_ref[0]
    scale = row_of(gain_ref)
    for number, piece in enumerate(pieces):
        held = piece.ref()
        count = held.shape[0]
        spans = [
            (at, slice(number * count + at, number * count + at + LANES))
            for at in range(0, count, LANES)
        ]

        @pl.when(which < 3)
        def _():
            for at, span in spans:
                own = held[at : at + LANES].astype(jnp.float32)
                own = (own * rms_factor(own) * scale).astype(jnp.bfloat16)
                left_ref[:, span] = own.T

        @pl.when(which == 3)
        def _():
            for at, span in spans:
                left_ref[:, span] = held[at : at + LANES].T

    left_ref.send()


def left_of(which, pieces, gain):
    count, width = pieces[0].shape
    total = count * len(pieces)
    kept = (shaped((width, total), jnp.bfloat16),)
    inputs = (*pieces, gain)
    (left,) = staged(
        left_kernel,
        "left",
        (which,),
        inputs,
        (),
        (),
        10 * total * width,
        6 * total * width,
        kept=kept,
        mib=60,
    )
    return left


gelu_scale = 0.7978845608028654
gelu_cubic = 0.044715


def expert_kernel(numbers, inputs, outputs, scratch):
    rows_ref, order_ref, in_a, out_a, in_b, out_b = inputs
    back_ref, rows_out, grads_out, act_ref, inner_ref = outputs
    count = rows_ref.shape[0]
    half = count // 2
    lanes = lax.broadcasted_iota(jnp.int32, (count, count), 1)
    sort = jnp.where(order_ref[:, 0:1] == lanes, 1.0, 0.0).astype(jnp.bfloat16)
    unsort = jnp.where(order_ref[:, 1:2] == lanes, 1.0, 0.0).astype(jnp.bfloat16)
    ordered = jnp.dot(sort, rows_ref[...], preferred_element_type=jnp.float32)
    ordered = ordered.astype(jnp.bfloat16)
    rows, slots = ordered[:half], ordered[half:]
    rows_out[...] = rows
    rows_out.send()
    grads_out[...] = slots
    grads_out.send()
    result, d_rows = 0.0, 0.0
    for part, (part_in, part_out) in enumerate(((in_a, out_a), (in_b, out_b))):
        inner = jnp.dot(rows, part_in[...], preferred_element_type=jnp.float32)
        upstream = dot_last(slots, part_out[...])
        square = inner * inner
        bent = jnp.tanh(gelu_scale * (inner + gelu_cubic * (square * inner)))
        active = (inner * (0.5 * (1.0 + bent))).astype(jnp.bfloat16)
        slope = 0.5 * (1.0 + bent) + 0.5 * inner * (1.0 - bent * bent) * (
            gelu_scale * (1.0 + 3.0 * gelu_cubic * square)
        )
        d_inner = (upstream * slope).astype(jnp.bfloat16)
        act_ref[part] = active
        inner_ref[part] = d_inner
        result = result + jnp.dot(active, part_out[...], preferred_element_type=jnp.float32)
        d_rows = d_rows + dot_last(d_inner, part_in[...])
    act_ref.send()
    inner_ref.send()
    both = jnp.concatenate([result.astype(jnp.bfloat16), d_rows.astype(jnp.bfloat16)], axis=0)
    back_ref[...] = jnp.dot(unsort, both, preferred_element_type=jnp.float32).astype(jnp.bfloat16)
    back_ref.send()


def expert_rows_of(rows, capacity, part_weights):
    count, width = rows.shape
    half = count // 2
    place = np.arange(count)
    sort = place % half // capacity * 2 * capacity + place // half * capacity + place % capacity
    unsort = np.empty_like(sort)
    unsort[sort] = place
    order = jnp.asarray(np.stack([sort, unsort], axis=1), jnp.int32)
    hidden_width = part_weights[0].shape[1]
    low = jnp.bfloat16
    outputs = (
        shaped((count, width), low),
        shaped((half, width), low),
        shaped((half, width), low),
        shaped((2, half, hidden_width), low),
        shaped((2, half, hidden_width), low),
    )
    return staged(
        expert_kernel,
        "expert_rows",
        (),
        (order, *part_weights),
        outputs,
        (),
        16 * half * width * hidden_width,
        12 * width * width,
        residents=(rows,),
        mib=62,
    )


def expert_grads_kernel(numbers, inputs, outputs, scratch):
    rows_ref, inner_ref, act_ref, slots_ref = inputs
    sent_in, sent_out, own_in, own_out = outputs
    sent_in[...] = dot_first(rows_ref[...], inner_ref[1]).astype(jnp.bfloat16)
    sent_in.send()
    sent_out[...] = dot_first(act_ref[1], slots_ref[...]).astype(jnp.bfloat16)
    sent_out.send()
    own_in[...] = dot_first(rows_ref[...], inner_ref[0])
    own_in.send()
    own_out[...] = dot_first(act_ref[0], slots_ref[...])
    own_out.send()


def expert_grads_of(rows, slots, active, d_inner):
    half, width = rows.shape
    hidden_width = active.shape[2]
    outputs = (
        shaped((width, hidden_width), jnp.bfloat16),
        shaped((hidden_width, width), jnp.bfloat16),
        shaped((width, hidden_width), jnp.float32),
        shaped((hidden_width, width), jnp.float32),
    )
    return staged(
        expert_grads_kernel,
        "expert_grads",
        (),
        (rows, d_inner, active, slots),
        outputs,
        (),
        8 * half * width * hidden_width,
        12 * width * width,
    )


def block_kernel(numbers, inputs, outputs, scratch):
    (bits_ref,), (late_ref, left_ref), (block_ref,) = numbers, inputs, outputs
    group = late_ref.shape[0]
    part = left_ref.shape[0] // 2
    block = left_ref.shape[0] * 4 // group
    edge = block - LANES
    half = part // 2
    small_rows = (block_ref.shape[1] - part - half) // 2
    odd = bits_ref[3] == 1
    which = bits_ref[0] * 2 + bits_ref[1]
    here = which * 4 + bits_ref[2] * 2 + bits_ref[3]
    right = jnp.concatenate(
        [late_ref[here ^ factor_order(i, which), :block] for i in range(group)], axis=1
    )
    right = jnp.where(odd, jnp.concatenate([right[edge:], right[:edge]], axis=0), right)
    total = dot_last(left_ref[...], right)
    first = pair_masks(half)
    tail = jnp.sum(late_ref[:, block:].astype(jnp.float32), axis=0)
    small = tail[:small_rows] + tail[small_rows:]
    high = small.astype(jnp.bfloat16).astype(jnp.float32)
    both = jnp.concatenate([high, small - high], axis=0).astype(jnp.bfloat16)
    for side in range(2):
        own = total[side * part : (side + 1) * part]
        block_ref[side, :part] = own[:, :LANES].astype(jnp.bfloat16)
        rest = own[:, LANES:]
        rest = jnp.concatenate([rest, rest], axis=1)
        upper, lower = rest[:half], rest[half:]
        even = jnp.where(first, upper, lower)
        packed = jnp.where(odd, jnp.where(first, lower, upper), even)
        block_ref[side, part : part + half] = packed.astype(jnp.bfloat16)
        block_ref[side, part + half :] = both


def block_of(bits, late, left, small_rows):
    group, rows, length = late.shape
    width = left.shape[0]
    kept = (shaped((2, 3 * width // 4 + 2 * small_rows, LANES), jnp.bfloat16),)
    (block,) = staged(
        block_kernel,
        "grad_block",
        (bits,),
        (),
        (),
        (),
        8 * width * width * length,
        2 * left.size,
        residents=(late, left),
        kept=kept,
        mib=24,
    )
    return block


def share_kernel(numbers, inputs, outputs, scratch):
    (own_ref, got_ref), (share_ref,) = inputs, outputs
    small_rows = scratch[0].shape[0]
    edge = own_ref.shape[1] - 2 * small_rows
    for side in range(2):
        own = own_ref[side, :edge].astype(jnp.float32) + got_ref[side, :edge].astype(jnp.float32)
        share_ref[side, :edge] = own.astype(jnp.bfloat16)
        own, got = own_ref[side, edge:].astype(jnp.float32), got_ref[side, edge:].astype(jnp.float32)
        small = (own[:small_rows] + own[small_rows:]) + (got[:small_rows] + got[small_rows:])
        high = small.astype(jnp.bfloat16).astype(jnp.float32)
        share_ref[side, edge:] = jnp.concatenate([high, small - high], axis=0).astype(jnp.bfloat16)


def share_of(own, got, small_rows):
    (share,) = staged(
        share_kernel,
        "share",
        (),
        (),
        (),
        (pltpu.VMEM((small_rows, LANES), jnp.float32),),
        own.size,
        6 * own.size,
        residents=(own, got),
        kept=(shaped(own.shape, own.dtype),),
        mib=8,
    )
    return share


def assemble_kernel(part, small_rows, bits_ref, *refs):
    sources, outs = refs[:16], refs[16:20]
    norm_out, ffn_out, bias_out, router_out = refs[20:24]
    held, made, tail, in_sems, out_sems = refs[24:]
    em, ey, dx, dc = [bits_ref[i] for i in range(4)]
    half = part // 2
    edge = part + half
    copies = [[] for _ in range(4)]
    for number, source in enumerate(sources):
        core, weight, step = dc ^ (number // 8), number // 2 % 4, number % 2
        copies[weight].append(
            pltpu.make_async_copy(
                source, held.at[weight, (dx ^ step) * 2 + core], in_sems.at[number]
            )
        )
    for weight in range(4):
        for copy in copies[weight]:
            copy.start()
    first = pair_masks(half)
    for weight in range(4):
        for copy in copies[weight]:
            copy.wait()
        for side in range(2):
            rows = slice(side * part, (side + 1) * part)
            upper = slice(side * part, side * part + half)
            lower = slice(side * part + half, (side + 1) * part)
            for twin in range(2):
                even, odd = 2 * twin, 2 * twin + 1
                at = 3 * twin * LANES
                made[weight, rows, at : at + LANES] = held[weight, even, side, :part].astype(
                    jnp.float32
                )
                made[weight, rows, at + 2 * LANES : at + 3 * LANES] = held[
                    weight, odd, side, :part
                ].astype(jnp.float32)
                left = held[weight, even, side, part:edge].astype(jnp.float32)
                right = held[weight, odd, side, part:edge].astype(jnp.float32)
                middle = slice(at + LANES, at + 2 * LANES)
                made[weight, upper, middle] = jnp.where(first, left, right)
                made[weight, lower, middle] = pltpu.roll(
                    jnp.where(first, right, left), HEAD_DIM, 1
                )
        truth = (em ^ (weight // 2)) * 2 + (ey ^ (weight % 2))
        for i in range(4):

            @pl.when(truth == i)
            def _():
                pltpu.make_async_copy(made.at[weight], outs[i], out_sems.at[weight]).start()

        for i in range(4):
            own = held[weight, i, 0, edge:].astype(jnp.float32)
            tail[truth, i] = own[:small_rows] + own[small_rows:]

    def small_row(at):
        at, row = divmod(at, small_rows)
        return tail[at // 4, at % 4, row : row + 1]

    chunks = made.shape[2] // LANES
    for chunk in range(chunks):
        lanes = slice(chunk * LANES, (chunk + 1) * LANES)
        norm_out[chunk : chunk + 1] = small_row(chunk)
        ffn_out[chunk : chunk + 1] = small_row(chunks + chunk)
        for expert in range(router_out.shape[0]):
            router_out[expert : expert + 1, lanes] = small_row(
                2 * chunks + HEADS // 4 + expert * chunks + chunk
            )
    for head in range(HEADS):
        at = head % 4 * BUCKETS
        bias_out[head : head + 1] = small_row(2 * chunks + head // 4)[:, at : at + BUCKETS]

    for weight in range(4):
        truth = (em ^ (weight // 2)) * 2 + (ey ^ (weight % 2))
        for i in range(4):

            @pl.when(truth == i)
            def _():
                pltpu.make_async_copy(made.at[weight], outs[i], out_sems.at[weight]).wait()


def assemble(bits, sources, small_rows, width, experts):
    return pl.pallas_call(
        functools.partial(assemble_kernel, width // 2, small_rows),
        out_shape=(shaped((width, width), jnp.float32),) * 4
        + (
            shaped((width // LANES, LANES), jnp.float32),
            shaped((width // LANES, LANES), jnp.float32),
            shaped((HEADS, BUCKETS), jnp.float32),
            shaped((experts, width), jnp.float32),
        ),
        in_specs=[pl.BlockSpec(memory_space=pltpu.SMEM)] + [whole_spec()] * 16,
        out_specs=(any_spec(),) * 4 + (whole_spec(),) * 4,
        scratch_shapes=[
            pltpu.VMEM((4, 4) + sources[0].shape, jnp.bfloat16),
            pltpu.VMEM((4, width, width), jnp.float32),
            pltpu.VMEM((4, 4, small_rows, LANES), jnp.float32),
            pltpu.SemaphoreType.DMA((16,)),
            pltpu.SemaphoreType.DMA((4,)),
        ],
        compiler_params=params(32),
        cost_estimate=cost(8 * width * width, 24 * width * width),
        name="assemble",
    )(bits, *sources)


def place_in_group():
    place = [lax.axis_index(axis) for axis in ("em", "ey", "dx", "dc")]
    return (2 * place[0] + place[1]).astype(jnp.int32), jnp.stack(place).astype(jnp.int32)


def factor_order(at, which):
    low, high = at & 1, at >> 1 & 1
    turned = jnp.where(which == 3, 2 * low + 8 * high, 8 * low + 2 * high)
    return turned + (at >> 2 & 1) * 4 + (at >> 3)


def with_other(rows, axis):
    return jnp.concatenate([rows, swap(rows, axis)], axis=0)


def gathered_grads(late, left, place, small_rows, experts, beside):
    width = left.shape[0]
    block = block_of(place, late, left, small_rows)
    block, beside = lax.optimization_barrier((block, beside))
    beside = [own + other.astype(jnp.float32) for own, other in beside]
    got, beside = lax.optimization_barrier((swap(block, "eh"), beside))
    near = share_of(block, got, small_rows)
    far, near_x, near_y = swap(near, "em"), swap(near, "dx"), swap(near, "ey")
    far_x, far_y = swap(far, "dx"), swap(far, "ey")
    near_both, far_both = swap(near_x, "ey"), swap(far_y, "dx")
    sources = (near, near_x, near_y, near_both, far, far_x, far_y, far_both)
    sources = sources + tuple(swap(source, "dc") for source in sources)
    return assemble(place, sources, small_rows, width, experts), beside


def gathered_grads_plain(late, left, place, small_rows, experts, beside):
    group, rows, length = late.shape
    width = left.shape[0]
    block = 4 * width // group
    small = jnp.sum(late[:, block:].astype(jnp.float32), axis=0)
    small = lax.psum(small[:small_rows] + small[small_rows:], "eh")
    which = place_in_group()[0]
    order = jnp.stack([factor_order(at, which) for at in range(group)])
    order = order ^ lax.axis_index(GROUP_AXES)
    late_block = jnp.take(late[:, :block], order, axis=0)
    late_block = late_block.transpose(1, 0, 2).reshape(block, group * length)
    grad_block = dot_last(late_block, left)
    mine = lax.psum_scatter(grad_block, "eh", scatter_dimension=0, tiled=True)
    grads = lax.all_gather(mine.astype(jnp.bfloat16), "eh", axis=0, tiled=True)
    grads = lax.all_gather(grads, GROUP_AXES, axis=0, tiled=True)
    small = lax.all_gather(small, GROUP_AXES, axis=0, tiled=True).reshape(-1)
    grads = grads.reshape(4, width, width).transpose(0, 2, 1).astype(jnp.float32)
    sizes = (width, width, HEADS * BUCKETS, experts * width)
    ends = np.cumsum(sizes)
    pieces = [small[end - size : end] for end, size in zip(ends, sizes)]
    pieces[2], pieces[3] = pieces[2].reshape(HEADS, BUCKETS), pieces[3].reshape(experts, width)
    return (*grads, *pieces), [own + other.astype(jnp.float32) for own, other in beside]


def per_device(
    tokens,
    norm_gain,
    w_query,
    w_key,
    w_value,
    w_output,
    rel_bias,
    ffn_gain,
    w_router,
    w_in,
    w_out,
    routes,
    lengths,
    cotangent,
):
    length, model_width = tokens.shape
    experts = w_router.shape[1]
    group = lax.axis_size(GROUP_AXES)
    capacity = max(2, (5 * length + 4 * experts - 1) // (4 * experts))
    small_rows = -(-small_count(model_width, experts) // group)
    gain_one, gain_two = norm_gain.reshape(-1, LANES), ffn_gain.reshape(-1, LANES)
    weights = (w_query, w_key, w_value, w_output)
    router = w_router.T

    w_in_own, w_out_own = w_in[0], w_out[0]
    w_in_other, w_out_other = swap(w_in_own, "dc"), swap(w_out_own, "dc")
    outgoing, attended, *saved = forward_of(
        lengths,
        tokens,
        gain_one,
        weights,
        rel_bias.T,
        gain_two,
        router,
        routes.reshape(1, length),
        cotangent,
        capacity,
    )
    which, place = place_in_group()
    outgoing, near_tokens = lax.optimization_barrier((outgoing, with_other(tokens, "em")))
    outgoing = outgoing.reshape(2 * experts, 2 * capacity, model_width)
    incoming = lax.all_to_all(outgoing, EXPERT_AXES, split_axis=0, concat_axis=0, tiled=True)
    far_tokens = swap(near_tokens, "dx")
    near_attended, own_near, given_near = picked(
        which[None], (attended, swap(attended, "dx")), near_tokens
    )
    incoming, far_tokens, near_attended, given_near = lax.optimization_barrier(
        (incoming, far_tokens, near_attended, given_near)
    )
    far_attended, got_near = swap(near_attended, "em"), swap(given_near, "ey")
    incoming = incoming.reshape(-1, model_width)
    sent_back, expert_rows, grad_slots, active, d_inner = expert_rows_of(
        incoming, capacity, (w_in_own, w_out_own, w_in_other, w_out_other)
    )
    sent_back, far_attended, got_near = lax.optimization_barrier(
        (sent_back, far_attended, got_near)
    )
    sent_back = sent_back.reshape(2 * experts, 2 * capacity, model_width)
    came_back = lax.all_to_all(sent_back, EXPERT_AXES, split_axis=0, concat_axis=0, tiled=True)
    own_far, given_far = picked(which[None], (far_attended,), far_tokens)
    expert_rows, given_far = lax.optimization_barrier((expert_rows, given_far))
    factors = [own_near, own_far, got_near, swap(given_far, "ey")]
    in_other, out_other, in_own, out_own = expert_grads_of(
        expert_rows, grad_slots, active, d_inner
    )
    came_back, factors, in_own, out_own, in_other, out_other = lax.optimization_barrier(
        (came_back, factors, in_own, out_own, in_other, out_other)
    )
    factors = factors + [swap(rows, "dc") for rows in factors]
    in_other, out_other = swap(in_other, "dc"), swap(out_other, "dc")

    output, grad_input, late = backward_of(
        came_back.reshape(experts, 2, 2 * capacity, model_width),
        tokens,
        gain_one,
        weights,
        gain_two,
        router,
        cotangent,
        saved,
        group,
    )

    late = lax.all_to_all(late, GROUP_AXES, split_axis=0, concat_axis=0, tiled=True)
    left = left_of(which[None], factors, gain_one)
    late, left = lax.optimization_barrier((late, left))
    gather = gathered_grads if lax.axis_size("eh") == 2 else gathered_grads_plain
    grads, (grad_in, grad_out) = gather(
        late, left, place, small_rows, experts, ((in_own, in_other), (out_own, out_other))
    )
    *grads, grad_norm, grad_ffn, grad_bias, grad_router = grads
    return (
        output,
        grad_input,
        grad_norm.reshape(model_width),
        *grads,
        grad_bias.T,
        grad_ffn.reshape(model_width),
        grad_router.T,
        grad_in[None],
        grad_out[None],
    )


def solution(mesh):
    exp_count, dp_count = mesh.shape["exp"], mesh.shape["dp"]
    fine = Mesh(
        mesh.devices.reshape(exp_count // 4, 2, 2, dp_count // 2, 2),
        TOKEN_AXES,
    )
    exp, dp = ("eh", "em", "ey"), ("dx", "dc")
    in_specs = (
        P(TOKEN_AXES, None),
        P(),
        P(),
        P(),
        P(),
        P(),
        P(),
        P(),
        P(),
        P(exp, None, dp),
        P(exp, dp, None),
        P(TOKEN_AXES, None),
        P(TOKEN_AXES),
        P(TOKEN_AXES, None),
    )
    out_specs = (
        P(TOKEN_AXES, None),
        P(TOKEN_AXES, None),
        P(),
        P(),
        P(),
        P(),
        P(),
        P(),
        P(),
        P(),
        P(exp, None, dp),
        P(exp, dp, None),
    )
    return jax.shard_map(
        per_device, mesh=fine, in_specs=in_specs, out_specs=out_specs, check_vma=False
    )
```

time: 215 us -> 171 us (0.80)
  Pallas kernels: 24.1 us -> 51.8 us
  other arithmetic: 23.4 us -> 4.54 us
  waiting for transfers between devices: 87.4 us -> 68.9 us
  local copies, waits for them, and re-layouts: 21.8 us -> 5.22 us
  matrix products: 15.9 us -> 0 us
  between operations: 15.9 us -> 1.78 us
  starting transfers between devices: 25.7 us -> 38.4 us
    pallas_call x5 -> x10, Pallas kernels: 24.1 us -> 51.8 us  [the longest x9 45.5 us: staged(): pl.pallas_call(body, out_shape=tuple(kept) + tuple(outputs), in_specs=[pl...]
    ppermute x15 -> x30, waiting for transfers between devices: 40.9 us -> 65.1 us  [swap(): return lax.ppermute(array, axis, perm=[(0, 1), (1, 0)])]
    all_to_all x1, waiting for transfers between devices: 20.7 us -> 0.01 us  [per_device(): lax.all_to_all(outgoing, EXPERT_AXES, split_axis=0, concat_axis=0, tiled=...]
    dot_general x23 -> x0, matrix products: 15.9 us -> none  [the longest x5 4.85 us: dot_last(): lax.dot_general(left_side, right_side, (((1,), (1,)), ((), ())), preferre...]
    all_to_all x1, waiting for transfers between devices: 18.2 us -> 3.28 us  [per_device(): lax.all_to_all(sent_back, EXPERT_AXES, split_axis=0, concat_axis=0, tiled...]
    ppermute x15 -> x30, starting transfers between devices: 8.86 us -> 23.8 us  [swap(): return lax.ppermute(array, axis, perm=[(0, 1), (1, 0)])]
    unnamed x146 -> x32, local copies, waits for them, and re-layouts: 13.9 us -> 5.22 us
    all_to_all x1, waiting for transfers between devices: 6.87 us -> 0.47 us  [per_device(): lax.all_to_all(late, GROUP_AXES, split_axis=0, concat_axis=0, tiled=True)]
  transfers between devices with their start and end apart: 20 -> 33, of which waited for: 11 -> 14; matrix products, arithmetic and copies ran while one was open for 22% -> 3% of each run, Pallas kernels for 6% -> 21%
where the time goes in v3:
time: 171 us
  waiting for transfers between devices  68.9 us (40%)
  Pallas kernels  51.8 us (30%)
  starting transfers between devices  38.4 us (22%)
  local copies, waits for them, and re-layouts  5.22 us (3%)
  other arithmetic  4.54 us (3%)
  between operations  1.78 us (1%)
    ppermute x30, waiting for transfers between devices, swap(): return lax.ppermute(array, axis, perm=[(0, 1), (1, 0)])  65.1 us
    pallas_call x9, Pallas kernels, staged(): pl.pallas_call(body, out_shape=tuple(kept) + tuple(outputs), in_specs=[pl...  45.5 us
    ppermute x30, starting transfers between devices, swap(): return lax.ppermute(array, axis, perm=[(0, 1), (1, 0)])  23.8 us
    pallas_call x1, Pallas kernels, assemble(): pl.pallas_call(functools.partial(assemble_kernel, width // 2, small_rows)...  6.32 us
    all_to_all x1, starting transfers between devices, per_device(): lax.all_to_all(outgoing, EXPERT_AXES, split_axis=0, concat_axis=0, tiled=...  6.04 us
    unnamed x32, local copies, waits for them, and re-layouts  5.22 us
    all_to_all x1, starting transfers between devices, per_device(): lax.all_to_all(late, GROUP_AXES, split_axis=0, concat_axis=0, tiled=True)  4.84 us
    add x1, other arithmetic, gathered_grads(): beside = [own + other.astype(jnp.float32) for own, other in beside]  4.44 us
  transfers between devices with their start and end apart: 33, of which 14 were waited for; matrix products, arithmetic and copies ran while one was open for 3% of the time, Pallas kernels for 21%

profile of v3, /device:TPU:0, one launch (start us, length us, event | category | flops | bytes accessed | tf_op | source)
XLA Modules:
  0.0 170.6 jit_solution(15505845194079609466)
XLA Ops:
  0.6 3.1 %collective-permute-start = (bf16[128,768]{1,0:T(8,128)(2,1)}, bf16[128,768]{1,0:T(8,128)(2,1)S(1)}, u32[]{:S(2)}, u32[]{:S(2)}) collective-permute-start(bf16[128,768]{1,0:T(8,128)(2,1)} %refs_16_.1), channel_id=1, source_target_pairs={{0,8},{8,0},{1,9},{9,1},{2,10},{10,2},{3,11},{11,3},{4,12},{12,4},... | collective-permute-start | bytes 589832 | tf_op jit(solution)/shard_map/ppermute | solution.py:59
  4.4 7.4 %forward.1 = (bf16[8,2,40,768]{3,2,1,0:T(8,128)(2,1)}, bf16[128,768]{1,0:T(8,128)(2,1)}, bf16[128,768]{1,0:T(8,128)(2,1)}, bf16[128,768]{1,0:T(8,128)(2,1)}, bf1...) custom-call(s32[1]{0:T(128)S(6)} %copy.27.refs_0_, ...), custom_call_target="tpu_custom_call" | custom-call | flops 754974720 | bytes 5898240 | tf_op jit(solution)/shard_map/forward/pallas_call | solution.py:173
  11.9 6.0 %all-to-all-start = ((bf16[16,40,768]{2,1,0:T(8,128)(2,1)}), bf16[16,40,768]{2,1,0:T(8,128)(2,1)}, u32[]{:S(2)}, u32[]{:S(2)}) async-start(bf16[16,40,768]{2,1,0:T(8,128)(2,1)} %bitcast.25), calls=%async_computation | async-start | bytes 1966080 | tf_op jit(solution)/shard_map/all_to_all | solution.py:1038
  18.0 0.5 collective-permute-start.4
  18.5 1.8 %collective-permute-start.1 = (bf16[256,768]{1,0:T(8,128)(2,1)S(1)}, bf16[256,768]{1,0:T(8,128)(2,1)S(1)}, u32[]{:S(2)}, u32[]{:S(2)}) collective-permute-start(bf16[256,768]{1,0:T(8,128)(2,1)S(1)} %pad_maximum_fusion.refs_3_), channel_id=1, source_target_pairs={{0,2},{2,0},{1,3},{3,1},{4,6},{6,4},{5,7},{7,5},{8,10},{10,8},{9,1... | collective-permute-start | bytes 1179656 | tf_op jit(solution)/shard_map/ppermute | solution.py:59
  20.5 22.6 %collective-permute-done.2.refs_2_ = bf16[128,768]{1,0:T(8,128)(2,1)S(1)} collective-permute-done((bf16[128,768]{1,0:T(8,128)(2,1)S(1)}, bf16[128,768]{1,0:T(8,128)(2,1)S(1)}, u32[]{:S(2)}, u32[]{:S(2)}) %collective-permute-start.2) | collective-permute-done | bytes 196640 | tf_op jit(solution)/shard_map/ppermute | solution.py:59
  43.1 0.7 copy-done.15
  43.8 2.3 %picked.2 = (bf16[256,768]{1,0:T(8,128)(2,1)}, bf16[256,768]{1,0:T(8,128)(2,1)}, bf16[256,768]{1,0:T(8,128)(2,1)}) custom-call(s32[1]{0:T(128)} %bitcast.6.refs_0_, bf16[128,768]{1,0:T(8,128)(2,1)} %get-tuple-element.80.refs_1_, bf16[128,768]{1,0:T(8,128)(2,1)} %copy-done.15, bf16[256,768]{1,0:T(8,128)(2,1)} %copy-done.5), custom_call_target="tpu_custom_call" | custom-call | bytes 1966080 | tf_op jit(solution)/shard_map/picked/pallas_call | solution.py:173
  46.1 1.8 %collective-permute-start.5 = (bf16[256,768]{1,0:T(8,128)(2,1)}, bf16[256,768]{1,0:T(8,128)(2,1)S(1)}, u32[]{:S(2)}, u32[]{:S(2)}) collective-permute-start(bf16[256,768]{1,0:T(8,128)(2,1)} %get-tuple-element.85), channel_id=1, source_target_pairs={{0,8},{8,0},{1,9},{9,1},{2,10},{10,2},{3,11},{11,3},{4,12},{12,4},... | collective-permute-start | bytes 1179656 | tf_op jit(solution)/shard_map/ppermute | solution.py:59
  47.9 1.5 collective-permute-start.6
  49.4 9.9 %expert_rows.1 = (bf16[640,768]{1,0:T(8,128)(2,1)}, bf16[320,768]{1,0:T(8,128)(2,1)}, bf16[320,768]{1,0:T(8,128)(2,1)}, bf16[2,320,768]{2,1,0:T(8,128)(2,1)}, bf16[2,320,768]{2,1,0:T(8,128)(2,1)}) custom-call(bf16[640,768]{1,0:T(8,128)(2,1)} %bitcast.7.refs_0_, s32[640,2]{1,0:T(8,128)} %constant.18.clone.refs_1_, bf16[768,768]{1,0:T(8,128)(2,1)} %bitcast.8.refs_2_, ...), custom_call_target="tpu_custom_call" | custom-call | flops 3019898880 | bytes 7077888 | tf_op jit(solution)/shard_map/expert_rows/pallas_call | solution.py:173
  59.3 0.8 copy-done.7
  60.2 3.8 %all-to-all-start.1 = ((bf16[16,40,768]{2,1,0:T(8,128)(2,1)}), bf16[16,40,768]{2,1,0:T(8,128)(2,1)S(1)}, u32[]{:S(2)}, u32[]{:S(2)}) async-start(bf16[16,40,768]{2,1,0:T(8,128)(2,1)} %bitcast.26), calls=%async_computation.1 | async-start | bytes 1966080 | tf_op jit(solution)/shard_map/all_to_all | solution.py:1055
  63.9 2.1 %picked.3 = (bf16[256,768]{1,0:T(8,128)(2,1)}, bf16[256,768]{1,0:T(8,128)(2,1)}) custom-call(s32[1]{0:T(128)} %bitcast.6.refs_0_, bf16[256,768]{1,0:T(8,128)(2,1)} %copy-done.13, bf16[256,768]{1,0:T(8,128)(2,1)} %copy-done.12), custom_call_target="tpu_custom_call" | custom-call | bytes 1966080 | tf_op jit(solution)/shard_map/picked/pallas_call | solution.py:173
  66.1 2.0 %collective-permute-start.7 = (bf16[256,768]{1,0:T(8,128)(2,1)}, bf16[256,768]{1,0:T(8,128)(2,1)}, u32[]{:S(2)}, u32[]{:S(2)}) collective-permute-start(bf16[256,768]{1,0:T(8,128)(2,1)} %get-tuple-element.95), channel_id=1, source_target_pairs={{0,4},{4,0},{1,5},{5,1},{2,6},{6,2},{3,7},{7,3},{8,12},{12,8},{9,1... | collective-permute-start | bytes 1179656 | tf_op jit(solution)/shard_map/ppermute | solution.py:59
  68.1 6.1 %expert_grads.1 = (bf16[768,768]{1,0:T(8,128)(2,1)}, bf16[768,768]{1,0:T(8,128)(2,1)}, f32[768,768]{1,0:T(8,128)}, f32[768,768]{1,0:T(8,128)}) custom-call(bf16[320,768]{1,0:T(8,128)(2,1)} %get-tuple-element.96.refs_0_, bf16[2,320,768]{2,1,0:T(8,128)(2,1)} %get-tuple-element.97.refs_1_, bf16[2,320,768]{2,1,0:T(8,128)(2,1)} %get-tuple-element.98.refs_2_, ...), custom_call_target="tpu_custom_call" | custom-call | flops 1509949440 | bytes 7077888 | tf_op jit(solution)/shard_map/expert_grads/pallas_call | solution.py:173
  74.2 9.0 %collective-permute-done.7.refs_4_ = bf16[256,768]{1,0:T(8,128)(2,1)} collective-permute-done((bf16[256,768]{1,0:T(8,128)(2,1)}, bf16[256,768]{1,0:T(8,128)(2,1)}, u32[]{:S(2)}, u32[]{:S(2)}) %collective-permute-start.7) | collective-permute-done | bytes 393248 | tf_op jit(solution)/shard_map/ppermute | solution.py:59
  83.2 3.3 %all-to-all-done.1 = bf16[16,40,768]{2,1,0:T(8,128)(2,1)S(1)} async-done(((bf16[16,40,768]{2,1,0:T(8,128)(2,1)}), bf16[16,40,768]{2,1,0:T(8,128)(2,1)S(1)}, u32[]{:S(2)}, u32[]{:S(2)}) %all-to-all-start.1) | async-done | bytes 983072 | tf_op jit(solution)/shard_map/all_to_all | solution.py:1055
  86.4 0.9 copy-done.1
  87.4 10.0 %backward.1 = (bf16[128,768]{1,0:T(8,128)(2,1)}, bf16[128,768]{1,0:T(8,128)(2,1)}, bf16[16,200,128]{2,1,0:T(8,128)(2,1)}) custom-call(bf16[8,2,40,768]{3,2,1,0:T(8,128)(2,1)} %bitcast.22, s32[1,128]{1,0:T(1,128)} %get-tuple-element.105.refs_1_, f32[128,768]{1,0:T(8,128)} %get-tuple-element.106.refs_2_, f32[128,8]{1,0:T(8,128)} %get-tuple-element.107.refs_3_, ...), custom_call_target="tpu_custom_call" | custom-call | flops 754974720 | bytes 5898240 | tf_op jit(solution)/shard_map/backward/pallas_call | solution.py:173
  97.4 4.8 %all-to-all-start.2 = ((bf16[16,200,128]{2,1,0:T(8,128)(2,1)}), bf16[16,200,128]{2,1,0:T(8,128)(2,1)S(1)}, u32[]{:S(2)}, u32[]{:S(2)}) async-start(bf16[16,200,128]{2,1,0:T(8,128)(2,1)} %get-tuple-element.115), calls=%async_computation.2 | async-start | bytes 1638400 | tf_op jit(solution)/shard_map/all_to_all | solution.py:1080
  102.2 0.4 collective-permute-start.12
  102.8 0.3 collective-permute-start.8
  103.3 0.3 collective-permute-start.10
  103.7 3.2 %collective-permute-done.8.refs_5_ = bf16[256,768]{1,0:T(8,128)(2,1)S(1)} collective-permute-done((bf16[256,768]{1,0:T(8,128)(2,1)S(1)}, bf16[256,768]{1,0:T(8,128)(2,1)S(1)}, u32[]{:S(2)}, u32[]{:S(2)}) %collective-permute-start.8) | collective-permute-done | bytes 393248 | tf_op jit(solution)/shard_map/ppermute | solution.py:59
  107.2 0.7 collective-permute-done.10.refs_7_
  108.0 0.8 copy-done.11
  108.8 0.6 collective-permute-done.11.refs_8_
  109.4 6.0 %left.1.refs_2_ = bf16[768,2048]{1,0:T(8,128)(2,1)} custom-call(s32[1]{0:T(128)} %bitcast.6.refs_0_, bf16[256,768]{1,0:T(8,128)(2,1)} %get-tuple-element.116.refs_1_, bf16[256,768]{1,0:T(8,128)(2,1)} %get-tuple-element.117.refs_2_, bf16[256,768]{1,0:T(8,128)(2,1)} %copy-done.7, bf16[256,768]{1,0:T(8,128)(2,1)} %collective-permute-done.7.refs_4_, ...), custom_call_target="tpu_custom_call" | custom-call | flops 15728640 | bytes 9437184 | tf_op jit(solution)/shard_map/left/pallas_call | solution.py:173
  115.5 0.5 all-to-all-done.2.refs_1_
  115.9 1.9 %copy-done = bf16[768,2048]{1,0:T(8,128)(2,1)S(1)} copy-done((bf16[768,2048]{1,0:T(8,128)(2,1)S(1)}, bf16[768,2048]{1,0:T(8,128)(2,1)}, u32[]{:S(2)}) %copy-start) | copy-done | bytes 3145752
  117.8 1.6 grad_block.1.refs_0_
  119.5 1.4 collective-permute-start.14
  120.9 4.4 %convert_add_fusion = (f32[768,768]{1,0:T(8,128)}, f32[768,768]{1,0:T(8,128)}) fusion(f32[768,768]{1,0:T(8,128)S(1)} %copy-done.3, bf16[768,768]{1,0:T(8,128)(2,1)} %collective-permute-done.13, f32[768,768]{1,0:T(8,128)S(1)} %copy-done.2, bf16[768,768]{1,0:T(8,128)(2,1)} %collective-permute-done.12), kind=kLoop, calls=%fused_computation | loop fusion | flops 2359296 | bytes 11796480 | tf_op jit(solution)/shard_map/add | solution.py:961
  125.4 10.4 %collective-permute-done.14.refs_1_ = bf16[2,584,128]{2,1,0:T(8,128)(2,1)S(1)} collective-permute-done((bf16[2,584,128]{2,1,0:T(8,128)(2,1)S(1)}, bf16[2,584,128]{2,1,0:T(8,128)(2,1)S(1)}, u32[]{:S(2)}, u32[]{:S(2)}) %collective-permute-start.14) | collective-permute-done | bytes 299040 | tf_op jit(solution)/shard_map/ppermute | solution.py:59
  136.0 1.7 %collective-permute-start.16 = (bf16[2,584,128]{2,1,0:T(8,128)(2,1)S(1)}, bf16[2,584,128]{2,1,0:T(8,128)(2,1)S(1)}, u32[]{:S(2)}, u32[]{:S(2)}) collective-permute-start(bf16[2,584,128]{2,1,0:T(8,128)(2,1)S(1)} %share.1.refs_0_), channel_id=1, source_target_pairs={{0,4},{4,0},{1,5},{5,1},{2,6},{6,2},{3,7},{7,3},{8,12},{12,8},{9,1... | collective-permute-start | bytes 897032 | tf_op jit(solution)/shard_map/ppermute | solution.py:59
  137.7 1.5 collective-permute-start.15
  139.2 4.7 %collective-permute-done.18.refs_4_ = bf16[2,584,128]{2,1,0:T(8,128)(2,1)S(1)} collective-permute-done((bf16[2,584,128]{2,1,0:T(8,128)(2,1)S(1)}, bf16[2,584,128]{2,1,0:T(8,128)(2,1)S(1)}, u32[]{:S(2)}, u32[]{:S(2)}) %collective-permute-start.18) | collective-permute-done | bytes 299040 | tf_op jit(solution)/shard_map/ppermute | solution.py:59
  143.9 2.7 %collective-permute-start.20 = (bf16[2,584,128]{2,1,0:T(8,128)(2,1)S(1)}, bf16[2,584,128]{2,1,0:T(8,128)(2,1)S(1)}, u32[]{:S(2)}, u32[]{:S(2)}) collective-permute-start(bf16[2,584,128]{2,1,0:T(8,128)(2,1)S(1)} %collective-permute-done.18.refs_4_), channel_id=1, source_target_pairs={{0,4},{4,0},{1,5},{5,1},{2,6},{6,2},{3,7},{7,3},{8,12},{12,8},{9,1... | collective-permute-start | bytes 897032 | tf_op jit(solution)/shard_map/ppermute | solution.py:59
  146.6 1.4 collective-permute-start.19
  148.3 6.3 %collective-permute-done.20.refs_6_ = bf16[2,584,128]{2,1,0:T(8,128)(2,1)S(1)} collective-permute-done((bf16[2,584,128]{2,1,0:T(8,128)(2,1)S(1)}, bf16[2,584,128]{2,1,0:T(8,128)(2,1)S(1)}, u32[]{:S(2)}, u32[]{:S(2)}) %collective-permute-start.20) | collective-permute-done | bytes 299040 | tf_op jit(solution)/shard_map/ppermute | solution.py:59
  154.6 1.4 collective-permute-start.21
  156.1 0.5 collective-permute-done.19.refs_5_
  156.6 0.5 collective-permute-start.27
  157.0 2.4 %collective-permute-done.17.refs_3_ = bf16[2,584,128]{2,1,0:T(8,128)(2,1)S(1)} collective-permute-done((bf16[2,584,128]{2,1,0:T(8,128)(2,1)S(1)}, bf16[2,584,128]{2,1,0:T(8,128)(2,1)S(1)}, u32[]{:S(2)}, u32[]{:S(2)}) %collective-permute-start.17) | collective-permute-done | bytes 299040 | tf_op jit(solution)/shard_map/ppermute | solution.py:59
  159.5 3.1 %collective-permute-done.21.refs_7_ = bf16[2,584,128]{2,1,0:T(8,128)(2,1)S(1)} collective-permute-done((bf16[2,584,128]{2,1,0:T(8,128)(2,1)S(1)}, bf16[2,584,128]{2,1,0:T(8,128)(2,1)S(1)}, u32[]{:S(2)}, u32[]{:S(2)}) %collective-permute-start.21) | collective-permute-done | bytes 299040 | tf_op jit(solution)/shard_map/ppermute | solution.py:59
  162.6 1.6 collective-permute-done.29.refs_15_
  164.1 6.3 %assemble.1 = (f32[768,768]{1,0:T(8,128)}, f32[768,768]{1,0:T(8,128)}, f32[768,768]{1,0:T(8,128)}, f32[768,768]{1,0:T(8,128)}, f32[6,128]{1,0:T(8,128)}, /*index...) custom-call(s32[4]{0:T(128)S(1)} %pad_add_fusion.refs_0_.bits_ref, bf16[2,584,128]{2,1,0:T(8,128)(2,1)S(1)} %share.1.refs_0_, ...), custom_call_target="tpu_custom_call" | custom-call | flops 4718592 | bytes 14155776 | tf_op jit(solution)/shard_map/assemble/pallas_call | solution.py:918
  (63 shorter events, 1.8 us)
Async XLA Ops:
  0.6 11.1 %collective-permute-start = (bf16[128,768]{1,0:T(8,128)(2,1)}, bf16[128,768]{1,0:T(8,128)(2,1)S(1)}, u32[]{:S(2)}, u32[]{:S(2)}) collective-permute-start(bf16[128,768]{1,0:T(8,128)(2,1)} %refs_16_.1), channel_id=1, source_target_pairs={{0,8},{8,0},{1,9},{9,1},{2,10},{10,2},{3,11},{11,3},{4,12},{12,4},... | collective-permute-start | bytes 589832 | tf_op jit(solution)/shard_map/ppermute | solution.py:59
  4.4 7.4 %copy-start.4 = (bf16[128,768]{1,0:T(8,128)(2,1)S(1)}, bf16[128,768]{1,0:T(8,128)(2,1)}, u32[]{:S(2)}) copy-start(bf16[128,768]{1,0:T(8,128)(2,1)} %refs_16_.1) | copy-start | bytes 589828
  11.8 8.5 %copy-start.14 = (bf16[128,768]{1,0:T(8,128)(2,1)S(1)}, bf16[128,768]{1,0:T(8,128)(2,1)}, u32[]{:S(2)}) copy-start(bf16[128,768]{1,0:T(8,128)(2,1)} %get-tuple-element.80.refs_1_) | copy-start | bytes 589828
  11.8 31.9 %copy-start.5 = (bf16[256,768]{1,0:T(8,128)(2,1)}, bf16[256,768]{1,0:T(8,128)(2,1)S(1)}, u32[]{:S(2)}) copy-start(bf16[256,768]{1,0:T(8,128)(2,1)S(1)} %pad_maximum_fusion.refs_3_) | copy-start | bytes 1179652
  11.9 34.2 %all-to-all-start = ((bf16[16,40,768]{2,1,0:T(8,128)(2,1)}), bf16[16,40,768]{2,1,0:T(8,128)(2,1)}, u32[]{:S(2)}, u32[]{:S(2)}) async-start(bf16[16,40,768]{2,1,0:T(8,128)(2,1)} %bitcast.25), calls=%async_computation | async-start | bytes 1966080 | tf_op jit(solution)/shard_map/all_to_all | solution.py:1038
  17.9 31.4 %collective-permute-start.3 = (bf16[768,768]{1,0:T(8,128)(2,1)}, bf16[768,768]{1,0:T(8,128)(2,1)}, u32[]{:S(2)}, u32[]{:S(2)}) collective-permute-start(bf16[768,768]{1,0:T(8,128)(2,1)} %bitcast.8.refs_2_), channel_id=1, source_target_pairs={{0,1},{1,0},{2,3},{3,2},{4,5},{5,4},{6,7},{7,6},{8,9},{9,8},{10,11... | collective-permute-start | bytes 3538952 | tf_op jit(solution)/shard_map/ppermute | solution.py:59
  18.0 31.4 %collective-permute-start.4 = (bf16[768,768]{1,0:T(8,128)(2,1)}, bf16[768,768]{1,0:T(8,128)(2,1)}, u32[]{:S(2)}, u32[]{:S(2)}) collective-permute-start(bf16[768,768]{1,0:T(8,128)(2,1)} %bitcast.9.refs_3_), channel_id=1, source_target_pairs={{0,1},{1,0},{2,3},{3,2},{4,5},{5,4},{6,7},{7,6},{8,9},{9,8},{10,11... | collective-permute-start | bytes 3538952 | tf_op jit(solution)/shard_map/ppermute | solution.py:59
  18.5 27.6 %collective-permute-start.1 = (bf16[256,768]{1,0:T(8,128)(2,1)S(1)}, bf16[256,768]{1,0:T(8,128)(2,1)S(1)}, u32[]{:S(2)}, u32[]{:S(2)}) collective-permute-start(bf16[256,768]{1,0:T(8,128)(2,1)S(1)} %pad_maximum_fusion.refs_3_), channel_id=1, source_target_pairs={{0,2},{2,0},{1,3},{3,1},{4,6},{6,4},{5,7},{7,5},{8,10},{10,8},{9,1... | collective-permute-start | bytes 1179656 | tf_op jit(solution)/shard_map/ppermute | solution.py:59
  20.3 22.8 %collective-permute-start.2 = (bf16[128,768]{1,0:T(8,128)(2,1)S(1)}, bf16[128,768]{1,0:T(8,128)(2,1)S(1)}, u32[]{:S(2)}, u32[]{:S(2)}) collective-permute-start(bf16[128,768]{1,0:T(8,128)(2,1)S(1)} %copy-done.14), channel_id=1, source_target_pairs={{0,2},{2,0},{1,3},{3,1},{4,6},{6,4},{5,7},{7,5},{8,10},{10,8},{9,1... | collective-permute-start | bytes 589832 | tf_op jit(solution)/shard_map/ppermute | solution.py:59
  46.1 13.2 %copy-start.12 = (bf16[256,768]{1,0:T(8,128)(2,1)}, bf16[256,768]{1,0:T(8,128)(2,1)S(1)}, u32[]{:S(2)}) copy-start(bf16[256,768]{1,0:T(8,128)(2,1)S(1)} %collective-permute-done.1.refs_2_) | copy-start | bytes 1179652
  46.1 13.2 %collective-permute-start.5 = (bf16[256,768]{1,0:T(8,128)(2,1)}, bf16[256,768]{1,0:T(8,128)(2,1)S(1)}, u32[]{:S(2)}, u32[]{:S(2)}) collective-permute-start(bf16[256,768]{1,0:T(8,128)(2,1)} %get-tuple-element.85), channel_id=1, source_target_pairs={{0,8},{8,0},{1,9},{9,1},{2,10},{10,2},{3,11},{11,3},{4,12},{12,4},... | collective-permute-start | bytes 1179656 | tf_op jit(solution)/shard_map/ppermute | solution.py:59
  47.9 11.4 %collective-permute-start.6 = (bf16[256,768]{1,0:T(8,128)(2,1)}, bf16[256,768]{1,0:T(8,128)(2,1)S(1)}, u32[]{:S(2)}, u32[]{:S(2)}) collective-permute-start(bf16[256,768]{1,0:T(8,128)(2,1)} %get-tuple-element.86), channel_id=1, source_target_pairs={{0,4},{4,0},{1,5},{5,1},{2,6},{6,2},{3,7},{7,3},{8,12},{12,8},{9,1... | collective-permute-start | bytes 1179656 | tf_op jit(solution)/shard_map/ppermute | solution.py:59
  59.3 0.9 copy-start.13
  59.3 0.8 copy-start.7
  60.2 26.3 %all-to-all-start.1 = ((bf16[16,40,768]{2,1,0:T(8,128)(2,1)}), bf16[16,40,768]{2,1,0:T(8,128)(2,1)S(1)}, u32[]{:S(2)}, u32[]{:S(2)}) async-start(bf16[16,40,768]{2,1,0:T(8,128)(2,1)} %bitcast.26), calls=%async_computation.1 | async-start | bytes 1966080 | tf_op jit(solution)/shard_map/all_to_all | solution.py:1055
  66.1 17.1 %collective-permute-start.7 = (bf16[256,768]{1,0:T(8,128)(2,1)}, bf16[256,768]{1,0:T(8,128)(2,1)}, u32[]{:S(2)}, u32[]{:S(2)}) collective-permute-start(bf16[256,768]{1,0:T(8,128)(2,1)} %get-tuple-element.95), channel_id=1, source_target_pairs={{0,4},{4,0},{1,5},{5,1},{2,6},{6,2},{3,7},{7,3},{8,12},{12,8},{9,1... | collective-permute-start | bytes 1179656 | tf_op jit(solution)/shard_map/ppermute | solution.py:59
  86.4 0.9 copy-start.1
  87.4 15.4 %copy-start.6 = (bf16[256,768]{1,0:T(8,128)(2,1)S(1)}, bf16[256,768]{1,0:T(8,128)(2,1)}, u32[]{:S(2)}) copy-start(bf16[256,768]{1,0:T(8,128)(2,1)} %get-tuple-element.116.refs_1_) | copy-start | bytes 1179652
  87.4 15.9 %copy-start.8 = (bf16[256,768]{1,0:T(8,128)(2,1)S(1)}, bf16[256,768]{1,0:T(8,128)(2,1)}, u32[]{:S(2)}) copy-start(bf16[256,768]{1,0:T(8,128)(2,1)} %copy-done.7) | copy-start | bytes 1179652
  97.4 18.6 %all-to-all-start.2 = ((bf16[16,200,128]{2,1,0:T(8,128)(2,1)}), bf16[16,200,128]{2,1,0:T(8,128)(2,1)S(1)}, u32[]{:S(2)}, u32[]{:S(2)}) async-start(bf16[16,200,128]{2,1,0:T(8,128)(2,1)} %get-tuple-element.115), calls=%async_computation.2 | async-start | bytes 1638400 | tf_op jit(solution)/shard_map/all_to_all | solution.py:1080
  102.2 17.2 %collective-permute-start.12 = (bf16[768,768]{1,0:T(8,128)(2,1)}, bf16[768,768]{1,0:T(8,128)(2,1)}, u32[]{:S(2)}, u32[]{:S(2)}) collective-permute-start(bf16[768,768]{1,0:T(8,128)(2,1)} %get-tuple-element.123), channel_id=1, source_target_pairs={{0,1},{1,0},{2,3},{3,2},{4,5},{5,4},{6,7},{7,6},{8,9},{9,8},{10,11... | collective-permute-start | bytes 3538952 | tf_op jit(solution)/shard_map/ppermute | solution.py:59
  102.6 16.8 %collective-permute-start.13 = (bf16[768,768]{1,0:T(8,128)(2,1)}, bf16[768,768]{1,0:T(8,128)(2,1)}, u32[]{:S(2)}, u32[]{:S(2)}) collective-permute-start(bf16[768,768]{1,0:T(8,128)(2,1)} %get-tuple-element.125), channel_id=1, source_target_pairs={{0,1},{1,0},{2,3},{3,2},{4,5},{5,4},{6,7},{7,6},{8,9},{9,8},{10,11... | collective-permute-start | bytes 3538952 | tf_op jit(solution)/shard_map/ppermute | solution.py:59
  102.8 4.0 %collective-permute-start.8 = (bf16[256,768]{1,0:T(8,128)(2,1)S(1)}, bf16[256,768]{1,0:T(8,128)(2,1)S(1)}, u32[]{:S(2)}, u32[]{:S(2)}) collective-permute-start(bf16[256,768]{1,0:T(8,128)(2,1)S(1)} %copy-done.6), channel_id=1, source_target_pairs={{0,1},{1,0},{2,3},{3,2},{4,5},{5,4},{6,7},{7,6},{8,9},{9,8},{10,11... | collective-permute-start | bytes 1179656 | tf_op jit(solution)/shard_map/ppermute | solution.py:59
  103.1 4.1 %collective-permute-start.9 = (bf16[256,768]{1,0:T(8,128)(2,1)}, bf16[256,768]{1,0:T(8,128)(2,1)S(1)}, u32[]{:S(2)}, u32[]{:S(2)}) collective-permute-start(bf16[256,768]{1,0:T(8,128)(2,1)} %get-tuple-element.117.refs_2_), channel_id=1, source_target_pairs={{0,1},{1,0},{2,3},{3,2},{4,5},{5,4},{6,7},{7,6},{8,9},{9,8},{10,11... | collective-permute-start | bytes 1179656 | tf_op jit(solution)/shard_map/ppermute | solution.py:59
  103.3 4.6 %collective-permute-start.10 = (bf16[256,768]{1,0:T(8,128)(2,1)S(1)}, bf16[256,768]{1,0:T(8,128)(2,1)S(1)}, u32[]{:S(2)}, u32[]{:S(2)}) collective-permute-start(bf16[256,768]{1,0:T(8,128)(2,1)S(1)} %copy-done.8), channel_id=1, source_target_pairs={{0,1},{1,0},{2,3},{3,2},{4,5},{5,4},{6,7},{7,6},{8,9},{9,8},{10,11... | collective-permute-start | bytes 1179656 | tf_op jit(solution)/shard_map/ppermute | solution.py:59
  106.8 1.1 copy-start.9
  106.8 2.6 %collective-permute-start.11 = (bf16[256,768]{1,0:T(8,128)(2,1)}, bf16[256,768]{1,0:T(8,128)(2,1)}, u32[]{:S(2)}, u32[]{:S(2)}) collective-permute-start(bf16[256,768]{1,0:T(8,128)(2,1)} %collective-permute-done.7.refs_4_), channel_id=1, source_target_pairs={{0,1},{1,0},{2,3},{3,2},{4,5},{5,4},{6,7},{7,6},{8,9},{9,8},{10,11... | collective-permute-start | bytes 1179656 | tf_op jit(solution)/shard_map/ppermute | solution.py:59
  107.2 0.7 copy-start.10
  108.0 0.8 copy-start.11
  109.4 11.5 %copy-start.3 = (f32[768,768]{1,0:T(8,128)S(1)}, f32[768,768]{1,0:T(8,128)}, u32[]{:S(2)}) copy-start(f32[768,768]{1,0:T(8,128)} %get-tuple-element.129) | copy-start | bytes 7077892
  115.9 1.9 %copy-start = (bf16[768,2048]{1,0:T(8,128)(2,1)S(1)}, bf16[768,2048]{1,0:T(8,128)(2,1)}, u32[]{:S(2)}) copy-start(bf16[768,2048]{1,0:T(8,128)(2,1)} %left.1.refs_2_) | copy-start | bytes 9437188
  117.8 3.1 %copy-start.2 = (f32[768,768]{1,0:T(8,128)S(1)}, f32[768,768]{1,0:T(8,128)}, u32[]{:S(2)}) copy-start(f32[768,768]{1,0:T(8,128)} %get-tuple-element.127) | copy-start | bytes 7077892
  119.5 16.3 %collective-permute-start.14 = (bf16[2,584,128]{2,1,0:T(8,128)(2,1)S(1)}, bf16[2,584,128]{2,1,0:T(8,128)(2,1)S(1)}, u32[]{:S(2)}, u32[]{:S(2)}) collective-permute-start(bf16[2,584,128]{2,1,0:T(8,128)(2,1)S(1)} %grad_block.1.refs_0_), channel_id=1, source_target_pairs={{0,16},{16,0},{1,17},{17,1},{2,18},{18,2},{3,19},{19,3},{4,20},{20... | collective-permute-start | bytes 897032 | tf_op jit(solution)/shard_map/ppermute | solution.py:59
  135.8 8.1 %collective-permute-start.18 = (bf16[2,584,128]{2,1,0:T(8,128)(2,1)S(1)}, bf16[2,584,128]{2,1,0:T(8,128)(2,1)S(1)}, u32[]{:S(2)}, u32[]{:S(2)}) collective-permute-start(bf16[2,584,128]{2,1,0:T(8,128)(2,1)S(1)} %share.1.refs_0_), channel_id=1, source_target_pairs={{0,8},{8,0},{1,9},{9,1},{2,10},{10,2},{3,11},{11,3},{4,12},{12,4},... | collective-permute-start | bytes 897032 | tf_op jit(solution)/shard_map/ppermute | solution.py:59
  135.9 10.7 %collective-permute-start.22 = (bf16[2,584,128]{2,1,0:T(8,128)(2,1)S(1)}, bf16[2,584,128]{2,1,0:T(8,128)(2,1)S(1)}, u32[]{:S(2)}, u32[]{:S(2)}) collective-permute-start(bf16[2,584,128]{2,1,0:T(8,128)(2,1)S(1)} %share.1.refs_0_), channel_id=1, source_target_pairs={{0,1},{1,0},{2,3},{3,2},{4,5},{5,4},{6,7},{7,6},{8,9},{9,8},{10,11... | collective-permute-start | bytes 897032 | tf_op jit(solution)/shard_map/ppermute | solution.py:59
  136.0 12.0 %collective-permute-start.16 = (bf16[2,584,128]{2,1,0:T(8,128)(2,1)S(1)}, bf16[2,584,128]{2,1,0:T(8,128)(2,1)S(1)}, u32[]{:S(2)}, u32[]{:S(2)}) collective-permute-start(bf16[2,584,128]{2,1,0:T(8,128)(2,1)S(1)} %share.1.refs_0_), channel_id=1, source_target_pairs={{0,4},{4,0},{1,5},{5,1},{2,6},{6,2},{3,7},{7,3},{8,12},{12,8},{9,1... | collective-permute-start | bytes 897032 | tf_op jit(solution)/shard_map/ppermute | solution.py:59
  137.7 10.5 %collective-permute-start.15 = (bf16[2,584,128]{2,1,0:T(8,128)(2,1)S(1)}, bf16[2,584,128]{2,1,0:T(8,128)(2,1)S(1)}, u32[]{:S(2)}, u32[]{:S(2)}) collective-permute-start(bf16[2,584,128]{2,1,0:T(8,128)(2,1)S(1)} %share.1.refs_0_), channel_id=1, source_target_pairs={{0,2},{2,0},{1,3},{3,1},{4,6},{6,4},{5,7},{7,5},{8,10},{10,8},{9,1... | collective-permute-start | bytes 897032 | tf_op jit(solution)/shard_map/ppermute | solution.py:59
  143.9 10.7 %collective-permute-start.20 = (bf16[2,584,128]{2,1,0:T(8,128)(2,1)S(1)}, bf16[2,584,128]{2,1,0:T(8,128)(2,1)S(1)}, u32[]{:S(2)}, u32[]{:S(2)}) collective-permute-start(bf16[2,584,128]{2,1,0:T(8,128)(2,1)S(1)} %collective-permute-done.18.refs_4_), channel_id=1, source_target_pairs={{0,4},{4,0},{1,5},{5,1},{2,6},{6,2},{3,7},{7,3},{8,12},{12,8},{9,1... | collective-permute-start | bytes 897032 | tf_op jit(solution)/shard_map/ppermute | solution.py:59
  146.6 9.4 %collective-permute-start.26 = (bf16[2,584,128]{2,1,0:T(8,128)(2,1)S(1)}, bf16[2,584,128]{2,1,0:T(8,128)(2,1)S(1)}, u32[]{:S(2)}, u32[]{:S(2)}) collective-permute-start(bf16[2,584,128]{2,1,0:T(8,128)(2,1)S(1)} %collective-permute-done.18.refs_4_), channel_id=1, source_target_pairs={{0,1},{1,0},{2,3},{3,2},{4,5},{5,4},{6,7},{7,6},{8,9},{9,8},{10,11... | collective-permute-start | bytes 897032 | tf_op jit(solution)/shard_map/ppermute | solution.py:59
  146.6 9.9 %collective-permute-start.19 = (bf16[2,584,128]{2,1,0:T(8,128)(2,1)S(1)}, bf16[2,584,128]{2,1,0:T(8,128)(2,1)S(1)}, u32[]{:S(2)}, u32[]{:S(2)}) collective-permute-start(bf16[2,584,128]{2,1,0:T(8,128)(2,1)S(1)} %collective-permute-done.18.refs_4_), channel_id=1, source_target_pairs={{0,2},{2,0},{1,3},{3,1},{4,6},{6,4},{5,7},{7,5},{8,10},{10,8},{9,1... | collective-permute-start | bytes 897032 | tf_op jit(solution)/shard_map/ppermute | solution.py:59
  148.0 8.5 %collective-permute-start.24 = (bf16[2,584,128]{2,1,0:T(8,128)(2,1)S(1)}, bf16[2,584,128]{2,1,0:T(8,128)(2,1)S(1)}, u32[]{:S(2)}, u32[]{:S(2)}) collective-permute-start(bf16[2,584,128]{2,1,0:T(8,128)(2,1)S(1)} %collective-permute-done.16.refs_2_), channel_id=1, source_target_pairs={{0,1},{1,0},{2,3},{3,2},{4,5},{5,4},{6,7},{7,6},{8,9},{9,8},{10,11... | collective-permute-start | bytes 897032 | tf_op jit(solution)/shard_map/ppermute | solution.py:59
  148.3 11.2 %collective-permute-start.17 = (bf16[2,584,128]{2,1,0:T(8,128)(2,1)S(1)}, bf16[2,584,128]{2,1,0:T(8,128)(2,1)S(1)}, u32[]{:S(2)}, u32[]{:S(2)}) collective-permute-start(bf16[2,584,128]{2,1,0:T(8,128)(2,1)S(1)} %collective-permute-done.15.refs_1_), channel_id=1, source_target_pairs={{0,4},{4,0},{1,5},{5,1},{2,6},{6,2},{3,7},{7,3},{8,12},{12,8},{9,1... | collective-permute-start | bytes 897032 | tf_op jit(solution)/shard_map/ppermute | solution.py:59
  154.6 7.9 %collective-permute-start.21 = (bf16[2,584,128]{2,1,0:T(8,128)(2,1)S(1)}, bf16[2,584,128]{2,1,0:T(8,128)(2,1)S(1)}, u32[]{:S(2)}, u32[]{:S(2)}) collective-permute-start(bf16[2,584,128]{2,1,0:T(8,128)(2,1)S(1)} %collective-permute-done.20.refs_6_), channel_id=1, source_target_pairs={{0,2},{2,0},{1,3},{3,1},{4,6},{6,4},{5,7},{7,5},{8,10},{10,8},{9,1... | collective-permute-start | bytes 897032 | tf_op jit(solution)/shard_map/ppermute | solution.py:59
  156.0 6.5 %collective-permute-start.23 = (bf16[2,584,128]{2,1,0:T(8,128)(2,1)S(1)}, bf16[2,584,128]{2,1,0:T(8,128)(2,1)S(1)}, u32[]{:S(2)}, u32[]{:S(2)}) collective-permute-start(bf16[2,584,128]{2,1,0:T(8,128)(2,1)S(1)} %collective-permute-done.15.refs_1_), channel_id=1, source_target_pairs={{0,1},{1,0},{2,3},{3,2},{4,5},{5,4},{6,7},{7,6},{8,9},{9,8},{10,11... | collective-permute-start | bytes 897032 | tf_op jit(solution)/shard_map/ppermute | solution.py:59
  156.5 6.0 %collective-permute-start.28 = (bf16[2,584,128]{2,1,0:T(8,128)(2,1)S(1)}, bf16[2,584,128]{2,1,0:T(8,128)(2,1)S(1)}, u32[]{:S(2)}, u32[]{:S(2)}) collective-permute-start(bf16[2,584,128]{2,1,0:T(8,128)(2,1)S(1)} %collective-permute-done.20.refs_6_), channel_id=1, source_target_pairs={{0,1},{1,0},{2,3},{3,2},{4,5},{5,4},{6,7},{7,6},{8,9},{9,8},{10,11... | collective-permute-start | bytes 897032 | tf_op jit(solution)/shard_map/ppermute | solution.py:59
  156.6 6.0 %collective-permute-start.27 = (bf16[2,584,128]{2,1,0:T(8,128)(2,1)S(1)}, bf16[2,584,128]{2,1,0:T(8,128)(2,1)S(1)}, u32[]{:S(2)}, u32[]{:S(2)}) collective-permute-start(bf16[2,584,128]{2,1,0:T(8,128)(2,1)S(1)} %collective-permute-done.19.refs_5_), channel_id=1, source_target_pairs={{0,1},{1,0},{2,3},{3,2},{4,5},{5,4},{6,7},{7,6},{8,9},{9,8},{10,11... | collective-permute-start | bytes 897032 | tf_op jit(solution)/shard_map/ppermute | solution.py:59
  159.5 3.1 %collective-permute-start.25 = (bf16[2,584,128]{2,1,0:T(8,128)(2,1)S(1)}, bf16[2,584,128]{2,1,0:T(8,128)(2,1)S(1)}, u32[]{:S(2)}, u32[]{:S(2)}) collective-permute-start(bf16[2,584,128]{2,1,0:T(8,128)(2,1)S(1)} %collective-permute-done.17.refs_3_), channel_id=1, source_target_pairs={{0,1},{1,0},{2,3},{3,2},{4,5},{5,4},{6,7},{7,6},{8,9},{9,8},{10,11... | collective-permute-start | bytes 897032 | tf_op jit(solution)/shard_map/ppermute | solution.py:59
  162.5 1.6 collective-permute-start.29
  (1 other events, 0.7 us)

commit v4 on v3

--- a/solution.py
+++ b/solution.py
@@ -98,6 +98,11 @@
         return self.held.shape
 
 
+def wait_all(*operands):
+    for operand in operands:
+        operand.ref()
+
+
 class Leaving:
     def __init__(self, held, target, sem):
         self.held, self.copy = held, pltpu.make_async_copy(held, target, sem)
@@ -135,6 +140,18 @@
 
     def send(self):
         pass
+
+
+def slot_rows(slot, capacity):
+    if not mixed_tiles(capacity):
+        return slot, slot + capacity
+    main = capacity - 4
+    tail = slot >= main
+    return jnp.where(tail, slot + main, slot), jnp.where(tail, slot + main + 4, slot + main)
+
+
+def mixed_tiles(capacity):
+    return capacity > 4 and (capacity - 4) % 16 == 0
 
 
 def staged(
@@ -237,6 +254,8 @@
         choose_ref,
         slot_ref,
     ) = outputs
+    early, later = inputs[:7], inputs[7:]
+    wait_all(*early)
     low = jnp.bfloat16
     length, width = tokens_ref.shape
     experts = router_ref.shape[0]
@@ -279,6 +298,7 @@
 
     attended_ref.send()
     probs_ref.send()
+    wait_all(*later)
     hidden = inputs + jnp.dot(
         attended_ref[...], output_ref[...], preferred_element_type=jnp.float32
     )
@@ -305,8 +325,10 @@
     )
     slot = jnp.sum(running * chosen, axis=0, keepdims=True).astype(jnp.int32) - 1
     kept = alive & (slot < capacity)
-    column = jnp.where(kept, routes * (2 * capacity) + slot, -2 * capacity)
-    slot_ref[...] = column
+    columns = [
+        jnp.where(kept, routes * (2 * capacity) + row, -1) for row in slot_rows(slot, capacity)
+    ]
+    slot_ref[...] = jnp.concatenate(columns, axis=0)
     slot_ref.send()
     unit = jnp.where(place == lane, 1.0, 0.0).astype(low)
     choose = dot_last(unit, chosen.astype(low))
@@ -317,8 +339,8 @@
     row = lax.broadcasted_iota(jnp.int32, (experts * 2 * capacity, length), 0)
     spread = jnp.concatenate(
         [
-            jnp.where(row == column, 1.0, 0.0).astype(low),
-            jnp.where(row == column + capacity, 1.0, 0.0).astype(low),
+            jnp.where(row == columns[0], 1.0, 0.0).astype(low),
+            jnp.where(row == columns[1], 1.0, 0.0).astype(low),
         ],
         axis=1,
     )
@@ -348,7 +370,7 @@
         shaped((length, width), jnp.float32),
         shaped((length, experts), jnp.float32),
         shaped((length, experts), jnp.float32),
-        shaped((1, length), jnp.int32),
+        shaped((2, length), jnp.int32),
     )
     query, key, value, output = weights
     inputs = (tokens, gain, query, key, value, bias, routes, output, gain_two, router, cotangent)
@@ -379,16 +401,12 @@
         probs_ref,
         q_ref,
         k_ref,
-        query_ref,
-        key_ref,
-        value_ref,
-        tokens_ref,
-        gain_ref,
     ) = inputs
-    out_ref, grad_ref, late_ref = outputs
-    turned, sums, tail = scratch
+    late_ref, turned, hidden_grad_ref, out_ref = outputs
+    sums, tail = scratch
+    wait_all(*inputs[1:])
     low = jnp.bfloat16
-    length, width = tokens_ref.shape
+    length, width = hidden_ref.shape
     experts = router_ref.shape[0]
     capacity = came_ref.shape[2] // 2
     group = late_ref.shape[0]
@@ -398,11 +416,10 @@
     came = came_ref[:, 0].astype(jnp.float32) + came_ref[:, 1].astype(jnp.float32)
     came = came.reshape(slots, width).astype(low)
     row = lax.broadcasted_iota(jnp.int32, (slots, length), 0)
-    column = slot_ref[...]
     spread = jnp.concatenate(
         [
-            jnp.where(row == column, 1.0, 0.0).astype(low),
-            jnp.where(row == column + capacity, 1.0, 0.0).astype(low),
+            jnp.where(row == slot_ref[0:1], 1.0, 0.0).astype(low),
+            jnp.where(row == slot_ref[1:2], 1.0, 0.0).astype(low),
         ],
         axis=1,
     )
@@ -428,6 +445,8 @@
     )
     d_from_norm, grad_ffn = norm_backward(hidden, factor, gain_two, d_normed_two)
     d_hidden = top + d_from_norm
+    hidden_grad_ref[...] = d_hidden
+    hidden_grad_ref.send()
     d_mixed = d_hidden.astype(low)
     d_attended = dot_last(d_mixed, output_ref[...]).astype(low)
     flipped = d_mixed.T
@@ -478,20 +497,7 @@
             at = 2 * pair + head
             sums[at % 4, at // 4 : at // 4 + 1] = jnp.sum(own, axis=0, keepdims=True)
 
-    d_normed = 0.0
-    for which, weight in enumerate((query_ref, key_ref, value_ref)):
-        d_normed = d_normed + lax.dot_general(
-            turned[which],
-            weight[...],
-            (((0,), (1,)), ((), ())),
-            preferred_element_type=jnp.float32,
-        )
-    inputs = tokens_ref[...].astype(jnp.float32)
-    d_first, grad_norm = norm_backward(
-        inputs, rms_factor(inputs), row_of(gain_ref), d_normed
-    )
-    grad_ref[...] = (d_hidden + d_first).astype(low)
-    grad_ref.send()
+    turned.send()
 
     shift = lax.broadcasted_iota(jnp.int32, (2 * length, LANES), 0) - (length - 1)
     bucket = bucket_of(shift)
@@ -509,12 +515,11 @@
     tail[...] = jnp.zeros_like(tail)
     for chunk in range(chunks):
         lanes = slice(chunk * LANES, (chunk + 1) * LANES)
-        tail[chunk : chunk + 1] = grad_norm[:, lanes]
-        tail[chunks + chunk : chunks + chunk + 1] = grad_ffn[:, lanes]
+        tail[chunk : chunk + 1] = grad_ffn[:, lanes]
         for expert in range(experts):
-            at = 2 * chunks + HEADS // 4 + expert * chunks + chunk
+            at = chunks + HEADS // 4 + expert * chunks + chunk
             tail[at : at + 1] = grad_router[expert : expert + 1, lanes]
-    tail[2 * chunks : 2 * chunks + HEADS // 4] = bias_rows[: HEADS // 4]
+    tail[chunks : chunks + HEADS // 4] = bias_rows[: HEADS // 4]
     block = 4 * width // group
     for at in range(group):
         own = tail[at * small_rows : (at + 1) * small_rows]
@@ -523,42 +528,82 @@
     late_ref.send()
 
 
-def backward_of(came, tokens, gain, weights, gain_two, router, cotangent, saved, group):
-    length, width = tokens.shape
+def backward_of(came, weight, gain_two, router, cotangent, saved, group):
+    length, width = cotangent.shape
     experts = router.shape[0]
     low = jnp.bfloat16
     small_rows = -(-small_count(width, experts) // group)
     block = 4 * width // group
     outputs = (
+        shaped((group, block + 2 * small_rows, length), low),
+        shaped((3, width, length), low),
+        shaped((length, width), jnp.float32),
         shaped((length, width), low),
-        shaped((length, width), low),
-        shaped((group, block + 2 * small_rows, length), low),
     )
     scratch = (
-        pltpu.VMEM((3, width, length), low),
         pltpu.VMEM((4, 8, 2 * length), jnp.float32),
         pltpu.VMEM((group * small_rows, LANES), jnp.float32),
     )
-    query, key, value, output = weights
     q, k, v, probs, hidden, router_probs, choose, slot = saved
-    inputs = (slot, hidden, router_probs, choose, cotangent, gain_two, router, output)
-    inputs = inputs + (v, probs, q, k, query, key, value, tokens, gain)
+    inputs = (slot, hidden, router_probs, choose, cotangent, gain_two, router, weight)
     return staged(
         backward_kernel,
         "backward",
         (),
-        inputs,
+        (*inputs, v, probs, q, k),
         outputs,
         scratch,
-        10 * length * width * width,
+        4 * length * width * width,
         10 * width * width,
         residents=(came,),
         mib=62,
     )
 
 
+def first_norm_kernel(numbers, inputs, outputs, scratch):
+    turned, hidden_grad_ref, query_ref, key_ref, value_ref, tokens_ref, gain_ref = inputs
+    gain_out, grad_ref = outputs
+    wait_all(*inputs)
+    d_normed = 0.0
+    for which, weight in enumerate((query_ref, key_ref, value_ref)):
+        d_normed = d_normed + lax.dot_general(
+            turned[which],
+            weight[...],
+            (((0,), (1,)), ((), ())),
+            preferred_element_type=jnp.float32,
+        )
+    inputs = tokens_ref[...].astype(jnp.float32)
+    d_first, grad_norm = norm_backward(
+        inputs, rms_factor(inputs), row_of(gain_ref), d_normed
+    )
+    grad_ref[...] = (hidden_grad_ref[...] + d_first).astype(jnp.bfloat16)
+    grad_ref.send()
+    gain_out[...] = jnp.zeros(gain_out.shape, jnp.float32)
+    for chunk in range(gain_ref.shape[0]):
+        gain_out[chunk : chunk + 1] = grad_norm[:, chunk * LANES : (chunk + 1) * LANES]
+    gain_out.send()
+
+
+def first_norm_of(turned, hidden_grad, weights, tokens, gain):
+    length, width = tokens.shape
+    low = jnp.bfloat16
+    rows = -(-gain.shape[0] // 8) * 8
+    return staged(
+        first_norm_kernel,
+        "first_norm",
+        (),
+        (turned, hidden_grad, *weights, tokens, gain),
+        (shaped((length, width), low),),
+        (),
+        6 * length * width * width,
+        8 * width * width,
+        kept=(shaped((rows, LANES), jnp.float32),),
+        mib=59,
+    )
+
+
 def small_count(width, experts):
-    return (2 + experts) * (width // LANES) + HEADS // 4
+    return (1 + experts) * (width // LANES) + HEADS // 4
 
 
 def pick_kernel(numbers, inputs, outputs, scratch):
@@ -571,7 +616,7 @@
         for part, piece in enumerate(pieces):
             outputs[0][part * rows : (part + 1) * rows] = piece[...]
         outputs[0].send()
-    for out, turn in zip(outputs[-2:], (3, 2)):
+    for out, turn in zip(outputs[-2:], (3, 1)):
 
         @pl.when(which == turn)
         def _():
@@ -603,25 +648,25 @@
     (which_ref,), (*pieces, gain_ref), (left_ref,) = numbers, inputs, outputs
     which = which_ref[0]
     scale = row_of(gain_ref)
-    for number, piece in enumerate(pieces):
-        held = piece.ref()
-        count = held.shape[0]
-        spans = [
-            (at, slice(number * count + at, number * count + at + LANES))
-            for at in range(0, count, LANES)
-        ]
-
-        @pl.when(which < 3)
-        def _():
-            for at, span in spans:
-                own = held[at : at + LANES].astype(jnp.float32)
-                own = (own * rms_factor(own) * scale).astype(jnp.bfloat16)
-                left_ref[:, span] = own.T
-
-        @pl.when(which == 3)
-        def _():
-            for at, span in spans:
-                left_ref[:, span] = held[at : at + LANES].T
+    wait_all(*pieces)
+    count = pieces[0].shape[0]
+    spans = [
+        (piece, at, slice(number * count + at, number * count + at + LANES))
+        for number, piece in enumerate(pieces)
+        for at in range(0, count, LANES)
+    ]
+
+    @pl.when(which < 3)
+    def _():
+        for piece, at, span in spans:
+            own = piece[at : at + LANES].astype(jnp.float32)
+            own = (own * rms_factor(own) * scale).astype(jnp.bfloat16)
+            left_ref[:, span] = own.T
+
+    @pl.when(which == 3)
+    def _():
+        for piece, at, span in spans:
+            left_ref[:, span] = piece[at : at + LANES].T
 
     left_ref.send()
 
@@ -641,7 +686,7 @@
         10 * total * width,
         6 * total * width,
         kept=kept,
-        mib=60,
+        mib=59,
     )
     return left
 
@@ -650,23 +695,9 @@
 gelu_cubic = 0.044715
 
 
-def expert_kernel(numbers, inputs, outputs, scratch):
-    rows_ref, order_ref, in_a, out_a, in_b, out_b = inputs
-    back_ref, rows_out, grads_out, act_ref, inner_ref = outputs
-    count = rows_ref.shape[0]
-    half = count // 2
-    lanes = lax.broadcasted_iota(jnp.int32, (count, count), 1)
-    sort = jnp.where(order_ref[:, 0:1] == lanes, 1.0, 0.0).astype(jnp.bfloat16)
-    unsort = jnp.where(order_ref[:, 1:2] == lanes, 1.0, 0.0).astype(jnp.bfloat16)
-    ordered = jnp.dot(sort, rows_ref[...], preferred_element_type=jnp.float32)
-    ordered = ordered.astype(jnp.bfloat16)
-    rows, slots = ordered[:half], ordered[half:]
-    rows_out[...] = rows
-    rows_out.send()
-    grads_out[...] = slots
-    grads_out.send()
+def expert_pass(rows, slots, weights, act_ref, inner_ref):
     result, d_rows = 0.0, 0.0
-    for part, (part_in, part_out) in enumerate(((in_a, out_a), (in_b, out_b))):
+    for part, (part_in, part_out) in enumerate(weights):
         inner = jnp.dot(rows, part_in[...], preferred_element_type=jnp.float32)
         upstream = dot_last(slots, part_out[...])
         square = inner * inner
@@ -682,97 +713,195 @@
         d_rows = d_rows + dot_last(d_inner, part_in[...])
     act_ref.send()
     inner_ref.send()
+    return result, d_rows
+
+
+def expert_kernel(numbers, inputs, outputs, scratch):
+    blocks_ref, in_a, out_a, in_b, out_b = inputs
+    back_ref, rows_out, slots_out, act_ref, inner_ref = outputs
+    low = jnp.bfloat16
+    blocks, height, width = blocks_ref.shape
+    main = height // 2 - 4
+    count = blocks * main
+    mixed = blocks_ref[:, 2 * main :].astype(jnp.float32).reshape(blocks * 8, width)
+    place = lax.broadcasted_iota(jnp.int32, mixed.shape, 0) & 7
+    ahead = place < 4
+    second = pltpu.roll(mixed, blocks * 8 - 4, 0)
+    zero = jnp.zeros_like(mixed)
+    first_main = blocks_ref[:, :main].reshape(count, width)
+    second_main = blocks_ref[:, main : 2 * main].reshape(count, width)
+    rows = jnp.concatenate([first_main, jnp.where(ahead, mixed, zero).astype(low)], axis=0)
+    slots = jnp.concatenate([second_main, jnp.where(ahead, second, zero).astype(low)], axis=0)
+    rows_out[...] = rows
+    rows_out.send()
+    slots_out[...] = slots
+    slots_out.send()
+    weights = ((in_a, out_a), (in_b, out_b))
+    wait_all(in_a, out_a, in_b, out_b)
+    result, d_rows = expert_pass(rows, slots, weights, act_ref, inner_ref)
+    back_ref[:, :main] = result[:count].reshape(blocks, main, width).astype(low)
+    back_ref[:, main : 2 * main] = d_rows[:count].reshape(blocks, main, width).astype(low)
+    mixed = jnp.where(ahead, result[count:], pltpu.roll(d_rows[count:], 4, 0))
+    back_ref[:, 2 * main :] = mixed.reshape(blocks, 8, width).astype(low)
+    back_ref.send()
+
+
+def expert_sorting_kernel(numbers, inputs, outputs, scratch):
+    rows_ref, order_ref, in_a, out_a, in_b, out_b = inputs
+    back_ref, rows_out, slots_out, act_ref, inner_ref = outputs
+    count = rows_ref.shape[0]
+    half = count // 2
+    lanes = lax.broadcasted_iota(jnp.int32, (count, count), 1)
+    sort = jnp.where(order_ref[:, 0:1] == lanes, 1.0, 0.0).astype(jnp.bfloat16)
+    unsort = jnp.where(order_ref[:, 1:2] == lanes, 1.0, 0.0).astype(jnp.bfloat16)
+    ordered = jnp.dot(sort, rows_ref[...], preferred_element_type=jnp.float32)
+    ordered = ordered.astype(jnp.bfloat16)
+    rows, slots = ordered[:half], ordered[half:]
+    rows_out[...] = rows
+    rows_out.send()
+    slots_out[...] = slots
+    slots_out.send()
+    weights = ((in_a, out_a), (in_b, out_b))
+    result, d_rows = expert_pass(rows, slots, weights, act_ref, inner_ref)
     both = jnp.concatenate([result.astype(jnp.bfloat16), d_rows.astype(jnp.bfloat16)], axis=0)
     back_ref[...] = jnp.dot(unsort, both, preferred_element_type=jnp.float32).astype(jnp.bfloat16)
     back_ref.send()
 
 
-def expert_rows_of(rows, capacity, part_weights):
-    count, width = rows.shape
-    half = count // 2
-    place = np.arange(count)
-    sort = place % half // capacity * 2 * capacity + place // half * capacity + place % capacity
-    unsort = np.empty_like(sort)
-    unsort[sort] = place
-    order = jnp.asarray(np.stack([sort, unsort], axis=1), jnp.int32)
+def expert_rows_of(blocks, part_weights):
+    number, height, width = blocks.shape
+    capacity = height // 2
     hidden_width = part_weights[0].shape[1]
     low = jnp.bfloat16
+    mixed = mixed_tiles(capacity)
+    half = number * (capacity + 4 if mixed else capacity)
+    back = shaped(blocks.shape if mixed else (number * height, width), low)
     outputs = (
-        shaped((count, width), low),
+        back,
         shaped((half, width), low),
         shaped((half, width), low),
         shaped((2, half, hidden_width), low),
         shaped((2, half, hidden_width), low),
     )
-    return staged(
-        expert_kernel,
+    flops, moved = 16 * half * width * hidden_width, 12 * width * width
+    if mixed:
+        return staged(
+            expert_kernel,
+            "expert_rows",
+            (),
+            part_weights,
+            outputs,
+            (),
+            flops,
+            moved,
+            residents=(blocks,),
+            mib=62,
+        )
+    place = np.arange(2 * half)
+    sort = place % half // capacity * height + place // half * capacity + place % capacity
+    unsort = np.empty_like(sort)
+    unsort[sort] = place
+    order = jnp.asarray(np.stack([sort, unsort], axis=1), jnp.int32)
+    back, *rest = staged(
+        expert_sorting_kernel,
         "expert_rows",
         (),
-        (order, *part_weights),
+        (blocks.reshape(-1, width), order, *part_weights),
         outputs,
         (),
-        16 * half * width * hidden_width,
-        12 * width * width,
-        residents=(rows,),
-        mib=62,
-    )
-
-
-def expert_grads_kernel(numbers, inputs, outputs, scratch):
+        flops,
+        moved,
+    )
+    return back.reshape(blocks.shape), *rest
+
+
+def sent_grads_kernel(numbers, inputs, outputs, scratch):
     rows_ref, inner_ref, act_ref, slots_ref = inputs
-    sent_in, sent_out, own_in, own_out = outputs
+    sent_in, sent_out = outputs
+    wait_all(*inputs)
     sent_in[...] = dot_first(rows_ref[...], inner_ref[1]).astype(jnp.bfloat16)
     sent_in.send()
     sent_out[...] = dot_first(act_ref[1], slots_ref[...]).astype(jnp.bfloat16)
     sent_out.send()
-    own_in[...] = dot_first(rows_ref[...], inner_ref[0])
-    own_in.send()
-    own_out[...] = dot_first(act_ref[0], slots_ref[...])
-    own_out.send()
-
-
-def expert_grads_of(rows, slots, active, d_inner):
+
+
+def sent_grads_of(rows, slots, active, d_inner):
     half, width = rows.shape
     hidden_width = active.shape[2]
     outputs = (
         shaped((width, hidden_width), jnp.bfloat16),
         shaped((hidden_width, width), jnp.bfloat16),
+    )
+    return staged(
+        sent_grads_kernel,
+        "sent_grads",
+        (),
+        (rows, d_inner, active, slots),
+        outputs,
+        (),
+        4 * half * width * hidden_width,
+        8 * width * width,
+    )
+
+
+def own_grads_kernel(numbers, inputs, outputs, scratch):
+    rows_ref, inner_ref, act_ref, slots_ref, got_in, got_out = inputs
+    own_in, own_out = outputs
+    wait_all(*inputs)
+    own_in[...] = dot_first(rows_ref[...], inner_ref[0]) + got_in[...].astype(jnp.float32)
+    own_in.send()
+    own_out[...] = dot_first(act_ref[0], slots_ref[...]) + got_out[...].astype(jnp.float32)
+    own_out.send()
+
+
+def own_grads_of(rows, slots, active, d_inner, got_in, got_out):
+    half, width = rows.shape
+    hidden_width = active.shape[2]
+    outputs = (
         shaped((width, hidden_width), jnp.float32),
         shaped((hidden_width, width), jnp.float32),
     )
     return staged(
-        expert_grads_kernel,
-        "expert_grads",
-        (),
-        (rows, d_inner, active, slots),
+        own_grads_kernel,
+        "own_grads",
+        (),
+        (rows, d_inner, active, slots, got_in, got_out),
         outputs,
         (),
-        8 * half * width * hidden_width,
-        12 * width * width,
-    )
+        0,
+        0,
+    )
+
+
+def in_parts(values):
+    high = values.astype(jnp.bfloat16).astype(jnp.float32)
+    return jnp.concatenate([high, values - high], axis=0).astype(jnp.bfloat16)
+
+
+def from_parts(parts):
+    parts = parts.astype(jnp.float32)
+    rows = parts.shape[0] // 2
+    return parts[:rows] + parts[rows:]
 
 
 def block_kernel(numbers, inputs, outputs, scratch):
-    (bits_ref,), (late_ref, left_ref), (block_ref,) = numbers, inputs, outputs
+    (bits_ref,), (late_ref, left_ref, gain_ref), (block_ref,) = numbers, inputs, outputs
     group = late_ref.shape[0]
     part = left_ref.shape[0] // 2
     block = left_ref.shape[0] * 4 // group
     edge = block - LANES
     half = part // 2
-    small_rows = (block_ref.shape[1] - part - half) // 2
+    gain_edge = block_ref.shape[1] - 2 * gain_ref.shape[0]
     odd = bits_ref[3] == 1
-    which = bits_ref[0] * 2 + bits_ref[1]
-    here = which * 4 + bits_ref[2] * 2 + bits_ref[3]
+    here = bits_ref[0] * 8 + bits_ref[1] * 4 + bits_ref[2] * 2 + bits_ref[3]
     right = jnp.concatenate(
-        [late_ref[here ^ factor_order(i, which), :block] for i in range(group)], axis=1
+        [late_ref[here ^ factor_order(i), :block] for i in range(group)], axis=1
     )
     right = jnp.where(odd, jnp.concatenate([right[edge:], right[:edge]], axis=0), right)
     total = dot_last(left_ref[...], right)
     first = pair_masks(half)
-    tail = jnp.sum(late_ref[:, block:].astype(jnp.float32), axis=0)
-    small = tail[:small_rows] + tail[small_rows:]
-    high = small.astype(jnp.bfloat16).astype(jnp.float32)
-    both = jnp.concatenate([high, small - high], axis=0).astype(jnp.bfloat16)
+    small = in_parts(from_parts(jnp.sum(late_ref[:, block:].astype(jnp.float32), axis=0)))
+    gain = in_parts(gain_ref[...])
     for side in range(2):
         own = total[side * part : (side + 1) * part]
         block_ref[side, :part] = own[:, :LANES].astype(jnp.bfloat16)
@@ -782,13 +911,14 @@
         even = jnp.where(first, upper, lower)
         packed = jnp.where(odd, jnp.where(first, lower, upper), even)
         block_ref[side, part : part + half] = packed.astype(jnp.bfloat16)
-        block_ref[side, part + half :] = both
-
-
-def block_of(bits, late, left, small_rows):
+        block_ref[side, part + half : gain_edge] = small
+        block_ref[side, gain_edge:] = gain
+
+
+def block_of(bits, late, left, gain, small_rows):
     group, rows, length = late.shape
     width = left.shape[0]
-    kept = (shaped((2, 3 * width // 4 + 2 * small_rows, LANES), jnp.bfloat16),)
+    height = 3 * width // 4 + 2 * (small_rows + gain.shape[0])
     (block,) = staged(
         block_kernel,
         "grad_block",
@@ -798,34 +928,33 @@
         (),
         8 * width * width * length,
         2 * left.size,
-        residents=(late, left),
-        kept=kept,
+        residents=(late, left, gain),
+        kept=(shaped((2, height, LANES), jnp.bfloat16),),
         mib=24,
     )
     return block
 
 
-def share_kernel(numbers, inputs, outputs, scratch):
+def share_kernel(edge, small_rows, numbers, inputs, outputs, scratch):
     (own_ref, got_ref), (share_ref,) = inputs, outputs
-    small_rows = scratch[0].shape[0]
-    edge = own_ref.shape[1] - 2 * small_rows
+    gain_edge = edge + 2 * small_rows
     for side in range(2):
         own = own_ref[side, :edge].astype(jnp.float32) + got_ref[side, :edge].astype(jnp.float32)
         share_ref[side, :edge] = own.astype(jnp.bfloat16)
-        own, got = own_ref[side, edge:].astype(jnp.float32), got_ref[side, edge:].astype(jnp.float32)
-        small = (own[:small_rows] + own[small_rows:]) + (got[:small_rows] + got[small_rows:])
-        high = small.astype(jnp.bfloat16).astype(jnp.float32)
-        share_ref[side, edge:] = jnp.concatenate([high, small - high], axis=0).astype(jnp.bfloat16)
-
-
-def share_of(own, got, small_rows):
+        for rows in (slice(edge, gain_edge), slice(gain_edge, None)):
+            share_ref[side, rows] = in_parts(
+                from_parts(own_ref[side, rows]) + from_parts(got_ref[side, rows])
+            )
+
+
+def share_of(own, got, edge, small_rows):
     (share,) = staged(
-        share_kernel,
+        functools.partial(share_kernel, edge, small_rows),
         "share",
         (),
         (),
         (),
-        (pltpu.VMEM((small_rows, LANES), jnp.float32),),
+        (),
         own.size,
         6 * own.size,
         residents=(own, got),
@@ -835,88 +964,133 @@
     return share
 
 
-def assemble_kernel(part, small_rows, bits_ref, *refs):
-    sources, outs = refs[:16], refs[16:20]
-    norm_out, ffn_out, bias_out, router_out = refs[20:24]
-    held, made, tail, in_sems, out_sems = refs[24:]
+def assemble_kernel(weights, small_rows, bits_ref, sources, outs, made, out_sems, put_small):
     em, ey, dx, dc = [bits_ref[i] for i in range(4)]
+    part = made.shape[1] // 2
     half = part // 2
     edge = part + half
-    copies = [[] for _ in range(4)]
-    for number, source in enumerate(sources):
-        core, weight, step = dc ^ (number // 8), number // 2 % 4, number % 2
-        copies[weight].append(
-            pltpu.make_async_copy(
-                source, held.at[weight, (dx ^ step) * 2 + core], in_sems.at[number]
-            )
-        )
-    for weight in range(4):
-        for copy in copies[weight]:
-            copy.start()
     first = pair_masks(half)
-    for weight in range(4):
-        for copy in copies[weight]:
-            copy.wait()
-        for side in range(2):
-            rows = slice(side * part, (side + 1) * part)
-            upper = slice(side * part, side * part + half)
-            lower = slice(side * part + half, (side + 1) * part)
-            for twin in range(2):
-                even, odd = 2 * twin, 2 * twin + 1
-                at = 3 * twin * LANES
-                made[weight, rows, at : at + LANES] = held[weight, even, side, :part].astype(
-                    jnp.float32
-                )
-                made[weight, rows, at + 2 * LANES : at + 3 * LANES] = held[
-                    weight, odd, side, :part
-                ].astype(jnp.float32)
-                left = held[weight, even, side, part:edge].astype(jnp.float32)
-                right = held[weight, odd, side, part:edge].astype(jnp.float32)
-                middle = slice(at + LANES, at + 2 * LANES)
-                made[weight, upper, middle] = jnp.where(first, left, right)
-                made[weight, lower, middle] = pltpu.roll(
-                    jnp.where(first, right, left), HEAD_DIM, 1
-                )
+    for number, weight in enumerate(weights):
+        for here in range(4):
+
+            @pl.when(dx * 2 + dc == here)
+            def _():
+                own = [sources[4 * number + 2 * ((i ^ here) & 1) + ((i ^ here) >> 1)] for i in range(4)]
+                for side in range(2):
+                    rows = slice(side * part, (side + 1) * part)
+                    upper = slice(side * part, side * part + half)
+                    lower = slice(side * part + half, (side + 1) * part)
+                    for twin in range(2):
+                        even, odd = own[2 * twin], own[2 * twin + 1]
+                        at = 3 * twin * LANES
+                        made[number, rows, at : at + LANES] = even[side, :part].astype(jnp.float32)
+                        made[number, rows, at + 2 * LANES : at + 3 * LANES] = odd[
+                            side, :part
+                        ].astype(jnp.float32)
+                        left = even[side, part:edge].astype(jnp.float32)
+                        right = odd[side, part:edge].astype(jnp.float32)
+                        middle = slice(at + LANES, at + 2 * LANES)
+                        made[number, upper, middle] = jnp.where(first, left, right)
+                        made[number, lower, middle] = pltpu.roll(
+                            jnp.where(first, right, left), HEAD_DIM, 1
+                        )
+                for i in range(4):
+                    tail = own[i][0, edge:].astype(jnp.float32)
+                    gain = tail[2 * small_rows :]
+                    gain_rows = gain.shape[0] // 2
+                    put_small(
+                        number,
+                        i,
+                        jnp.concatenate(
+                            [
+                                tail[:small_rows] + tail[small_rows : 2 * small_rows],
+                                gain[:gain_rows] + gain[gain_rows:],
+                            ],
+                            axis=0,
+                        ),
+                    )
+
         truth = (em ^ (weight // 2)) * 2 + (ey ^ (weight % 2))
         for i in range(4):
 
             @pl.when(truth == i)
             def _():
-                pltpu.make_async_copy(made.at[weight], outs[i], out_sems.at[weight]).start()
-
+                pltpu.make_async_copy(made.at[number], outs[i], out_sems.at[number]).start()
+
+    for number, weight in enumerate(weights):
+        truth = (em ^ (weight // 2)) * 2 + (ey ^ (weight % 2))
         for i in range(4):
-            own = held[weight, i, 0, edge:].astype(jnp.float32)
-            tail[truth, i] = own[:small_rows] + own[small_rows:]
+
+            @pl.when(truth == i)
+            def _():
+                pltpu.make_async_copy(made.at[number], outs[i], out_sems.at[number]).wait()
+
+
+def first_half_kernel(small_rows, bits_ref, *refs):
+    sources, outs, small_out, made, out_sems = refs[:8], refs[8:12], refs[12], refs[13], refs[14]
+
+    def put_small(number, i, rows):
+        small_out[number, i] = rows
+
+    assemble_kernel((0, 2), small_rows, bits_ref, sources, outs, made, out_sems, put_small)
+
+
+def second_half_kernel(small_rows, bits_ref, *refs):
+    sources, small_ref, outs = refs[:8], refs[8], refs[13:17]
+    norm_out, ffn_out, bias_out, router_out = refs[17:21]
+    made, tail, out_sems = refs[21:]
+    em, ey = bits_ref[0], bits_ref[1]
+    for number in range(2):
+        tail[(em ^ number) * 2 + ey] = small_ref[number]
+
+    def put_small(number, i, rows):
+        tail[(em ^ number) * 2 + (ey ^ 1), i] = rows
+
+    assemble_kernel((1, 3), small_rows, bits_ref, sources, outs, made, out_sems, put_small)
 
     def small_row(at):
         at, row = divmod(at, small_rows)
         return tail[at // 4, at % 4, row : row + 1]
 
     chunks = made.shape[2] // LANES
+    total = 0.0
+    for at in range(16):
+        total = total + tail[at // 4, at % 4, small_rows:]
+    norm_out[...] = total[:chunks]
     for chunk in range(chunks):
         lanes = slice(chunk * LANES, (chunk + 1) * LANES)
-        norm_out[chunk : chunk + 1] = small_row(chunk)
-        ffn_out[chunk : chunk + 1] = small_row(chunks + chunk)
+        ffn_out[chunk : chunk + 1] = small_row(chunk)
         for expert in range(router_out.shape[0]):
             router_out[expert : expert + 1, lanes] = small_row(
-                2 * chunks + HEADS // 4 + expert * chunks + chunk
+                chunks + HEADS // 4 + expert * chunks + chunk
             )
     for head in range(HEADS):
         at = head % 4 * BUCKETS
-        bias_out[head : head + 1] = small_row(2 * chunks + head // 4)[:, at : at + BUCKETS]
-
-    for weight in range(4):
-        truth = (em ^ (weight // 2)) * 2 + (ey ^ (weight % 2))
-        for i in range(4):
-
-            @pl.when(truth == i)
-            def _():
-                pltpu.make_async_copy(made.at[weight], outs[i], out_sems.at[weight]).wait()
-
-
-def assemble(bits, sources, small_rows, width, experts):
+        bias_out[head : head + 1] = small_row(chunks + head // 4)[:, at : at + BUCKETS]
+
+
+def first_half(bits, sources, small_rows, width):
+    gain_rows = (sources[0].shape[1] - 3 * width // 4 - 2 * small_rows) // 2
+    *grads, small = pl.pallas_call(
+        functools.partial(first_half_kernel, small_rows),
+        out_shape=(shaped((width, width), jnp.float32),) * 4
+        + (shaped((2, 4, small_rows + gain_rows, LANES), jnp.float32),),
+        in_specs=[pl.BlockSpec(memory_space=pltpu.SMEM)] + [whole_spec()] * 8,
+        out_specs=(any_spec(),) * 4 + (whole_spec(),),
+        scratch_shapes=[
+            pltpu.VMEM((2, width, width), jnp.float32),
+            pltpu.SemaphoreType.DMA((2,)),
+        ],
+        compiler_params=params(16),
+        cost_estimate=cost(8 * width * width, 12 * width * width),
+        name="first_half",
+    )(bits, *sources)
+    return grads, small
+
+
+def second_half(bits, sources, small, grads, small_rows, width, experts):
     return pl.pallas_call(
-        functools.partial(assemble_kernel, width // 2, small_rows),
+        functools.partial(second_half_kernel, small_rows),
         out_shape=(shaped((width, width), jnp.float32),) * 4
         + (
             shaped((width // LANES, LANES), jnp.float32),
@@ -924,19 +1098,20 @@
             shaped((HEADS, BUCKETS), jnp.float32),
             shaped((experts, width), jnp.float32),
         ),
-        in_specs=[pl.BlockSpec(memory_space=pltpu.SMEM)] + [whole_spec()] * 16,
+        in_specs=[pl.BlockSpec(memory_space=pltpu.SMEM)]
+        + [whole_spec()] * 9
+        + [any_spec()] * 4,
         out_specs=(any_spec(),) * 4 + (whole_spec(),) * 4,
+        input_output_aliases={10 + i: i for i in range(4)},
         scratch_shapes=[
-            pltpu.VMEM((4, 4) + sources[0].shape, jnp.bfloat16),
-            pltpu.VMEM((4, width, width), jnp.float32),
-            pltpu.VMEM((4, 4, small_rows, LANES), jnp.float32),
-            pltpu.SemaphoreType.DMA((16,)),
-            pltpu.SemaphoreType.DMA((4,)),
+            pltpu.VMEM((2, width, width), jnp.float32),
+            pltpu.VMEM((4, 4) + small.shape[2:], jnp.float32),
+            pltpu.SemaphoreType.DMA((2,)),
         ],
-        compiler_params=params(32),
-        cost_estimate=cost(8 * width * width, 24 * width * width),
-        name="assemble",
-    )(bits, *sources)
+        compiler_params=params(16),
+        cost_estimate=cost(8 * width * width, 12 * width * width),
+        name="second_half",
+    )(bits, *sources, small, *grads)
 
 
 def place_in_group():
@@ -944,39 +1119,42 @@
     return (2 * place[0] + place[1]).astype(jnp.int32), jnp.stack(place).astype(jnp.int32)
 
 
-def factor_order(at, which):
-    low, high = at & 1, at >> 1 & 1
-    turned = jnp.where(which == 3, 2 * low + 8 * high, 8 * low + 2 * high)
-    return turned + (at >> 2 & 1) * 4 + (at >> 3)
+def factor_order(at):
+    return (at & 1) * 2 + (at >> 1 & 1) * 4 + (at >> 2 & 1) * 8 + (at >> 3)
 
 
 def with_other(rows, axis):
     return jnp.concatenate([rows, swap(rows, axis)], axis=0)
 
 
-def gathered_grads(late, left, place, small_rows, experts, beside):
+def gathered_grads(late, left, gain_rows, place, small_rows, experts, beside):
     width = left.shape[0]
-    block = block_of(place, late, left, small_rows)
+    block = block_of(place, late, left, gain_rows, small_rows)
     block, beside = lax.optimization_barrier((block, beside))
-    beside = [own + other.astype(jnp.float32) for own, other in beside]
+    beside = own_grads_of(*beside)
     got, beside = lax.optimization_barrier((swap(block, "eh"), beside))
-    near = share_of(block, got, small_rows)
+    near = share_of(block, got, 3 * width // 4, small_rows)
     far, near_x, near_y = swap(near, "em"), swap(near, "dx"), swap(near, "ey")
     far_x, far_y = swap(far, "dx"), swap(far, "ey")
     near_both, far_both = swap(near_x, "ey"), swap(far_y, "dx")
-    sources = (near, near_x, near_y, near_both, far, far_x, far_y, far_both)
-    sources = sources + tuple(swap(source, "dc") for source in sources)
-    return assemble(place, sources, small_rows, width, experts), beside
-
-
-def gathered_grads_plain(late, left, place, small_rows, experts, beside):
+
+    def both_cores(*sources):
+        return sources + tuple(swap(source, "dc") for source in sources)
+
+    sources = both_cores(near, near_x) + both_cores(far, far_x)
+    grads, small = first_half(place, sources, small_rows, width)
+    sources = both_cores(near_y, near_both) + both_cores(far_y, far_both)
+    grads = second_half(place, sources, small, grads, small_rows, width, experts)
+    return grads, beside
+
+
+def gathered_grads_plain(late, left, gain_rows, place, small_rows, experts, beside):
     group, rows, length = late.shape
     width = left.shape[0]
     block = 4 * width // group
     small = jnp.sum(late[:, block:].astype(jnp.float32), axis=0)
     small = lax.psum(small[:small_rows] + small[small_rows:], "eh")
-    which = place_in_group()[0]
-    order = jnp.stack([factor_order(at, which) for at in range(group)])
+    order = jnp.asarray([factor_order(at) for at in range(group)], jnp.int32)
     order = order ^ lax.axis_index(GROUP_AXES)
     late_block = jnp.take(late[:, :block], order, axis=0)
     late_block = late_block.transpose(1, 0, 2).reshape(block, group * length)
@@ -986,11 +1164,12 @@
     grads = lax.all_gather(grads, GROUP_AXES, axis=0, tiled=True)
     small = lax.all_gather(small, GROUP_AXES, axis=0, tiled=True).reshape(-1)
     grads = grads.reshape(4, width, width).transpose(0, 2, 1).astype(jnp.float32)
-    sizes = (width, width, HEADS * BUCKETS, experts * width)
+    sizes = (width, HEADS * BUCKETS, experts * width)
     ends = np.cumsum(sizes)
     pieces = [small[end - size : end] for end, size in zip(ends, sizes)]
-    pieces[2], pieces[3] = pieces[2].reshape(HEADS, BUCKETS), pieces[3].reshape(experts, width)
-    return (*grads, *pieces), [own + other.astype(jnp.float32) for own, other in beside]
+    pieces[1], pieces[2] = pieces[1].reshape(HEADS, BUCKETS), pieces[2].reshape(experts, width)
+    grad_norm = lax.psum(gain_rows, TOKEN_AXES)[: width // LANES]
+    return (*grads, grad_norm, *pieces), own_grads_of(*beside)
 
 
 def per_device(
@@ -1033,56 +1212,50 @@
         capacity,
     )
     which, place = place_in_group()
-    outgoing, near_tokens = lax.optimization_barrier((outgoing, with_other(tokens, "em")))
+    outgoing, near_tokens = lax.optimization_barrier((outgoing, with_other(tokens, "dx")))
     outgoing = outgoing.reshape(2 * experts, 2 * capacity, model_width)
     incoming = lax.all_to_all(outgoing, EXPERT_AXES, split_axis=0, concat_axis=0, tiled=True)
-    far_tokens = swap(near_tokens, "dx")
+    far_tokens = swap(near_tokens, "ey")
     near_attended, own_near, given_near = picked(
         which[None], (attended, swap(attended, "dx")), near_tokens
     )
-    incoming, far_tokens, near_attended, given_near = lax.optimization_barrier(
-        (incoming, far_tokens, near_attended, given_near)
-    )
-    far_attended, got_near = swap(near_attended, "em"), swap(given_near, "ey")
-    incoming = incoming.reshape(-1, model_width)
+    far_attended, got_near = swap(near_attended, "ey"), swap(given_near, "em")
+    incoming, far_tokens, _ = lax.optimization_barrier((incoming, far_tokens, given_near))
     sent_back, expert_rows, grad_slots, active, d_inner = expert_rows_of(
-        incoming, capacity, (w_in_own, w_out_own, w_in_other, w_out_other)
+        incoming, (w_in_own, w_out_own, w_in_other, w_out_other)
     )
     sent_back, far_attended, got_near = lax.optimization_barrier(
         (sent_back, far_attended, got_near)
     )
-    sent_back = sent_back.reshape(2 * experts, 2 * capacity, model_width)
     came_back = lax.all_to_all(sent_back, EXPERT_AXES, split_axis=0, concat_axis=0, tiled=True)
     own_far, given_far = picked(which[None], (far_attended,), far_tokens)
-    expert_rows, given_far = lax.optimization_barrier((expert_rows, given_far))
-    factors = [own_near, own_far, got_near, swap(given_far, "ey")]
-    in_other, out_other, in_own, out_own = expert_grads_of(
-        expert_rows, grad_slots, active, d_inner
-    )
-    came_back, factors, in_own, out_own, in_other, out_other = lax.optimization_barrier(
-        (came_back, factors, in_own, out_own, in_other, out_other)
-    )
+    in_other, out_other = sent_grads_of(expert_rows, grad_slots, active, d_inner)
+    factors = [own_near, own_far, got_near]
     factors = factors + [swap(rows, "dc") for rows in factors]
-    in_other, out_other = swap(in_other, "dc"), swap(out_other, "dc")
-
-    output, grad_input, late = backward_of(
+    came_back, factors, given_far, in_other, out_other = lax.optimization_barrier(
+        (came_back, factors, given_far, in_other, out_other)
+    )
+    got_far = swap(given_far, "em")
+    beside = (expert_rows, grad_slots, active, d_inner, swap(in_other, "dc"), swap(out_other, "dc"))
+
+    late, turned, hidden_grad, output = backward_of(
         came_back.reshape(experts, 2, 2 * capacity, model_width),
-        tokens,
-        gain_one,
-        weights,
+        w_output,
         gain_two,
         router,
         cotangent,
         saved,
         group,
     )
-
+    late, got_far = lax.optimization_barrier((late, got_far))
+    factors = factors[:3] + [got_far] + factors[3:] + [swap(got_far, "dc")]
     late = lax.all_to_all(late, GROUP_AXES, split_axis=0, concat_axis=0, tiled=True)
     left = left_of(which[None], factors, gain_one)
-    late, left = lax.optimization_barrier((late, left))
+    gain_rows, grad_input = first_norm_of(turned, hidden_grad, weights[:3], tokens, gain_one)
+    late, left, gain_rows = lax.optimization_barrier((late, left, gain_rows))
     gather = gathered_grads if lax.axis_size("eh") == 2 else gathered_grads_plain
     grads, (grad_in, grad_out) = gather(
-        late, left, place, small_rows, experts, ((in_own, in_other), (out_own, out_other))
+        late, left, gain_rows, place, small_rows, experts, beside
     )
     *grads, grad_norm, grad_ffn, grad_bias, grad_router = grads
     return (

time: 171 us -> 160 us (0.936)
  waiting for transfers between devices: 68.9 us -> 53.8 us
  Pallas kernels: 51.8 us -> 56.7 us
  other arithmetic: 4.54 us -> 0.1 us
  starting transfers between devices: 38.4 us -> 41.7 us
    ppermute x30, waiting for transfers between devices: 65.1 us -> 36.4 us  [swap(): return lax.ppermute(array, axis, perm=[(0, 1), (1, 0)])]
    all_to_all x1, waiting for transfers between devices: 3.28 us -> 14.4 us  [per_device(): lax.all_to_all(sent_back, EXPERT_AXES, split_axis=0, concat_axis=0, tiled...]
    pallas_call x9 -> x11, Pallas kernels: 45.5 us -> 50.1 us  [staged(): pl.pallas_call(body, out_shape=tuple(kept) + tuple(outputs), in_specs=[pl...]
    add x1 -> x0, other arithmetic: 4.44 us -> none  [gathered_grads(): beside = [own + other.astype(jnp.float32) for own, other in beside]]
    all_to_all x1, starting transfers between devices: 3.77 us -> 6.07 us  [per_device(): lax.all_to_all(sent_back, EXPERT_AXES, split_axis=0, concat_axis=0, tiled...]
    all_to_all x1, waiting for transfers between devices: 0.01 us -> 1.78 us  [per_device(): lax.all_to_all(outgoing, EXPERT_AXES, split_axis=0, concat_axis=0, tiled=...]
    pallas_call x1 -> x2, Pallas kernels: 6.32 us -> 6.6 us  [the longest x1 3.65 us: second_half(): pl.pallas_call(functools.partial(second_half_kernel, small_rows), out_sha...]
    unnamed x32 -> x26, local copies, waits for them, and re-layouts: 5.22 us -> 5.21 us
  transfers between devices with their start and end apart: 33 -> 33, of which waited for: 14 -> 10; matrix products, arithmetic and copies ran while one was open for 3% -> 0% of each run, Pallas kernels for 21% -> 33%
where the time goes in v4:
time: 160 us; the launch traced here: 159 us
  Pallas kernels  56.7 us (35%)
  waiting for transfers between devices  53.8 us (34%)
  starting transfers between devices  41.7 us (26%)
  local copies, waits for them, and re-layouts  5.21 us (3%)
  between operations  1.85 us (1%)
    pallas_call x11, Pallas kernels, staged(): pl.pallas_call(body, out_shape=tuple(kept) + tuple(outputs), in_specs=[pl...  50.1 us
    ppermute x30, waiting for transfers between devices, swap(): return lax.ppermute(array, axis, perm=[(0, 1), (1, 0)])  36.4 us
    ppermute x30, starting transfers between devices, swap(): return lax.ppermute(array, axis, perm=[(0, 1), (1, 0)])  25.1 us
    all_to_all x1, waiting for transfers between devices, per_device(): lax.all_to_all(sent_back, EXPERT_AXES, split_axis=0, concat_axis=0, tiled...  14.4 us
    all_to_all x1, starting transfers between devices, per_device(): lax.all_to_all(outgoing, EXPERT_AXES, split_axis=0, concat_axis=0, tiled=...  6.13 us
    all_to_all x1, starting transfers between devices, per_device(): lax.all_to_all(sent_back, EXPERT_AXES, split_axis=0, concat_axis=0, tiled...  6.07 us
    unnamed x26, local copies, waits for them, and re-layouts  5.21 us
    all_to_all x1, starting transfers between devices, per_device(): lax.all_to_all(late, GROUP_AXES, split_axis=0, concat_axis=0, tiled=True)  4.37 us
  transfers between devices with their start and end apart: 33, of which 10 were waited for; matrix products, arithmetic and copies ran while one was open for 0% of the time, Pallas kernels for 33%

profile of v4, /device:TPU:0, one launch (start us, length us, event | category | flops | bytes accessed | tf_op | source)
XLA Modules:
  0.0 159.4 jit_solution(8545926994878613994)
XLA Ops:
  0.6 3.0 %collective-permute-start = (bf16[128,768]{1,0:T(8,128)(2,1)}, bf16[128,768]{1,0:T(8,128)(2,1)S(1)}, u32[]{:S(2)}, u32[]{:S(2)}) collective-permute-start(bf16[128,768]{1,0:T(8,128)(2,1)} %refs_5_.5), channel_id=1, source_target_pairs={{0,2},{2,0},{1,3},{3,1},{4,6},{6,4},{5,7},{7,5},{8,10},{10,8},{9,1... | collective-permute-start | bytes 589832 | tf_op jit(solution)/shard_map/ppermute | solution.py:59
  4.3 6.4 %forward.1 = (bf16[8,2,40,768]{3,2,1,0:T(8,128)(2,1)}, bf16[128,768]{1,0:T(8,128)(2,1)}, bf16[128,768]{1,0:T(8,128)(2,1)}, bf16[128,768]{1,0:T(8,128)(2,1)}, bf1...) custom-call(s32[1]{0:T(128)S(6)} %copy.34.refs_0_, ...), custom_call_target="tpu_custom_call" | custom-call | flops 754974720 | bytes 5898240 | tf_op jit(solution)/shard_map/forward/pallas_call | solution.py:190
  10.8 6.1 %all-to-all-start = ((bf16[16,40,768]{2,1,0:T(8,128)(2,1)}), bf16[16,40,768]{2,1,0:T(8,128)(2,1)}, u32[]{:S(2)}, u32[]{:S(2)}) async-start(bf16[16,40,768]{2,1,0:T(8,128)(2,1)} %bitcast.21), calls=%async_computation | async-start | bytes 1966080 | tf_op jit(solution)/shard_map/all_to_all | solution.py:1217
  17.0 0.5 collective-permute-start.4
  17.5 1.8 %collective-permute-start.1 = (bf16[256,768]{1,0:T(8,128)(2,1)S(1)}, bf16[256,768]{1,0:T(8,128)(2,1)S(1)}, u32[]{:S(2)}, u32[]{:S(2)}) collective-permute-start(bf16[256,768]{1,0:T(8,128)(2,1)S(1)} %pad_maximum_fusion.refs_3_), channel_id=1, source_target_pairs={{0,4},{4,0},{1,5},{5,1},{2,6},{6,2},{3,7},{7,3},{8,12},{12,8},{9,1... | collective-permute-start | bytes 1179656 | tf_op jit(solution)/shard_map/ppermute | solution.py:59
  19.4 1.5 collective-permute-start.2
  20.8 5.8 %collective-permute-done.2.refs_2_ = bf16[128,768]{1,0:T(8,128)(2,1)S(1)} collective-permute-done((bf16[128,768]{1,0:T(8,128)(2,1)S(1)}, bf16[128,768]{1,0:T(8,128)(2,1)S(1)}, u32[]{:S(2)}, u32[]{:S(2)}) %collective-permute-start.2) | collective-permute-done | bytes 196640 | tf_op jit(solution)/shard_map/ppermute | solution.py:59
  26.6 0.7 copy-done.12
  27.3 2.3 %picked.2 = (bf16[256,768]{1,0:T(8,128)(2,1)}, bf16[256,768]{1,0:T(8,128)(2,1)}, bf16[256,768]{1,0:T(8,128)(2,1)}) custom-call(s32[1]{0:T(128)} %bitcast.6.refs_0_, bf16[128,768]{1,0:T(8,128)(2,1)} %get-tuple-element.90.refs_1_, bf16[128,768]{1,0:T(8,128)(2,1)} %copy-done.12, bf16[256,768]{1,0:T(8,128)(2,1)} %copy-done.4), custom_call_target="tpu_custom_call" | custom-call | bytes 1966080 | tf_op jit(solution)/shard_map/picked/pallas_call | solution.py:190
  29.6 4.0 %collective-permute-start.5 = (bf16[256,768]{1,0:T(8,128)(2,1)}, bf16[256,768]{1,0:T(8,128)(2,1)S(1)}, u32[]{:S(2)}, u32[]{:S(2)}) collective-permute-start(bf16[256,768]{1,0:T(8,128)(2,1)} %get-tuple-element.94), channel_id=1, source_target_pairs={{0,4},{4,0},{1,5},{5,1},{2,6},{6,2},{3,7},{7,3},{8,12},{12,8},{9,1... | collective-permute-start | bytes 1179656 | tf_op jit(solution)/shard_map/ppermute | solution.py:59
  33.6 4.3 %collective-permute-done.1.refs_2_ = bf16[256,768]{1,0:T(8,128)(2,1)S(1)} collective-permute-done((bf16[256,768]{1,0:T(8,128)(2,1)S(1)}, bf16[256,768]{1,0:T(8,128)(2,1)S(1)}, u32[]{:S(2)}, u32[]{:S(2)}) %collective-permute-start.1) | collective-permute-done | bytes 393248 | tf_op jit(solution)/shard_map/ppermute | solution.py:59
  37.9 1.8 %all-to-all-done.refs_0_ = bf16[16,40,768]{2,1,0:T(8,128)(2,1)} async-done(((bf16[16,40,768]{2,1,0:T(8,128)(2,1)}), bf16[16,40,768]{2,1,0:T(8,128)(2,1)}, u32[]{:S(2)}, u32[]{:S(2)}) %all-to-all-start) | async-done | bytes 983072 | tf_op jit(solution)/shard_map/all_to_all | solution.py:1217
  39.7 9.1 %expert_rows.1 = (bf16[16,40,768]{2,1,0:T(8,128)(2,1)}, bf16[384,768]{1,0:T(8,128)(2,1)}, bf16[384,768]{1,0:T(8,128)(2,1)}, bf16[2,384,768]{2,1,0:T(8,128)(2,1)}, bf16[2,384,768]{2,1,0:T(8,128)(2,1)}) custom-call(bf16[16,40,768]{2,1,0:T(8,128)(2,1)} %all-to-all-done.refs_0_, bf16[768,768]{1,0:T(8,128)(2,1)} %bitcast.7.refs_1_, ...), custom_call_target="tpu_custom_call" | custom-call | flops 3623878656 | bytes 7077888 | tf_op jit(solution)/shard_map/expert_rows/pallas_call | solution.py:190
  48.8 0.8 copy-done.6
  49.7 6.1 %all-to-all-start.1 = ((bf16[16,40,768]{2,1,0:T(8,128)(2,1)}), bf16[16,40,768]{2,1,0:T(8,128)(2,1)S(1)}, u32[]{:S(2)}, u32[]{:S(2)}) async-start(bf16[16,40,768]{2,1,0:T(8,128)(2,1)} %get-tuple-element.95), calls=%async_computation.1 | async-start | bytes 1966080 | tf_op jit(solution)/shard_map/all_to_all | solution.py:1230
  55.8 2.1 %picked.3 = (bf16[256,768]{1,0:T(8,128)(2,1)}, bf16[256,768]{1,0:T(8,128)(2,1)}) custom-call(s32[1]{0:T(128)} %bitcast.6.refs_0_, bf16[256,768]{1,0:T(8,128)(2,1)} %copy-done.10, bf16[256,768]{1,0:T(8,128)(2,1)} %copy-done.9), custom_call_target="tpu_custom_call" | custom-call | bytes 1966080 | tf_op jit(solution)/shard_map/picked/pallas_call | solution.py:190
  57.9 0.6 collective-permute-start.8
  58.5 4.4 %sent_grads.1 = (bf16[768,768]{1,0:T(8,128)(2,1)}, bf16[768,768]{1,0:T(8,128)(2,1)}) custom-call(bf16[384,768]{1,0:T(8,128)(2,1)} %get-tuple-element.138.refs_0_, bf16[2,384,768]{2,1,0:T(8,128)(2,1)} %get-tuple-element.139.refs_1_, bf16[2,384,768]{2,1,0:T(8,128)(2,1)} %get-tuple-element.140.refs_2_, bf16[384,768]{1,0:T(8,128)(2,1)} %get-tuple-element.141.refs_3_), custom_call_target="tpu_custom_call" | custom-call | flops 905969664 | bytes 4718592 | tf_op jit(solution)/shard_map/sent_grads/pallas_call | solution.py:190
  63.0 14.4 %all-to-all-done.1 = bf16[16,40,768]{2,1,0:T(8,128)(2,1)S(1)} async-done(((bf16[16,40,768]{2,1,0:T(8,128)(2,1)}), bf16[16,40,768]{2,1,0:T(8,128)(2,1)S(1)}, u32[]{:S(2)}, u32[]{:S(2)}) %all-to-all-start.1) | async-done | bytes 983072 | tf_op jit(solution)/shard_map/all_to_all | solution.py:1230
  77.4 2.8 %collective-permute-start.10 = (bf16[256,768]{1,0:T(8,128)(2,1)}, bf16[256,768]{1,0:T(8,128)(2,1)S(1)}, u32[]{:S(2)}, u32[]{:S(2)}) collective-permute-start(bf16[256,768]{1,0:T(8,128)(2,1)} %get-tuple-element.122), channel_id=1, source_target_pairs={{0,8},{8,0},{1,9},{9,1},{2,10},{10,2},{3,11},{11,3},{4,12},{12,4},... | collective-permute-start | bytes 1179656 | tf_op jit(solution)/shard_map/ppermute | solution.py:59
  80.2 7.6 %backward.1 = (bf16[16,200,128]{2,1,0:T(8,128)(2,1)}, bf16[3,768,128]{2,1,0:T(8,128)(2,1)}, f32[128,768]{1,0:T(8,128)}, bf16[128,768]{1,0:T(8,128)(2,1)}) custom-call(bf16[8,2,40,768]{3,2,1,0:T(8,128)(2,1)} %bitcast.20, s32[2,128]{1,0:T(2,128)} %get-tuple-element.109.refs_1_, f32[128,768]{1,0:T(8,128)} %get-tuple-element.110.refs_2_, ...), custom_call_target="tpu_custom_call" | custom-call | flops 301989888 | bytes 5898240 | tf_op jit(solution)/shard_map/backward/pallas_call | solution.py:190
  87.8 4.4 %all-to-all-start.2 = ((bf16[16,200,128]{2,1,0:T(8,128)(2,1)}), bf16[16,200,128]{2,1,0:T(8,128)(2,1)S(1)}, u32[]{:S(2)}, u32[]{:S(2)}) async-start(bf16[16,200,128]{2,1,0:T(8,128)(2,1)} %get-tuple-element.123), calls=%async_computation.2 | async-start | bytes 1638400 | tf_op jit(solution)/shard_map/all_to_all | solution.py:1252
  92.2 0.5 collective-permute-start.12
  92.7 0.1 collective-permute-start.13
  92.8 0.4 collective-permute-start.11
  93.3 5.1 %first_norm.1 = (f32[8,128]{1,0:T(8,128)}, bf16[128,768]{1,0:T(8,128)(2,1)}) custom-call(bf16[3,768,128]{2,1,0:T(8,128)(2,1)} %get-tuple-element.118.refs_0_, f32[128,768]{1,0:T(8,128)} %get-tuple-element.119.refs_1_, bf16[768,768]{1,0:T(8,128)(2,1)} %refs_2_.1, bf16[768,768]{1,0:T(8,128)(2,1)} %refs_3_.3, bf16[768,768]{1,0:T(8,128)(2,1)} %refs_4_.3, ...), custom_call_target="tpu_custom_call" | custom-call | flops 452984832 | bytes 4718592 | tf_op jit(solution)/shard_map/first_norm/pallas_call | solution.py:190
  98.4 0.7 copy-done.8
  99.1 5.5 %left.1.refs_2_ = bf16[768,2048]{1,0:T(8,128)(2,1)} custom-call(s32[1]{0:T(128)} %bitcast.6.refs_0_, bf16[256,768]{1,0:T(8,128)(2,1)} %get-tuple-element.124.refs_1_, bf16[256,768]{1,0:T(8,128)(2,1)} %get-tuple-element.125.refs_2_, bf16[256,768]{1,0:T(8,128)(2,1)} %copy-done.6, bf16[256,768]{1,0:T(8,128)(2,1)} %copy-done.7, ...), custom_call_target="tpu_custom_call" | custom-call | flops 15728640 | bytes 9437184 | tf_op jit(solution)/shard_map/left/pallas_call | solution.py:190
  104.6 1.3 all-to-all-done.2.refs_1_
  105.9 1.9 %copy-done = bf16[768,2048]{1,0:T(8,128)(2,1)S(1)} copy-done((bf16[768,2048]{1,0:T(8,128)(2,1)S(1)}, bf16[768,2048]{1,0:T(8,128)(2,1)}, u32[]{:S(2)}) %copy-start) | copy-done | bytes 3145752
  107.8 1.6 %grad_block.1.refs_0_ = bf16[2,600,128]{2,1,0:T(8,128)(2,1)S(1)} custom-call(s32[4]{0:T(128)S(1)} %pad_add_fusion.refs_0_.bits_ref, bf16[16,200,128]{2,1,0:T(8,128)(2,1)S(1)} %all-to-all-done.2.refs_1_, bf16[768,2048]{1,0:T(8,128)(2,1)S(1)} %copy-done, f32[8,128]{1,0:T(8,128)S(1)} %copy-done.1), custom_call_target="tpu_custom_call" | custom-call | flops 603979776 | bytes 3145728 | tf_op jit(solution)/shard_map/grad_block/pallas_call | solution.py:190
  109.5 1.0 copy-done.5
  110.5 1.5 collective-permute-start.14
  112.0 6.0 %own_grads.1 = (f32[768,768]{1,0:T(8,128)}, f32[768,768]{1,0:T(8,128)}) custom-call(bf16[384,768]{1,0:T(8,128)(2,1)} %get-tuple-element.138.refs_0_, bf16[2,384,768]{2,1,0:T(8,128)(2,1)} %get-tuple-element.139.refs_1_, bf16[2,384,768]{2,1,0:T(8,128)(2,1)} %get-tuple-element.140.refs_2_, bf16[384,768]{1,0:T(8,128)(2,1)} %get-tuple-element.141.refs_3_, ...), custom_call_target="tpu_custom_call" | custom-call | tf_op jit(solution)/shard_map/own_grads/pallas_call | solution.py:190
  118.0 8.8 %collective-permute-done.14.refs_1_ = bf16[2,600,128]{2,1,0:T(8,128)(2,1)S(1)} collective-permute-done((bf16[2,600,128]{2,1,0:T(8,128)(2,1)S(1)}, bf16[2,600,128]{2,1,0:T(8,128)(2,1)S(1)}, u32[]{:S(2)}, u32[]{:S(2)}) %collective-permute-start.14) | collective-permute-done | bytes 307232 | tf_op jit(solution)/shard_map/ppermute | solution.py:59
  127.1 1.2 collective-permute-start.16
  128.2 1.5 collective-permute-start.15
  129.7 5.9 %collective-permute-done.20.refs_4_ = bf16[2,600,128]{2,1,0:T(8,128)(2,1)S(1)} collective-permute-done((bf16[2,600,128]{2,1,0:T(8,128)(2,1)S(1)}, bf16[2,600,128]{2,1,0:T(8,128)(2,1)S(1)}, u32[]{:S(2)}, u32[]{:S(2)}) %collective-permute-start.20) | collective-permute-done | bytes 307232 | tf_op jit(solution)/shard_map/ppermute | solution.py:59
  135.6 1.7 %collective-permute-start.21 = (bf16[2,600,128]{2,1,0:T(8,128)(2,1)S(1)}, bf16[2,600,128]{2,1,0:T(8,128)(2,1)S(1)}, u32[]{:S(2)}, u32[]{:S(2)}) collective-permute-start(bf16[2,600,128]{2,1,0:T(8,128)(2,1)S(1)} %collective-permute-done.20.refs_4_), channel_id=1, source_target_pairs={{0,4},{4,0},{1,5},{5,1},{2,6},{6,2},{3,7},{7,3},{8,12},{12,8},{9,1... | collective-permute-start | bytes 921608 | tf_op jit(solution)/shard_map/ppermute | solution.py:59
  137.2 1.5 collective-permute-start.27
  138.7 0.5 collective-permute-start.26
  139.3 6.5 %collective-permute-done.21.refs_4_ = bf16[2,600,128]{2,1,0:T(8,128)(2,1)S(1)} collective-permute-done((bf16[2,600,128]{2,1,0:T(8,128)(2,1)S(1)}, bf16[2,600,128]{2,1,0:T(8,128)(2,1)S(1)}, u32[]{:S(2)}, u32[]{:S(2)}) %collective-permute-start.21) | collective-permute-done | bytes 307232 | tf_op jit(solution)/shard_map/ppermute | solution.py:59
  145.8 1.2 collective-permute-start.22
  147.0 0.5 collective-permute-start.18
  147.6 3.1 %collective-permute-done.17.refs_1_ = bf16[2,600,128]{2,1,0:T(8,128)(2,1)S(1)} collective-permute-done((bf16[2,600,128]{2,1,0:T(8,128)(2,1)S(1)}, bf16[2,600,128]{2,1,0:T(8,128)(2,1)S(1)}, u32[]{:S(2)}, u32[]{:S(2)}) %collective-permute-start.17) | collective-permute-done | bytes 307232 | tf_op jit(solution)/shard_map/ppermute | solution.py:59
  150.7 1.9 %collective-permute-done.22.refs_5_ = bf16[2,600,128]{2,1,0:T(8,128)(2,1)S(1)} collective-permute-done((bf16[2,600,128]{2,1,0:T(8,128)(2,1)S(1)}, bf16[2,600,128]{2,1,0:T(8,128)(2,1)S(1)}, u32[]{:S(2)}, u32[]{:S(2)}) %collective-permute-start.22) | collective-permute-done | bytes 307232 | tf_op jit(solution)/shard_map/ppermute | solution.py:59
  152.6 3.0 %first_half.1 = (f32[768,768]{1,0:T(8,128)}, f32[768,768]{1,0:T(8,128)}, f32[768,768]{1,0:T(8,128)}, f32[768,768]{1,0:T(8,128)}, f32[2,4,12,128]{3,2,1,0:T(8,128)S(1)}) custom-call(s32[4]{0:T(128)S(1)} %pad_add_fusion.refs_0_.bits_ref, bf16[2,600,128]{2,1,0:T(8,128)(2,1)S(1)} %share.1.refs_0_, bf16[2,600,128]{2,1,0:T(8,128)(2,1)S(1)} %collective-permute-done.16.refs_1_, ...), custom_call_target="tpu_custom_call" | custom-call | flops 4718592 | bytes 7077888 | tf_op jit(solution)/shard_map/first_half/pallas_call | solution.py:1074
  155.6 3.6 %second_half.1 = (f32[768,768]{1,0:T(8,128)}, f32[768,768]{1,0:T(8,128)}, f32[768,768]{1,0:T(8,128)}, f32[768,768]{1,0:T(8,128)}, f32[6,128]{1,0:T(8,128)}, /*in...) custom-call(s32[4]{0:T(128)S(1)} %pad_add_fusion.refs_0_.bits_ref, ...), custom_call_target="tpu_custom_call", output_to_operand_aliasing={{0}: (10, {}), {1}: (11, {}), {2}: (12, {}), {3}: (13, {})} | custom-call | flops 4718592 | bytes 7077888 | tf_op jit(solution)/shard_map/second_half/pallas_call | solution.py:1092
  (59 shorter events, 0.9 us)
Async XLA Ops:
  0.6 10.1 %collective-permute-start = (bf16[128,768]{1,0:T(8,128)(2,1)}, bf16[128,768]{1,0:T(8,128)(2,1)S(1)}, u32[]{:S(2)}, u32[]{:S(2)}) collective-permute-start(bf16[128,768]{1,0:T(8,128)(2,1)} %refs_5_.5), channel_id=1, source_target_pairs={{0,2},{2,0},{1,3},{3,1},{4,6},{6,4},{5,7},{7,5},{8,10},{10,8},{9,1... | collective-permute-start | bytes 589832 | tf_op jit(solution)/shard_map/ppermute | solution.py:59
  4.3 6.5 %copy-start.3 = (bf16[128,768]{1,0:T(8,128)(2,1)S(1)}, bf16[128,768]{1,0:T(8,128)(2,1)}, u32[]{:S(2)}) copy-start(bf16[128,768]{1,0:T(8,128)(2,1)} %refs_5_.5) | copy-start | bytes 589828
  10.8 16.5 %copy-start.4 = (bf16[256,768]{1,0:T(8,128)(2,1)}, bf16[256,768]{1,0:T(8,128)(2,1)S(1)}, u32[]{:S(2)}) copy-start(bf16[256,768]{1,0:T(8,128)(2,1)S(1)} %pad_maximum_fusion.refs_3_) | copy-start | bytes 1179652
  10.8 8.5 %copy-start.11 = (bf16[128,768]{1,0:T(8,128)(2,1)S(1)}, bf16[128,768]{1,0:T(8,128)(2,1)}, u32[]{:S(2)}) copy-start(bf16[128,768]{1,0:T(8,128)(2,1)} %get-tuple-element.90.refs_1_) | copy-start | bytes 589828
  10.8 28.9 %all-to-all-start = ((bf16[16,40,768]{2,1,0:T(8,128)(2,1)}), bf16[16,40,768]{2,1,0:T(8,128)(2,1)}, u32[]{:S(2)}, u32[]{:S(2)}) async-start(bf16[16,40,768]{2,1,0:T(8,128)(2,1)} %bitcast.21), calls=%async_computation | async-start | bytes 1966080 | tf_op jit(solution)/shard_map/all_to_all | solution.py:1217
  17.0 22.7 %collective-permute-start.3 = (bf16[768,768]{1,0:T(8,128)(2,1)}, bf16[768,768]{1,0:T(8,128)(2,1)}, u32[]{:S(2)}, u32[]{:S(2)}) collective-permute-start(bf16[768,768]{1,0:T(8,128)(2,1)} %bitcast.7.refs_1_), channel_id=1, source_target_pairs={{0,1},{1,0},{2,3},{3,2},{4,5},{5,4},{6,7},{7,6},{8,9},{9,8},{10,11... | collective-permute-start | bytes 3538952 | tf_op jit(solution)/shard_map/ppermute | solution.py:59
  17.0 22.6 %collective-permute-start.4 = (bf16[768,768]{1,0:T(8,128)(2,1)}, bf16[768,768]{1,0:T(8,128)(2,1)}, u32[]{:S(2)}, u32[]{:S(2)}) collective-permute-start(bf16[768,768]{1,0:T(8,128)(2,1)} %bitcast.8.refs_2_), channel_id=1, source_target_pairs={{0,1},{1,0},{2,3},{3,2},{4,5},{5,4},{6,7},{7,6},{8,9},{9,8},{10,11... | collective-permute-start | bytes 3538952 | tf_op jit(solution)/shard_map/ppermute | solution.py:59
  17.5 20.4 %collective-permute-start.1 = (bf16[256,768]{1,0:T(8,128)(2,1)S(1)}, bf16[256,768]{1,0:T(8,128)(2,1)S(1)}, u32[]{:S(2)}, u32[]{:S(2)}) collective-permute-start(bf16[256,768]{1,0:T(8,128)(2,1)S(1)} %pad_maximum_fusion.refs_3_), channel_id=1, source_target_pairs={{0,4},{4,0},{1,5},{5,1},{2,6},{6,2},{3,7},{7,3},{8,12},{12,8},{9,1... | collective-permute-start | bytes 1179656 | tf_op jit(solution)/shard_map/ppermute | solution.py:59
  19.4 7.3 %collective-permute-start.2 = (bf16[128,768]{1,0:T(8,128)(2,1)S(1)}, bf16[128,768]{1,0:T(8,128)(2,1)S(1)}, u32[]{:S(2)}, u32[]{:S(2)}) collective-permute-start(bf16[128,768]{1,0:T(8,128)(2,1)S(1)} %copy-done.11), channel_id=1, source_target_pairs={{0,2},{2,0},{1,3},{3,1},{4,6},{6,4},{5,7},{7,5},{8,10},{10,8},{9,1... | collective-permute-start | bytes 589832 | tf_op jit(solution)/shard_map/ppermute | solution.py:59
  26.6 0.7 copy-start.12
  29.6 19.2 %collective-permute-start.5 = (bf16[256,768]{1,0:T(8,128)(2,1)}, bf16[256,768]{1,0:T(8,128)(2,1)S(1)}, u32[]{:S(2)}, u32[]{:S(2)}) collective-permute-start(bf16[256,768]{1,0:T(8,128)(2,1)} %get-tuple-element.94), channel_id=1, source_target_pairs={{0,4},{4,0},{1,5},{5,1},{2,6},{6,2},{3,7},{7,3},{8,12},{12,8},{9,1... | collective-permute-start | bytes 1179656 | tf_op jit(solution)/shard_map/ppermute | solution.py:59
  33.6 15.2 %collective-permute-start.6 = (bf16[256,768]{1,0:T(8,128)(2,1)}, bf16[256,768]{1,0:T(8,128)(2,1)S(1)}, u32[]{:S(2)}, u32[]{:S(2)}) collective-permute-start(bf16[256,768]{1,0:T(8,128)(2,1)} %get-tuple-element.91), channel_id=1, source_target_pairs={{0,8},{8,0},{1,9},{9,1},{2,10},{10,2},{3,11},{11,3},{4,12},{12,4},... | collective-permute-start | bytes 1179656 | tf_op jit(solution)/shard_map/ppermute | solution.py:59
  37.9 10.9 %copy-start.9 = (bf16[256,768]{1,0:T(8,128)(2,1)}, bf16[256,768]{1,0:T(8,128)(2,1)S(1)}, u32[]{:S(2)}) copy-start(bf16[256,768]{1,0:T(8,128)(2,1)S(1)} %collective-permute-done.1.refs_2_) | copy-start | bytes 1179652
  48.8 0.9 copy-start.10
  48.8 0.8 copy-start.6
  49.7 27.7 %all-to-all-start.1 = ((bf16[16,40,768]{2,1,0:T(8,128)(2,1)}), bf16[16,40,768]{2,1,0:T(8,128)(2,1)S(1)}, u32[]{:S(2)}, u32[]{:S(2)}) async-start(bf16[16,40,768]{2,1,0:T(8,128)(2,1)} %get-tuple-element.95), calls=%async_computation.1 | async-start | bytes 1966080 | tf_op jit(solution)/shard_map/all_to_all | solution.py:1230
  55.7 7.2 %collective-permute-start.7 = (bf16[256,768]{1,0:T(8,128)(2,1)}, bf16[256,768]{1,0:T(8,128)(2,1)}, u32[]{:S(2)}, u32[]{:S(2)}) collective-permute-start(bf16[256,768]{1,0:T(8,128)(2,1)} %get-tuple-element.124.refs_1_), channel_id=1, source_target_pairs={{0,1},{1,0},{2,3},{3,2},{4,5},{5,4},{6,7},{7,6},{8,9},{9,8},{10,11... | collective-permute-start | bytes 1179656 | tf_op jit(solution)/shard_map/ppermute | solution.py:59
  57.9 5.1 %collective-permute-start.8 = (bf16[256,768]{1,0:T(8,128)(2,1)}, bf16[256,768]{1,0:T(8,128)(2,1)}, u32[]{:S(2)}, u32[]{:S(2)}) collective-permute-start(bf16[256,768]{1,0:T(8,128)(2,1)} %get-tuple-element.125.refs_2_), channel_id=1, source_target_pairs={{0,1},{1,0},{2,3},{3,2},{4,5},{5,4},{6,7},{7,6},{8,9},{9,8},{10,11... | collective-permute-start | bytes 1179656 | tf_op jit(solution)/shard_map/ppermute | solution.py:59
  58.5 4.5 %collective-permute-start.9 = (bf16[256,768]{1,0:T(8,128)(2,1)}, bf16[256,768]{1,0:T(8,128)(2,1)}, u32[]{:S(2)}, u32[]{:S(2)}) collective-permute-start(bf16[256,768]{1,0:T(8,128)(2,1)} %copy-done.6), channel_id=1, source_target_pairs={{0,1},{1,0},{2,3},{3,2},{4,5},{5,4},{6,7},{7,6},{8,9},{9,8},{10,11... | collective-permute-start | bytes 1179656 | tf_op jit(solution)/shard_map/ppermute | solution.py:59
  77.4 2.8 %copy-start.2 = (bf16[16,40,768]{2,1,0:T(8,128)(2,1)}, bf16[16,40,768]{2,1,0:T(8,128)(2,1)S(1)}, u32[]{:S(2)}) copy-start(bf16[16,40,768]{2,1,0:T(8,128)(2,1)S(1)} %all-to-all-done.1) | copy-start | bytes 2949124
  77.4 10.4 %collective-permute-start.10 = (bf16[256,768]{1,0:T(8,128)(2,1)}, bf16[256,768]{1,0:T(8,128)(2,1)S(1)}, u32[]{:S(2)}, u32[]{:S(2)}) collective-permute-start(bf16[256,768]{1,0:T(8,128)(2,1)} %get-tuple-element.122), channel_id=1, source_target_pairs={{0,8},{8,0},{1,9},{9,1},{2,10},{10,2},{3,11},{11,3},{4,12},{12,4},... | collective-permute-start | bytes 1179656 | tf_op jit(solution)/shard_map/ppermute | solution.py:59
  87.8 10.5 %copy-start.7 = (bf16[256,768]{1,0:T(8,128)(2,1)}, bf16[256,768]{1,0:T(8,128)(2,1)S(1)}, u32[]{:S(2)}) copy-start(bf16[256,768]{1,0:T(8,128)(2,1)S(1)} %collective-permute-done.10.refs_4_) | copy-start | bytes 1179652
  87.8 18.1 %all-to-all-start.2 = ((bf16[16,200,128]{2,1,0:T(8,128)(2,1)}), bf16[16,200,128]{2,1,0:T(8,128)(2,1)S(1)}, u32[]{:S(2)}, u32[]{:S(2)}) async-start(bf16[16,200,128]{2,1,0:T(8,128)(2,1)} %get-tuple-element.123), calls=%async_computation.2 | async-start | bytes 1638400 | tf_op jit(solution)/shard_map/all_to_all | solution.py:1252
  92.2 17.2 %collective-permute-start.12 = (bf16[768,768]{1,0:T(8,128)(2,1)}, bf16[768,768]{1,0:T(8,128)(2,1)S(1)}, u32[]{:S(2)}, u32[]{:S(2)}) collective-permute-start(bf16[768,768]{1,0:T(8,128)(2,1)} %get-tuple-element.135), channel_id=1, source_target_pairs={{0,1},{1,0},{2,3},{3,2},{4,5},{5,4},{6,7},{7,6},{8,9},{9,8},{10,11... | collective-permute-start | bytes 3538952 | tf_op jit(solution)/shard_map/ppermute | solution.py:59
  92.7 17.8 %collective-permute-start.13 = (bf16[768,768]{1,0:T(8,128)(2,1)}, bf16[768,768]{1,0:T(8,128)(2,1)}, u32[]{:S(2)}, u32[]{:S(2)}) collective-permute-start(bf16[768,768]{1,0:T(8,128)(2,1)} %get-tuple-element.136), channel_id=1, source_target_pairs={{0,1},{1,0},{2,3},{3,2},{4,5},{5,4},{6,7},{7,6},{8,9},{9,8},{10,11... | collective-permute-start | bytes 3538952 | tf_op jit(solution)/shard_map/ppermute | solution.py:59
  92.8 5.6 %collective-permute-start.11 = (bf16[256,768]{1,0:T(8,128)(2,1)S(1)}, bf16[256,768]{1,0:T(8,128)(2,1)S(1)}, u32[]{:S(2)}, u32[]{:S(2)}) collective-permute-start(bf16[256,768]{1,0:T(8,128)(2,1)S(1)} %collective-permute-done.10.refs_4_), channel_id=1, source_target_pairs={{0,1},{1,0},{2,3},{3,2},{4,5},{5,4},{6,7},{7,6},{8,9},{9,8},{10,11... | collective-permute-start | bytes 1179656 | tf_op jit(solution)/shard_map/ppermute | solution.py:59
  98.4 7.6 %copy-start.1 = (f32[8,128]{1,0:T(8,128)S(1)}, f32[8,128]{1,0:T(8,128)}, u32[]{:S(2)}) copy-start(f32[8,128]{1,0:T(8,128)} %get-tuple-element.134.refs_3_) | copy-start | bytes 12292
  98.4 0.8 copy-start.8
  105.9 1.9 %copy-start = (bf16[768,2048]{1,0:T(8,128)(2,1)S(1)}, bf16[768,2048]{1,0:T(8,128)(2,1)}, u32[]{:S(2)}) copy-start(bf16[768,2048]{1,0:T(8,128)(2,1)} %left.1.refs_2_) | copy-start | bytes 9437188
  109.5 1.0 copy-start.5
  110.5 16.3 %collective-permute-start.14 = (bf16[2,600,128]{2,1,0:T(8,128)(2,1)S(1)}, bf16[2,600,128]{2,1,0:T(8,128)(2,1)S(1)}, u32[]{:S(2)}, u32[]{:S(2)}) collective-permute-start(bf16[2,600,128]{2,1,0:T(8,128)(2,1)S(1)} %grad_block.1.refs_0_), channel_id=1, source_target_pairs={{0,16},{16,0},{1,17},{17,1},{2,18},{18,2},{3,19},{19,3},{4,20},{20... | collective-permute-start | bytes 921608 | tf_op jit(solution)/shard_map/ppermute | solution.py:59
  126.9 8.7 %collective-permute-start.20 = (bf16[2,600,128]{2,1,0:T(8,128)(2,1)S(1)}, bf16[2,600,128]{2,1,0:T(8,128)(2,1)S(1)}, u32[]{:S(2)}, u32[]{:S(2)}) collective-permute-start(bf16[2,600,128]{2,1,0:T(8,128)(2,1)S(1)} %share.1.refs_0_), channel_id=1, source_target_pairs={{0,8},{8,0},{1,9},{9,1},{2,10},{10,2},{3,11},{11,3},{4,12},{12,4},... | collective-permute-start | bytes 921608 | tf_op jit(solution)/shard_map/ppermute | solution.py:59
  127.0 11.7 %collective-permute-start.25 = (bf16[2,600,128]{2,1,0:T(8,128)(2,1)S(1)}, bf16[2,600,128]{2,1,0:T(8,128)(2,1)S(1)}, u32[]{:S(2)}, u32[]{:S(2)}) collective-permute-start(bf16[2,600,128]{2,1,0:T(8,128)(2,1)S(1)} %share.1.refs_0_), channel_id=1, source_target_pairs={{0,1},{1,0},{2,3},{3,2},{4,5},{5,4},{6,7},{7,6},{8,9},{9,8},{10,11... | collective-permute-start | bytes 921608 | tf_op jit(solution)/shard_map/ppermute | solution.py:59
  127.1 11.7 %collective-permute-start.16 = (bf16[2,600,128]{2,1,0:T(8,128)(2,1)S(1)}, bf16[2,600,128]{2,1,0:T(8,128)(2,1)S(1)}, u32[]{:S(2)}, u32[]{:S(2)}) collective-permute-start(bf16[2,600,128]{2,1,0:T(8,128)(2,1)S(1)} %share.1.refs_0_), channel_id=1, source_target_pairs={{0,2},{2,0},{1,3},{3,1},{4,6},{6,4},{5,7},{7,5},{8,10},{10,8},{9,1... | collective-permute-start | bytes 921608 | tf_op jit(solution)/shard_map/ppermute | solution.py:59
  128.2 11.0 %collective-permute-start.15 = (bf16[2,600,128]{2,1,0:T(8,128)(2,1)S(1)}, bf16[2,600,128]{2,1,0:T(8,128)(2,1)S(1)}, u32[]{:S(2)}, u32[]{:S(2)}) collective-permute-start(bf16[2,600,128]{2,1,0:T(8,128)(2,1)S(1)} %share.1.refs_0_), channel_id=1, source_target_pairs={{0,4},{4,0},{1,5},{5,1},{2,6},{6,2},{3,7},{7,3},{8,12},{12,8},{9,1... | collective-permute-start | bytes 921608 | tf_op jit(solution)/shard_map/ppermute | solution.py:59
  135.6 10.2 %collective-permute-start.21 = (bf16[2,600,128]{2,1,0:T(8,128)(2,1)S(1)}, bf16[2,600,128]{2,1,0:T(8,128)(2,1)S(1)}, u32[]{:S(2)}, u32[]{:S(2)}) collective-permute-start(bf16[2,600,128]{2,1,0:T(8,128)(2,1)S(1)} %collective-permute-done.20.refs_4_), channel_id=1, source_target_pairs={{0,4},{4,0},{1,5},{5,1},{2,6},{6,2},{3,7},{7,3},{8,12},{12,8},{9,1... | collective-permute-start | bytes 921608 | tf_op jit(solution)/shard_map/ppermute | solution.py:59
  137.2 9.8 %collective-permute-start.27 = (bf16[2,600,128]{2,1,0:T(8,128)(2,1)S(1)}, bf16[2,600,128]{2,1,0:T(8,128)(2,1)S(1)}, u32[]{:S(2)}, u32[]{:S(2)}) collective-permute-start(bf16[2,600,128]{2,1,0:T(8,128)(2,1)S(1)} %collective-permute-done.20.refs_4_), channel_id=1, source_target_pairs={{0,2},{2,0},{1,3},{3,1},{4,6},{6,4},{5,7},{7,5},{8,10},{10,8},{9,1... | collective-permute-start | bytes 921608 | tf_op jit(solution)/shard_map/ppermute | solution.py:59
  138.7 8.3 %collective-permute-start.28 = (bf16[2,600,128]{2,1,0:T(8,128)(2,1)S(1)}, bf16[2,600,128]{2,1,0:T(8,128)(2,1)S(1)}, u32[]{:S(2)}, u32[]{:S(2)}) collective-permute-start(bf16[2,600,128]{2,1,0:T(8,128)(2,1)S(1)} %collective-permute-done.20.refs_4_), channel_id=1, source_target_pairs={{0,1},{1,0},{2,3},{3,2},{4,5},{5,4},{6,7},{7,6},{8,9},{9,8},{10,11... | collective-permute-start | bytes 921608 | tf_op jit(solution)/shard_map/ppermute | solution.py:59
  138.7 8.8 %collective-permute-start.26 = (bf16[2,600,128]{2,1,0:T(8,128)(2,1)S(1)}, bf16[2,600,128]{2,1,0:T(8,128)(2,1)S(1)}, u32[]{:S(2)}, u32[]{:S(2)}) collective-permute-start(bf16[2,600,128]{2,1,0:T(8,128)(2,1)S(1)} %collective-permute-done.16.refs_1_), channel_id=1, source_target_pairs={{0,1},{1,0},{2,3},{3,2},{4,5},{5,4},{6,7},{7,6},{8,9},{9,8},{10,11... | collective-permute-start | bytes 921608 | tf_op jit(solution)/shard_map/ppermute | solution.py:59
  139.2 11.5 %collective-permute-start.17 = (bf16[2,600,128]{2,1,0:T(8,128)(2,1)S(1)}, bf16[2,600,128]{2,1,0:T(8,128)(2,1)S(1)}, u32[]{:S(2)}, u32[]{:S(2)}) collective-permute-start(bf16[2,600,128]{2,1,0:T(8,128)(2,1)S(1)} %collective-permute-done.16.refs_1_), channel_id=1, source_target_pairs={{0,4},{4,0},{1,5},{5,1},{2,6},{6,2},{3,7},{7,3},{8,12},{12,8},{9,1... | collective-permute-start | bytes 921608 | tf_op jit(solution)/shard_map/ppermute | solution.py:59
  145.8 6.9 %collective-permute-start.22 = (bf16[2,600,128]{2,1,0:T(8,128)(2,1)S(1)}, bf16[2,600,128]{2,1,0:T(8,128)(2,1)S(1)}, u32[]{:S(2)}, u32[]{:S(2)}) collective-permute-start(bf16[2,600,128]{2,1,0:T(8,128)(2,1)S(1)} %collective-permute-done.21.refs_4_), channel_id=1, source_target_pairs={{0,2},{2,0},{1,3},{3,1},{4,6},{6,4},{5,7},{7,5},{8,10},{10,8},{9,1... | collective-permute-start | bytes 921608 | tf_op jit(solution)/shard_map/ppermute | solution.py:59
  147.0 5.7 %collective-permute-start.29 = (bf16[2,600,128]{2,1,0:T(8,128)(2,1)S(1)}, bf16[2,600,128]{2,1,0:T(8,128)(2,1)S(1)}, u32[]{:S(2)}, u32[]{:S(2)}) collective-permute-start(bf16[2,600,128]{2,1,0:T(8,128)(2,1)S(1)} %collective-permute-done.27.refs_5_), channel_id=1, source_target_pairs={{0,1},{1,0},{2,3},{3,2},{4,5},{5,4},{6,7},{7,6},{8,9},{9,8},{10,11... | collective-permute-start | bytes 921608 | tf_op jit(solution)/shard_map/ppermute | solution.py:59
  147.0 8.6 %collective-permute-start.18 = (bf16[2,600,128]{2,1,0:T(8,128)(2,1)S(1)}, bf16[2,600,128]{2,1,0:T(8,128)(2,1)S(1)}, u32[]{:S(2)}, u32[]{:S(2)}) collective-permute-start(bf16[2,600,128]{2,1,0:T(8,128)(2,1)S(1)} %collective-permute-done.15.refs_0_), channel_id=1, source_target_pairs={{0,1},{1,0},{2,3},{3,2},{4,5},{5,4},{6,7},{7,6},{8,9},{9,8},{10,11... | collective-permute-start | bytes 921608 | tf_op jit(solution)/shard_map/ppermute | solution.py:59
  147.5 8.1 %collective-permute-start.23 = (bf16[2,600,128]{2,1,0:T(8,128)(2,1)S(1)}, bf16[2,600,128]{2,1,0:T(8,128)(2,1)S(1)}, u32[]{:S(2)}, u32[]{:S(2)}) collective-permute-start(bf16[2,600,128]{2,1,0:T(8,128)(2,1)S(1)} %collective-permute-done.21.refs_4_), channel_id=1, source_target_pairs={{0,1},{1,0},{2,3},{3,2},{4,5},{5,4},{6,7},{7,6},{8,9},{9,8},{10,11... | collective-permute-start | bytes 921608 | tf_op jit(solution)/shard_map/ppermute | solution.py:59
  150.7 4.9 %collective-permute-start.19 = (bf16[2,600,128]{2,1,0:T(8,128)(2,1)S(1)}, bf16[2,600,128]{2,1,0:T(8,128)(2,1)S(1)}, u32[]{:S(2)}, u32[]{:S(2)}) collective-permute-start(bf16[2,600,128]{2,1,0:T(8,128)(2,1)S(1)} %collective-permute-done.17.refs_1_), channel_id=1, source_target_pairs={{0,1},{1,0},{2,3},{3,2},{4,5},{5,4},{6,7},{7,6},{8,9},{9,8},{10,11... | collective-permute-start | bytes 921608 | tf_op jit(solution)/shard_map/ppermute | solution.py:59
  152.6 3.0 %collective-permute-start.24 = (bf16[2,600,128]{2,1,0:T(8,128)(2,1)S(1)}, bf16[2,600,128]{2,1,0:T(8,128)(2,1)S(1)}, u32[]{:S(2)}, u32[]{:S(2)}) collective-permute-start(bf16[2,600,128]{2,1,0:T(8,128)(2,1)S(1)} %collective-permute-done.22.refs_5_), channel_id=1, source_target_pairs={{0,1},{1,0},{2,3},{3,2},{4,5},{5,4},{6,7},{7,6},{8,9},{9,8},{10,11... | collective-permute-start | bytes 921608 | tf_op jit(solution)/shard_map/ppermute | solution.py:59

commit v5 on v4

--- a/solution.py
+++ b/solution.py
@@ -598,7 +598,7 @@
         6 * length * width * width,
         8 * width * width,
         kept=(shaped((rows, LANES), jnp.float32),),
-        mib=59,
+        mib=56,
     )
 
 
@@ -686,7 +686,7 @@
         10 * total * width,
         6 * total * width,
         kept=kept,
-        mib=59,
+        mib=44,
     )
     return left
 
@@ -695,74 +695,92 @@
 gelu_cubic = 0.044715
 
 
-def expert_pass(rows, slots, weights, act_ref, inner_ref):
+def hidden_pass(rows, slots, part_in, part_out):
+    inner = jnp.dot(rows, part_in[...], preferred_element_type=jnp.float32)
+    upstream = dot_last(slots, part_out[...])
+    square = inner * inner
+    bent = jnp.tanh(gelu_scale * (inner + gelu_cubic * (square * inner)))
+    active = (inner * (0.5 * (1.0 + bent))).astype(jnp.bfloat16)
+    slope = 0.5 * (1.0 + bent) + 0.5 * inner * (1.0 - bent * bent) * (
+        gelu_scale * (1.0 + 3.0 * gelu_cubic * square)
+    )
+    return active, (upstream * slope).astype(jnp.bfloat16)
+
+
+def expert_pass(rows, slots, weights):
     result, d_rows = 0.0, 0.0
-    for part, (part_in, part_out) in enumerate(weights):
-        inner = jnp.dot(rows, part_in[...], preferred_element_type=jnp.float32)
-        upstream = dot_last(slots, part_out[...])
-        square = inner * inner
-        bent = jnp.tanh(gelu_scale * (inner + gelu_cubic * (square * inner)))
-        active = (inner * (0.5 * (1.0 + bent))).astype(jnp.bfloat16)
-        slope = 0.5 * (1.0 + bent) + 0.5 * inner * (1.0 - bent * bent) * (
-            gelu_scale * (1.0 + 3.0 * gelu_cubic * square)
-        )
-        d_inner = (upstream * slope).astype(jnp.bfloat16)
-        act_ref[part] = active
-        inner_ref[part] = d_inner
+    for part_in, part_out in weights:
+        active, d_inner = hidden_pass(rows, slots, part_in, part_out)
         result = result + jnp.dot(active, part_out[...], preferred_element_type=jnp.float32)
         d_rows = d_rows + dot_last(d_inner, part_in[...])
-    act_ref.send()
-    inner_ref.send()
     return result, d_rows
+
+
+def four_of_eight(shape):
+    return lax.broadcasted_iota(jnp.int32, shape, 0) & 7 < 4
+
+
+def sorted_rows(blocks_ref):
+    number, height, width = blocks_ref.shape
+    main = height // 2 - 4
+    mixed = blocks_ref[:, 2 * main :].astype(jnp.float32).reshape(number * 8, width)
+    ahead = four_of_eight(mixed.shape)
+    second = pltpu.roll(mixed, number * 8 - 4, 0)
+    zero = jnp.zeros_like(mixed)
+    sorted_kinds = []
+    for whole, rest in (
+        (blocks_ref[:, :main], mixed),
+        (blocks_ref[:, main : 2 * main], second),
+    ):
+        rest = jnp.where(ahead, rest, zero).astype(jnp.bfloat16)
+        sorted_kinds.append(jnp.concatenate([whole.reshape(number * main, width), rest], axis=0))
+    return sorted_kinds
 
 
 def expert_kernel(numbers, inputs, outputs, scratch):
     blocks_ref, in_a, out_a, in_b, out_b = inputs
-    back_ref, rows_out, slots_out, act_ref, inner_ref = outputs
+    (back_ref,) = outputs
     low = jnp.bfloat16
     blocks, height, width = blocks_ref.shape
     main = height // 2 - 4
     count = blocks * main
-    mixed = blocks_ref[:, 2 * main :].astype(jnp.float32).reshape(blocks * 8, width)
-    place = lax.broadcasted_iota(jnp.int32, mixed.shape, 0) & 7
-    ahead = place < 4
-    second = pltpu.roll(mixed, blocks * 8 - 4, 0)
-    zero = jnp.zeros_like(mixed)
-    first_main = blocks_ref[:, :main].reshape(count, width)
-    second_main = blocks_ref[:, main : 2 * main].reshape(count, width)
-    rows = jnp.concatenate([first_main, jnp.where(ahead, mixed, zero).astype(low)], axis=0)
-    slots = jnp.concatenate([second_main, jnp.where(ahead, second, zero).astype(low)], axis=0)
-    rows_out[...] = rows
-    rows_out.send()
-    slots_out[...] = slots
-    slots_out.send()
-    weights = ((in_a, out_a), (in_b, out_b))
+    rows, slots = sorted_rows(blocks_ref)
     wait_all(in_a, out_a, in_b, out_b)
-    result, d_rows = expert_pass(rows, slots, weights, act_ref, inner_ref)
+    result, d_rows = expert_pass(rows, slots, ((in_a, out_a), (in_b, out_b)))
     back_ref[:, :main] = result[:count].reshape(blocks, main, width).astype(low)
     back_ref[:, main : 2 * main] = d_rows[:count].reshape(blocks, main, width).astype(low)
-    mixed = jnp.where(ahead, result[count:], pltpu.roll(d_rows[count:], 4, 0))
+    mixed = result[count:]
+    mixed = jnp.where(four_of_eight(mixed.shape), mixed, pltpu.roll(d_rows[count:], 4, 0))
     back_ref[:, 2 * main :] = mixed.reshape(blocks, 8, width).astype(low)
     back_ref.send()
 
 
+def sorting(number, height):
+    half, capacity = number * height // 2, height // 2
+    place = np.arange(2 * half)
+    sort = place % half // capacity * height + place // half * capacity + place % capacity
+    unsort = np.empty_like(sort)
+    unsort[sort] = place
+    return jnp.asarray(np.stack([sort, unsort], axis=1), jnp.int32)
+
+
+def rows_by_product(rows_ref, order_ref):
+    count = rows_ref.shape[0]
+    lanes = lax.broadcasted_iota(jnp.int32, (count, count), 1)
+    sort = jnp.where(order_ref[:, 0:1] == lanes, 1.0, 0.0).astype(jnp.bfloat16)
+    ordered = jnp.dot(sort, rows_ref[...], preferred_element_type=jnp.float32)
+    ordered = ordered.astype(jnp.bfloat16)
+    return ordered[: count // 2], ordered[count // 2 :]
+
+
 def expert_sorting_kernel(numbers, inputs, outputs, scratch):
     rows_ref, order_ref, in_a, out_a, in_b, out_b = inputs
-    back_ref, rows_out, slots_out, act_ref, inner_ref = outputs
+    (back_ref,) = outputs
     count = rows_ref.shape[0]
-    half = count // 2
+    rows, slots = rows_by_product(rows_ref, order_ref)
+    result, d_rows = expert_pass(rows, slots, ((in_a, out_a), (in_b, out_b)))
     lanes = lax.broadcasted_iota(jnp.int32, (count, count), 1)
-    sort = jnp.where(order_ref[:, 0:1] == lanes, 1.0, 0.0).astype(jnp.bfloat16)
     unsort = jnp.where(order_ref[:, 1:2] == lanes, 1.0, 0.0).astype(jnp.bfloat16)
-    ordered = jnp.dot(sort, rows_ref[...], preferred_element_type=jnp.float32)
-    ordered = ordered.astype(jnp.bfloat16)
-    rows, slots = ordered[:half], ordered[half:]
-    rows_out[...] = rows
-    rows_out.send()
-    slots_out[...] = slots
-    slots_out.send()
-    weights = ((in_a, out_a), (in_b, out_b))
-    result, d_rows = expert_pass(rows, slots, weights, act_ref, inner_ref)
     both = jnp.concatenate([result.astype(jnp.bfloat16), d_rows.astype(jnp.bfloat16)], axis=0)
     back_ref[...] = jnp.dot(unsort, both, preferred_element_type=jnp.float32).astype(jnp.bfloat16)
     back_ref.send()
@@ -770,106 +788,69 @@
 
 def expert_rows_of(blocks, part_weights):
     number, height, width = blocks.shape
-    capacity = height // 2
     hidden_width = part_weights[0].shape[1]
-    low = jnp.bfloat16
-    mixed = mixed_tiles(capacity)
-    half = number * (capacity + 4 if mixed else capacity)
-    back = shaped(blocks.shape if mixed else (number * height, width), low)
-    outputs = (
-        back,
-        shaped((half, width), low),
-        shaped((half, width), low),
-        shaped((2, half, hidden_width), low),
-        shaped((2, half, hidden_width), low),
-    )
-    flops, moved = 16 * half * width * hidden_width, 12 * width * width
-    if mixed:
-        return staged(
+    flops, moved = 8 * number * height * width * hidden_width, 12 * width * width
+    if mixed_tiles(height // 2):
+        (back,) = staged(
             expert_kernel,
             "expert_rows",
             (),
             part_weights,
-            outputs,
+            (shaped(blocks.shape, blocks.dtype),),
             (),
             flops,
             moved,
             residents=(blocks,),
             mib=62,
         )
-    place = np.arange(2 * half)
-    sort = place % half // capacity * height + place // half * capacity + place % capacity
-    unsort = np.empty_like(sort)
-    unsort[sort] = place
-    order = jnp.asarray(np.stack([sort, unsort], axis=1), jnp.int32)
-    back, *rest = staged(
+        return back
+    (back,) = staged(
         expert_sorting_kernel,
         "expert_rows",
         (),
-        (blocks.reshape(-1, width), order, *part_weights),
-        outputs,
+        (blocks.reshape(-1, width), sorting(number, height), *part_weights),
+        (shaped((number * height, width), blocks.dtype),),
         (),
         flops,
         moved,
     )
-    return back.reshape(blocks.shape), *rest
-
-
-def sent_grads_kernel(numbers, inputs, outputs, scratch):
-    rows_ref, inner_ref, act_ref, slots_ref = inputs
-    sent_in, sent_out = outputs
+    return back.reshape(blocks.shape)
+
+
+def grads_kernel(mixed, numbers, inputs, outputs, scratch):
     wait_all(*inputs)
-    sent_in[...] = dot_first(rows_ref[...], inner_ref[1]).astype(jnp.bfloat16)
-    sent_in.send()
-    sent_out[...] = dot_first(act_ref[1], slots_ref[...]).astype(jnp.bfloat16)
-    sent_out.send()
-
-
-def sent_grads_of(rows, slots, active, d_inner):
-    half, width = rows.shape
-    hidden_width = active.shape[2]
-    outputs = (
-        shaped((width, hidden_width), jnp.bfloat16),
-        shaped((hidden_width, width), jnp.bfloat16),
-    )
+    if mixed:
+        blocks_ref, part_in, part_out, *got = inputs
+        rows, slots = sorted_rows(blocks_ref)
+    else:
+        rows_ref, order_ref, part_in, part_out, *got = inputs
+        rows, slots = rows_by_product(rows_ref, order_ref)
+    active, d_inner = hidden_pass(rows, slots, part_in, part_out)
+    for number, (left, right) in enumerate(((rows, d_inner), (active, slots))):
+        grad = dot_first(left, right)
+        if got:
+            outputs[number][...] = grad + got[number][...].astype(jnp.float32)
+        else:
+            outputs[number][...] = grad.astype(jnp.bfloat16)
+        outputs[number].send()
+
+
+def expert_grads_of(blocks, part_in, part_out, *got):
+    number, height, width = blocks.shape
+    hidden_width = part_in.shape[1]
+    mixed = mixed_tiles(height // 2)
+    kind = jnp.float32 if got else jnp.bfloat16
+    outputs = (shaped((width, hidden_width), kind), shaped((hidden_width, width), kind))
+    rows = (blocks,) if mixed else (blocks.reshape(-1, width), sorting(number, height))
     return staged(
-        sent_grads_kernel,
-        "sent_grads",
-        (),
-        (rows, d_inner, active, slots),
+        functools.partial(grads_kernel, mixed),
+        "own_grads" if got else "sent_grads",
+        (),
+        (*rows, part_in, part_out, *got),
         outputs,
         (),
-        4 * half * width * hidden_width,
-        8 * width * width,
-    )
-
-
-def own_grads_kernel(numbers, inputs, outputs, scratch):
-    rows_ref, inner_ref, act_ref, slots_ref, got_in, got_out = inputs
-    own_in, own_out = outputs
-    wait_all(*inputs)
-    own_in[...] = dot_first(rows_ref[...], inner_ref[0]) + got_in[...].astype(jnp.float32)
-    own_in.send()
-    own_out[...] = dot_first(act_ref[0], slots_ref[...]) + got_out[...].astype(jnp.float32)
-    own_out.send()
-
-
-def own_grads_of(rows, slots, active, d_inner, got_in, got_out):
-    half, width = rows.shape
-    hidden_width = active.shape[2]
-    outputs = (
-        shaped((width, hidden_width), jnp.float32),
-        shaped((hidden_width, width), jnp.float32),
-    )
-    return staged(
-        own_grads_kernel,
-        "own_grads",
-        (),
-        (rows, d_inner, active, slots, got_in, got_out),
-        outputs,
-        (),
-        0,
-        0,
+        0 if got else 4 * number * height * width * hidden_width,
+        0 if got else 8 * width * width,
     )
 
 
@@ -970,13 +951,23 @@
     half = part // 2
     edge = part + half
     first = pair_masks(half)
+    def copy_of(number, side, target):
+        rows = pl.ds(side * part, part)
+        return pltpu.make_async_copy(
+            made.at[number, rows], target.at[rows], out_sems.at[2 * number + side]
+        )
+
     for number, weight in enumerate(weights):
-        for here in range(4):
-
-            @pl.when(dx * 2 + dc == here)
-            def _():
-                own = [sources[4 * number + 2 * ((i ^ here) & 1) + ((i ^ here) >> 1)] for i in range(4)]
-                for side in range(2):
+        truth = (em ^ (weight // 2)) * 2 + (ey ^ (weight % 2))
+        for side in range(2):
+            for here in range(4):
+
+                @pl.when(dx * 2 + dc == here)
+                def _():
+                    own = [
+                        sources[4 * number + 2 * ((i ^ here) & 1) + ((i ^ here) >> 1)]
+                        for i in range(4)
+                    ]
                     rows = slice(side * part, (side + 1) * part)
                     upper = slice(side * part, side * part + half)
                     lower = slice(side * part + half, (side + 1) * part)
@@ -994,28 +985,27 @@
                         made[number, lower, middle] = pltpu.roll(
                             jnp.where(first, right, left), HEAD_DIM, 1
                         )
-                for i in range(4):
-                    tail = own[i][0, edge:].astype(jnp.float32)
-                    gain = tail[2 * small_rows :]
-                    gain_rows = gain.shape[0] // 2
-                    put_small(
-                        number,
-                        i,
-                        jnp.concatenate(
-                            [
-                                tail[:small_rows] + tail[small_rows : 2 * small_rows],
-                                gain[:gain_rows] + gain[gain_rows:],
-                            ],
-                            axis=0,
-                        ),
-                    )
-
-        truth = (em ^ (weight // 2)) * 2 + (ey ^ (weight % 2))
-        for i in range(4):
-
-            @pl.when(truth == i)
-            def _():
-                pltpu.make_async_copy(made.at[number], outs[i], out_sems.at[number]).start()
+                    for i in range(4 if side == 0 else 0):
+                        tail = own[i][0, edge:].astype(jnp.float32)
+                        gain = tail[2 * small_rows :]
+                        gain_rows = gain.shape[0] // 2
+                        put_small(
+                            number,
+                            i,
+                            jnp.concatenate(
+                                [
+                                    tail[:small_rows] + tail[small_rows : 2 * small_rows],
+                                    gain[:gain_rows] + gain[gain_rows:],
+                                ],
+                                axis=0,
+                            ),
+                        )
+
+            for i in range(4):
+
+                @pl.when(truth == i)
+                def _():
+                    copy_of(number, side, outs[i]).start()
 
     for number, weight in enumerate(weights):
         truth = (em ^ (weight // 2)) * 2 + (ey ^ (weight % 2))
@@ -1023,7 +1013,8 @@
 
             @pl.when(truth == i)
             def _():
-                pltpu.make_async_copy(made.at[number], outs[i], out_sems.at[number]).wait()
+                for side in range(2):
+                    copy_of(number, side, outs[i]).wait()
 
 
 def first_half_kernel(small_rows, bits_ref, *refs):
@@ -1079,7 +1070,7 @@
         out_specs=(any_spec(),) * 4 + (whole_spec(),),
         scratch_shapes=[
             pltpu.VMEM((2, width, width), jnp.float32),
-            pltpu.SemaphoreType.DMA((2,)),
+            pltpu.SemaphoreType.DMA((4,)),
         ],
         compiler_params=params(16),
         cost_estimate=cost(8 * width * width, 12 * width * width),
@@ -1106,7 +1097,7 @@
         scratch_shapes=[
             pltpu.VMEM((2, width, width), jnp.float32),
             pltpu.VMEM((4, 4) + small.shape[2:], jnp.float32),
-            pltpu.SemaphoreType.DMA((2,)),
+            pltpu.SemaphoreType.DMA((4,)),
         ],
         compiler_params=params(16),
         cost_estimate=cost(8 * width * width, 12 * width * width),
@@ -1131,7 +1122,7 @@
     width = left.shape[0]
     block = block_of(place, late, left, gain_rows, small_rows)
     block, beside = lax.optimization_barrier((block, beside))
-    beside = own_grads_of(*beside)
+    beside = expert_grads_of(*beside)
     got, beside = lax.optimization_barrier((swap(block, "eh"), beside))
     near = share_of(block, got, 3 * width // 4, small_rows)
     far, near_x, near_y = swap(near, "em"), swap(near, "dx"), swap(near, "ey")
@@ -1169,7 +1160,7 @@
     pieces = [small[end - size : end] for end, size in zip(ends, sizes)]
     pieces[1], pieces[2] = pieces[1].reshape(HEADS, BUCKETS), pieces[2].reshape(experts, width)
     grad_norm = lax.psum(gain_rows, TOKEN_AXES)[: width // LANES]
-    return (*grads, grad_norm, *pieces), own_grads_of(*beside)
+    return (*grads, grad_norm, *pieces), expert_grads_of(*beside)
 
 
 def per_device(
@@ -1221,22 +1212,21 @@
     )
     far_attended, got_near = swap(near_attended, "ey"), swap(given_near, "em")
     incoming, far_tokens, _ = lax.optimization_barrier((incoming, far_tokens, given_near))
-    sent_back, expert_rows, grad_slots, active, d_inner = expert_rows_of(
-        incoming, (w_in_own, w_out_own, w_in_other, w_out_other)
-    )
+    sent_back = expert_rows_of(incoming, (w_in_own, w_out_own, w_in_other, w_out_other))
     sent_back, far_attended, got_near = lax.optimization_barrier(
         (sent_back, far_attended, got_near)
     )
     came_back = lax.all_to_all(sent_back, EXPERT_AXES, split_axis=0, concat_axis=0, tiled=True)
     own_far, given_far = picked(which[None], (far_attended,), far_tokens)
-    in_other, out_other = sent_grads_of(expert_rows, grad_slots, active, d_inner)
+    incoming, _ = lax.optimization_barrier((incoming, sent_back))
+    in_other, out_other = expert_grads_of(incoming, w_in_other, w_out_other)
     factors = [own_near, own_far, got_near]
     factors = factors + [swap(rows, "dc") for rows in factors]
     came_back, factors, given_far, in_other, out_other = lax.optimization_barrier(
         (came_back, factors, given_far, in_other, out_other)
     )
     got_far = swap(given_far, "em")
-    beside = (expert_rows, grad_slots, active, d_inner, swap(in_other, "dc"), swap(out_other, "dc"))
+    beside = (incoming, w_in_own, w_out_own, swap(in_other, "dc"), swap(out_other, "dc"))
 
     late, turned, hidden_grad, output = backward_of(
         came_back.reshape(experts, 2, 2 * capacity, model_width),
@@ -1252,7 +1242,7 @@
     late = lax.all_to_all(late, GROUP_AXES, split_axis=0, concat_axis=0, tiled=True)
     left = left_of(which[None], factors, gain_one)
     gain_rows, grad_input = first_norm_of(turned, hidden_grad, weights[:3], tokens, gain_one)
-    late, left, gain_rows = lax.optimization_barrier((late, left, gain_rows))
+    late, left, gain_rows, beside = lax.optimization_barrier((late, left, gain_rows, beside))
     gather = gathered_grads if lax.axis_size("eh") == 2 else gathered_grads_plain
     grads, (grad_in, grad_out) = gather(
         late, left, gain_rows, place, small_rows, experts, beside

time: 160 us -> 157 us (0.981)
  waiting for transfers between devices: 53.8 us -> 48.6 us
  starting transfers between devices: 41.7 us -> 44.8 us
  local copies, waits for them, and re-layouts: 5.21 us -> 3.45 us
    ppermute x30, waiting for transfers between devices: 36.4 us -> 33 us  [swap(): return lax.ppermute(array, axis, perm=[(0, 1), (1, 0)])]
    ppermute x30, starting transfers between devices: 25.1 us -> 28 us  [swap(): return lax.ppermute(array, axis, perm=[(0, 1), (1, 0)])]
    unnamed x26 -> x30, local copies, waits for them, and re-layouts: 5.21 us -> 3.45 us
where the time goes in v5:
time: 157 us; the launch traced here: 156 us
  Pallas kernels  57.5 us (37%)
  waiting for transfers between devices  48.6 us (31%)
  starting transfers between devices  44.8 us (29%)
  local copies, waits for them, and re-layouts  3.45 us (2%)
  between operations  1.87 us (1%)
    pallas_call x11, Pallas kernels, staged(): pl.pallas_call(body, out_shape=tuple(kept) + tuple(outputs), in_specs=[pl...  51.1 us
    ppermute x30, waiting for transfers between devices, swap(): return lax.ppermute(array, axis, perm=[(0, 1), (1, 0)])  33 us
    ppermute x30, starting transfers between devices, swap(): return lax.ppermute(array, axis, perm=[(0, 1), (1, 0)])  28 us
    all_to_all x1, waiting for transfers between devices, per_device(): lax.all_to_all(sent_back, EXPERT_AXES, split_axis=0, concat_axis=0, tiled...  13.2 us
    all_to_all x1, starting transfers between devices, per_device(): lax.all_to_all(sent_back, EXPERT_AXES, split_axis=0, concat_axis=0, tiled...  6.26 us
    all_to_all x1, starting transfers between devices, per_device(): lax.all_to_all(outgoing, EXPERT_AXES, split_axis=0, concat_axis=0, tiled=...  6.13 us
    all_to_all x1, starting transfers between devices, per_device(): lax.all_to_all(late, GROUP_AXES, split_axis=0, concat_axis=0, tiled=True)  4.41 us
    pallas_call x1, Pallas kernels, second_half(): pl.pallas_call(functools.partial(second_half_kernel, small_rows), out_sha...  3.57 us
  transfers between devices with their start and end apart: 33, of which 10 were waited for; matrix products, arithmetic and copies ran while one was open for 0% of the time, Pallas kernels for 33%

profile of v5, /device:TPU:0, one launch (start us, length us, event | category | flops | bytes accessed | tf_op | source)
XLA Modules:
  0.0 156.4 jit_solution(2498526685699220076)
XLA Ops:
  0.6 3.0 %collective-permute-start = (bf16[128,768]{1,0:T(8,128)(2,1)}, bf16[128,768]{1,0:T(8,128)(2,1)S(1)}, u32[]{:S(2)}, u32[]{:S(2)}) collective-permute-start(bf16[128,768]{1,0:T(8,128)(2,1)} %refs_5_.5), channel_id=1, source_target_pairs={{0,2},{2,0},{1,3},{3,1},{4,6},{6,4},{5,7},{7,5},{8,10},{10,8},{9,1... | collective-permute-start | bytes 589832 | tf_op jit(solution)/shard_map/ppermute | solution.py:59
  4.3 6.4 %forward.1 = (bf16[8,2,40,768]{3,2,1,0:T(8,128)(2,1)}, bf16[128,768]{1,0:T(8,128)(2,1)}, bf16[128,768]{1,0:T(8,128)(2,1)}, bf16[128,768]{1,0:T(8,128)(2,1)}, bf1...) custom-call(s32[1]{0:T(128)S(6)} %copy.34.refs_0_, ...), custom_call_target="tpu_custom_call" | custom-call | flops 754974720 | bytes 5898240 | tf_op jit(solution)/shard_map/forward/pallas_call | solution.py:190
  10.8 6.1 %all-to-all-start = ((bf16[16,40,768]{2,1,0:T(8,128)(2,1)}), bf16[16,40,768]{2,1,0:T(8,128)(2,1)}, u32[]{:S(2)}, u32[]{:S(2)}) async-start(bf16[16,40,768]{2,1,0:T(8,128)(2,1)} %bitcast.23), calls=%async_computation | async-start | bytes 1966080 | tf_op jit(solution)/shard_map/all_to_all | solution.py:1208
  17.0 0.5 collective-permute-start.4
  17.5 1.8 %collective-permute-start.1 = (bf16[256,768]{1,0:T(8,128)(2,1)S(1)}, bf16[256,768]{1,0:T(8,128)(2,1)}, u32[]{:S(2)}, u32[]{:S(2)}) collective-permute-start(bf16[256,768]{1,0:T(8,128)(2,1)S(1)} %pad_maximum_fusion.refs_3_), channel_id=1, source_target_pairs={{0,4},{4,0},{1,5},{5,1},{2,6},{6,2},{3,7},{7,3},{8,12},{12,8},{9,1... | collective-permute-start | bytes 1179656 | tf_op jit(solution)/shard_map/ppermute | solution.py:59
  19.4 1.5 collective-permute-start.2
  20.8 5.8 %collective-permute-done.2.refs_2_ = bf16[128,768]{1,0:T(8,128)(2,1)S(1)} collective-permute-done((bf16[128,768]{1,0:T(8,128)(2,1)S(1)}, bf16[128,768]{1,0:T(8,128)(2,1)S(1)}, u32[]{:S(2)}, u32[]{:S(2)}) %collective-permute-start.2) | collective-permute-done | bytes 196640 | tf_op jit(solution)/shard_map/ppermute | solution.py:59
  26.6 0.7 copy-done.14
  27.3 2.3 %picked.2 = (bf16[256,768]{1,0:T(8,128)(2,1)}, bf16[256,768]{1,0:T(8,128)(2,1)}, bf16[256,768]{1,0:T(8,128)(2,1)}) custom-call(s32[1]{0:T(128)} %bitcast.6.refs_0_, bf16[128,768]{1,0:T(8,128)(2,1)} %get-tuple-element.90.refs_1_, bf16[128,768]{1,0:T(8,128)(2,1)} %copy-done.14, bf16[256,768]{1,0:T(8,128)(2,1)} %copy-done.11), custom_call_target="tpu_custom_call" | custom-call | bytes 1966080 | tf_op jit(solution)/shard_map/picked/pallas_call | solution.py:190
  29.6 4.0 %collective-permute-start.5 = (bf16[256,768]{1,0:T(8,128)(2,1)}, bf16[256,768]{1,0:T(8,128)(2,1)S(1)}, u32[]{:S(2)}, u32[]{:S(2)}) collective-permute-start(bf16[256,768]{1,0:T(8,128)(2,1)} %get-tuple-element.93), channel_id=1, source_target_pairs={{0,4},{4,0},{1,5},{5,1},{2,6},{6,2},{3,7},{7,3},{8,12},{12,8},{9,1... | collective-permute-start | bytes 1179656 | tf_op jit(solution)/shard_map/ppermute | solution.py:59
  33.6 4.4 %collective-permute-done.1.refs_2_ = bf16[256,768]{1,0:T(8,128)(2,1)} collective-permute-done((bf16[256,768]{1,0:T(8,128)(2,1)S(1)}, bf16[256,768]{1,0:T(8,128)(2,1)}, u32[]{:S(2)}, u32[]{:S(2)}) %collective-permute-start.1) | collective-permute-done | bytes 393248 | tf_op jit(solution)/shard_map/ppermute | solution.py:59
  38.0 1.7 %all-to-all-done.refs_0_ = bf16[16,40,768]{2,1,0:T(8,128)(2,1)} async-done(((bf16[16,40,768]{2,1,0:T(8,128)(2,1)}), bf16[16,40,768]{2,1,0:T(8,128)(2,1)}, u32[]{:S(2)}, u32[]{:S(2)}) %all-to-all-start) | async-done | bytes 983072 | tf_op jit(solution)/shard_map/all_to_all | solution.py:1208
  39.7 8.5 %expert_rows.1 = bf16[16,40,768]{2,1,0:T(8,128)(2,1)} custom-call(bf16[16,40,768]{2,1,0:T(8,128)(2,1)} %all-to-all-done.refs_0_, bf16[768,768]{1,0:T(8,128)(2,1)} %bitcast.7.refs_1_, bf16[768,768]{1,0:T(8,128)(2,1)} %bitcast.8.refs_2_, bf16[768,768]{1,0:T(8,128)(2,1)} %collective-permute-done.3.refs_3_.refs_1_, ...), custom_call_target="tpu_custom_call" | custom-call | flops 3019898880 | bytes 7077888 | tf_op jit(solution)/shard_map/expert_rows/pallas_call | solution.py:190
  48.2 6.3 %all-to-all-start.1 = ((bf16[16,40,768]{2,1,0:T(8,128)(2,1)}), bf16[16,40,768]{2,1,0:T(8,128)(2,1)}, u32[]{:S(2)}, u32[]{:S(2)}) async-start(bf16[16,40,768]{2,1,0:T(8,128)(2,1)} %expert_rows.1), calls=%async_computation.1 | async-start | bytes 1966080 | tf_op jit(solution)/shard_map/all_to_all | solution.py:1219
  54.6 2.1 %picked.3 = (bf16[256,768]{1,0:T(8,128)(2,1)}, bf16[256,768]{1,0:T(8,128)(2,1)}) custom-call(s32[1]{0:T(128)} %bitcast.6.refs_0_, bf16[256,768]{1,0:T(8,128)(2,1)} %copy-done.12, bf16[256,768]{1,0:T(8,128)(2,1)} %collective-permute-done.1.refs_2_), custom_call_target="tpu_custom_call" | custom-call | bytes 1966080 | tf_op jit(solution)/shard_map/picked/pallas_call | solution.py:190
  56.8 0.6 collective-permute-start.8
  57.4 5.5 %sent_grads.1 = (bf16[768,768]{1,0:T(8,128)(2,1)}, bf16[768,768]{1,0:T(8,128)(2,1)}) custom-call(bf16[16,40,768]{2,1,0:T(8,128)(2,1)} %all-to-all-done.refs_0_, bf16[768,768]{1,0:T(8,128)(2,1)} %collective-permute-done.3.refs_3_.refs_1_, bf16[768,768]{1,0:T(8,128)(2,1)} %collective-permute-done.4.refs_4_.refs_2_), custom_call_target="tpu_custom_call" | custom-call | flops 1509949440 | bytes 4718592 | tf_op jit(solution)/shard_map/sent_grads/pallas_call | solution.py:190
  63.0 13.2 %all-to-all-done.1 = bf16[16,40,768]{2,1,0:T(8,128)(2,1)} async-done(((bf16[16,40,768]{2,1,0:T(8,128)(2,1)}), bf16[16,40,768]{2,1,0:T(8,128)(2,1)}, u32[]{:S(2)}, u32[]{:S(2)}) %all-to-all-start.1) | async-done | bytes 983072 | tf_op jit(solution)/shard_map/all_to_all | solution.py:1219
  76.2 2.8 %collective-permute-start.10 = (bf16[256,768]{1,0:T(8,128)(2,1)}, bf16[256,768]{1,0:T(8,128)(2,1)S(1)}, u32[]{:S(2)}, u32[]{:S(2)}) collective-permute-start(bf16[256,768]{1,0:T(8,128)(2,1)} %get-tuple-element.118), channel_id=1, source_target_pairs={{0,8},{8,0},{1,9},{9,1},{2,10},{10,2},{3,11},{11,3},{4,12},{12,4},... | collective-permute-start | bytes 1179656 | tf_op jit(solution)/shard_map/ppermute | solution.py:59
  79.0 7.6 %backward.1 = (bf16[16,200,128]{2,1,0:T(8,128)(2,1)}, bf16[3,768,128]{2,1,0:T(8,128)(2,1)}, f32[128,768]{1,0:T(8,128)}, bf16[128,768]{1,0:T(8,128)(2,1)}) custom-call(bf16[8,2,40,768]{3,2,1,0:T(8,128)(2,1)} %bitcast.9.refs_0_, s32[2,128]{1,0:T(2,128)} %get-tuple-element.105.refs_1_, f32[128,768]{1,0:T(8,128)} %get-tuple-element.106.refs_2_, ...), custom_call_target="tpu_custom_call" | custom-call | flops 301989888 | bytes 5898240 | tf_op jit(solution)/shard_map/backward/pallas_call | solution.py:190
  86.7 4.4 %all-to-all-start.2 = ((bf16[16,200,128]{2,1,0:T(8,128)(2,1)}), bf16[16,200,128]{2,1,0:T(8,128)(2,1)}, u32[]{:S(2)}, u32[]{:S(2)}) async-start(bf16[16,200,128]{2,1,0:T(8,128)(2,1)} %get-tuple-element.119), calls=%async_computation.2 | async-start | bytes 1638400 | tf_op jit(solution)/shard_map/all_to_all | solution.py:1242
  91.1 0.4 collective-permute-start.12
  91.5 0.2 collective-permute-start.13
  91.7 0.3 collective-permute-start.11
  92.1 5.1 %first_norm.1 = (f32[8,128]{1,0:T(8,128)}, bf16[128,768]{1,0:T(8,128)(2,1)}) custom-call(bf16[3,768,128]{2,1,0:T(8,128)(2,1)} %get-tuple-element.114.refs_0_, f32[128,768]{1,0:T(8,128)} %get-tuple-element.115.refs_1_, bf16[768,768]{1,0:T(8,128)(2,1)} %refs_2_.1, bf16[768,768]{1,0:T(8,128)(2,1)} %refs_3_.3, bf16[768,768]{1,0:T(8,128)(2,1)} %refs_4_.3, ...), custom_call_target="tpu_custom_call" | custom-call | flops 452984832 | bytes 4718592 | tf_op jit(solution)/shard_map/first_norm/pallas_call | solution.py:190
  97.2 0.7 copy-done.6
  98.0 1.0 copy-done.5
  99.0 1.0 copy-done.7
  100.0 4.1 %left.1.refs_2_ = bf16[768,2048]{1,0:T(8,128)(2,1)S(1)} custom-call(s32[1]{0:T(128)} %bitcast.6.refs_0_, bf16[256,768]{1,0:T(8,128)(2,1)S(1)} %copy-done, bf16[256,768]{1,0:T(8,128)(2,1)S(1)} %copy-done.3, bf16[256,768]{1,0:T(8,128)(2,1)S(1)} %copy-done.2, bf16[256,768]{1,0:T(8,128)(2,1)S(1)} %copy-done.5, bf16[256,768]{1,0:T(8,128)(2,1)} %collective-permute-done.7.refs_5_, ...), custom_call_target="tpu_custom_call" | custom-call | flops 15728640 | bytes 9437184 | tf_op jit(solution)/shard_map/left/pallas_call | solution.py:190
  104.2 0.7 all-to-all-done.2.refs_1_
  104.9 2.2 %grad_block.1.refs_0_ = bf16[2,600,128]{2,1,0:T(8,128)(2,1)S(1)} custom-call(s32[4]{0:T(128)S(1)} %pad_add_fusion.refs_0_.bits_ref, bf16[16,200,128]{2,1,0:T(8,128)(2,1)} %all-to-all-done.2.refs_1_, bf16[768,2048]{1,0:T(8,128)(2,1)S(1)} %left.1.refs_2_, f32[8,128]{1,0:T(8,128)S(1)} %copy-done.9), custom_call_target="tpu_custom_call" | custom-call | flops 603979776 | bytes 3145728 | tf_op jit(solution)/shard_map/grad_block/pallas_call | solution.py:190
  107.1 2.2 %collective-permute-start.14 = (bf16[2,600,128]{2,1,0:T(8,128)(2,1)S(1)}, bf16[2,600,128]{2,1,0:T(8,128)(2,1)S(1)}, u32[]{:S(2)}, u32[]{:S(2)}) collective-permute-start(bf16[2,600,128]{2,1,0:T(8,128)(2,1)S(1)} %grad_block.1.refs_0_), channel_id=1, source_target_pairs={{0,16},{16,0},{1,17},{17,1},{2,18},{18,2},{3,19},{19,3},{4,20},{20... | collective-permute-start | bytes 921608 | tf_op jit(solution)/shard_map/ppermute | solution.py:59
  109.3 6.9 %own_grads.1 = (f32[768,768]{1,0:T(8,128)}, f32[768,768]{1,0:T(8,128)}) custom-call(bf16[16,40,768]{2,1,0:T(8,128)(2,1)} %all-to-all-done.refs_0_, bf16[768,768]{1,0:T(8,128)(2,1)} %bitcast.7.refs_1_, bf16[768,768]{1,0:T(8,128)(2,1)} %bitcast.8.refs_2_, bf16[768,768]{1,0:T(8,128)(2,1)} %collective-permute-done.12.refs_3_, ...), custom_call_target="tpu_custom_call" | custom-call | tf_op jit(solution)/shard_map/own_grads/pallas_call | solution.py:190
  116.3 7.2 %collective-permute-done.14.refs_1_ = bf16[2,600,128]{2,1,0:T(8,128)(2,1)S(1)} collective-permute-done((bf16[2,600,128]{2,1,0:T(8,128)(2,1)S(1)}, bf16[2,600,128]{2,1,0:T(8,128)(2,1)S(1)}, u32[]{:S(2)}, u32[]{:S(2)}) %collective-permute-start.14) | collective-permute-done | bytes 307232 | tf_op jit(solution)/shard_map/ppermute | solution.py:59
  123.6 0.3 collective-permute-start.20
  123.9 1.6 %collective-permute-start.16 = (bf16[2,600,128]{2,1,0:T(8,128)(2,1)S(1)}, bf16[2,600,128]{2,1,0:T(8,128)(2,1)S(1)}, u32[]{:S(2)}, u32[]{:S(2)}) collective-permute-start(bf16[2,600,128]{2,1,0:T(8,128)(2,1)S(1)} %share.1.refs_0_), channel_id=1, source_target_pairs={{0,2},{2,0},{1,3},{3,1},{4,6},{6,4},{5,7},{7,5},{8,10},{10,8},{9,1... | collective-permute-start | bytes 921608 | tf_op jit(solution)/shard_map/ppermute | solution.py:59
  125.5 1.4 collective-permute-start.15
  127.0 4.7 %collective-permute-done.20.refs_4_ = bf16[2,600,128]{2,1,0:T(8,128)(2,1)S(1)} collective-permute-done((bf16[2,600,128]{2,1,0:T(8,128)(2,1)S(1)}, bf16[2,600,128]{2,1,0:T(8,128)(2,1)S(1)}, u32[]{:S(2)}, u32[]{:S(2)}) %collective-permute-start.20) | collective-permute-done | bytes 307232 | tf_op jit(solution)/shard_map/ppermute | solution.py:59
  131.7 2.8 %collective-permute-start.21 = (bf16[2,600,128]{2,1,0:T(8,128)(2,1)S(1)}, bf16[2,600,128]{2,1,0:T(8,128)(2,1)S(1)}, u32[]{:S(2)}, u32[]{:S(2)}) collective-permute-start(bf16[2,600,128]{2,1,0:T(8,128)(2,1)S(1)} %collective-permute-done.20.refs_4_), channel_id=1, source_target_pairs={{0,4},{4,0},{1,5},{5,1},{2,6},{6,2},{3,7},{7,3},{8,12},{12,8},{9,1... | collective-permute-start | bytes 921608 | tf_op jit(solution)/shard_map/ppermute | solution.py:59
  134.4 1.5 collective-permute-start.27
  136.0 0.5 collective-permute-start.26
  136.6 6.0 %collective-permute-done.21.refs_4_ = bf16[2,600,128]{2,1,0:T(8,128)(2,1)S(1)} collective-permute-done((bf16[2,600,128]{2,1,0:T(8,128)(2,1)S(1)}, bf16[2,600,128]{2,1,0:T(8,128)(2,1)S(1)}, u32[]{:S(2)}, u32[]{:S(2)}) %collective-permute-start.21) | collective-permute-done | bytes 307232 | tf_op jit(solution)/shard_map/ppermute | solution.py:59
  142.6 1.7 %collective-permute-start.22 = (bf16[2,600,128]{2,1,0:T(8,128)(2,1)S(1)}, bf16[2,600,128]{2,1,0:T(8,128)(2,1)S(1)}, u32[]{:S(2)}, u32[]{:S(2)}) collective-permute-start(bf16[2,600,128]{2,1,0:T(8,128)(2,1)S(1)} %collective-permute-done.21.refs_4_), channel_id=1, source_target_pairs={{0,2},{2,0},{1,3},{3,1},{4,6},{6,4},{5,7},{7,5},{8,10},{10,8},{9,1... | collective-permute-start | bytes 921608 | tf_op jit(solution)/shard_map/ppermute | solution.py:59
  144.3 0.5 collective-permute-start.18
  144.9 3.2 %collective-permute-done.17.refs_1_ = bf16[2,600,128]{2,1,0:T(8,128)(2,1)S(1)} collective-permute-done((bf16[2,600,128]{2,1,0:T(8,128)(2,1)S(1)}, bf16[2,600,128]{2,1,0:T(8,128)(2,1)S(1)}, u32[]{:S(2)}, u32[]{:S(2)}) %collective-permute-start.17) | collective-permute-done | bytes 307232 | tf_op jit(solution)/shard_map/ppermute | solution.py:59
  148.1 1.6 %collective-permute-done.22.refs_5_ = bf16[2,600,128]{2,1,0:T(8,128)(2,1)S(1)} collective-permute-done((bf16[2,600,128]{2,1,0:T(8,128)(2,1)S(1)}, bf16[2,600,128]{2,1,0:T(8,128)(2,1)S(1)}, u32[]{:S(2)}, u32[]{:S(2)}) %collective-permute-start.22) | collective-permute-done | bytes 307232 | tf_op jit(solution)/shard_map/ppermute | solution.py:59
  149.7 2.9 %first_half.1 = (f32[768,768]{1,0:T(8,128)}, f32[768,768]{1,0:T(8,128)}, f32[768,768]{1,0:T(8,128)}, f32[768,768]{1,0:T(8,128)}, f32[2,4,12,128]{3,2,1,0:T(8,128)S(1)}) custom-call(s32[4]{0:T(128)S(1)} %pad_add_fusion.refs_0_.bits_ref, bf16[2,600,128]{2,1,0:T(8,128)(2,1)S(1)} %share.1.refs_0_, bf16[2,600,128]{2,1,0:T(8,128)(2,1)S(1)} %collective-permute-done.16.refs_1_, ...), custom_call_target="tpu_custom_call" | custom-call | flops 4718592 | bytes 7077888 | tf_op jit(solution)/shard_map/first_half/pallas_call | solution.py:1065
  152.6 3.6 %second_half.1 = (f32[768,768]{1,0:T(8,128)}, f32[768,768]{1,0:T(8,128)}, f32[768,768]{1,0:T(8,128)}, f32[768,768]{1,0:T(8,128)}, f32[6,128]{1,0:T(8,128)}, /*in...) custom-call(s32[4]{0:T(128)S(1)} %pad_add_fusion.refs_0_.bits_ref, ...), custom_call_target="tpu_custom_call", output_to_operand_aliasing={{0}: (10, {}), {1}: (11, {}), {2}: (12, {}), {3}: (13, {})} | custom-call | flops 4718592 | bytes 7077888 | tf_op jit(solution)/shard_map/second_half/pallas_call | solution.py:1083
  (63 shorter events, 0.8 us)
Async XLA Ops:
  0.6 10.1 %collective-permute-start = (bf16[128,768]{1,0:T(8,128)(2,1)}, bf16[128,768]{1,0:T(8,128)(2,1)S(1)}, u32[]{:S(2)}, u32[]{:S(2)}) collective-permute-start(bf16[128,768]{1,0:T(8,128)(2,1)} %refs_5_.5), channel_id=1, source_target_pairs={{0,2},{2,0},{1,3},{3,1},{4,6},{6,4},{5,7},{7,5},{8,10},{10,8},{9,1... | collective-permute-start | bytes 589832 | tf_op jit(solution)/shard_map/ppermute | solution.py:59
  4.3 6.5 %copy-start.10 = (bf16[128,768]{1,0:T(8,128)(2,1)S(1)}, bf16[128,768]{1,0:T(8,128)(2,1)}, u32[]{:S(2)}) copy-start(bf16[128,768]{1,0:T(8,128)(2,1)} %refs_5_.5) | copy-start | bytes 589828
  10.8 15.8 %copy-start.11 = (bf16[256,768]{1,0:T(8,128)(2,1)}, bf16[256,768]{1,0:T(8,128)(2,1)S(1)}, u32[]{:S(2)}) copy-start(bf16[256,768]{1,0:T(8,128)(2,1)S(1)} %pad_maximum_fusion.refs_3_) | copy-start | bytes 1179652
  10.8 8.5 %copy-start.13 = (bf16[128,768]{1,0:T(8,128)(2,1)S(1)}, bf16[128,768]{1,0:T(8,128)(2,1)}, u32[]{:S(2)}) copy-start(bf16[128,768]{1,0:T(8,128)(2,1)} %get-tuple-element.90.refs_1_) | copy-start | bytes 589828
  10.8 28.9 %all-to-all-start = ((bf16[16,40,768]{2,1,0:T(8,128)(2,1)}), bf16[16,40,768]{2,1,0:T(8,128)(2,1)}, u32[]{:S(2)}, u32[]{:S(2)}) async-start(bf16[16,40,768]{2,1,0:T(8,128)(2,1)} %bitcast.23), calls=%async_computation | async-start | bytes 1966080 | tf_op jit(solution)/shard_map/all_to_all | solution.py:1208
  17.0 22.7 %collective-permute-start.3 = (bf16[768,768]{1,0:T(8,128)(2,1)}, bf16[768,768]{1,0:T(8,128)(2,1)}, u32[]{:S(2)}, u32[]{:S(2)}) collective-permute-start(bf16[768,768]{1,0:T(8,128)(2,1)} %bitcast.7.refs_1_), channel_id=1, source_target_pairs={{0,1},{1,0},{2,3},{3,2},{4,5},{5,4},{6,7},{7,6},{8,9},{9,8},{10,11... | collective-permute-start | bytes 3538952 | tf_op jit(solution)/shard_map/ppermute | solution.py:59
  17.0 22.6 %collective-permute-start.4 = (bf16[768,768]{1,0:T(8,128)(2,1)}, bf16[768,768]{1,0:T(8,128)(2,1)}, u32[]{:S(2)}, u32[]{:S(2)}) collective-permute-start(bf16[768,768]{1,0:T(8,128)(2,1)} %bitcast.8.refs_2_), channel_id=1, source_target_pairs={{0,1},{1,0},{2,3},{3,2},{4,5},{5,4},{6,7},{7,6},{8,9},{9,8},{10,11... | collective-permute-start | bytes 3538952 | tf_op jit(solution)/shard_map/ppermute | solution.py:59
  17.5 20.5 %collective-permute-start.1 = (bf16[256,768]{1,0:T(8,128)(2,1)S(1)}, bf16[256,768]{1,0:T(8,128)(2,1)}, u32[]{:S(2)}, u32[]{:S(2)}) collective-permute-start(bf16[256,768]{1,0:T(8,128)(2,1)S(1)} %pad_maximum_fusion.refs_3_), channel_id=1, source_target_pairs={{0,4},{4,0},{1,5},{5,1},{2,6},{6,2},{3,7},{7,3},{8,12},{12,8},{9,1... | collective-permute-start | bytes 1179656 | tf_op jit(solution)/shard_map/ppermute | solution.py:59
  19.4 7.3 %collective-permute-start.2 = (bf16[128,768]{1,0:T(8,128)(2,1)S(1)}, bf16[128,768]{1,0:T(8,128)(2,1)S(1)}, u32[]{:S(2)}, u32[]{:S(2)}) collective-permute-start(bf16[128,768]{1,0:T(8,128)(2,1)S(1)} %copy-done.13), channel_id=1, source_target_pairs={{0,2},{2,0},{1,3},{3,1},{4,6},{6,4},{5,7},{7,5},{8,10},{10,8},{9,1... | collective-permute-start | bytes 589832 | tf_op jit(solution)/shard_map/ppermute | solution.py:59
  26.6 0.7 copy-start.14
  29.6 18.6 %collective-permute-start.5 = (bf16[256,768]{1,0:T(8,128)(2,1)}, bf16[256,768]{1,0:T(8,128)(2,1)S(1)}, u32[]{:S(2)}, u32[]{:S(2)}) collective-permute-start(bf16[256,768]{1,0:T(8,128)(2,1)} %get-tuple-element.93), channel_id=1, source_target_pairs={{0,4},{4,0},{1,5},{5,1},{2,6},{6,2},{3,7},{7,3},{8,12},{12,8},{9,1... | collective-permute-start | bytes 1179656 | tf_op jit(solution)/shard_map/ppermute | solution.py:59
  33.6 14.7 %collective-permute-start.6 = (bf16[256,768]{1,0:T(8,128)(2,1)}, bf16[256,768]{1,0:T(8,128)(2,1)S(1)}, u32[]{:S(2)}, u32[]{:S(2)}) collective-permute-start(bf16[256,768]{1,0:T(8,128)(2,1)} %get-tuple-element.91), channel_id=1, source_target_pairs={{0,8},{8,0},{1,9},{9,1},{2,10},{10,2},{3,11},{11,3},{4,12},{12,4},... | collective-permute-start | bytes 1179656 | tf_op jit(solution)/shard_map/ppermute | solution.py:59
  48.2 6.3 %copy-start = (bf16[256,768]{1,0:T(8,128)(2,1)S(1)}, bf16[256,768]{1,0:T(8,128)(2,1)}, u32[]{:S(2)}) copy-start(bf16[256,768]{1,0:T(8,128)(2,1)} %get-tuple-element.120.refs_1_) | copy-start | bytes 1179652
  48.2 6.3 %copy-start.12 = (bf16[256,768]{1,0:T(8,128)(2,1)}, bf16[256,768]{1,0:T(8,128)(2,1)S(1)}, u32[]{:S(2)}) copy-start(bf16[256,768]{1,0:T(8,128)(2,1)S(1)} %collective-permute-done.5.refs_1_) | copy-start | bytes 1179652
  48.2 9.1 %copy-start.1 = (bf16[256,768]{1,0:T(8,128)(2,1)}, bf16[256,768]{1,0:T(8,128)(2,1)S(1)}, u32[]{:S(2)}) copy-start(bf16[256,768]{1,0:T(8,128)(2,1)S(1)} %collective-permute-done.6.refs_3_) | copy-start | bytes 1179652
  48.2 28.0 %all-to-all-start.1 = ((bf16[16,40,768]{2,1,0:T(8,128)(2,1)}), bf16[16,40,768]{2,1,0:T(8,128)(2,1)}, u32[]{:S(2)}, u32[]{:S(2)}) async-start(bf16[16,40,768]{2,1,0:T(8,128)(2,1)} %expert_rows.1), calls=%async_computation.1 | async-start | bytes 1966080 | tf_op jit(solution)/shard_map/all_to_all | solution.py:1219
  54.5 8.4 %collective-permute-start.7 = (bf16[256,768]{1,0:T(8,128)(2,1)S(1)}, bf16[256,768]{1,0:T(8,128)(2,1)}, u32[]{:S(2)}, u32[]{:S(2)}) collective-permute-start(bf16[256,768]{1,0:T(8,128)(2,1)S(1)} %copy-done), channel_id=1, source_target_pairs={{0,1},{1,0},{2,3},{3,2},{4,5},{5,4},{6,7},{7,6},{8,9},{9,8},{10,11... | collective-permute-start | bytes 1179656 | tf_op jit(solution)/shard_map/ppermute | solution.py:59
  56.8 6.2 %collective-permute-start.8 = (bf16[256,768]{1,0:T(8,128)(2,1)}, bf16[256,768]{1,0:T(8,128)(2,1)}, u32[]{:S(2)}, u32[]{:S(2)}) collective-permute-start(bf16[256,768]{1,0:T(8,128)(2,1)} %get-tuple-element.121.refs_2_), channel_id=1, source_target_pairs={{0,1},{1,0},{2,3},{3,2},{4,5},{5,4},{6,7},{7,6},{8,9},{9,8},{10,11... | collective-permute-start | bytes 1179656 | tf_op jit(solution)/shard_map/ppermute | solution.py:59
  57.3 5.7 %collective-permute-start.9 = (bf16[256,768]{1,0:T(8,128)(2,1)S(1)}, bf16[256,768]{1,0:T(8,128)(2,1)}, u32[]{:S(2)}, u32[]{:S(2)}) collective-permute-start(bf16[256,768]{1,0:T(8,128)(2,1)S(1)} %collective-permute-done.6.refs_3_), channel_id=1, source_target_pairs={{0,1},{1,0},{2,3},{3,2},{4,5},{5,4},{6,7},{7,6},{8,9},{9,8},{10,11... | collective-permute-start | bytes 1179656 | tf_op jit(solution)/shard_map/ppermute | solution.py:59
  76.2 10.4 %collective-permute-start.10 = (bf16[256,768]{1,0:T(8,128)(2,1)}, bf16[256,768]{1,0:T(8,128)(2,1)S(1)}, u32[]{:S(2)}, u32[]{:S(2)}) collective-permute-start(bf16[256,768]{1,0:T(8,128)(2,1)} %get-tuple-element.118), channel_id=1, source_target_pairs={{0,8},{8,0},{1,9},{9,1},{2,10},{10,2},{3,11},{11,3},{4,12},{12,4},... | collective-permute-start | bytes 1179656 | tf_op jit(solution)/shard_map/ppermute | solution.py:59
  86.7 10.5 %copy-start.4 = (bf16[256,768]{1,0:T(8,128)(2,1)}, bf16[256,768]{1,0:T(8,128)(2,1)S(1)}, u32[]{:S(2)}) copy-start(bf16[256,768]{1,0:T(8,128)(2,1)S(1)} %collective-permute-done.10.refs_4_) | copy-start | bytes 1179652
  86.7 18.2 %all-to-all-start.2 = ((bf16[16,200,128]{2,1,0:T(8,128)(2,1)}), bf16[16,200,128]{2,1,0:T(8,128)(2,1)}, u32[]{:S(2)}, u32[]{:S(2)}) async-start(bf16[16,200,128]{2,1,0:T(8,128)(2,1)} %get-tuple-element.119), calls=%async_computation.2 | async-start | bytes 1638400 | tf_op jit(solution)/shard_map/all_to_all | solution.py:1242
  91.1 13.0 %collective-permute-start.12 = (bf16[768,768]{1,0:T(8,128)(2,1)}, bf16[768,768]{1,0:T(8,128)(2,1)}, u32[]{:S(2)}, u32[]{:S(2)}) collective-permute-start(bf16[768,768]{1,0:T(8,128)(2,1)} %get-tuple-element.128), channel_id=1, source_target_pairs={{0,1},{1,0},{2,3},{3,2},{4,5},{5,4},{6,7},{7,6},{8,9},{9,8},{10,11... | collective-permute-start | bytes 3538952 | tf_op jit(solution)/shard_map/ppermute | solution.py:59
  91.5 12.7 %collective-permute-start.13 = (bf16[768,768]{1,0:T(8,128)(2,1)}, bf16[768,768]{1,0:T(8,128)(2,1)}, u32[]{:S(2)}, u32[]{:S(2)}) collective-permute-start(bf16[768,768]{1,0:T(8,128)(2,1)} %get-tuple-element.129), channel_id=1, source_target_pairs={{0,1},{1,0},{2,3},{3,2},{4,5},{5,4},{6,7},{7,6},{8,9},{9,8},{10,11... | collective-permute-start | bytes 3538952 | tf_op jit(solution)/shard_map/ppermute | solution.py:59
  91.7 5.5 %collective-permute-start.11 = (bf16[256,768]{1,0:T(8,128)(2,1)S(1)}, bf16[256,768]{1,0:T(8,128)(2,1)S(1)}, u32[]{:S(2)}, u32[]{:S(2)}) collective-permute-start(bf16[256,768]{1,0:T(8,128)(2,1)S(1)} %collective-permute-done.10.refs_4_), channel_id=1, source_target_pairs={{0,1},{1,0},{2,3},{3,2},{4,5},{5,4},{6,7},{7,6},{8,9},{9,8},{10,11... | collective-permute-start | bytes 1179656 | tf_op jit(solution)/shard_map/ppermute | solution.py:59
  92.1 5.9 %copy-start.2 = (bf16[256,768]{1,0:T(8,128)(2,1)S(1)}, bf16[256,768]{1,0:T(8,128)(2,1)}, u32[]{:S(2)}) copy-start(bf16[256,768]{1,0:T(8,128)(2,1)} %copy-done.1) | copy-start | bytes 1179652
  92.1 5.9 %copy-start.3 = (bf16[256,768]{1,0:T(8,128)(2,1)S(1)}, bf16[256,768]{1,0:T(8,128)(2,1)}, u32[]{:S(2)}) copy-start(bf16[256,768]{1,0:T(8,128)(2,1)} %get-tuple-element.121.refs_2_) | copy-start | bytes 1179652
  92.1 5.9 %copy-start.8 = (f32[768]{0:T(1024)S(1)}, f32[768]{0:T(1024)}, u32[]{:S(2)}) copy-start(f32[768]{0:T(1024)} %param.15) | copy-start | bytes 9220
  97.2 0.7 copy-start.6
  98.0 1.0 copy-start.5
  99.0 1.0 copy-start.7
  100.0 4.9 %copy-start.9 = (f32[8,128]{1,0:T(8,128)S(1)}, f32[8,128]{1,0:T(8,128)}, u32[]{:S(2)}) copy-start(f32[8,128]{1,0:T(8,128)} %get-tuple-element.132.refs_3_) | copy-start | bytes 12292
  107.1 16.4 %collective-permute-start.14 = (bf16[2,600,128]{2,1,0:T(8,128)(2,1)S(1)}, bf16[2,600,128]{2,1,0:T(8,128)(2,1)S(1)}, u32[]{:S(2)}, u32[]{:S(2)}) collective-permute-start(bf16[2,600,128]{2,1,0:T(8,128)(2,1)S(1)} %grad_block.1.refs_0_), channel_id=1, source_target_pairs={{0,16},{16,0},{1,17},{17,1},{2,18},{18,2},{3,19},{19,3},{4,20},{20... | collective-permute-start | bytes 921608 | tf_op jit(solution)/shard_map/ppermute | solution.py:59
  123.6 8.1 %collective-permute-start.20 = (bf16[2,600,128]{2,1,0:T(8,128)(2,1)S(1)}, bf16[2,600,128]{2,1,0:T(8,128)(2,1)S(1)}, u32[]{:S(2)}, u32[]{:S(2)}) collective-permute-start(bf16[2,600,128]{2,1,0:T(8,128)(2,1)S(1)} %share.1.refs_0_), channel_id=1, source_target_pairs={{0,8},{8,0},{1,9},{9,1},{2,10},{10,2},{3,11},{11,3},{4,12},{12,4},... | collective-permute-start | bytes 921608 | tf_op jit(solution)/shard_map/ppermute | solution.py:59
  123.9 12.1 %collective-permute-start.25 = (bf16[2,600,128]{2,1,0:T(8,128)(2,1)S(1)}, bf16[2,600,128]{2,1,0:T(8,128)(2,1)S(1)}, u32[]{:S(2)}, u32[]{:S(2)}) collective-permute-start(bf16[2,600,128]{2,1,0:T(8,128)(2,1)S(1)} %share.1.refs_0_), channel_id=1, source_target_pairs={{0,1},{1,0},{2,3},{3,2},{4,5},{5,4},{6,7},{7,6},{8,9},{9,8},{10,11... | collective-permute-start | bytes 921608 | tf_op jit(solution)/shard_map/ppermute | solution.py:59
  123.9 12.1 %collective-permute-start.16 = (bf16[2,600,128]{2,1,0:T(8,128)(2,1)S(1)}, bf16[2,600,128]{2,1,0:T(8,128)(2,1)S(1)}, u32[]{:S(2)}, u32[]{:S(2)}) collective-permute-start(bf16[2,600,128]{2,1,0:T(8,128)(2,1)S(1)} %share.1.refs_0_), channel_id=1, source_target_pairs={{0,2},{2,0},{1,3},{3,1},{4,6},{6,4},{5,7},{7,5},{8,10},{10,8},{9,1... | collective-permute-start | bytes 921608 | tf_op jit(solution)/shard_map/ppermute | solution.py:59
  125.5 11.0 %collective-permute-start.15 = (bf16[2,600,128]{2,1,0:T(8,128)(2,1)S(1)}, bf16[2,600,128]{2,1,0:T(8,128)(2,1)S(1)}, u32[]{:S(2)}, u32[]{:S(2)}) collective-permute-start(bf16[2,600,128]{2,1,0:T(8,128)(2,1)S(1)} %share.1.refs_0_), channel_id=1, source_target_pairs={{0,4},{4,0},{1,5},{5,1},{2,6},{6,2},{3,7},{7,3},{8,12},{12,8},{9,1... | collective-permute-start | bytes 921608 | tf_op jit(solution)/shard_map/ppermute | solution.py:59
  131.7 11.0 %collective-permute-start.21 = (bf16[2,600,128]{2,1,0:T(8,128)(2,1)S(1)}, bf16[2,600,128]{2,1,0:T(8,128)(2,1)S(1)}, u32[]{:S(2)}, u32[]{:S(2)}) collective-permute-start(bf16[2,600,128]{2,1,0:T(8,128)(2,1)S(1)} %collective-permute-done.20.refs_4_), channel_id=1, source_target_pairs={{0,4},{4,0},{1,5},{5,1},{2,6},{6,2},{3,7},{7,3},{8,12},{12,8},{9,1... | collective-permute-start | bytes 921608 | tf_op jit(solution)/shard_map/ppermute | solution.py:59
  134.4 9.9 %collective-permute-start.27 = (bf16[2,600,128]{2,1,0:T(8,128)(2,1)S(1)}, bf16[2,600,128]{2,1,0:T(8,128)(2,1)S(1)}, u32[]{:S(2)}, u32[]{:S(2)}) collective-permute-start(bf16[2,600,128]{2,1,0:T(8,128)(2,1)S(1)} %collective-permute-done.20.refs_4_), channel_id=1, source_target_pairs={{0,2},{2,0},{1,3},{3,1},{4,6},{6,4},{5,7},{7,5},{8,10},{10,8},{9,1... | collective-permute-start | bytes 921608 | tf_op jit(solution)/shard_map/ppermute | solution.py:59
  136.0 8.3 %collective-permute-start.28 = (bf16[2,600,128]{2,1,0:T(8,128)(2,1)S(1)}, bf16[2,600,128]{2,1,0:T(8,128)(2,1)S(1)}, u32[]{:S(2)}, u32[]{:S(2)}) collective-permute-start(bf16[2,600,128]{2,1,0:T(8,128)(2,1)S(1)} %collective-permute-done.20.refs_4_), channel_id=1, source_target_pairs={{0,1},{1,0},{2,3},{3,2},{4,5},{5,4},{6,7},{7,6},{8,9},{9,8},{10,11... | collective-permute-start | bytes 921608 | tf_op jit(solution)/shard_map/ppermute | solution.py:59
  136.0 8.8 %collective-permute-start.26 = (bf16[2,600,128]{2,1,0:T(8,128)(2,1)S(1)}, bf16[2,600,128]{2,1,0:T(8,128)(2,1)S(1)}, u32[]{:S(2)}, u32[]{:S(2)}) collective-permute-start(bf16[2,600,128]{2,1,0:T(8,128)(2,1)S(1)} %collective-permute-done.16.refs_1_), channel_id=1, source_target_pairs={{0,1},{1,0},{2,3},{3,2},{4,5},{5,4},{6,7},{7,6},{8,9},{9,8},{10,11... | collective-permute-start | bytes 921608 | tf_op jit(solution)/shard_map/ppermute | solution.py:59
  136.5 11.6 %collective-permute-start.17 = (bf16[2,600,128]{2,1,0:T(8,128)(2,1)S(1)}, bf16[2,600,128]{2,1,0:T(8,128)(2,1)S(1)}, u32[]{:S(2)}, u32[]{:S(2)}) collective-permute-start(bf16[2,600,128]{2,1,0:T(8,128)(2,1)S(1)} %collective-permute-done.16.refs_1_), channel_id=1, source_target_pairs={{0,4},{4,0},{1,5},{5,1},{2,6},{6,2},{3,7},{7,3},{8,12},{12,8},{9,1... | collective-permute-start | bytes 921608 | tf_op jit(solution)/shard_map/ppermute | solution.py:59
  142.6 7.1 %collective-permute-start.22 = (bf16[2,600,128]{2,1,0:T(8,128)(2,1)S(1)}, bf16[2,600,128]{2,1,0:T(8,128)(2,1)S(1)}, u32[]{:S(2)}, u32[]{:S(2)}) collective-permute-start(bf16[2,600,128]{2,1,0:T(8,128)(2,1)S(1)} %collective-permute-done.21.refs_4_), channel_id=1, source_target_pairs={{0,2},{2,0},{1,3},{3,1},{4,6},{6,4},{5,7},{7,5},{8,10},{10,8},{9,1... | collective-permute-start | bytes 921608 | tf_op jit(solution)/shard_map/ppermute | solution.py:59
  144.3 5.4 %collective-permute-start.29 = (bf16[2,600,128]{2,1,0:T(8,128)(2,1)S(1)}, bf16[2,600,128]{2,1,0:T(8,128)(2,1)S(1)}, u32[]{:S(2)}, u32[]{:S(2)}) collective-permute-start(bf16[2,600,128]{2,1,0:T(8,128)(2,1)S(1)} %collective-permute-done.27.refs_5_), channel_id=1, source_target_pairs={{0,1},{1,0},{2,3},{3,2},{4,5},{5,4},{6,7},{7,6},{8,9},{9,8},{10,11... | collective-permute-start | bytes 921608 | tf_op jit(solution)/shard_map/ppermute | solution.py:59
  144.3 8.3 %collective-permute-start.18 = (bf16[2,600,128]{2,1,0:T(8,128)(2,1)S(1)}, bf16[2,600,128]{2,1,0:T(8,128)(2,1)S(1)}, u32[]{:S(2)}, u32[]{:S(2)}) collective-permute-start(bf16[2,600,128]{2,1,0:T(8,128)(2,1)S(1)} %collective-permute-done.15.refs_0_), channel_id=1, source_target_pairs={{0,1},{1,0},{2,3},{3,2},{4,5},{5,4},{6,7},{7,6},{8,9},{9,8},{10,11... | collective-permute-start | bytes 921608 | tf_op jit(solution)/shard_map/ppermute | solution.py:59
  144.8 7.8 %collective-permute-start.23 = (bf16[2,600,128]{2,1,0:T(8,128)(2,1)S(1)}, bf16[2,600,128]{2,1,0:T(8,128)(2,1)S(1)}, u32[]{:S(2)}, u32[]{:S(2)}) collective-permute-start(bf16[2,600,128]{2,1,0:T(8,128)(2,1)S(1)} %collective-permute-done.21.refs_4_), channel_id=1, source_target_pairs={{0,1},{1,0},{2,3},{3,2},{4,5},{5,4},{6,7},{7,6},{8,9},{9,8},{10,11... | collective-permute-start | bytes 921608 | tf_op jit(solution)/shard_map/ppermute | solution.py:59
  148.1 4.5 %collective-permute-start.19 = (bf16[2,600,128]{2,1,0:T(8,128)(2,1)S(1)}, bf16[2,600,128]{2,1,0:T(8,128)(2,1)S(1)}, u32[]{:S(2)}, u32[]{:S(2)}) collective-permute-start(bf16[2,600,128]{2,1,0:T(8,128)(2,1)S(1)} %collective-permute-done.17.refs_1_), channel_id=1, source_target_pairs={{0,1},{1,0},{2,3},{3,2},{4,5},{5,4},{6,7},{7,6},{8,9},{9,8},{10,11... | collective-permute-start | bytes 921608 | tf_op jit(solution)/shard_map/ppermute | solution.py:59
  149.7 2.9 %collective-permute-start.24 = (bf16[2,600,128]{2,1,0:T(8,128)(2,1)S(1)}, bf16[2,600,128]{2,1,0:T(8,128)(2,1)S(1)}, u32[]{:S(2)}, u32[]{:S(2)}) collective-permute-start(bf16[2,600,128]{2,1,0:T(8,128)(2,1)S(1)} %collective-permute-done.22.refs_5_), channel_id=1, source_target_pairs={{0,1},{1,0},{2,3},{3,2},{4,5},{5,4},{6,7},{7,6},{8,9},{9,8},{10,11... | collective-permute-start | bytes 921608 | tf_op jit(solution)/shard_map/ppermute | solution.py:59

commit v6 on v5

--- a/solution.py
+++ b/solution.py
@@ -402,9 +402,10 @@
         q_ref,
         k_ref,
     ) = inputs
-    late_ref, turned, hidden_grad_ref, out_ref = outputs
+    late_ref, hidden_grad_ref, out_ref = outputs
     sums, tail = scratch
-    wait_all(*inputs[1:])
+    early, later = inputs[1:9], inputs[9:]
+    wait_all(*early)
     low = jnp.bfloat16
     length, width = hidden_ref.shape
     experts = router_ref.shape[0]
@@ -456,6 +457,7 @@
             head * HEAD_DIM : (head + 1) * HEAD_DIM
         ]
 
+    wait_all(*later)
     first = pair_masks(length)
     upper = lax.broadcasted_iota(jnp.int32, (LANES, length), 0) < HEAD_DIM
     lane = lax.broadcasted_iota(jnp.int32, (length, length), 1)
@@ -483,7 +485,6 @@
         for which, value in enumerate(
             (d_queries.T, d_keys.astype(low), d_values.astype(low))
         ):
-            turned[which, lanes] = value
             for head in range(2):
                 at = which * HEADS + 2 * pair + head
                 late_ref[at // 3, at % 3 * HEAD_DIM : (at % 3 + 1) * HEAD_DIM] = value[
@@ -496,8 +497,6 @@
             own = pltpu.roll(own, 0, 1, stride=1, stride_axis=0)
             at = 2 * pair + head
             sums[at % 4, at // 4 : at // 4 + 1] = jnp.sum(own, axis=0, keepdims=True)
-
-    turned.send()
 
     shift = lax.broadcasted_iota(jnp.int32, (2 * length, LANES), 0) - (length - 1)
     bucket = bucket_of(shift)
@@ -536,7 +535,6 @@
     block = 4 * width // group
     outputs = (
         shaped((group, block + 2 * small_rows, length), low),
-        shaped((3, width, length), low),
         shaped((length, width), jnp.float32),
         shaped((length, width), low),
     )
@@ -561,13 +559,16 @@
 
 
 def first_norm_kernel(numbers, inputs, outputs, scratch):
-    turned, hidden_grad_ref, query_ref, key_ref, value_ref, tokens_ref, gain_ref = inputs
+    late_ref, hidden_grad_ref, query_ref, key_ref, value_ref, tokens_ref, gain_ref = inputs
     gain_out, grad_ref = outputs
     wait_all(*inputs)
     d_normed = 0.0
+    each = late_ref.shape[0] // 4
+    block = query_ref.shape[0] // each
     for which, weight in enumerate((query_ref, key_ref, value_ref)):
+        turned = [late_ref[i, :block] for i in range(which * each, (which + 1) * each)]
         d_normed = d_normed + lax.dot_general(
-            turned[which],
+            jnp.concatenate(turned, axis=0),
             weight[...],
             (((0,), (1,)), ((), ())),
             preferred_element_type=jnp.float32,
@@ -584,7 +585,7 @@
     gain_out.send()
 
 
-def first_norm_of(turned, hidden_grad, weights, tokens, gain):
+def first_norm_of(late, hidden_grad, weights, tokens, gain):
     length, width = tokens.shape
     low = jnp.bfloat16
     rows = -(-gain.shape[0] // 8) * 8
@@ -592,7 +593,7 @@
         first_norm_kernel,
         "first_norm",
         (),
-        (turned, hidden_grad, *weights, tokens, gain),
+        (late, hidden_grad, *weights, tokens, gain),
         (shaped((length, width), low),),
         (),
         6 * length * width * width,
@@ -745,8 +746,11 @@
     main = height // 2 - 4
     count = blocks * main
     rows, slots = sorted_rows(blocks_ref)
-    wait_all(in_a, out_a, in_b, out_b)
-    result, d_rows = expert_pass(rows, slots, ((in_a, out_a), (in_b, out_b)))
+    result, d_rows = 0.0, 0.0
+    for part_in, part_out in ((in_a, out_a), (in_b, out_b)):
+        wait_all(part_in, part_out)
+        part_result, part_rows = expert_pass(rows, slots, ((part_in, part_out),))
+        result, d_rows = result + part_result, d_rows + part_rows
     back_ref[:, :main] = result[:count].reshape(blocks, main, width).astype(low)
     back_ref[:, main : 2 * main] = d_rows[:count].reshape(blocks, main, width).astype(low)
     mixed = result[count:]
@@ -1228,7 +1232,7 @@
     got_far = swap(given_far, "em")
     beside = (incoming, w_in_own, w_out_own, swap(in_other, "dc"), swap(out_other, "dc"))
 
-    late, turned, hidden_grad, output = backward_of(
+    late, hidden_grad, output = backward_of(
         came_back.reshape(experts, 2, 2 * capacity, model_width),
         w_output,
         gain_two,
@@ -1238,10 +1242,11 @@
         group,
     )
     late, got_far = lax.optimization_barrier((late, got_far))
+    own_late = late
     factors = factors[:3] + [got_far] + factors[3:] + [swap(got_far, "dc")]
     late = lax.all_to_all(late, GROUP_AXES, split_axis=0, concat_axis=0, tiled=True)
     left = left_of(which[None], factors, gain_one)
-    gain_rows, grad_input = first_norm_of(turned, hidden_grad, weights[:3], tokens, gain_one)
+    gain_rows, grad_input = first_norm_of(own_late, hidden_grad, weights[:3], tokens, gain_one)
     late, left, gain_rows, beside = lax.optimization_barrier((late, left, gain_rows, beside))
     gather = gathered_grads if lax.axis_size("eh") == 2 else gathered_grads_plain
     grads, (grad_in, grad_out) = gather(

time: 157 us -> 157 us (level)
  transfers between devices with their start and end apart: 33 -> 33, of which waited for: 10 -> 11; matrix products, arithmetic and copies ran while one was open for 0% -> 0% of each run, Pallas kernels for 33% -> 33%
where the time goes in v6:
time: 157 us; the launch traced here: 156 us
  Pallas kernels  56.7 us (36%)
  waiting for transfers between devices  48.7 us (31%)
  starting transfers between devices  45.1 us (29%)
  local copies, waits for them, and re-layouts  3.45 us (2%)
  between operations  1.85 us (1%)
    pallas_call x11, Pallas kernels, staged(): pl.pallas_call(body, out_shape=tuple(kept) + tuple(outputs), in_specs=[pl...  50.3 us
    ppermute x30, waiting for transfers between devices, swap(): return lax.ppermute(array, axis, perm=[(0, 1), (1, 0)])  33.1 us
    ppermute x30, starting transfers between devices, swap(): return lax.ppermute(array, axis, perm=[(0, 1), (1, 0)])  28.2 us
    all_to_all x1, waiting for transfers between devices, per_device(): lax.all_to_all(sent_back, EXPERT_AXES, split_axis=0, concat_axis=0, tiled...  13.2 us
    all_to_all x1, starting transfers between devices, per_device(): lax.all_to_all(sent_back, EXPERT_AXES, split_axis=0, concat_axis=0, tiled...  6.26 us
    all_to_all x1, starting transfers between devices, per_device(): lax.all_to_all(outgoing, EXPERT_AXES, split_axis=0, concat_axis=0, tiled=...  6.13 us
    all_to_all x1, starting transfers between devices, per_device(): lax.all_to_all(late, GROUP_AXES, split_axis=0, concat_axis=0, tiled=True)  4.5 us
    pallas_call x1, Pallas kernels, second_half(): pl.pallas_call(functools.partial(second_half_kernel, small_rows), out_sha...  3.57 us
  transfers between devices with their start and end apart: 33, of which 11 were waited for; matrix products, arithmetic and copies ran while one was open for 0% of the time, Pallas kernels for 33%

profile of v6, /device:TPU:0, one launch (start us, length us, event | category | flops | bytes accessed | tf_op | source)
XLA Modules:
  0.0 155.9 jit_solution(14325958020494792086)
XLA Ops:
  0.6 3.0 %collective-permute-start = (bf16[128,768]{1,0:T(8,128)(2,1)}, bf16[128,768]{1,0:T(8,128)(2,1)S(1)}, u32[]{:S(2)}, u32[]{:S(2)}) collective-permute-start(bf16[128,768]{1,0:T(8,128)(2,1)} %refs_5_.5), channel_id=1, source_target_pairs={{0,2},{2,0},{1,3},{3,1},{4,6},{6,4},{5,7},{7,5},{8,10},{10,8},{9,1... | collective-permute-start | bytes 589832 | tf_op jit(solution)/shard_map/ppermute | solution.py:59
  4.3 6.4 %forward.1 = (bf16[8,2,40,768]{3,2,1,0:T(8,128)(2,1)}, bf16[128,768]{1,0:T(8,128)(2,1)}, bf16[128,768]{1,0:T(8,128)(2,1)}, bf16[128,768]{1,0:T(8,128)(2,1)}, bf1...) custom-call(s32[1]{0:T(128)S(6)} %copy.34.refs_0_, ...), custom_call_target="tpu_custom_call" | custom-call | flops 754974720 | bytes 5898240 | tf_op jit(solution)/shard_map/forward/pallas_call | solution.py:190
  10.8 6.1 %all-to-all-start = ((bf16[16,40,768]{2,1,0:T(8,128)(2,1)}), bf16[16,40,768]{2,1,0:T(8,128)(2,1)}, u32[]{:S(2)}, u32[]{:S(2)}) async-start(bf16[16,40,768]{2,1,0:T(8,128)(2,1)} %bitcast.23), calls=%async_computation | async-start | bytes 1966080 | tf_op jit(solution)/shard_map/all_to_all | solution.py:1212
  17.0 0.5 collective-permute-start.4
  17.5 1.8 %collective-permute-start.1 = (bf16[256,768]{1,0:T(8,128)(2,1)S(1)}, bf16[256,768]{1,0:T(8,128)(2,1)}, u32[]{:S(2)}, u32[]{:S(2)}) collective-permute-start(bf16[256,768]{1,0:T(8,128)(2,1)S(1)} %pad_maximum_fusion.refs_3_), channel_id=1, source_target_pairs={{0,4},{4,0},{1,5},{5,1},{2,6},{6,2},{3,7},{7,3},{8,12},{12,8},{9,1... | collective-permute-start | bytes 1179656 | tf_op jit(solution)/shard_map/ppermute | solution.py:59
  19.4 1.5 collective-permute-start.2
  20.8 5.8 %collective-permute-done.2.refs_2_ = bf16[128,768]{1,0:T(8,128)(2,1)S(1)} collective-permute-done((bf16[128,768]{1,0:T(8,128)(2,1)S(1)}, bf16[128,768]{1,0:T(8,128)(2,1)S(1)}, u32[]{:S(2)}, u32[]{:S(2)}) %collective-permute-start.2) | collective-permute-done | bytes 196640 | tf_op jit(solution)/shard_map/ppermute | solution.py:59
  26.6 0.7 copy-done.14
  27.3 2.3 %picked.2 = (bf16[256,768]{1,0:T(8,128)(2,1)}, bf16[256,768]{1,0:T(8,128)(2,1)}, bf16[256,768]{1,0:T(8,128)(2,1)}) custom-call(s32[1]{0:T(128)} %bitcast.6.refs_0_, bf16[128,768]{1,0:T(8,128)(2,1)} %get-tuple-element.89.refs_1_, bf16[128,768]{1,0:T(8,128)(2,1)} %copy-done.14, bf16[256,768]{1,0:T(8,128)(2,1)} %copy-done.11), custom_call_target="tpu_custom_call" | custom-call | bytes 1966080 | tf_op jit(solution)/shard_map/picked/pallas_call | solution.py:190
  29.6 4.0 %collective-permute-start.5 = (bf16[256,768]{1,0:T(8,128)(2,1)}, bf16[256,768]{1,0:T(8,128)(2,1)S(1)}, u32[]{:S(2)}, u32[]{:S(2)}) collective-permute-start(bf16[256,768]{1,0:T(8,128)(2,1)} %get-tuple-element.92), channel_id=1, source_target_pairs={{0,4},{4,0},{1,5},{5,1},{2,6},{6,2},{3,7},{7,3},{8,12},{12,8},{9,1... | collective-permute-start | bytes 1179656 | tf_op jit(solution)/shard_map/ppermute | solution.py:59
  33.6 4.4 %collective-permute-done.1.refs_2_ = bf16[256,768]{1,0:T(8,128)(2,1)} collective-permute-done((bf16[256,768]{1,0:T(8,128)(2,1)S(1)}, bf16[256,768]{1,0:T(8,128)(2,1)}, u32[]{:S(2)}, u32[]{:S(2)}) %collective-permute-start.1) | collective-permute-done | bytes 393248 | tf_op jit(solution)/shard_map/ppermute | solution.py:59
  38.0 1.7 %all-to-all-done.refs_0_ = bf16[16,40,768]{2,1,0:T(8,128)(2,1)} async-done(((bf16[16,40,768]{2,1,0:T(8,128)(2,1)}), bf16[16,40,768]{2,1,0:T(8,128)(2,1)}, u32[]{:S(2)}, u32[]{:S(2)}) %all-to-all-start) | async-done | bytes 983072 | tf_op jit(solution)/shard_map/all_to_all | solution.py:1212
  39.7 8.0 %expert_rows.1 = bf16[16,40,768]{2,1,0:T(8,128)(2,1)} custom-call(bf16[16,40,768]{2,1,0:T(8,128)(2,1)} %all-to-all-done.refs_0_, bf16[768,768]{1,0:T(8,128)(2,1)} %bitcast.7.refs_1_, bf16[768,768]{1,0:T(8,128)(2,1)} %bitcast.8.refs_2_, bf16[768,768]{1,0:T(8,128)(2,1)} %collective-permute-done.3.refs_3_.refs_1_, ...), custom_call_target="tpu_custom_call" | custom-call | flops 3019898880 | bytes 7077888 | tf_op jit(solution)/shard_map/expert_rows/pallas_call | solution.py:190
  47.7 6.3 %all-to-all-start.1 = ((bf16[16,40,768]{2,1,0:T(8,128)(2,1)}), bf16[16,40,768]{2,1,0:T(8,128)(2,1)}, u32[]{:S(2)}, u32[]{:S(2)}) async-start(bf16[16,40,768]{2,1,0:T(8,128)(2,1)} %expert_rows.1), calls=%async_computation.1 | async-start | bytes 1966080 | tf_op jit(solution)/shard_map/all_to_all | solution.py:1223
  54.1 2.1 %picked.3 = (bf16[256,768]{1,0:T(8,128)(2,1)}, bf16[256,768]{1,0:T(8,128)(2,1)}) custom-call(s32[1]{0:T(128)} %bitcast.6.refs_0_, bf16[256,768]{1,0:T(8,128)(2,1)} %copy-done.12, bf16[256,768]{1,0:T(8,128)(2,1)} %collective-permute-done.1.refs_2_), custom_call_target="tpu_custom_call" | custom-call | bytes 1966080 | tf_op jit(solution)/shard_map/picked/pallas_call | solution.py:190
  56.2 0.6 collective-permute-start.8
  56.9 5.5 %sent_grads.1 = (bf16[768,768]{1,0:T(8,128)(2,1)}, bf16[768,768]{1,0:T(8,128)(2,1)}) custom-call(bf16[16,40,768]{2,1,0:T(8,128)(2,1)} %all-to-all-done.refs_0_, bf16[768,768]{1,0:T(8,128)(2,1)} %collective-permute-done.3.refs_3_.refs_1_, bf16[768,768]{1,0:T(8,128)(2,1)} %collective-permute-done.4.refs_4_.refs_2_), custom_call_target="tpu_custom_call" | custom-call | flops 1509949440 | bytes 4718592 | tf_op jit(solution)/shard_map/sent_grads/pallas_call | solution.py:190
  62.5 13.2 %all-to-all-done.1 = bf16[16,40,768]{2,1,0:T(8,128)(2,1)} async-done(((bf16[16,40,768]{2,1,0:T(8,128)(2,1)}), bf16[16,40,768]{2,1,0:T(8,128)(2,1)}, u32[]{:S(2)}, u32[]{:S(2)}) %all-to-all-start.1) | async-done | bytes 983072 | tf_op jit(solution)/shard_map/all_to_all | solution.py:1223
  75.7 2.8 %collective-permute-start.10 = (bf16[256,768]{1,0:T(8,128)(2,1)}, bf16[256,768]{1,0:T(8,128)(2,1)S(1)}, u32[]{:S(2)}, u32[]{:S(2)}) collective-permute-start(bf16[256,768]{1,0:T(8,128)(2,1)} %get-tuple-element.114), channel_id=1, source_target_pairs={{0,8},{8,0},{1,9},{9,1},{2,10},{10,2},{3,11},{11,3},{4,12},{12,4},... | collective-permute-start | bytes 1179656 | tf_op jit(solution)/shard_map/ppermute | solution.py:59
  78.5 7.3 %backward.1 = (bf16[16,200,128]{2,1,0:T(8,128)(2,1)}, f32[128,768]{1,0:T(8,128)}, bf16[128,768]{1,0:T(8,128)(2,1)}) custom-call(bf16[8,2,40,768]{3,2,1,0:T(8,128)(2,1)} %bitcast.9.refs_0_, s32[2,128]{1,0:T(2,128)} %get-tuple-element.104.refs_1_, f32[128,768]{1,0:T(8,128)} %get-tuple-element.105.refs_2_, f32[128,8]{1,0:T(8,128)} %get-tuple-element.106.refs_3_, ...), custom_call_target="tpu_custom_call" | custom-call | flops 301989888 | bytes 5898240 | tf_op jit(solution)/shard_map/backward/pallas_call | solution.py:190
  85.8 0.3 collective-permute-done.10.refs_4_
  86.1 4.5 %all-to-all-start.2 = ((bf16[16,200,128]{2,1,0:T(8,128)(2,1)}), bf16[16,200,128]{2,1,0:T(8,128)(2,1)}, u32[]{:S(2)}, u32[]{:S(2)}) async-start(bf16[16,200,128]{2,1,0:T(8,128)(2,1)} %get-tuple-element.115.refs_0_), calls=%async_computation.2 | async-start | bytes 1638400 | tf_op jit(solution)/shard_map/all_to_all | solution.py:1247
  90.6 0.4 collective-permute-start.12
  91.2 0.3 collective-permute-start.11
  91.5 5.2 %first_norm.1 = (f32[8,128]{1,0:T(8,128)}, bf16[128,768]{1,0:T(8,128)(2,1)}) custom-call(bf16[16,200,128]{2,1,0:T(8,128)(2,1)} %get-tuple-element.115.refs_0_, f32[128,768]{1,0:T(8,128)} %get-tuple-element.116.refs_1_, bf16[768,768]{1,0:T(8,128)(2,1)} %refs_2_.1, bf16[768,768]{1,0:T(8,128)(2,1)} %refs_3_.3, bf16[768,768]{1,0:T(8,128)(2,1)} %refs_4_.3, ...), custom_call_target="tpu_custom_call" | custom-call | flops 452984832 | bytes 4718592 | tf_op jit(solution)/shard_map/first_norm/pallas_call | solution.py:190
  96.8 0.7 copy-done.6
  97.5 1.0 copy-done.5
  98.5 1.0 copy-done.7
  99.5 4.1 %left.1.refs_2_ = bf16[768,2048]{1,0:T(8,128)(2,1)S(1)} custom-call(s32[1]{0:T(128)} %bitcast.6.refs_0_, bf16[256,768]{1,0:T(8,128)(2,1)S(1)} %copy-done, bf16[256,768]{1,0:T(8,128)(2,1)S(1)} %copy-done.3, bf16[256,768]{1,0:T(8,128)(2,1)S(1)} %copy-done.2, bf16[256,768]{1,0:T(8,128)(2,1)S(1)} %copy-done.5, bf16[256,768]{1,0:T(8,128)(2,1)} %collective-permute-done.7.refs_5_, ...), custom_call_target="tpu_custom_call" | custom-call | flops 15728640 | bytes 9437184 | tf_op jit(solution)/shard_map/left/pallas_call | solution.py:190
  103.7 0.7 all-to-all-done.2.refs_1_
  104.3 2.2 %grad_block.1.refs_0_ = bf16[2,600,128]{2,1,0:T(8,128)(2,1)S(1)} custom-call(s32[4]{0:T(128)S(1)} %pad_add_fusion.refs_0_.bits_ref, bf16[16,200,128]{2,1,0:T(8,128)(2,1)} %all-to-all-done.2.refs_1_, bf16[768,2048]{1,0:T(8,128)(2,1)S(1)} %left.1.refs_2_, f32[8,128]{1,0:T(8,128)S(1)} %copy-done.9), custom_call_target="tpu_custom_call" | custom-call | flops 603979776 | bytes 3145728 | tf_op jit(solution)/shard_map/grad_block/pallas_call | solution.py:190
  106.6 2.2 %collective-permute-start.14 = (bf16[2,600,128]{2,1,0:T(8,128)(2,1)S(1)}, bf16[2,600,128]{2,1,0:T(8,128)(2,1)S(1)}, u32[]{:S(2)}, u32[]{:S(2)}) collective-permute-start(bf16[2,600,128]{2,1,0:T(8,128)(2,1)S(1)} %grad_block.1.refs_0_), channel_id=1, source_target_pairs={{0,16},{16,0},{1,17},{17,1},{2,18},{18,2},{3,19},{19,3},{4,20},{20... | collective-permute-start | bytes 921608 | tf_op jit(solution)/shard_map/ppermute | solution.py:59
  108.8 6.9 %own_grads.1 = (f32[768,768]{1,0:T(8,128)}, f32[768,768]{1,0:T(8,128)}) custom-call(bf16[16,40,768]{2,1,0:T(8,128)(2,1)} %all-to-all-done.refs_0_, bf16[768,768]{1,0:T(8,128)(2,1)} %bitcast.7.refs_1_, bf16[768,768]{1,0:T(8,128)(2,1)} %bitcast.8.refs_2_, bf16[768,768]{1,0:T(8,128)(2,1)} %collective-permute-done.12.refs_3_, ...), custom_call_target="tpu_custom_call" | custom-call | tf_op jit(solution)/shard_map/own_grads/pallas_call | solution.py:190
  115.7 7.2 %collective-permute-done.14.refs_1_ = bf16[2,600,128]{2,1,0:T(8,128)(2,1)S(1)} collective-permute-done((bf16[2,600,128]{2,1,0:T(8,128)(2,1)S(1)}, bf16[2,600,128]{2,1,0:T(8,128)(2,1)S(1)}, u32[]{:S(2)}, u32[]{:S(2)}) %collective-permute-start.14) | collective-permute-done | bytes 307232 | tf_op jit(solution)/shard_map/ppermute | solution.py:59
  123.1 0.3 collective-permute-start.20
  123.4 1.7 %collective-permute-start.16 = (bf16[2,600,128]{2,1,0:T(8,128)(2,1)S(1)}, bf16[2,600,128]{2,1,0:T(8,128)(2,1)S(1)}, u32[]{:S(2)}, u32[]{:S(2)}) collective-permute-start(bf16[2,600,128]{2,1,0:T(8,128)(2,1)S(1)} %share.1.refs_0_), channel_id=1, source_target_pairs={{0,2},{2,0},{1,3},{3,1},{4,6},{6,4},{5,7},{7,5},{8,10},{10,8},{9,1... | collective-permute-start | bytes 921608 | tf_op jit(solution)/shard_map/ppermute | solution.py:59
  125.0 1.5 collective-permute-start.15
  126.5 4.6 %collective-permute-done.20.refs_4_ = bf16[2,600,128]{2,1,0:T(8,128)(2,1)S(1)} collective-permute-done((bf16[2,600,128]{2,1,0:T(8,128)(2,1)S(1)}, bf16[2,600,128]{2,1,0:T(8,128)(2,1)S(1)}, u32[]{:S(2)}, u32[]{:S(2)}) %collective-permute-start.20) | collective-permute-done | bytes 307232 | tf_op jit(solution)/shard_map/ppermute | solution.py:59
  131.1 2.9 %collective-permute-start.21 = (bf16[2,600,128]{2,1,0:T(8,128)(2,1)S(1)}, bf16[2,600,128]{2,1,0:T(8,128)(2,1)S(1)}, u32[]{:S(2)}, u32[]{:S(2)}) collective-permute-start(bf16[2,600,128]{2,1,0:T(8,128)(2,1)S(1)} %collective-permute-done.20.refs_4_), channel_id=1, source_target_pairs={{0,4},{4,0},{1,5},{5,1},{2,6},{6,2},{3,7},{7,3},{8,12},{12,8},{9,1... | collective-permute-start | bytes 921608 | tf_op jit(solution)/shard_map/ppermute | solution.py:59
  134.0 1.5 collective-permute-start.27
  135.5 0.5 collective-permute-start.26
  136.2 6.0 %collective-permute-done.21.refs_4_ = bf16[2,600,128]{2,1,0:T(8,128)(2,1)S(1)} collective-permute-done((bf16[2,600,128]{2,1,0:T(8,128)(2,1)S(1)}, bf16[2,600,128]{2,1,0:T(8,128)(2,1)S(1)}, u32[]{:S(2)}, u32[]{:S(2)}) %collective-permute-start.21) | collective-permute-done | bytes 307232 | tf_op jit(solution)/shard_map/ppermute | solution.py:59
  142.2 1.6 %collective-permute-start.22 = (bf16[2,600,128]{2,1,0:T(8,128)(2,1)S(1)}, bf16[2,600,128]{2,1,0:T(8,128)(2,1)S(1)}, u32[]{:S(2)}, u32[]{:S(2)}) collective-permute-start(bf16[2,600,128]{2,1,0:T(8,128)(2,1)S(1)} %collective-permute-done.21.refs_4_), channel_id=1, source_target_pairs={{0,2},{2,0},{1,3},{3,1},{4,6},{6,4},{5,7},{7,5},{8,10},{10,8},{9,1... | collective-permute-start | bytes 921608 | tf_op jit(solution)/shard_map/ppermute | solution.py:59
  143.8 0.5 collective-permute-start.18
  144.4 3.2 %collective-permute-done.17.refs_1_ = bf16[2,600,128]{2,1,0:T(8,128)(2,1)S(1)} collective-permute-done((bf16[2,600,128]{2,1,0:T(8,128)(2,1)S(1)}, bf16[2,600,128]{2,1,0:T(8,128)(2,1)S(1)}, u32[]{:S(2)}, u32[]{:S(2)}) %collective-permute-start.17) | collective-permute-done | bytes 307232 | tf_op jit(solution)/shard_map/ppermute | solution.py:59
  147.6 1.6 %collective-permute-done.22.refs_5_ = bf16[2,600,128]{2,1,0:T(8,128)(2,1)S(1)} collective-permute-done((bf16[2,600,128]{2,1,0:T(8,128)(2,1)S(1)}, bf16[2,600,128]{2,1,0:T(8,128)(2,1)S(1)}, u32[]{:S(2)}, u32[]{:S(2)}) %collective-permute-start.22) | collective-permute-done | bytes 307232 | tf_op jit(solution)/shard_map/ppermute | solution.py:59
  149.2 2.9 %first_half.1 = (f32[768,768]{1,0:T(8,128)}, f32[768,768]{1,0:T(8,128)}, f32[768,768]{1,0:T(8,128)}, f32[768,768]{1,0:T(8,128)}, f32[2,4,12,128]{3,2,1,0:T(8,128)S(1)}) custom-call(s32[4]{0:T(128)S(1)} %pad_add_fusion.refs_0_.bits_ref, bf16[2,600,128]{2,1,0:T(8,128)(2,1)S(1)} %share.1.refs_0_, bf16[2,600,128]{2,1,0:T(8,128)(2,1)S(1)} %collective-permute-done.16.refs_1_, ...), custom_call_target="tpu_custom_call" | custom-call | flops 4718592 | bytes 7077888 | tf_op jit(solution)/shard_map/first_half/pallas_call | solution.py:1069
  152.1 3.6 %second_half.1 = (f32[768,768]{1,0:T(8,128)}, f32[768,768]{1,0:T(8,128)}, f32[768,768]{1,0:T(8,128)}, f32[768,768]{1,0:T(8,128)}, f32[6,128]{1,0:T(8,128)}, /*in...) custom-call(s32[4]{0:T(128)S(1)} %pad_add_fusion.refs_0_.bits_ref, ...), custom_call_target="tpu_custom_call", output_to_operand_aliasing={{0}: (10, {}), {1}: (11, {}), {2}: (12, {}), {3}: (13, {})} | custom-call | flops 4718592 | bytes 7077888 | tf_op jit(solution)/shard_map/second_half/pallas_call | solution.py:1087
  (63 shorter events, 1.0 us)
Async XLA Ops:
  0.6 10.1 %collective-permute-start = (bf16[128,768]{1,0:T(8,128)(2,1)}, bf16[128,768]{1,0:T(8,128)(2,1)S(1)}, u32[]{:S(2)}, u32[]{:S(2)}) collective-permute-start(bf16[128,768]{1,0:T(8,128)(2,1)} %refs_5_.5), channel_id=1, source_target_pairs={{0,2},{2,0},{1,3},{3,1},{4,6},{6,4},{5,7},{7,5},{8,10},{10,8},{9,1... | collective-permute-start | bytes 589832 | tf_op jit(solution)/shard_map/ppermute | solution.py:59
  4.3 6.5 %copy-start.10 = (bf16[128,768]{1,0:T(8,128)(2,1)S(1)}, bf16[128,768]{1,0:T(8,128)(2,1)}, u32[]{:S(2)}) copy-start(bf16[128,768]{1,0:T(8,128)(2,1)} %refs_5_.5) | copy-start | bytes 589828
  10.8 15.8 %copy-start.11 = (bf16[256,768]{1,0:T(8,128)(2,1)}, bf16[256,768]{1,0:T(8,128)(2,1)S(1)}, u32[]{:S(2)}) copy-start(bf16[256,768]{1,0:T(8,128)(2,1)S(1)} %pad_maximum_fusion.refs_3_) | copy-start | bytes 1179652
  10.8 8.5 %copy-start.13 = (bf16[128,768]{1,0:T(8,128)(2,1)S(1)}, bf16[128,768]{1,0:T(8,128)(2,1)}, u32[]{:S(2)}) copy-start(bf16[128,768]{1,0:T(8,128)(2,1)} %get-tuple-element.89.refs_1_) | copy-start | bytes 589828
  10.8 28.9 %all-to-all-start = ((bf16[16,40,768]{2,1,0:T(8,128)(2,1)}), bf16[16,40,768]{2,1,0:T(8,128)(2,1)}, u32[]{:S(2)}, u32[]{:S(2)}) async-start(bf16[16,40,768]{2,1,0:T(8,128)(2,1)} %bitcast.23), calls=%async_computation | async-start | bytes 1966080 | tf_op jit(solution)/shard_map/all_to_all | solution.py:1212
  17.0 22.7 %collective-permute-start.3 = (bf16[768,768]{1,0:T(8,128)(2,1)}, bf16[768,768]{1,0:T(8,128)(2,1)}, u32[]{:S(2)}, u32[]{:S(2)}) collective-permute-start(bf16[768,768]{1,0:T(8,128)(2,1)} %bitcast.7.refs_1_), channel_id=1, source_target_pairs={{0,1},{1,0},{2,3},{3,2},{4,5},{5,4},{6,7},{7,6},{8,9},{9,8},{10,11... | collective-permute-start | bytes 3538952 | tf_op jit(solution)/shard_map/ppermute | solution.py:59
  17.0 22.6 %collective-permute-start.4 = (bf16[768,768]{1,0:T(8,128)(2,1)}, bf16[768,768]{1,0:T(8,128)(2,1)}, u32[]{:S(2)}, u32[]{:S(2)}) collective-permute-start(bf16[768,768]{1,0:T(8,128)(2,1)} %bitcast.8.refs_2_), channel_id=1, source_target_pairs={{0,1},{1,0},{2,3},{3,2},{4,5},{5,4},{6,7},{7,6},{8,9},{9,8},{10,11... | collective-permute-start | bytes 3538952 | tf_op jit(solution)/shard_map/ppermute | solution.py:59
  17.5 20.5 %collective-permute-start.1 = (bf16[256,768]{1,0:T(8,128)(2,1)S(1)}, bf16[256,768]{1,0:T(8,128)(2,1)}, u32[]{:S(2)}, u32[]{:S(2)}) collective-permute-start(bf16[256,768]{1,0:T(8,128)(2,1)S(1)} %pad_maximum_fusion.refs_3_), channel_id=1, source_target_pairs={{0,4},{4,0},{1,5},{5,1},{2,6},{6,2},{3,7},{7,3},{8,12},{12,8},{9,1... | collective-permute-start | bytes 1179656 | tf_op jit(solution)/shard_map/ppermute | solution.py:59
  19.4 7.3 %collective-permute-start.2 = (bf16[128,768]{1,0:T(8,128)(2,1)S(1)}, bf16[128,768]{1,0:T(8,128)(2,1)S(1)}, u32[]{:S(2)}, u32[]{:S(2)}) collective-permute-start(bf16[128,768]{1,0:T(8,128)(2,1)S(1)} %copy-done.13), channel_id=1, source_target_pairs={{0,2},{2,0},{1,3},{3,1},{4,6},{6,4},{5,7},{7,5},{8,10},{10,8},{9,1... | collective-permute-start | bytes 589832 | tf_op jit(solution)/shard_map/ppermute | solution.py:59
  26.6 0.7 copy-start.14
  29.6 18.1 %collective-permute-start.5 = (bf16[256,768]{1,0:T(8,128)(2,1)}, bf16[256,768]{1,0:T(8,128)(2,1)S(1)}, u32[]{:S(2)}, u32[]{:S(2)}) collective-permute-start(bf16[256,768]{1,0:T(8,128)(2,1)} %get-tuple-element.92), channel_id=1, source_target_pairs={{0,4},{4,0},{1,5},{5,1},{2,6},{6,2},{3,7},{7,3},{8,12},{12,8},{9,1... | collective-permute-start | bytes 1179656 | tf_op jit(solution)/shard_map/ppermute | solution.py:59
  33.6 14.1 %collective-permute-start.6 = (bf16[256,768]{1,0:T(8,128)(2,1)}, bf16[256,768]{1,0:T(8,128)(2,1)S(1)}, u32[]{:S(2)}, u32[]{:S(2)}) collective-permute-start(bf16[256,768]{1,0:T(8,128)(2,1)} %get-tuple-element.90), channel_id=1, source_target_pairs={{0,8},{8,0},{1,9},{9,1},{2,10},{10,2},{3,11},{11,3},{4,12},{12,4},... | collective-permute-start | bytes 1179656 | tf_op jit(solution)/shard_map/ppermute | solution.py:59
  47.7 6.3 %copy-start = (bf16[256,768]{1,0:T(8,128)(2,1)S(1)}, bf16[256,768]{1,0:T(8,128)(2,1)}, u32[]{:S(2)}) copy-start(bf16[256,768]{1,0:T(8,128)(2,1)} %get-tuple-element.118.refs_1_) | copy-start | bytes 1179652
  47.7 6.3 %copy-start.12 = (bf16[256,768]{1,0:T(8,128)(2,1)}, bf16[256,768]{1,0:T(8,128)(2,1)S(1)}, u32[]{:S(2)}) copy-start(bf16[256,768]{1,0:T(8,128)(2,1)S(1)} %collective-permute-done.5.refs_1_) | copy-start | bytes 1179652
  47.7 9.1 %copy-start.1 = (bf16[256,768]{1,0:T(8,128)(2,1)}, bf16[256,768]{1,0:T(8,128)(2,1)S(1)}, u32[]{:S(2)}) copy-start(bf16[256,768]{1,0:T(8,128)(2,1)S(1)} %collective-permute-done.6.refs_3_) | copy-start | bytes 1179652
  47.7 28.0 %all-to-all-start.1 = ((bf16[16,40,768]{2,1,0:T(8,128)(2,1)}), bf16[16,40,768]{2,1,0:T(8,128)(2,1)}, u32[]{:S(2)}, u32[]{:S(2)}) async-start(bf16[16,40,768]{2,1,0:T(8,128)(2,1)} %expert_rows.1), calls=%async_computation.1 | async-start | bytes 1966080 | tf_op jit(solution)/shard_map/all_to_all | solution.py:1223
  54.0 8.4 %collective-permute-start.7 = (bf16[256,768]{1,0:T(8,128)(2,1)S(1)}, bf16[256,768]{1,0:T(8,128)(2,1)}, u32[]{:S(2)}, u32[]{:S(2)}) collective-permute-start(bf16[256,768]{1,0:T(8,128)(2,1)S(1)} %copy-done), channel_id=1, source_target_pairs={{0,1},{1,0},{2,3},{3,2},{4,5},{5,4},{6,7},{7,6},{8,9},{9,8},{10,11... | collective-permute-start | bytes 1179656 | tf_op jit(solution)/shard_map/ppermute | solution.py:59
  56.2 6.2 %collective-permute-start.8 = (bf16[256,768]{1,0:T(8,128)(2,1)}, bf16[256,768]{1,0:T(8,128)(2,1)}, u32[]{:S(2)}, u32[]{:S(2)}) collective-permute-start(bf16[256,768]{1,0:T(8,128)(2,1)} %get-tuple-element.119.refs_2_), channel_id=1, source_target_pairs={{0,1},{1,0},{2,3},{3,2},{4,5},{5,4},{6,7},{7,6},{8,9},{9,8},{10,11... | collective-permute-start | bytes 1179656 | tf_op jit(solution)/shard_map/ppermute | solution.py:59
  56.8 5.7 %collective-permute-start.9 = (bf16[256,768]{1,0:T(8,128)(2,1)S(1)}, bf16[256,768]{1,0:T(8,128)(2,1)}, u32[]{:S(2)}, u32[]{:S(2)}) collective-permute-start(bf16[256,768]{1,0:T(8,128)(2,1)S(1)} %collective-permute-done.6.refs_3_), channel_id=1, source_target_pairs={{0,1},{1,0},{2,3},{3,2},{4,5},{5,4},{6,7},{7,6},{8,9},{9,8},{10,11... | collective-permute-start | bytes 1179656 | tf_op jit(solution)/shard_map/ppermute | solution.py:59
  75.7 10.4 %collective-permute-start.10 = (bf16[256,768]{1,0:T(8,128)(2,1)}, bf16[256,768]{1,0:T(8,128)(2,1)S(1)}, u32[]{:S(2)}, u32[]{:S(2)}) collective-permute-start(bf16[256,768]{1,0:T(8,128)(2,1)} %get-tuple-element.114), channel_id=1, source_target_pairs={{0,8},{8,0},{1,9},{9,1},{2,10},{10,2},{3,11},{11,3},{4,12},{12,4},... | collective-permute-start | bytes 1179656 | tf_op jit(solution)/shard_map/ppermute | solution.py:59
  86.1 10.7 %copy-start.4 = (bf16[256,768]{1,0:T(8,128)(2,1)}, bf16[256,768]{1,0:T(8,128)(2,1)S(1)}, u32[]{:S(2)}) copy-start(bf16[256,768]{1,0:T(8,128)(2,1)S(1)} %collective-permute-done.10.refs_4_) | copy-start | bytes 1179652
  86.1 18.3 %all-to-all-start.2 = ((bf16[16,200,128]{2,1,0:T(8,128)(2,1)}), bf16[16,200,128]{2,1,0:T(8,128)(2,1)}, u32[]{:S(2)}, u32[]{:S(2)}) async-start(bf16[16,200,128]{2,1,0:T(8,128)(2,1)} %get-tuple-element.115.refs_0_), calls=%async_computation.2 | async-start | bytes 1638400 | tf_op jit(solution)/shard_map/all_to_all | solution.py:1247
  90.6 13.1 %collective-permute-start.12 = (bf16[768,768]{1,0:T(8,128)(2,1)}, bf16[768,768]{1,0:T(8,128)(2,1)}, u32[]{:S(2)}, u32[]{:S(2)}) collective-permute-start(bf16[768,768]{1,0:T(8,128)(2,1)} %get-tuple-element.126), channel_id=1, source_target_pairs={{0,1},{1,0},{2,3},{3,2},{4,5},{5,4},{6,7},{7,6},{8,9},{9,8},{10,11... | collective-permute-start | bytes 3538952 | tf_op jit(solution)/shard_map/ppermute | solution.py:59
  90.9 12.7 %collective-permute-start.13 = (bf16[768,768]{1,0:T(8,128)(2,1)}, bf16[768,768]{1,0:T(8,128)(2,1)}, u32[]{:S(2)}, u32[]{:S(2)}) collective-permute-start(bf16[768,768]{1,0:T(8,128)(2,1)} %get-tuple-element.127), channel_id=1, source_target_pairs={{0,1},{1,0},{2,3},{3,2},{4,5},{5,4},{6,7},{7,6},{8,9},{9,8},{10,11... | collective-permute-start | bytes 3538952 | tf_op jit(solution)/shard_map/ppermute | solution.py:59
  91.2 5.6 %collective-permute-start.11 = (bf16[256,768]{1,0:T(8,128)(2,1)S(1)}, bf16[256,768]{1,0:T(8,128)(2,1)S(1)}, u32[]{:S(2)}, u32[]{:S(2)}) collective-permute-start(bf16[256,768]{1,0:T(8,128)(2,1)S(1)} %collective-permute-done.10.refs_4_), channel_id=1, source_target_pairs={{0,1},{1,0},{2,3},{3,2},{4,5},{5,4},{6,7},{7,6},{8,9},{9,8},{10,11... | collective-permute-start | bytes 1179656 | tf_op jit(solution)/shard_map/ppermute | solution.py:59
  91.5 6.0 %copy-start.2 = (bf16[256,768]{1,0:T(8,128)(2,1)S(1)}, bf16[256,768]{1,0:T(8,128)(2,1)}, u32[]{:S(2)}) copy-start(bf16[256,768]{1,0:T(8,128)(2,1)} %copy-done.1) | copy-start | bytes 1179652
  91.5 6.0 %copy-start.3 = (bf16[256,768]{1,0:T(8,128)(2,1)S(1)}, bf16[256,768]{1,0:T(8,128)(2,1)}, u32[]{:S(2)}) copy-start(bf16[256,768]{1,0:T(8,128)(2,1)} %get-tuple-element.119.refs_2_) | copy-start | bytes 1179652
  91.5 6.0 %copy-start.8 = (f32[768]{0:T(1024)S(1)}, f32[768]{0:T(1024)}, u32[]{:S(2)}) copy-start(f32[768]{0:T(1024)} %param.15) | copy-start | bytes 9220
  96.8 0.7 copy-start.6
  97.5 1.0 copy-start.5
  98.5 1.0 copy-start.7
  99.5 4.8 %copy-start.9 = (f32[8,128]{1,0:T(8,128)S(1)}, f32[8,128]{1,0:T(8,128)}, u32[]{:S(2)}) copy-start(f32[8,128]{1,0:T(8,128)} %get-tuple-element.130.refs_3_) | copy-start | bytes 12292
  106.6 16.4 %collective-permute-start.14 = (bf16[2,600,128]{2,1,0:T(8,128)(2,1)S(1)}, bf16[2,600,128]{2,1,0:T(8,128)(2,1)S(1)}, u32[]{:S(2)}, u32[]{:S(2)}) collective-permute-start(bf16[2,600,128]{2,1,0:T(8,128)(2,1)S(1)} %grad_block.1.refs_0_), channel_id=1, source_target_pairs={{0,16},{16,0},{1,17},{17,1},{2,18},{18,2},{3,19},{19,3},{4,20},{20... | collective-permute-start | bytes 921608 | tf_op jit(solution)/shard_map/ppermute | solution.py:59
  123.1 8.0 %collective-permute-start.20 = (bf16[2,600,128]{2,1,0:T(8,128)(2,1)S(1)}, bf16[2,600,128]{2,1,0:T(8,128)(2,1)S(1)}, u32[]{:S(2)}, u32[]{:S(2)}) collective-permute-start(bf16[2,600,128]{2,1,0:T(8,128)(2,1)S(1)} %share.1.refs_0_), channel_id=1, source_target_pairs={{0,8},{8,0},{1,9},{9,1},{2,10},{10,2},{3,11},{11,3},{4,12},{12,4},... | collective-permute-start | bytes 921608 | tf_op jit(solution)/shard_map/ppermute | solution.py:59
  123.4 12.1 %collective-permute-start.25 = (bf16[2,600,128]{2,1,0:T(8,128)(2,1)S(1)}, bf16[2,600,128]{2,1,0:T(8,128)(2,1)S(1)}, u32[]{:S(2)}, u32[]{:S(2)}) collective-permute-start(bf16[2,600,128]{2,1,0:T(8,128)(2,1)S(1)} %share.1.refs_0_), channel_id=1, source_target_pairs={{0,1},{1,0},{2,3},{3,2},{4,5},{5,4},{6,7},{7,6},{8,9},{9,8},{10,11... | collective-permute-start | bytes 921608 | tf_op jit(solution)/shard_map/ppermute | solution.py:59
  123.4 12.2 %collective-permute-start.16 = (bf16[2,600,128]{2,1,0:T(8,128)(2,1)S(1)}, bf16[2,600,128]{2,1,0:T(8,128)(2,1)S(1)}, u32[]{:S(2)}, u32[]{:S(2)}) collective-permute-start(bf16[2,600,128]{2,1,0:T(8,128)(2,1)S(1)} %share.1.refs_0_), channel_id=1, source_target_pairs={{0,2},{2,0},{1,3},{3,1},{4,6},{6,4},{5,7},{7,5},{8,10},{10,8},{9,1... | collective-permute-start | bytes 921608 | tf_op jit(solution)/shard_map/ppermute | solution.py:59
  125.0 11.0 %collective-permute-start.15 = (bf16[2,600,128]{2,1,0:T(8,128)(2,1)S(1)}, bf16[2,600,128]{2,1,0:T(8,128)(2,1)S(1)}, u32[]{:S(2)}, u32[]{:S(2)}) collective-permute-start(bf16[2,600,128]{2,1,0:T(8,128)(2,1)S(1)} %share.1.refs_0_), channel_id=1, source_target_pairs={{0,4},{4,0},{1,5},{5,1},{2,6},{6,2},{3,7},{7,3},{8,12},{12,8},{9,1... | collective-permute-start | bytes 921608 | tf_op jit(solution)/shard_map/ppermute | solution.py:59
  131.1 11.1 %collective-permute-start.21 = (bf16[2,600,128]{2,1,0:T(8,128)(2,1)S(1)}, bf16[2,600,128]{2,1,0:T(8,128)(2,1)S(1)}, u32[]{:S(2)}, u32[]{:S(2)}) collective-permute-start(bf16[2,600,128]{2,1,0:T(8,128)(2,1)S(1)} %collective-permute-done.20.refs_4_), channel_id=1, source_target_pairs={{0,4},{4,0},{1,5},{5,1},{2,6},{6,2},{3,7},{7,3},{8,12},{12,8},{9,1... | collective-permute-start | bytes 921608 | tf_op jit(solution)/shard_map/ppermute | solution.py:59
  134.0 9.8 %collective-permute-start.27 = (bf16[2,600,128]{2,1,0:T(8,128)(2,1)S(1)}, bf16[2,600,128]{2,1,0:T(8,128)(2,1)S(1)}, u32[]{:S(2)}, u32[]{:S(2)}) collective-permute-start(bf16[2,600,128]{2,1,0:T(8,128)(2,1)S(1)} %collective-permute-done.20.refs_4_), channel_id=1, source_target_pairs={{0,2},{2,0},{1,3},{3,1},{4,6},{6,4},{5,7},{7,5},{8,10},{10,8},{9,1... | collective-permute-start | bytes 921608 | tf_op jit(solution)/shard_map/ppermute | solution.py:59
  135.5 8.3 %collective-permute-start.28 = (bf16[2,600,128]{2,1,0:T(8,128)(2,1)S(1)}, bf16[2,600,128]{2,1,0:T(8,128)(2,1)S(1)}, u32[]{:S(2)}, u32[]{:S(2)}) collective-permute-start(bf16[2,600,128]{2,1,0:T(8,128)(2,1)S(1)} %collective-permute-done.20.refs_4_), channel_id=1, source_target_pairs={{0,1},{1,0},{2,3},{3,2},{4,5},{5,4},{6,7},{7,6},{8,9},{9,8},{10,11... | collective-permute-start | bytes 921608 | tf_op jit(solution)/shard_map/ppermute | solution.py:59
  135.5 8.8 %collective-permute-start.26 = (bf16[2,600,128]{2,1,0:T(8,128)(2,1)S(1)}, bf16[2,600,128]{2,1,0:T(8,128)(2,1)S(1)}, u32[]{:S(2)}, u32[]{:S(2)}) collective-permute-start(bf16[2,600,128]{2,1,0:T(8,128)(2,1)S(1)} %collective-permute-done.16.refs_1_), channel_id=1, source_target_pairs={{0,1},{1,0},{2,3},{3,2},{4,5},{5,4},{6,7},{7,6},{8,9},{9,8},{10,11... | collective-permute-start | bytes 921608 | tf_op jit(solution)/shard_map/ppermute | solution.py:59
  136.0 11.6 %collective-permute-start.17 = (bf16[2,600,128]{2,1,0:T(8,128)(2,1)S(1)}, bf16[2,600,128]{2,1,0:T(8,128)(2,1)S(1)}, u32[]{:S(2)}, u32[]{:S(2)}) collective-permute-start(bf16[2,600,128]{2,1,0:T(8,128)(2,1)S(1)} %collective-permute-done.16.refs_1_), channel_id=1, source_target_pairs={{0,4},{4,0},{1,5},{5,1},{2,6},{6,2},{3,7},{7,3},{8,12},{12,8},{9,1... | collective-permute-start | bytes 921608 | tf_op jit(solution)/shard_map/ppermute | solution.py:59
  142.2 7.0 %collective-permute-start.22 = (bf16[2,600,128]{2,1,0:T(8,128)(2,1)S(1)}, bf16[2,600,128]{2,1,0:T(8,128)(2,1)S(1)}, u32[]{:S(2)}, u32[]{:S(2)}) collective-permute-start(bf16[2,600,128]{2,1,0:T(8,128)(2,1)S(1)} %collective-permute-done.21.refs_4_), channel_id=1, source_target_pairs={{0,2},{2,0},{1,3},{3,1},{4,6},{6,4},{5,7},{7,5},{8,10},{10,8},{9,1... | collective-permute-start | bytes 921608 | tf_op jit(solution)/shard_map/ppermute | solution.py:59
  143.8 5.4 %collective-permute-start.29 = (bf16[2,600,128]{2,1,0:T(8,128)(2,1)S(1)}, bf16[2,600,128]{2,1,0:T(8,128)(2,1)S(1)}, u32[]{:S(2)}, u32[]{:S(2)}) collective-permute-start(bf16[2,600,128]{2,1,0:T(8,128)(2,1)S(1)} %collective-permute-done.27.refs_5_), channel_id=1, source_target_pairs={{0,1},{1,0},{2,3},{3,2},{4,5},{5,4},{6,7},{7,6},{8,9},{9,8},{10,11... | collective-permute-start | bytes 921608 | tf_op jit(solution)/shard_map/ppermute | solution.py:59
  143.8 8.2 %collective-permute-start.18 = (bf16[2,600,128]{2,1,0:T(8,128)(2,1)S(1)}, bf16[2,600,128]{2,1,0:T(8,128)(2,1)S(1)}, u32[]{:S(2)}, u32[]{:S(2)}) collective-permute-start(bf16[2,600,128]{2,1,0:T(8,128)(2,1)S(1)} %collective-permute-done.15.refs_0_), channel_id=1, source_target_pairs={{0,1},{1,0},{2,3},{3,2},{4,5},{5,4},{6,7},{7,6},{8,9},{9,8},{10,11... | collective-permute-start | bytes 921608 | tf_op jit(solution)/shard_map/ppermute | solution.py:59
  144.3 7.8 %collective-permute-start.23 = (bf16[2,600,128]{2,1,0:T(8,128)(2,1)S(1)}, bf16[2,600,128]{2,1,0:T(8,128)(2,1)S(1)}, u32[]{:S(2)}, u32[]{:S(2)}) collective-permute-start(bf16[2,600,128]{2,1,0:T(8,128)(2,1)S(1)} %collective-permute-done.21.refs_4_), channel_id=1, source_target_pairs={{0,1},{1,0},{2,3},{3,2},{4,5},{5,4},{6,7},{7,6},{8,9},{9,8},{10,11... | collective-permute-start | bytes 921608 | tf_op jit(solution)/shard_map/ppermute | solution.py:59
  147.6 4.5 %collective-permute-start.19 = (bf16[2,600,128]{2,1,0:T(8,128)(2,1)S(1)}, bf16[2,600,128]{2,1,0:T(8,128)(2,1)S(1)}, u32[]{:S(2)}, u32[]{:S(2)}) collective-permute-start(bf16[2,600,128]{2,1,0:T(8,128)(2,1)S(1)} %collective-permute-done.17.refs_1_), channel_id=1, source_target_pairs={{0,1},{1,0},{2,3},{3,2},{4,5},{5,4},{6,7},{7,6},{8,9},{9,8},{10,11... | collective-permute-start | bytes 921608 | tf_op jit(solution)/shard_map/ppermute | solution.py:59
  149.2 2.9 %collective-permute-start.24 = (bf16[2,600,128]{2,1,0:T(8,128)(2,1)S(1)}, bf16[2,600,128]{2,1,0:T(8,128)(2,1)S(1)}, u32[]{:S(2)}, u32[]{:S(2)}) collective-permute-start(bf16[2,600,128]{2,1,0:T(8,128)(2,1)S(1)} %collective-permute-done.22.refs_5_), channel_id=1, source_target_pairs={{0,1},{1,0},{2,3},{3,2},{4,5},{5,4},{6,7},{7,6},{8,9},{9,8},{10,11... | collective-permute-start | bytes 921608 | tf_op jit(solution)/shard_map/ppermute | solution.py:59

commit v7 on v6

--- a/solution.py
+++ b/solution.py
@@ -1130,8 +1130,9 @@
     got, beside = lax.optimization_barrier((swap(block, "eh"), beside))
     near = share_of(block, got, 3 * width // 4, small_rows)
     far, near_x, near_y = swap(near, "em"), swap(near, "dx"), swap(near, "ey")
-    far_x, far_y = swap(far, "dx"), swap(far, "ey")
-    near_both, far_both = swap(near_x, "ey"), swap(far_y, "dx")
+    far_x, far_y = swap(near_x, "em"), swap(far, "ey")
+    near_both = swap(near_y, "dx")
+    far_both = swap(near_both, "em")
 
     def both_cores(*sources):
         return sources + tuple(swap(source, "dc") for source in sources)

time: 157 us -> 156 us (level)
  starting transfers between devices: 45.1 us -> 41.7 us
  waiting for transfers between devices: 48.7 us -> 51.1 us
    ppermute x30, starting transfers between devices: 28.2 us -> 24.8 us  [swap(): return lax.ppermute(array, axis, perm=[(0, 1), (1, 0)])]
    ppermute x30, waiting for transfers between devices: 33.1 us -> 35.5 us  [swap(): return lax.ppermute(array, axis, perm=[(0, 1), (1, 0)])]
  transfers between devices with their start and end apart: 33 -> 33, of which waited for: 11 -> 13; matrix products, arithmetic and copies ran while one was open for 0% -> 0% of each run, Pallas kernels for 33% -> 33%
where the time goes in v7:
time: 156 us; the launch traced here: 155 us
  Pallas kernels  56.7 us (36%)
  waiting for transfers between devices  51.1 us (33%)
  starting transfers between devices  41.7 us (27%)
  local copies, waits for them, and re-layouts  3.45 us (2%)
  between operations  1.85 us (1%)
    pallas_call x11, Pallas kernels, staged(): pl.pallas_call(body, out_shape=tuple(kept) + tuple(outputs), in_specs=[pl...  50.3 us
    ppermute x30, waiting for transfers between devices, swap(): return lax.ppermute(array, axis, perm=[(0, 1), (1, 0)])  35.5 us
    ppermute x30, starting transfers between devices, swap(): return lax.ppermute(array, axis, perm=[(0, 1), (1, 0)])  24.8 us
    all_to_all x1, waiting for transfers between devices, per_device(): lax.all_to_all(sent_back, EXPERT_AXES, split_axis=0, concat_axis=0, tiled...  13.2 us
    all_to_all x1, starting transfers between devices, per_device(): lax.all_to_all(sent_back, EXPERT_AXES, split_axis=0, concat_axis=0, tiled...  6.26 us
    all_to_all x1, starting transfers between devices, per_device(): lax.all_to_all(outgoing, EXPERT_AXES, split_axis=0, concat_axis=0, tiled=...  6.13 us
    all_to_all x1, starting transfers between devices, per_device(): lax.all_to_all(late, GROUP_AXES, split_axis=0, concat_axis=0, tiled=True)  4.5 us
    pallas_call x1, Pallas kernels, second_half(): pl.pallas_call(functools.partial(second_half_kernel, small_rows), out_sha...  3.57 us
  transfers between devices with their start and end apart: 33, of which 13 were waited for; matrix products, arithmetic and copies ran while one was open for 0% of the time, Pallas kernels for 33%

profile of v7, /device:TPU:0, one launch (start us, length us, event | category | flops | bytes accessed | tf_op | source)
XLA Modules:
  0.0 154.9 jit_solution(8161727356154362612)
XLA Ops:
  0.6 3.0 %collective-permute-start = (bf16[128,768]{1,0:T(8,128)(2,1)}, bf16[128,768]{1,0:T(8,128)(2,1)S(1)}, u32[]{:S(2)}, u32[]{:S(2)}) collective-permute-start(bf16[128,768]{1,0:T(8,128)(2,1)} %refs_5_.5), channel_id=1, source_target_pairs={{0,2},{2,0},{1,3},{3,1},{4,6},{6,4},{5,7},{7,5},{8,10},{10,8},{9,1... | collective-permute-start | bytes 589832 | tf_op jit(solution)/shard_map/ppermute | solution.py:59
  4.3 6.4 %forward.1 = (bf16[8,2,40,768]{3,2,1,0:T(8,128)(2,1)}, bf16[128,768]{1,0:T(8,128)(2,1)}, bf16[128,768]{1,0:T(8,128)(2,1)}, bf16[128,768]{1,0:T(8,128)(2,1)}, bf1...) custom-call(s32[1]{0:T(128)S(6)} %copy.34.refs_0_, ...), custom_call_target="tpu_custom_call" | custom-call | flops 754974720 | bytes 5898240 | tf_op jit(solution)/shard_map/forward/pallas_call | solution.py:190
  10.8 6.1 %all-to-all-start = ((bf16[16,40,768]{2,1,0:T(8,128)(2,1)}), bf16[16,40,768]{2,1,0:T(8,128)(2,1)}, u32[]{:S(2)}, u32[]{:S(2)}) async-start(bf16[16,40,768]{2,1,0:T(8,128)(2,1)} %bitcast.23), calls=%async_computation | async-start | bytes 1966080 | tf_op jit(solution)/shard_map/all_to_all | solution.py:1213
  17.0 0.5 collective-permute-start.4
  17.5 1.8 %collective-permute-start.1 = (bf16[256,768]{1,0:T(8,128)(2,1)S(1)}, bf16[256,768]{1,0:T(8,128)(2,1)}, u32[]{:S(2)}, u32[]{:S(2)}) collective-permute-start(bf16[256,768]{1,0:T(8,128)(2,1)S(1)} %pad_maximum_fusion.refs_3_), channel_id=1, source_target_pairs={{0,4},{4,0},{1,5},{5,1},{2,6},{6,2},{3,7},{7,3},{8,12},{12,8},{9,1... | collective-permute-start | bytes 1179656 | tf_op jit(solution)/shard_map/ppermute | solution.py:59
  19.4 1.5 collective-permute-start.2
  20.8 5.8 %collective-permute-done.2.refs_2_ = bf16[128,768]{1,0:T(8,128)(2,1)S(1)} collective-permute-done((bf16[128,768]{1,0:T(8,128)(2,1)S(1)}, bf16[128,768]{1,0:T(8,128)(2,1)S(1)}, u32[]{:S(2)}, u32[]{:S(2)}) %collective-permute-start.2) | collective-permute-done | bytes 196640 | tf_op jit(solution)/shard_map/ppermute | solution.py:59
  26.6 0.7 copy-done.14
  27.3 2.3 %picked.2 = (bf16[256,768]{1,0:T(8,128)(2,1)}, bf16[256,768]{1,0:T(8,128)(2,1)}, bf16[256,768]{1,0:T(8,128)(2,1)}) custom-call(s32[1]{0:T(128)} %bitcast.6.refs_0_, bf16[128,768]{1,0:T(8,128)(2,1)} %get-tuple-element.89.refs_1_, bf16[128,768]{1,0:T(8,128)(2,1)} %copy-done.14, bf16[256,768]{1,0:T(8,128)(2,1)} %copy-done.11), custom_call_target="tpu_custom_call" | custom-call | bytes 1966080 | tf_op jit(solution)/shard_map/picked/pallas_call | solution.py:190
  29.6 4.0 %collective-permute-start.5 = (bf16[256,768]{1,0:T(8,128)(2,1)}, bf16[256,768]{1,0:T(8,128)(2,1)S(1)}, u32[]{:S(2)}, u32[]{:S(2)}) collective-permute-start(bf16[256,768]{1,0:T(8,128)(2,1)} %get-tuple-element.92), channel_id=1, source_target_pairs={{0,4},{4,0},{1,5},{5,1},{2,6},{6,2},{3,7},{7,3},{8,12},{12,8},{9,1... | collective-permute-start | bytes 1179656 | tf_op jit(solution)/shard_map/ppermute | solution.py:59
  33.6 4.4 %collective-permute-done.1.refs_2_ = bf16[256,768]{1,0:T(8,128)(2,1)} collective-permute-done((bf16[256,768]{1,0:T(8,128)(2,1)S(1)}, bf16[256,768]{1,0:T(8,128)(2,1)}, u32[]{:S(2)}, u32[]{:S(2)}) %collective-permute-start.1) | collective-permute-done | bytes 393248 | tf_op jit(solution)/shard_map/ppermute | solution.py:59
  38.0 1.7 %all-to-all-done.refs_0_ = bf16[16,40,768]{2,1,0:T(8,128)(2,1)} async-done(((bf16[16,40,768]{2,1,0:T(8,128)(2,1)}), bf16[16,40,768]{2,1,0:T(8,128)(2,1)}, u32[]{:S(2)}, u32[]{:S(2)}) %all-to-all-start) | async-done | bytes 983072 | tf_op jit(solution)/shard_map/all_to_all | solution.py:1213
  39.7 8.0 %expert_rows.1 = bf16[16,40,768]{2,1,0:T(8,128)(2,1)} custom-call(bf16[16,40,768]{2,1,0:T(8,128)(2,1)} %all-to-all-done.refs_0_, bf16[768,768]{1,0:T(8,128)(2,1)} %bitcast.7.refs_1_, bf16[768,768]{1,0:T(8,128)(2,1)} %bitcast.8.refs_2_, bf16[768,768]{1,0:T(8,128)(2,1)} %collective-permute-done.3.refs_3_.refs_1_, ...), custom_call_target="tpu_custom_call" | custom-call | flops 3019898880 | bytes 7077888 | tf_op jit(solution)/shard_map/expert_rows/pallas_call | solution.py:190
  47.7 6.3 %all-to-all-start.1 = ((bf16[16,40,768]{2,1,0:T(8,128)(2,1)}), bf16[16,40,768]{2,1,0:T(8,128)(2,1)}, u32[]{:S(2)}, u32[]{:S(2)}) async-start(bf16[16,40,768]{2,1,0:T(8,128)(2,1)} %expert_rows.1), calls=%async_computation.1 | async-start | bytes 1966080 | tf_op jit(solution)/shard_map/all_to_all | solution.py:1224
  54.1 2.1 %picked.3 = (bf16[256,768]{1,0:T(8,128)(2,1)}, bf16[256,768]{1,0:T(8,128)(2,1)}) custom-call(s32[1]{0:T(128)} %bitcast.6.refs_0_, bf16[256,768]{1,0:T(8,128)(2,1)} %copy-done.12, bf16[256,768]{1,0:T(8,128)(2,1)} %collective-permute-done.1.refs_2_), custom_call_target="tpu_custom_call" | custom-call | bytes 1966080 | tf_op jit(solution)/shard_map/picked/pallas_call | solution.py:190
  56.2 0.6 collective-permute-start.8
  56.9 5.5 %sent_grads.1 = (bf16[768,768]{1,0:T(8,128)(2,1)}, bf16[768,768]{1,0:T(8,128)(2,1)}) custom-call(bf16[16,40,768]{2,1,0:T(8,128)(2,1)} %all-to-all-done.refs_0_, bf16[768,768]{1,0:T(8,128)(2,1)} %collective-permute-done.3.refs_3_.refs_1_, bf16[768,768]{1,0:T(8,128)(2,1)} %collective-permute-done.4.refs_4_.refs_2_), custom_call_target="tpu_custom_call" | custom-call | flops 1509949440 | bytes 4718592 | tf_op jit(solution)/shard_map/sent_grads/pallas_call | solution.py:190
  62.5 13.2 %all-to-all-done.1 = bf16[16,40,768]{2,1,0:T(8,128)(2,1)} async-done(((bf16[16,40,768]{2,1,0:T(8,128)(2,1)}), bf16[16,40,768]{2,1,0:T(8,128)(2,1)}, u32[]{:S(2)}, u32[]{:S(2)}) %all-to-all-start.1) | async-done | bytes 983072 | tf_op jit(solution)/shard_map/all_to_all | solution.py:1224
  75.7 2.8 %collective-permute-start.10 = (bf16[256,768]{1,0:T(8,128)(2,1)}, bf16[256,768]{1,0:T(8,128)(2,1)S(1)}, u32[]{:S(2)}, u32[]{:S(2)}) collective-permute-start(bf16[256,768]{1,0:T(8,128)(2,1)} %get-tuple-element.114), channel_id=1, source_target_pairs={{0,8},{8,0},{1,9},{9,1},{2,10},{10,2},{3,11},{11,3},{4,12},{12,4},... | collective-permute-start | bytes 1179656 | tf_op jit(solution)/shard_map/ppermute | solution.py:59
  78.5 7.3 %backward.1 = (bf16[16,200,128]{2,1,0:T(8,128)(2,1)}, f32[128,768]{1,0:T(8,128)}, bf16[128,768]{1,0:T(8,128)(2,1)}) custom-call(bf16[8,2,40,768]{3,2,1,0:T(8,128)(2,1)} %bitcast.9.refs_0_, s32[2,128]{1,0:T(2,128)} %get-tuple-element.104.refs_1_, f32[128,768]{1,0:T(8,128)} %get-tuple-element.105.refs_2_, f32[128,8]{1,0:T(8,128)} %get-tuple-element.106.refs_3_, ...), custom_call_target="tpu_custom_call" | custom-call | flops 301989888 | bytes 5898240 | tf_op jit(solution)/shard_map/backward/pallas_call | solution.py:190
  86.1 4.5 %all-to-all-start.2 = ((bf16[16,200,128]{2,1,0:T(8,128)(2,1)}), bf16[16,200,128]{2,1,0:T(8,128)(2,1)}, u32[]{:S(2)}, u32[]{:S(2)}) async-start(bf16[16,200,128]{2,1,0:T(8,128)(2,1)} %get-tuple-element.115.refs_0_), calls=%async_computation.2 | async-start | bytes 1638400 | tf_op jit(solution)/shard_map/all_to_all | solution.py:1248
  90.6 0.4 collective-permute-start.12
  91.2 0.3 collective-permute-start.11
  91.5 5.2 %first_norm.1 = (f32[8,128]{1,0:T(8,128)}, bf16[128,768]{1,0:T(8,128)(2,1)}) custom-call(bf16[16,200,128]{2,1,0:T(8,128)(2,1)} %get-tuple-element.115.refs_0_, f32[128,768]{1,0:T(8,128)} %get-tuple-element.116.refs_1_, bf16[768,768]{1,0:T(8,128)(2,1)} %refs_2_.1, bf16[768,768]{1,0:T(8,128)(2,1)} %refs_3_.3, bf16[768,768]{1,0:T(8,128)(2,1)} %refs_4_.3, ...), custom_call_target="tpu_custom_call" | custom-call | flops 452984832 | bytes 4718592 | tf_op jit(solution)/shard_map/first_norm/pallas_call | solution.py:190
  96.8 0.7 copy-done.6
  97.5 1.0 copy-done.5
  98.5 1.0 copy-done.7
  99.5 4.1 %left.1.refs_2_ = bf16[768,2048]{1,0:T(8,128)(2,1)S(1)} custom-call(s32[1]{0:T(128)} %bitcast.6.refs_0_, bf16[256,768]{1,0:T(8,128)(2,1)S(1)} %copy-done, bf16[256,768]{1,0:T(8,128)(2,1)S(1)} %copy-done.3, bf16[256,768]{1,0:T(8,128)(2,1)S(1)} %copy-done.2, bf16[256,768]{1,0:T(8,128)(2,1)S(1)} %copy-done.5, bf16[256,768]{1,0:T(8,128)(2,1)} %collective-permute-done.7.refs_5_, ...), custom_call_target="tpu_custom_call" | custom-call | flops 15728640 | bytes 9437184 | tf_op jit(solution)/shard_map/left/pallas_call | solution.py:190
  103.7 0.7 all-to-all-done.2.refs_1_
  104.3 2.2 %grad_block.1.refs_0_ = bf16[2,600,128]{2,1,0:T(8,128)(2,1)S(1)} custom-call(s32[4]{0:T(128)S(1)} %pad_add_fusion.refs_0_.bits_ref, bf16[16,200,128]{2,1,0:T(8,128)(2,1)} %all-to-all-done.2.refs_1_, bf16[768,2048]{1,0:T(8,128)(2,1)S(1)} %left.1.refs_2_, f32[8,128]{1,0:T(8,128)S(1)} %copy-done.9), custom_call_target="tpu_custom_call" | custom-call | flops 603979776 | bytes 3145728 | tf_op jit(solution)/shard_map/grad_block/pallas_call | solution.py:190
  106.6 2.2 %collective-permute-start.14 = (bf16[2,600,128]{2,1,0:T(8,128)(2,1)S(1)}, bf16[2,600,128]{2,1,0:T(8,128)(2,1)S(1)}, u32[]{:S(2)}, u32[]{:S(2)}) collective-permute-start(bf16[2,600,128]{2,1,0:T(8,128)(2,1)S(1)} %grad_block.1.refs_0_), channel_id=1, source_target_pairs={{0,16},{16,0},{1,17},{17,1},{2,18},{18,2},{3,19},{19,3},{4,20},{20... | collective-permute-start | bytes 921608 | tf_op jit(solution)/shard_map/ppermute | solution.py:59
  108.8 6.9 %own_grads.1 = (f32[768,768]{1,0:T(8,128)}, f32[768,768]{1,0:T(8,128)}) custom-call(bf16[16,40,768]{2,1,0:T(8,128)(2,1)} %all-to-all-done.refs_0_, bf16[768,768]{1,0:T(8,128)(2,1)} %bitcast.7.refs_1_, bf16[768,768]{1,0:T(8,128)(2,1)} %bitcast.8.refs_2_, bf16[768,768]{1,0:T(8,128)(2,1)} %collective-permute-done.12.refs_3_, ...), custom_call_target="tpu_custom_call" | custom-call | tf_op jit(solution)/shard_map/own_grads/pallas_call | solution.py:190
  115.7 7.2 %collective-permute-done.14.refs_1_ = bf16[2,600,128]{2,1,0:T(8,128)(2,1)S(1)} collective-permute-done((bf16[2,600,128]{2,1,0:T(8,128)(2,1)S(1)}, bf16[2,600,128]{2,1,0:T(8,128)(2,1)S(1)}, u32[]{:S(2)}, u32[]{:S(2)}) %collective-permute-start.14) | collective-permute-done | bytes 307232 | tf_op jit(solution)/shard_map/ppermute | solution.py:59
  123.1 1.8 %collective-permute-start.15 = (bf16[2,600,128]{2,1,0:T(8,128)(2,1)S(1)}, bf16[2,600,128]{2,1,0:T(8,128)(2,1)S(1)}, u32[]{:S(2)}, u32[]{:S(2)}) collective-permute-start(bf16[2,600,128]{2,1,0:T(8,128)(2,1)S(1)} %share.1.refs_0_), channel_id=1, source_target_pairs={{0,4},{4,0},{1,5},{5,1},{2,6},{6,2},{3,7},{7,3},{8,12},{12,8},{9,1... | collective-permute-start | bytes 921608 | tf_op jit(solution)/shard_map/ppermute | solution.py:59
  124.9 1.5 collective-permute-start.24
  126.4 5.9 %collective-permute-done.15.refs_0_ = bf16[2,600,128]{2,1,0:T(8,128)(2,1)S(1)} collective-permute-done((bf16[2,600,128]{2,1,0:T(8,128)(2,1)S(1)}, bf16[2,600,128]{2,1,0:T(8,128)(2,1)S(1)}, u32[]{:S(2)}, u32[]{:S(2)}) %collective-permute-start.15) | collective-permute-done | bytes 307232 | tf_op jit(solution)/shard_map/ppermute | solution.py:59
  132.2 1.5 collective-permute-start.16
  133.8 0.5 collective-permute-start.27
  134.3 0.7 collective-permute-done.19.refs_4_
  135.0 1.1 collective-permute-start.20
  136.0 4.5 %collective-permute-done.16.refs_1_ = bf16[2,600,128]{2,1,0:T(8,128)(2,1)S(1)} collective-permute-done((bf16[2,600,128]{2,1,0:T(8,128)(2,1)S(1)}, bf16[2,600,128]{2,1,0:T(8,128)(2,1)S(1)}, u32[]{:S(2)}, u32[]{:S(2)}) %collective-permute-start.16) | collective-permute-done | bytes 307232 | tf_op jit(solution)/shard_map/ppermute | solution.py:59
  140.5 0.4 collective-permute-start.21
  140.9 1.0 collective-permute-done.27.refs_5_
  141.9 0.5 collective-permute-start.17
  142.5 2.1 %collective-permute-done.20.refs_4_ = bf16[2,600,128]{2,1,0:T(8,128)(2,1)S(1)} collective-permute-done((bf16[2,600,128]{2,1,0:T(8,128)(2,1)S(1)}, bf16[2,600,128]{2,1,0:T(8,128)(2,1)S(1)}, u32[]{:S(2)}, u32[]{:S(2)}) %collective-permute-start.20) | collective-permute-done | bytes 307232 | tf_op jit(solution)/shard_map/ppermute | solution.py:59
  144.7 3.6 %collective-permute-done.21.refs_5_ = bf16[2,600,128]{2,1,0:T(8,128)(2,1)S(1)} collective-permute-done((bf16[2,600,128]{2,1,0:T(8,128)(2,1)S(1)}, bf16[2,600,128]{2,1,0:T(8,128)(2,1)S(1)}, u32[]{:S(2)}, u32[]{:S(2)}) %collective-permute-start.21) | collective-permute-done | bytes 307232 | tf_op jit(solution)/shard_map/ppermute | solution.py:59
  148.2 2.9 %first_half.1 = (f32[768,768]{1,0:T(8,128)}, f32[768,768]{1,0:T(8,128)}, f32[768,768]{1,0:T(8,128)}, f32[768,768]{1,0:T(8,128)}, f32[2,4,12,128]{3,2,1,0:T(8,128)S(1)}) custom-call(s32[4]{0:T(128)S(1)} %pad_add_fusion.refs_0_.bits_ref, bf16[2,600,128]{2,1,0:T(8,128)(2,1)S(1)} %share.1.refs_0_, bf16[2,600,128]{2,1,0:T(8,128)(2,1)S(1)} %collective-permute-done.24.refs_1_, ...), custom_call_target="tpu_custom_call" | custom-call | flops 4718592 | bytes 7077888 | tf_op jit(solution)/shard_map/first_half/pallas_call | solution.py:1069
  151.1 3.6 %second_half.1 = (f32[768,768]{1,0:T(8,128)}, f32[768,768]{1,0:T(8,128)}, f32[768,768]{1,0:T(8,128)}, f32[768,768]{1,0:T(8,128)}, f32[6,128]{1,0:T(8,128)}, /*in...) custom-call(s32[4]{0:T(128)S(1)} %pad_add_fusion.refs_0_.bits_ref, ...), custom_call_target="tpu_custom_call", output_to_operand_aliasing={{0}: (10, {}), {1}: (11, {}), {2}: (12, {}), {3}: (13, {})} | custom-call | flops 4718592 | bytes 7077888 | tf_op jit(solution)/shard_map/second_half/pallas_call | solution.py:1087
  (63 shorter events, 1.2 us)
Async XLA Ops:
  0.6 10.1 %collective-permute-start = (bf16[128,768]{1,0:T(8,128)(2,1)}, bf16[128,768]{1,0:T(8,128)(2,1)S(1)}, u32[]{:S(2)}, u32[]{:S(2)}) collective-permute-start(bf16[128,768]{1,0:T(8,128)(2,1)} %refs_5_.5), channel_id=1, source_target_pairs={{0,2},{2,0},{1,3},{3,1},{4,6},{6,4},{5,7},{7,5},{8,10},{10,8},{9,1... | collective-permute-start | bytes 589832 | tf_op jit(solution)/shard_map/ppermute | solution.py:59
  4.3 6.5 %copy-start.10 = (bf16[128,768]{1,0:T(8,128)(2,1)S(1)}, bf16[128,768]{1,0:T(8,128)(2,1)}, u32[]{:S(2)}) copy-start(bf16[128,768]{1,0:T(8,128)(2,1)} %refs_5_.5) | copy-start | bytes 589828
  10.8 15.8 %copy-start.11 = (bf16[256,768]{1,0:T(8,128)(2,1)}, bf16[256,768]{1,0:T(8,128)(2,1)S(1)}, u32[]{:S(2)}) copy-start(bf16[256,768]{1,0:T(8,128)(2,1)S(1)} %pad_maximum_fusion.refs_3_) | copy-start | bytes 1179652
  10.8 8.5 %copy-start.13 = (bf16[128,768]{1,0:T(8,128)(2,1)S(1)}, bf16[128,768]{1,0:T(8,128)(2,1)}, u32[]{:S(2)}) copy-start(bf16[128,768]{1,0:T(8,128)(2,1)} %get-tuple-element.89.refs_1_) | copy-start | bytes 589828
  10.8 28.9 %all-to-all-start = ((bf16[16,40,768]{2,1,0:T(8,128)(2,1)}), bf16[16,40,768]{2,1,0:T(8,128)(2,1)}, u32[]{:S(2)}, u32[]{:S(2)}) async-start(bf16[16,40,768]{2,1,0:T(8,128)(2,1)} %bitcast.23), calls=%async_computation | async-start | bytes 1966080 | tf_op jit(solution)/shard_map/all_to_all | solution.py:1213
  17.0 22.7 %collective-permute-start.3 = (bf16[768,768]{1,0:T(8,128)(2,1)}, bf16[768,768]{1,0:T(8,128)(2,1)}, u32[]{:S(2)}, u32[]{:S(2)}) collective-permute-start(bf16[768,768]{1,0:T(8,128)(2,1)} %bitcast.7.refs_1_), channel_id=1, source_target_pairs={{0,1},{1,0},{2,3},{3,2},{4,5},{5,4},{6,7},{7,6},{8,9},{9,8},{10,11... | collective-permute-start | bytes 3538952 | tf_op jit(solution)/shard_map/ppermute | solution.py:59
  17.0 22.6 %collective-permute-start.4 = (bf16[768,768]{1,0:T(8,128)(2,1)}, bf16[768,768]{1,0:T(8,128)(2,1)}, u32[]{:S(2)}, u32[]{:S(2)}) collective-permute-start(bf16[768,768]{1,0:T(8,128)(2,1)} %bitcast.8.refs_2_), channel_id=1, source_target_pairs={{0,1},{1,0},{2,3},{3,2},{4,5},{5,4},{6,7},{7,6},{8,9},{9,8},{10,11... | collective-permute-start | bytes 3538952 | tf_op jit(solution)/shard_map/ppermute | solution.py:59
  17.5 20.5 %collective-permute-start.1 = (bf16[256,768]{1,0:T(8,128)(2,1)S(1)}, bf16[256,768]{1,0:T(8,128)(2,1)}, u32[]{:S(2)}, u32[]{:S(2)}) collective-permute-start(bf16[256,768]{1,0:T(8,128)(2,1)S(1)} %pad_maximum_fusion.refs_3_), channel_id=1, source_target_pairs={{0,4},{4,0},{1,5},{5,1},{2,6},{6,2},{3,7},{7,3},{8,12},{12,8},{9,1... | collective-permute-start | bytes 1179656 | tf_op jit(solution)/shard_map/ppermute | solution.py:59
  19.4 7.3 %collective-permute-start.2 = (bf16[128,768]{1,0:T(8,128)(2,1)S(1)}, bf16[128,768]{1,0:T(8,128)(2,1)S(1)}, u32[]{:S(2)}, u32[]{:S(2)}) collective-permute-start(bf16[128,768]{1,0:T(8,128)(2,1)S(1)} %copy-done.13), channel_id=1, source_target_pairs={{0,2},{2,0},{1,3},{3,1},{4,6},{6,4},{5,7},{7,5},{8,10},{10,8},{9,1... | collective-permute-start | bytes 589832 | tf_op jit(solution)/shard_map/ppermute | solution.py:59
  26.6 0.7 copy-start.14
  29.6 18.1 %collective-permute-start.5 = (bf16[256,768]{1,0:T(8,128)(2,1)}, bf16[256,768]{1,0:T(8,128)(2,1)S(1)}, u32[]{:S(2)}, u32[]{:S(2)}) collective-permute-start(bf16[256,768]{1,0:T(8,128)(2,1)} %get-tuple-element.92), channel_id=1, source_target_pairs={{0,4},{4,0},{1,5},{5,1},{2,6},{6,2},{3,7},{7,3},{8,12},{12,8},{9,1... | collective-permute-start | bytes 1179656 | tf_op jit(solution)/shard_map/ppermute | solution.py:59
  33.6 14.1 %collective-permute-start.6 = (bf16[256,768]{1,0:T(8,128)(2,1)}, bf16[256,768]{1,0:T(8,128)(2,1)S(1)}, u32[]{:S(2)}, u32[]{:S(2)}) collective-permute-start(bf16[256,768]{1,0:T(8,128)(2,1)} %get-tuple-element.90), channel_id=1, source_target_pairs={{0,8},{8,0},{1,9},{9,1},{2,10},{10,2},{3,11},{11,3},{4,12},{12,4},... | collective-permute-start | bytes 1179656 | tf_op jit(solution)/shard_map/ppermute | solution.py:59
  47.7 6.3 %copy-start = (bf16[256,768]{1,0:T(8,128)(2,1)S(1)}, bf16[256,768]{1,0:T(8,128)(2,1)}, u32[]{:S(2)}) copy-start(bf16[256,768]{1,0:T(8,128)(2,1)} %get-tuple-element.118.refs_1_) | copy-start | bytes 1179652
  47.7 6.3 %copy-start.12 = (bf16[256,768]{1,0:T(8,128)(2,1)}, bf16[256,768]{1,0:T(8,128)(2,1)S(1)}, u32[]{:S(2)}) copy-start(bf16[256,768]{1,0:T(8,128)(2,1)S(1)} %collective-permute-done.5.refs_1_) | copy-start | bytes 1179652
  47.7 9.1 %copy-start.1 = (bf16[256,768]{1,0:T(8,128)(2,1)}, bf16[256,768]{1,0:T(8,128)(2,1)S(1)}, u32[]{:S(2)}) copy-start(bf16[256,768]{1,0:T(8,128)(2,1)S(1)} %collective-permute-done.6.refs_3_) | copy-start | bytes 1179652
  47.7 28.0 %all-to-all-start.1 = ((bf16[16,40,768]{2,1,0:T(8,128)(2,1)}), bf16[16,40,768]{2,1,0:T(8,128)(2,1)}, u32[]{:S(2)}, u32[]{:S(2)}) async-start(bf16[16,40,768]{2,1,0:T(8,128)(2,1)} %expert_rows.1), calls=%async_computation.1 | async-start | bytes 1966080 | tf_op jit(solution)/shard_map/all_to_all | solution.py:1224
  54.0 8.4 %collective-permute-start.7 = (bf16[256,768]{1,0:T(8,128)(2,1)S(1)}, bf16[256,768]{1,0:T(8,128)(2,1)}, u32[]{:S(2)}, u32[]{:S(2)}) collective-permute-start(bf16[256,768]{1,0:T(8,128)(2,1)S(1)} %copy-done), channel_id=1, source_target_pairs={{0,1},{1,0},{2,3},{3,2},{4,5},{5,4},{6,7},{7,6},{8,9},{9,8},{10,11... | collective-permute-start | bytes 1179656 | tf_op jit(solution)/shard_map/ppermute | solution.py:59
  56.2 6.2 %collective-permute-start.8 = (bf16[256,768]{1,0:T(8,128)(2,1)}, bf16[256,768]{1,0:T(8,128)(2,1)}, u32[]{:S(2)}, u32[]{:S(2)}) collective-permute-start(bf16[256,768]{1,0:T(8,128)(2,1)} %get-tuple-element.119.refs_2_), channel_id=1, source_target_pairs={{0,1},{1,0},{2,3},{3,2},{4,5},{5,4},{6,7},{7,6},{8,9},{9,8},{10,11... | collective-permute-start | bytes 1179656 | tf_op jit(solution)/shard_map/ppermute | solution.py:59
  56.8 5.7 %collective-permute-start.9 = (bf16[256,768]{1,0:T(8,128)(2,1)S(1)}, bf16[256,768]{1,0:T(8,128)(2,1)}, u32[]{:S(2)}, u32[]{:S(2)}) collective-permute-start(bf16[256,768]{1,0:T(8,128)(2,1)S(1)} %collective-permute-done.6.refs_3_), channel_id=1, source_target_pairs={{0,1},{1,0},{2,3},{3,2},{4,5},{5,4},{6,7},{7,6},{8,9},{9,8},{10,11... | collective-permute-start | bytes 1179656 | tf_op jit(solution)/shard_map/ppermute | solution.py:59
  75.7 10.4 %collective-permute-start.10 = (bf16[256,768]{1,0:T(8,128)(2,1)}, bf16[256,768]{1,0:T(8,128)(2,1)S(1)}, u32[]{:S(2)}, u32[]{:S(2)}) collective-permute-start(bf16[256,768]{1,0:T(8,128)(2,1)} %get-tuple-element.114), channel_id=1, source_target_pairs={{0,8},{8,0},{1,9},{9,1},{2,10},{10,2},{3,11},{11,3},{4,12},{12,4},... | collective-permute-start | bytes 1179656 | tf_op jit(solution)/shard_map/ppermute | solution.py:59
  86.1 10.7 %copy-start.4 = (bf16[256,768]{1,0:T(8,128)(2,1)}, bf16[256,768]{1,0:T(8,128)(2,1)S(1)}, u32[]{:S(2)}) copy-start(bf16[256,768]{1,0:T(8,128)(2,1)S(1)} %collective-permute-done.10.refs_4_) | copy-start | bytes 1179652
  86.1 18.3 %all-to-all-start.2 = ((bf16[16,200,128]{2,1,0:T(8,128)(2,1)}), bf16[16,200,128]{2,1,0:T(8,128)(2,1)}, u32[]{:S(2)}, u32[]{:S(2)}) async-start(bf16[16,200,128]{2,1,0:T(8,128)(2,1)} %get-tuple-element.115.refs_0_), calls=%async_computation.2 | async-start | bytes 1638400 | tf_op jit(solution)/shard_map/all_to_all | solution.py:1248
  90.6 13.1 %collective-permute-start.12 = (bf16[768,768]{1,0:T(8,128)(2,1)}, bf16[768,768]{1,0:T(8,128)(2,1)}, u32[]{:S(2)}, u32[]{:S(2)}) collective-permute-start(bf16[768,768]{1,0:T(8,128)(2,1)} %get-tuple-element.126), channel_id=1, source_target_pairs={{0,1},{1,0},{2,3},{3,2},{4,5},{5,4},{6,7},{7,6},{8,9},{9,8},{10,11... | collective-permute-start | bytes 3538952 | tf_op jit(solution)/shard_map/ppermute | solution.py:59
  90.9 12.7 %collective-permute-start.13 = (bf16[768,768]{1,0:T(8,128)(2,1)}, bf16[768,768]{1,0:T(8,128)(2,1)}, u32[]{:S(2)}, u32[]{:S(2)}) collective-permute-start(bf16[768,768]{1,0:T(8,128)(2,1)} %get-tuple-element.127), channel_id=1, source_target_pairs={{0,1},{1,0},{2,3},{3,2},{4,5},{5,4},{6,7},{7,6},{8,9},{9,8},{10,11... | collective-permute-start | bytes 3538952 | tf_op jit(solution)/shard_map/ppermute | solution.py:59
  91.2 5.6 %collective-permute-start.11 = (bf16[256,768]{1,0:T(8,128)(2,1)S(1)}, bf16[256,768]{1,0:T(8,128)(2,1)S(1)}, u32[]{:S(2)}, u32[]{:S(2)}) collective-permute-start(bf16[256,768]{1,0:T(8,128)(2,1)S(1)} %collective-permute-done.10.refs_4_), channel_id=1, source_target_pairs={{0,1},{1,0},{2,3},{3,2},{4,5},{5,4},{6,7},{7,6},{8,9},{9,8},{10,11... | collective-permute-start | bytes 1179656 | tf_op jit(solution)/shard_map/ppermute | solution.py:59
  91.5 6.0 %copy-start.2 = (bf16[256,768]{1,0:T(8,128)(2,1)S(1)}, bf16[256,768]{1,0:T(8,128)(2,1)}, u32[]{:S(2)}) copy-start(bf16[256,768]{1,0:T(8,128)(2,1)} %copy-done.1) | copy-start | bytes 1179652
  91.5 6.0 %copy-start.3 = (bf16[256,768]{1,0:T(8,128)(2,1)S(1)}, bf16[256,768]{1,0:T(8,128)(2,1)}, u32[]{:S(2)}) copy-start(bf16[256,768]{1,0:T(8,128)(2,1)} %get-tuple-element.119.refs_2_) | copy-start | bytes 1179652
  91.5 6.0 %copy-start.8 = (f32[768]{0:T(1024)S(1)}, f32[768]{0:T(1024)}, u32[]{:S(2)}) copy-start(f32[768]{0:T(1024)} %param.15) | copy-start | bytes 9220
  96.8 0.7 copy-start.6
  97.5 1.0 copy-start.5
  98.5 1.0 copy-start.7
  99.5 4.8 %copy-start.9 = (f32[8,128]{1,0:T(8,128)S(1)}, f32[8,128]{1,0:T(8,128)}, u32[]{:S(2)}) copy-start(f32[8,128]{1,0:T(8,128)} %get-tuple-element.130.refs_3_) | copy-start | bytes 12292
  106.6 16.4 %collective-permute-start.14 = (bf16[2,600,128]{2,1,0:T(8,128)(2,1)S(1)}, bf16[2,600,128]{2,1,0:T(8,128)(2,1)S(1)}, u32[]{:S(2)}, u32[]{:S(2)}) collective-permute-start(bf16[2,600,128]{2,1,0:T(8,128)(2,1)S(1)} %grad_block.1.refs_0_), channel_id=1, source_target_pairs={{0,16},{16,0},{1,17},{17,1},{2,18},{18,2},{3,19},{19,3},{4,20},{20... | collective-permute-start | bytes 921608 | tf_op jit(solution)/shard_map/ppermute | solution.py:59
  123.1 9.2 %collective-permute-start.15 = (bf16[2,600,128]{2,1,0:T(8,128)(2,1)S(1)}, bf16[2,600,128]{2,1,0:T(8,128)(2,1)S(1)}, u32[]{:S(2)}, u32[]{:S(2)}) collective-permute-start(bf16[2,600,128]{2,1,0:T(8,128)(2,1)S(1)} %share.1.refs_0_), channel_id=1, source_target_pairs={{0,4},{4,0},{1,5},{5,1},{2,6},{6,2},{3,7},{7,3},{8,12},{12,8},{9,1... | collective-permute-start | bytes 921608 | tf_op jit(solution)/shard_map/ppermute | solution.py:59
  124.9 8.9 %collective-permute-start.24 = (bf16[2,600,128]{2,1,0:T(8,128)(2,1)S(1)}, bf16[2,600,128]{2,1,0:T(8,128)(2,1)S(1)}, u32[]{:S(2)}, u32[]{:S(2)}) collective-permute-start(bf16[2,600,128]{2,1,0:T(8,128)(2,1)S(1)} %share.1.refs_0_), channel_id=1, source_target_pairs={{0,2},{2,0},{1,3},{3,1},{4,6},{6,4},{5,7},{7,5},{8,10},{10,8},{9,1... | collective-permute-start | bytes 921608 | tf_op jit(solution)/shard_map/ppermute | solution.py:59
  126.3 8.6 %collective-permute-start.19 = (bf16[2,600,128]{2,1,0:T(8,128)(2,1)S(1)}, bf16[2,600,128]{2,1,0:T(8,128)(2,1)S(1)}, u32[]{:S(2)}, u32[]{:S(2)}) collective-permute-start(bf16[2,600,128]{2,1,0:T(8,128)(2,1)S(1)} %share.1.refs_0_), channel_id=1, source_target_pairs={{0,8},{8,0},{1,9},{9,1},{2,10},{10,2},{3,11},{11,3},{4,12},{12,4},... | collective-permute-start | bytes 921608 | tf_op jit(solution)/shard_map/ppermute | solution.py:59
  126.4 8.6 %collective-permute-start.25 = (bf16[2,600,128]{2,1,0:T(8,128)(2,1)S(1)}, bf16[2,600,128]{2,1,0:T(8,128)(2,1)S(1)}, u32[]{:S(2)}, u32[]{:S(2)}) collective-permute-start(bf16[2,600,128]{2,1,0:T(8,128)(2,1)S(1)} %share.1.refs_0_), channel_id=1, source_target_pairs={{0,1},{1,0},{2,3},{3,2},{4,5},{5,4},{6,7},{7,6},{8,9},{9,8},{10,11... | collective-permute-start | bytes 921608 | tf_op jit(solution)/shard_map/ppermute | solution.py:59
  132.2 8.3 %collective-permute-start.16 = (bf16[2,600,128]{2,1,0:T(8,128)(2,1)S(1)}, bf16[2,600,128]{2,1,0:T(8,128)(2,1)S(1)}, u32[]{:S(2)}, u32[]{:S(2)}) collective-permute-start(bf16[2,600,128]{2,1,0:T(8,128)(2,1)S(1)} %collective-permute-done.15.refs_0_), channel_id=1, source_target_pairs={{0,2},{2,0},{1,3},{3,1},{4,6},{6,4},{5,7},{7,5},{8,10},{10,8},{9,1... | collective-permute-start | bytes 921608 | tf_op jit(solution)/shard_map/ppermute | solution.py:59
  133.8 8.1 %collective-permute-start.27 = (bf16[2,600,128]{2,1,0:T(8,128)(2,1)S(1)}, bf16[2,600,128]{2,1,0:T(8,128)(2,1)S(1)}, u32[]{:S(2)}, u32[]{:S(2)}) collective-permute-start(bf16[2,600,128]{2,1,0:T(8,128)(2,1)S(1)} %collective-permute-done.24.refs_1_), channel_id=1, source_target_pairs={{0,8},{8,0},{1,9},{9,1},{2,10},{10,2},{3,11},{11,3},{4,12},{12,4},... | collective-permute-start | bytes 921608 | tf_op jit(solution)/shard_map/ppermute | solution.py:59
  134.3 7.7 %collective-permute-start.26 = (bf16[2,600,128]{2,1,0:T(8,128)(2,1)S(1)}, bf16[2,600,128]{2,1,0:T(8,128)(2,1)S(1)}, u32[]{:S(2)}, u32[]{:S(2)}) collective-permute-start(bf16[2,600,128]{2,1,0:T(8,128)(2,1)S(1)} %collective-permute-done.24.refs_1_), channel_id=1, source_target_pairs={{0,1},{1,0},{2,3},{3,2},{4,5},{5,4},{6,7},{7,6},{8,9},{9,8},{10,11... | collective-permute-start | bytes 921608 | tf_op jit(solution)/shard_map/ppermute | solution.py:59
  135.0 7.5 %collective-permute-start.28 = (bf16[2,600,128]{2,1,0:T(8,128)(2,1)S(1)}, bf16[2,600,128]{2,1,0:T(8,128)(2,1)S(1)}, u32[]{:S(2)}, u32[]{:S(2)}) collective-permute-start(bf16[2,600,128]{2,1,0:T(8,128)(2,1)S(1)} %collective-permute-done.19.refs_4_), channel_id=1, source_target_pairs={{0,1},{1,0},{2,3},{3,2},{4,5},{5,4},{6,7},{7,6},{8,9},{9,8},{10,11... | collective-permute-start | bytes 921608 | tf_op jit(solution)/shard_map/ppermute | solution.py:59
  135.0 9.7 %collective-permute-start.20 = (bf16[2,600,128]{2,1,0:T(8,128)(2,1)S(1)}, bf16[2,600,128]{2,1,0:T(8,128)(2,1)S(1)}, u32[]{:S(2)}, u32[]{:S(2)}) collective-permute-start(bf16[2,600,128]{2,1,0:T(8,128)(2,1)S(1)} %collective-permute-done.19.refs_4_), channel_id=1, source_target_pairs={{0,4},{4,0},{1,5},{5,1},{2,6},{6,2},{3,7},{7,3},{8,12},{12,8},{9,1... | collective-permute-start | bytes 921608 | tf_op jit(solution)/shard_map/ppermute | solution.py:59
  140.5 7.7 %collective-permute-start.21 = (bf16[2,600,128]{2,1,0:T(8,128)(2,1)S(1)}, bf16[2,600,128]{2,1,0:T(8,128)(2,1)S(1)}, u32[]{:S(2)}, u32[]{:S(2)}) collective-permute-start(bf16[2,600,128]{2,1,0:T(8,128)(2,1)S(1)} %collective-permute-done.16.refs_1_), channel_id=1, source_target_pairs={{0,8},{8,0},{1,9},{9,1},{2,10},{10,2},{3,11},{11,3},{4,12},{12,4},... | collective-permute-start | bytes 921608 | tf_op jit(solution)/shard_map/ppermute | solution.py:59
  141.9 6.3 %collective-permute-start.29 = (bf16[2,600,128]{2,1,0:T(8,128)(2,1)S(1)}, bf16[2,600,128]{2,1,0:T(8,128)(2,1)S(1)}, u32[]{:S(2)}, u32[]{:S(2)}) collective-permute-start(bf16[2,600,128]{2,1,0:T(8,128)(2,1)S(1)} %collective-permute-done.27.refs_5_), channel_id=1, source_target_pairs={{0,1},{1,0},{2,3},{3,2},{4,5},{5,4},{6,7},{7,6},{8,9},{9,8},{10,11... | collective-permute-start | bytes 921608 | tf_op jit(solution)/shard_map/ppermute | solution.py:59
  141.9 9.2 %collective-permute-start.17 = (bf16[2,600,128]{2,1,0:T(8,128)(2,1)S(1)}, bf16[2,600,128]{2,1,0:T(8,128)(2,1)S(1)}, u32[]{:S(2)}, u32[]{:S(2)}) collective-permute-start(bf16[2,600,128]{2,1,0:T(8,128)(2,1)S(1)} %collective-permute-done.15.refs_0_), channel_id=1, source_target_pairs={{0,1},{1,0},{2,3},{3,2},{4,5},{5,4},{6,7},{7,6},{8,9},{9,8},{10,11... | collective-permute-start | bytes 921608 | tf_op jit(solution)/shard_map/ppermute | solution.py:59
  142.4 8.7 %collective-permute-start.18 = (bf16[2,600,128]{2,1,0:T(8,128)(2,1)S(1)}, bf16[2,600,128]{2,1,0:T(8,128)(2,1)S(1)}, u32[]{:S(2)}, u32[]{:S(2)}) collective-permute-start(bf16[2,600,128]{2,1,0:T(8,128)(2,1)S(1)} %collective-permute-done.16.refs_1_), channel_id=1, source_target_pairs={{0,1},{1,0},{2,3},{3,2},{4,5},{5,4},{6,7},{7,6},{8,9},{9,8},{10,11... | collective-permute-start | bytes 921608 | tf_op jit(solution)/shard_map/ppermute | solution.py:59
  144.6 6.5 %collective-permute-start.22 = (bf16[2,600,128]{2,1,0:T(8,128)(2,1)S(1)}, bf16[2,600,128]{2,1,0:T(8,128)(2,1)S(1)}, u32[]{:S(2)}, u32[]{:S(2)}) collective-permute-start(bf16[2,600,128]{2,1,0:T(8,128)(2,1)S(1)} %collective-permute-done.20.refs_4_), channel_id=1, source_target_pairs={{0,1},{1,0},{2,3},{3,2},{4,5},{5,4},{6,7},{7,6},{8,9},{9,8},{10,11... | collective-permute-start | bytes 921608 | tf_op jit(solution)/shard_map/ppermute | solution.py:59
  148.2 2.9 %collective-permute-start.23 = (bf16[2,600,128]{2,1,0:T(8,128)(2,1)S(1)}, bf16[2,600,128]{2,1,0:T(8,128)(2,1)S(1)}, u32[]{:S(2)}, u32[]{:S(2)}) collective-permute-start(bf16[2,600,128]{2,1,0:T(8,128)(2,1)S(1)} %collective-permute-done.21.refs_5_), channel_id=1, source_target_pairs={{0,1},{1,0},{2,3},{3,2},{4,5},{5,4},{6,7},{7,6},{8,9},{9,8},{10,11... | collective-permute-start | bytes 921608 | tf_op jit(solution)/shard_map/ppermute | solution.py:59
